TPU v7x, 256 devices: a whole 4x4x8 slice. The times are simulated.
256 devices in a mesh: ctx: 8 (over y, x_hi), exp: 32 (over x_lo, z, core).
Axes of the slice: x: 4 (x_hi: 2, x_lo: 2; x = x_hi * 2 + x_lo), y: 4, z: 8, core: 2. Of those that a mesh axis runs over, the one named last changes fastest.
Arguments:
- states: bfloat16 [32, 128, 2560], P('exp'), may hold values from -13 to 13
- out_grad: bfloat16 [32, 128, 2560], P('exp'), may hold values from -6 to 6
- doc_keys: bfloat16 [32, 1024, 2560], P('exp', 'ctx'), may hold values from -60 to 60
- doc_values: bfloat16 [32, 1024, 2560], P('exp', 'ctx'), may hold values from -18 to 18
- norm_gain: float32 [2560], replicated, may hold values from 0.5 to 1.5
- expert_ids: int32 [32, 128, 2], P('exp'), may hold values from 0 to 31, all different within a row; in each aligned block of 128 rows (0 to 127, 128 to 255, ..., all dimensions but the last counted through in order) at most 16 rows name the same one
- gate_values: float32 [32, 128, 2], P('exp'), may hold values from 0.5 to 2.5
- expert_weights: bfloat16 [32, 2048, 2, 2560], P('exp', 'ctx'), may hold values from -0.125 to 0.125
Outputs:
- states_grad: bfloat16 [32, 128, 2560], P('exp')
- keys_grad: bfloat16 [32, 1024, 2560], P('exp', 'ctx')
- values_grad: bfloat16 [32, 1024, 2560], P('exp', 'ctx')
- weights_grad: bfloat16 [32, 2048, 2, 2560], P('exp', 'ctx')
Inputs may be any that keep to these rules, and one draw needn't show every extreme that they name: `expert_ids`: within one sequence's 128 tokens, every expert is named by at most 16 tokens.
All inputs are finite; a program needn't handle non-finite values.
Results may differ from a plain program's by a relative error of at most 0.04.
Values may be sent and summed in bfloat16 or wider, within the bound.
No kernel may reach another device: no remote copies, remote signals or barrier semaphores. Data moves between devices by JAX's collectives and lax.ppermute only.
A program may use at most 128 MiB of HBM per device.

v0:
```python
import jax
import jax.numpy as jnp
from jax import lax
from jax.sharding import Mesh
from jax.sharding import PartitionSpec as P

HEADS = 20
HEAD = 128
TOP = 2
CTX = ("ctx_0", "ctx_1")


EPSILON = 1e-05


def all_in_one(array, axis):
    leaves = jax.tree.leaves(array)
    order = sorted(range(len(leaves)), key=lambda k: -leaves[k].size)
    width = (1, *leaves[order[0]].shape)[-1]
    lines = [
        jnp.pad(leaves[k].reshape(-1), (0, -leaves[k].size % width)).reshape(-1, width)
        for k in order
    ]
    both, at, found = (lax.all_gather(jnp.concatenate(lines), axis), 0, {})
    for k, line in zip(order, lines):
        share = both[:, at : at + len(line)].reshape(len(both), -1)
        found[k] = share[:, : leaves[k].size].reshape(-1, *leaves[k].shape)
        at += len(line)
    numbers = iter(range(len(leaves)))
    return jax.tree.map(lambda _: found[next(numbers)], array)


def joined_all(array, axes, combine):
    for axis in axes:
        pieces = all_in_one(array, axis)
        array = jax.tree.map(lambda part: part[0], pieces)
        for k in range(1, lax.axis_size(axis)):
            array = combine(array, jax.tree.map(lambda part: part[k], pieces))
    return array


def sent_together(arrays, axis, split_dim, concat_dim, along):
    both = jnp.concatenate(arrays, axis=along)
    filled, at, outs = (
        lax.all_to_all(both, axis, split_axis=split_dim, concat_axis=concat_dim, tiled=True),
        0,
        [],
    )
    for a in arrays:
        outs.append(lax.slice_in_dim(filled, at, at + a.shape[along], axis=along))
        at += a.shape[along]
    return tuple(outs)


def side_by_side(arrays, axis, dim, along):
    ends, at = ([], 0)
    for a in arrays[:-1]:
        at += a.shape[along]
        ends.append(at)
    both = jnp.concatenate(arrays, axis=along)
    return tuple(jnp.split(lax.all_gather(both, axis, axis=dim, tiled=True), ends, axis=along))


def total_of_pieces(array, axis):
    return lax.all_gather(array, axis).astype(jnp.float32).sum(0)


def combine_scores(one_side, other_side):
    top_score = jnp.maximum(one_side[0], other_side[0])
    factor_one = jnp.exp(one_side[0] - top_score)
    factor_two = jnp.exp(other_side[0] - top_score)
    summed = one_side[1] * factor_one + other_side[1] * factor_two
    weighted = one_side[2] * factor_one + other_side[2] * factor_two
    return (top_score, summed, weighted)


def on_device(
    states, out_grad, doc_keys, doc_values, norm_gain, expert_ids, gate_values, expert_weights
):
    tokens = states.shape[1]
    model_width = states.shape[2]
    key_count = doc_keys.shape[1]
    scale = HEAD ** (-0.5)
    inputs = states[0].astype(jnp.float32)
    inverse = lax.rsqrt(jnp.mean(inputs * inputs, axis=-1, keepdims=True) + EPSILON)
    unit = inputs * inverse
    normed = (unit * norm_gain).astype(jnp.bfloat16)
    upstream = out_grad[0]
    queries = normed.reshape(tokens, HEADS, HEAD)
    key_heads = doc_keys[0].reshape(key_count, HEADS, HEAD)
    value_heads = doc_values[0].reshape(key_count, HEADS, HEAD)
    grad_heads = upstream.reshape(tokens, HEADS, HEAD)
    scores = (
        jnp.einsum("qhd,khd->hqk", queries, key_heads, preferred_element_type=jnp.float32) * scale
    )
    local_peak = jnp.max(scores, axis=-1)
    local_weights = jnp.exp(scores - local_peak[..., None])
    local_total = jnp.sum(local_weights, axis=-1)
    slopes = jnp.einsum("qhd,khd->hqk", grad_heads, value_heads, preferred_element_type=jnp.float32)
    local_inner = jnp.sum(local_weights * slopes, axis=-1)
    peak, total, merged = joined_all((local_peak, local_total, local_inner), CTX, combine_scores)
    delta = merged / total
    probs = jnp.exp(scores - peak[..., None]) / total[..., None]
    score_grad = (probs * (slopes - delta[..., None])).astype(jnp.bfloat16)
    probs_low = probs.astype(jnp.bfloat16)
    values_grad = jnp.einsum(
        "hqk,qhd->khd", probs_low, grad_heads, preferred_element_type=jnp.float32
    )
    keys_grad = (
        jnp.einsum("hqk,qhd->khd", score_grad, queries, preferred_element_type=jnp.float32) * scale
    )
    query_grad = (
        jnp.einsum(
            "hqk,khd->qhd", score_grad, key_heads, preferred_element_type=jnp.float32
        ).reshape(tokens, model_width)
        * scale
    )
    ctx_count = lax.axis_size(CTX)
    expert_count = lax.axis_size("exp")
    capacity = ctx_count * (
        (5 * TOP * tokens + 4 * expert_count * ctx_count - 1) // (4 * expert_count * ctx_count)
    )
    assigned = tokens * TOP
    flat_ids = expert_ids[0].reshape(assigned)
    onehot = (flat_ids[:, None] == jnp.arange(expert_count, dtype=jnp.int32)[None, :]).astype(
        jnp.int32
    )
    earlier = jnp.cumsum(onehot, axis=0) - onehot
    slot = jnp.sum(earlier * onehot, axis=1)
    placed = flat_ids * capacity + slot
    table = (
        jnp.full((expert_count * capacity,), assigned, jnp.int32)
        .at[placed]
        .set(jnp.arange(assigned, dtype=jnp.int32))
    )
    filled = table < assigned
    safe_index = jnp.minimum(table, assigned - 1)
    source = safe_index // TOP
    slot_gate = jnp.where(filled, gate_values[0].reshape(assigned)[safe_index], 0.0)
    send_rows = jnp.where(filled[:, None], normed[source], jnp.zeros((), jnp.bfloat16))
    send_rows = send_rows.reshape(expert_count, capacity, model_width)
    send_grads = (slot_gate[:, None] * upstream[source].astype(jnp.float32)).astype(jnp.bfloat16)
    send_grads = send_grads.reshape(expert_count, capacity, model_width)
    share = capacity // ctx_count
    offset = lax.axis_index(CTX) * share
    piece_rows = lax.dynamic_slice_in_dim(send_rows, offset, share, 1)
    piece_grads = lax.dynamic_slice_in_dim(send_grads, offset, share, 1)
    sent_rows, sent_grads = sent_together((piece_rows, piece_grads), "exp", 0, 0, 1)
    got_rows, got_grads = side_by_side((sent_rows, sent_grads), CTX, 1, 0)
    slot_rows = got_rows.shape[0] * got_rows.shape[1]
    rows = got_rows.reshape(slot_rows, model_width)
    douts = got_grads.reshape(slot_rows, model_width)
    w_in = expert_weights[0, :, 0, :]
    w_out = expert_weights[0, :, 1, :]
    pre = jnp.einsum("sd,hd->sh", rows, w_in, preferred_element_type=jnp.float32)
    activ, pull = jax.vjp(jax.nn.gelu, pre)
    activ_low = activ.astype(jnp.bfloat16)
    act_grad = jnp.einsum("sd,hd->sh", douts, w_out, preferred_element_type=jnp.float32)
    pre_grad = pull(act_grad)[0].astype(jnp.bfloat16)
    grad_in = jnp.einsum("sh,sd->hd", pre_grad, rows, preferred_element_type=jnp.float32)
    grad_proj = jnp.einsum("sh,sd->hd", activ_low, douts, preferred_element_type=jnp.float32)
    weights_grad = jnp.stack([grad_in, grad_proj], axis=1).astype(jnp.bfloat16)[None]
    partial_rows = jnp.einsum("sh,hd->sd", pre_grad, w_in, preferred_element_type=jnp.float32)
    partial_rows = partial_rows.astype(jnp.bfloat16).reshape(got_rows.shape)
    returned = lax.all_to_all(partial_rows, "exp", split_axis=0, concat_axis=0, tiled=True)
    picked_rows = returned.reshape(expert_count * capacity, model_width)[placed]
    moe_part = jnp.sum(picked_rows.astype(jnp.float32).reshape(tokens, TOP, model_width), axis=1)
    total_grad = total_of_pieces((query_grad + moe_part).astype(jnp.bfloat16), CTX).astype(
        jnp.float32
    )
    scaled = total_grad * norm_gain
    states_grad = upstream.astype(jnp.float32) + inverse * (
        scaled - unit * jnp.mean(scaled * unit, axis=-1, keepdims=True)
    )
    return (
        states_grad.astype(jnp.bfloat16)[None],
        keys_grad.reshape(key_count, model_width).astype(jnp.bfloat16)[None],
        values_grad.reshape(key_count, model_width).astype(jnp.bfloat16)[None],
        weights_grad,
    )


def solution(mesh):
    finer = Mesh(mesh.devices.reshape(4, 2, mesh.shape["exp"]), ("ctx_0", "ctx_1", "exp"))
    return jax.shard_map(
        on_device,
        mesh=finer,
        in_specs=(
            P("exp", None, None),
            P("exp", None, None),
            P("exp", CTX, None),
            P("exp", CTX, None),
            P(),
            P("exp", None, None),
            P("exp", None, None),
            P("exp", CTX, None, None),
        ),
        out_specs=(
            P("exp", None, None),
            P("exp", CTX, None),
            P("exp", CTX, None),
            P("exp", CTX, None, None),
        ),
        check_vma=False,
    )
```

profile of v0, /device:TPU:32, one launch (start us, length us, event | category | flops | bytes accessed | tf_op | source)
XLA Modules:
  0.0 330.0 jit_solution(12507527570165740859)
XLA Ops:
  7.2 0.8 copy.122
  10.8 1.4 scatter_custom_fusion
  12.2 0.8 copy.125
  13.2 3.5 %gather_fusion.1 = f32[512]{0:T(512)S(1)} fusion(f32[256]{0:T(256)S(1)} %reshape_squeeze.16, s32[1024]{0:T(1024)S(1)} %get-tuple-element.44), kind=kCustom, calls=%fused_computation.1 | custom fusion | bytes 6144 | tf_op jit(solution)/shard_map/gather | solution.py:139
  17.5 3.5 %gather_fusion = bf16[512,2560]{1,0:T(8,128)(2,1)} fusion(bf16[128,2560]{1,0:T(8,128)(2,1)S(1)} %multiply_convert_fusion, s32[1024]{0:T(1024)S(1)} %get-tuple-element.45), kind=kCustom, calls=%fused_computation | custom fusion | bytes 5244928 | tf_op jit(solution)/shard_map/gather | solution.py:140
  21.0 2.6 gather_fusion.2
  23.6 1.8 broadcast_select_fusion
  26.6 30.0 %all_to_all.10 = bf16[32,4,2560]{2,1,0:T(4,128)(2,1)S(1)} all-to-all(bf16[32,4,2560]{2,1,0:T(4,128)(2,1)S(1)} %pad_maximum_fusion.1), channel_id=1, replica_groups=mesh['ctx_0'=4,'ctx_1'=2,'exp'=32] {'exp'}, dimensions={0} | all-to-all | bytes 1310720 | tf_op jit(solution)/shard_map/all_to_all | solution.py:45
  57.1 0.8 pad_maximum_fusion.2
  58.0 0.9 copy.126
  58.9 5.1 %fusion.71 = (bf16[1,256,1,2560]{3,2,1,0:T(2,128)(2,1)}, bf16[1,256,1,2560]{3,2,1,0:T(2,128)(2,1)}) fusion(bf16[1,256,2,2560]{3,2,1,0:T(2,128)(2,1)S(1)} %copy-done.6), kind=kLoop, calls=%fused_computation.153 | loop fusion | bytes 5242880 | tf_op jit(solution)/shard_map/slice | solution.py:154
  64.0 77.3 %all-gather.7.cloned.1.call-done = bf16[64,16,2560]{2,0,1:T(8,128)(2,1)} async-done(((bf16[64,2,2560]{2,0,1:T(8,128)(2,1)}), bf16[64,16,2560]{2,0,1:T(8,128)(2,1)}) %all-gather.7.cloned.1.call-update) | async-done | bytes 5242896 | tf_op jit(solution)/shard_map/all_gather | solution.py:61
  141.3 2.9 fusion.70
  144.2 1.4 copy.153
  145.6 1.4 copy.151
  147.2 1.8 copy-done.11
  148.9 0.9 fusion.21
  149.8 0.8 copy-done.15
  150.7 1.1 fusion.20
  151.8 2.3 convolution_convert_fusion
  154.1 7.6 %all-to-all-start.1 = ((bf16[32,16,2560]{2,1,0:T(8,128)(2,1)}), bf16[32,16,2560]{2,1,0:T(8,128)(2,1)S(1)}, u32[]{:S(2)}, u32[]{:S(2)}) async-start(bf16[32,16,2560]{2,1,0:T(8,128)(2,1)} %bitcast.282), calls=%async_computation.1 | async-start | bytes 5242880 | tf_op jit(solution)/shard_map/all_to_all | solution.py:165
  161.8 2.4 copy.112
  164.2 1.1 copy.116
  165.3 2.2 copy.113
  167.4 2.2 copy.117
  169.6 2.4 fusion.73
  172.5 12.0 %all-gather.2 = f32[4,60,128]{2,1,0:T(8,128)S(1)} all-gather(f32[1,60,128]{2,1,0:T(8,128)S(1)} %maximum_bitcast_fusion), channel_id=2, replica_groups=mesh['ctx_0'=4,'ctx_1'=2,'exp'=32] {'ctx_0'}, dimensions={0}, use_global_device_ids=true | all-gather | bytes 153600 | tf_op jit(solution)/shard_map/all_gather | solution.py:24
  184.6 7.3 %all-gather.3 = f32[2,60,128]{2,1,0:T(8,128)S(1)} all-gather(f32[1,60,128]{2,1,0:T(8,128)S(1)} %maximum_bitcast_fusion.1), channel_id=3, replica_groups=mesh['ctx_0'=4,'ctx_1'=2,'exp'=32] {'ctx_1'}, dimensions={0}, use_global_device_ids=true | all-gather | bytes 92160 | tf_op jit(solution)/shard_map/all_gather | solution.py:24
  193.1 1.4 convolution_multiply_fusion
  194.5 2.8 copy.131
  197.3 1.3 pad_clamp_fusion
  198.5 24.9 %all-to-all-done.1 = bf16[32,16,2560]{2,1,0:T(8,128)(2,1)S(1)} async-done(((bf16[32,16,2560]{2,1,0:T(8,128)(2,1)}), bf16[32,16,2560]{2,1,0:T(8,128)(2,1)S(1)}, u32[]{:S(2)}, u32[]{:S(2)}) %all-to-all-start.1) | async-done | bytes 2621472 | tf_op jit(solution)/shard_map/all_to_all | solution.py:165
  223.4 2.6 gather_fusion.3
  226.1 3.3 reshape.329
  229.4 4.5 %reduce_sum.74 = f32[128,2560]{1,0:T(8,128)} reduce(f32[128,2,2560]{2,1,0:T(2,128)S(1)} %reshape.329, f32[]{:T(128)} %constant.25.clone.1), dimensions={1}, to_apply=%region_8.9 | reduce | flops 327680 | bytes 3932164 | tf_op jit(solution)/shard_map/reduce_sum | solution.py:167
  233.9 2.8 fusion.8
  236.8 2.2 convolution_convert_fusion.3
  239.0 2.3 copy.140
  241.3 1.5 fusion.10
  242.7 2.3 copy.137
  245.1 2.2 copy.139
  247.3 0.9 fusion
  248.2 0.9 copy-done.10
  249.1 0.9 fusion.1
  250.3 4.2 %copy.141 = bf16[1,256,2,2560]{3,2,1,0:T(2,128)(2,1)} copy(bf16[1,256,2,2560]{3,1,2,0:T(8,128)(2,1)S(1)} %pad_maximum_fusion) | data formatting | bytes 5242880
  254.5 63.6 %all-gather.9.cloned.1.call-done = bf16[8,128,2560]{2,1,0:T(8,128)(2,1)} async-done(((bf16[1,128,2560]{2,1,0:T(8,128)(2,1)}), bf16[8,128,2560]{2,1,0:T(8,128)(2,1)}) %all-gather.9.cloned.1.call-update) | async-done | bytes 5242896 | tf_op jit(solution)/shard_map/all_gather | solution.py:65
  318.1 3.3 %convert_reduce_fusion = f32[128,2560]{1,0:T(8,128)S(1)} fusion(bf16[8,128,2560]{2,1,0:T(8,128)(2,1)} %all-gather.9.cloned.1.call-done), kind=kLoop, calls=%fused_computation.5 | loop fusion | flops 4915200 | bytes 6553600 | tf_op jit(solution)/shard_map/reduce_sum | solution.py:65
  321.8 1.3 fusion.7
  (88 shorter events, 8.0 us)
Async XLA Ops:
  7.2 134.1 %all-gather.7.cloned.1.call-start = ((), (), s32[]{:S(2)}) async-start(), calls=%async_computation.2 | async-start | bytes 5898240 | tf_op jit(solution)/shard_map/all_gather | solution.py:61
  8.3 8.5 %copy-start.1 = (bf16[1,128,2560]{2,1,0:T(8,128)(2,1)S(1)}, bf16[1,128,2560]{2,1,0:T(8,128)(2,1)}, u32[]{:S(2)}) copy-start(bf16[1,128,2560]{2,1,0:T(8,128)(2,1)} %param.8) | copy-start | bytes 1966084
  10.2 0.6 copy-start.24
  13.2 4.1 %copy-start.21 = (f32[2560]{0:T(1024)S(1)}, f32[2560]{0:T(1024)}, u32[]{:S(2)}) copy-start(f32[2560]{0:T(1024)} %param.12) | copy-start | bytes 30724
  17.5 3.5 %copy-start = (bf16[1,128,2560]{2,1,0:T(8,128)(2,1)S(1)}, bf16[1,128,2560]{2,1,0:T(8,128)(2,1)}, u32[]{:S(2)}) copy-start(bf16[1,128,2560]{2,1,0:T(8,128)(2,1)} %param.9) | copy-start | bytes 1966084
  57.1 1.8 copy-start.6
  145.6 1.6 copy-start.7
  145.6 3.3 %copy-start.11 = (bf16[1,256,1,2560]{3,2,1,0:T(2,128)(2,1)S(1)}, bf16[1,256,1,2560]{3,2,1,0:T(2,128)(2,1)}, u32[]{:S(2)}) copy-start(bf16[1,256,1,2560]{3,2,1,0:T(2,128)(2,1)} %get-tuple-element.36) | copy-start | bytes 3932164
  147.1 2.8 copy-start.9
  148.9 1.7 copy-start.15
  149.8 1.9 copy-start.19
  154.1 69.3 %all-to-all-start.1 = ((bf16[32,16,2560]{2,1,0:T(8,128)(2,1)}), bf16[32,16,2560]{2,1,0:T(8,128)(2,1)S(1)}, u32[]{:S(2)}, u32[]{:S(2)}) async-start(bf16[32,16,2560]{2,1,0:T(8,128)(2,1)} %bitcast.282), calls=%async_computation.1 | async-start | bytes 5242880 | tf_op jit(solution)/shard_map/all_to_all | solution.py:165
  161.8 156.3 %all-gather.9.cloned.1.call-start = ((), (), s32[]{:S(2)}) async-start(), calls=%async_computation.3 | async-start | bytes 5898240 | tf_op jit(solution)/shard_map/all_gather | solution.py:65
  169.6 2.4 copy-start.16
  169.6 2.4 copy-start.18
  172.0 20.0 %copy-start.3 = (f32[20,128,128]{1,2,0:T(8,128)}, f32[20,128,128]{1,2,0:T(8,128)S(1)}, u32[]{:S(2)}) copy-start(f32[20,128,128]{1,2,0:T(8,128)S(1)} %get-tuple-element.42) | copy-start | bytes 3932164
  191.9 0.6 copy-start.22
  192.0 0.6 copy-start.23
  192.0 1.1 copy-start.14
  193.1 1.4 copy-start.12
  233.9 2.8 copy-start.4
  233.9 2.9 copy-start.17
  236.8 4.5 %copy-start.13 = (bf16[20,128,128]{1,2,0:T(8,128)(2,1)S(1)}, bf16[20,128,128]{1,2,0:T(8,128)(2,1)}, u32[]{:S(2)}) copy-start(bf16[20,128,128]{1,2,0:T(8,128)(2,1)} %copy-done.12) | copy-start | bytes 1966084
  239.0 2.3 copy-start.5
  242.7 4.6 %copy-start.8 = (bf16[32,16,2560]{2,1,0:T(8,128)(2,1)S(1)}, bf16[32,16,2560]{2,1,0:T(8,128)(2,1)}, u32[]{:S(2)}) copy-start(bf16[32,16,2560]{2,1,0:T(8,128)(2,1)} %copy-done.7) | copy-start | bytes 7864324
  247.3 1.7 copy-start.10
  247.3 1.8 copy-start.20
  254.5 66.9 %copy-start.2 = (bf16[1,128,2560]{2,1,0:T(8,128)(2,1)S(1)}, bf16[1,128,2560]{2,1,0:T(8,128)(2,1)}, u32[]{:S(2)}) copy-start(bf16[1,128,2560]{2,1,0:T(8,128)(2,1)} %param.8) | copy-start | bytes 1966084
Sparse Core Ops, SparseCore 0:
  59.0 82.2 all-gather.6
  236.9 81.1 all-gather.8
where the time goes:
time: 332 us; the launch traced here: 330 us
  waiting for transfers between devices  166 us (50%)
  local copies, waits for them, and re-layouts  58.5 us (18%)
  blocking collectives  49.3 us (15%)
  other arithmetic  20.1 us (6%)
  between operations  14.5 us (4%)
  matrix products  14 us (4%)
  starting transfers between devices  7.72 us (2%)
    all_gather x1, waiting for transfers between devices, side_by_side(): lax.all_gather(both, axis, axis=dim, tiled=True)  77.3 us
    all_gather x1, waiting for transfers between devices, total_of_pieces(): return lax.all_gather(array, axis).astype(jnp.float32).sum(0)  63.6 us
    all_to_all x1, blocking collectives, sent_together(): lax.all_to_all(both, axis, split_axis=split_dim, concat_axis=concat_dim,...  30 us
    all_to_all x1, waiting for transfers between devices, on_device(): lax.all_to_all(partial_rows, 'exp', split_axis=0, concat_axis=0, tiled=True)  24.9 us
    unnamed x60, local copies, waits for them, and re-layouts  23.6 us
    all_gather x2, blocking collectives, all_in_one(): both, at, found = (lax.all_gather(jnp.concatenate(lines), axis), 0, {})  19.3 us
    all_to_all x1, starting transfers between devices, on_device(): lax.all_to_all(partial_rows, 'exp', split_axis=0, concat_axis=0, tiled=True)  7.64 us
  transfers between devices with their start and end apart: 3, of which 3 were waited for; matrix products, arithmetic and copies ran while one was open for 12% of the time, Pallas kernels for 0%

commit v1 on v0

--- a/solution.py
+++ b/solution.py
@@ -122,11 +122,9 @@
     )
     assigned = tokens * TOP
     flat_ids = expert_ids[0].reshape(assigned)
-    onehot = (flat_ids[:, None] == jnp.arange(expert_count, dtype=jnp.int32)[None, :]).astype(
-        jnp.int32
-    )
-    earlier = jnp.cumsum(onehot, axis=0) - onehot
-    slot = jnp.sum(earlier * onehot, axis=1)
+    order = jnp.arange(assigned, dtype=jnp.int32)
+    same = (flat_ids[:, None] == flat_ids[None, :]) & (order[None, :] < order[:, None])
+    slot = jnp.sum(same.astype(jnp.int32), axis=1)
     placed = flat_ids * capacity + slot
     table = (
         jnp.full((expert_count * capacity,), assigned, jnp.int32)

time: 332 us -> 330 us (level)
  no operation moved by 1% of the time
where the time goes in v1:
time: 330 us; the launch traced here: 329 us
  waiting for transfers between devices  166 us (50%)
  local copies, waits for them, and re-layouts  57.7 us (17%)
  blocking collectives  49.4 us (15%)
  other arithmetic  19.5 us (6%)
  between operations  14.5 us (4%)
  matrix products  14 us (4%)
  starting transfers between devices  7.72 us (2%)
    all_gather x1, waiting for transfers between devices, side_by_side(): lax.all_gather(both, axis, axis=dim, tiled=True)  77.3 us
    all_gather x1, waiting for transfers between devices, total_of_pieces(): return lax.all_gather(array, axis).astype(jnp.float32).sum(0)  63.6 us
    all_to_all x1, blocking collectives, sent_together(): lax.all_to_all(both, axis, split_axis=split_dim, concat_axis=concat_dim,...  30 us
    all_to_all x1, waiting for transfers between devices, on_device(): lax.all_to_all(partial_rows, 'exp', split_axis=0, concat_axis=0, tiled=True)  24.9 us
    unnamed x60, local copies, waits for them, and re-layouts  23 us
    all_gather x2, blocking collectives, all_in_one(): both, at, found = (lax.all_gather(jnp.concatenate(lines), axis), 0, {})  19.3 us
    all_to_all x1, starting transfers between devices, on_device(): lax.all_to_all(partial_rows, 'exp', split_axis=0, concat_axis=0, tiled=True)  7.64 us
  transfers between devices with their start and end apart: 3, of which 3 were waited for; matrix products, arithmetic and copies ran while one was open for 12% of the time, Pallas kernels for 0%

profile of v1, /device:TPU:32, one launch (start us, length us, event | category | flops | bytes accessed | tf_op | source)
XLA Modules:
  0.0 328.5 jit_solution(3053327792871167622)
XLA Ops:
  7.2 0.8 copy.144
  9.4 1.4 scatter_custom_fusion
  10.8 0.8 copy.145
  11.8 3.5 %gather_fusion.1 = f32[512]{0:T(512)S(1)} fusion(f32[256]{0:T(256)S(1)} %reshape_squeeze.16, s32[1024]{0:T(1024)S(1)} %get-tuple-element.48), kind=kCustom, calls=%fused_computation.1 | custom fusion | bytes 6144 | tf_op jit(solution)/shard_map/gather | solution.py:137
  16.1 3.5 %gather_fusion = bf16[512,2560]{1,0:T(8,128)(2,1)} fusion(bf16[128,2560]{1,0:T(8,128)(2,1)S(1)} %multiply_convert_fusion, s32[1024]{0:T(1024)S(1)} %get-tuple-element.49), kind=kCustom, calls=%fused_computation | custom fusion | bytes 5244928 | tf_op jit(solution)/shard_map/gather | solution.py:138
  19.6 2.6 gather_fusion.2
  22.2 1.8 broadcast_select_fusion
  25.2 30.0 %all_to_all.10 = bf16[32,4,2560]{2,1,0:T(4,128)(2,1)S(1)} all-to-all(bf16[32,4,2560]{2,1,0:T(4,128)(2,1)S(1)} %pad_maximum_fusion.1), channel_id=1, replica_groups=mesh['ctx_0'=4,'ctx_1'=2,'exp'=32] {'exp'}, dimensions={0} | all-to-all | bytes 1310720 | tf_op jit(solution)/shard_map/all_to_all | solution.py:45
  55.7 0.8 pad_maximum_fusion.2
  56.5 0.9 copy.146
  57.5 5.1 %fusion.68 = (bf16[1,256,1,2560]{3,2,1,0:T(2,128)(2,1)}, bf16[1,256,1,2560]{3,2,1,0:T(2,128)(2,1)}) fusion(bf16[1,256,2,2560]{3,2,1,0:T(2,128)(2,1)S(1)} %copy-done.6), kind=kLoop, calls=%fused_computation.147 | loop fusion | bytes 5242880 | tf_op jit(solution)/shard_map/slice | solution.py:152
  62.5 77.3 %all-gather.7.cloned.1.call-done = bf16[64,16,2560]{2,0,1:T(8,128)(2,1)} async-done(((bf16[64,2,2560]{2,0,1:T(8,128)(2,1)}), bf16[64,16,2560]{2,0,1:T(8,128)(2,1)}) %all-gather.7.cloned.1.call-update) | async-done | bytes 5242896 | tf_op jit(solution)/shard_map/all_gather | solution.py:61
  139.8 2.9 fusion.67
  142.7 1.4 copy.173
  144.2 1.4 copy.171
  145.7 1.8 copy-done.11
  147.5 0.9 fusion.21
  148.4 0.8 copy-done.15
  149.2 1.1 fusion.20
  150.3 2.3 convolution_convert_fusion
  152.7 7.6 %all-to-all-start.1 = ((bf16[32,16,2560]{2,1,0:T(8,128)(2,1)}), bf16[32,16,2560]{2,1,0:T(8,128)(2,1)S(1)}, u32[]{:S(2)}, u32[]{:S(2)}) async-start(bf16[32,16,2560]{2,1,0:T(8,128)(2,1)} %bitcast.263), calls=%async_computation.1 | async-start | bytes 5242880 | tf_op jit(solution)/shard_map/all_to_all | solution.py:163
  160.4 2.4 copy.134
  162.8 1.1 copy.138
  163.8 2.2 copy.135
  166.0 2.2 copy.139
  168.2 2.4 fusion.70
  171.1 12.0 %all-gather.2 = f32[4,60,128]{2,1,0:T(8,128)S(1)} all-gather(f32[1,60,128]{2,1,0:T(8,128)S(1)} %maximum_bitcast_fusion), channel_id=2, replica_groups=mesh['ctx_0'=4,'ctx_1'=2,'exp'=32] {'ctx_0'}, dimensions={0}, use_global_device_ids=true | all-gather | bytes 153600 | tf_op jit(solution)/shard_map/all_gather | solution.py:24
  183.1 7.3 %all-gather.3 = f32[2,60,128]{2,1,0:T(8,128)S(1)} all-gather(f32[1,60,128]{2,1,0:T(8,128)S(1)} %maximum_bitcast_fusion.1), channel_id=3, replica_groups=mesh['ctx_0'=4,'ctx_1'=2,'exp'=32] {'ctx_1'}, dimensions={0}, use_global_device_ids=true | all-gather | bytes 92160 | tf_op jit(solution)/shard_map/all_gather | solution.py:24
  191.6 1.4 convolution_multiply_fusion
  193.0 2.8 copy.151
  195.8 1.3 pad_clamp_fusion
  197.1 24.9 %all-to-all-done.1 = bf16[32,16,2560]{2,1,0:T(8,128)(2,1)S(1)} async-done(((bf16[32,16,2560]{2,1,0:T(8,128)(2,1)}), bf16[32,16,2560]{2,1,0:T(8,128)(2,1)S(1)}, u32[]{:S(2)}, u32[]{:S(2)}) %all-to-all-start.1) | async-done | bytes 2621472 | tf_op jit(solution)/shard_map/all_to_all | solution.py:163
  222.0 2.6 gather_fusion.3
  224.6 3.3 %reshape.313 = f32[128,2,2560]{2,1,0:T(2,128)S(1)} reshape(bf16[256,2560]{1,0:T(8,128)(2,1)} %gather_fusion.3) | data formatting | bytes 3932160 | tf_op jit(solution)/shard_map/convert_element_type | solution.py:165
  227.9 4.5 %reduce_sum.74 = f32[128,2560]{1,0:T(8,128)} reduce(f32[128,2,2560]{2,1,0:T(2,128)S(1)} %reshape.313, f32[]{:T(128)} %constant.25.clone.1), dimensions={1}, to_apply=%region_6.7 | reduce | flops 327680 | bytes 3932164 | tf_op jit(solution)/shard_map/reduce_sum | solution.py:165
  232.5 2.8 fusion.8
  235.3 2.2 convolution_convert_fusion.3
  237.5 2.3 copy.160
  239.8 1.5 fusion.10
  241.3 2.3 copy.157
  243.6 2.2 copy.159
  245.9 0.9 fusion
  246.7 0.9 copy-done.10
  247.7 0.9 fusion.1
  248.8 4.2 %copy.161 = bf16[1,256,2,2560]{3,2,1,0:T(2,128)(2,1)} copy(bf16[1,256,2,2560]{3,1,2,0:T(8,128)(2,1)S(1)} %pad_maximum_fusion) | data formatting | bytes 5242880
  253.0 63.6 %all-gather.9.cloned.1.call-done = bf16[8,128,2560]{2,1,0:T(8,128)(2,1)} async-done(((bf16[1,128,2560]{2,1,0:T(8,128)(2,1)}), bf16[8,128,2560]{2,1,0:T(8,128)(2,1)}) %all-gather.9.cloned.1.call-update) | async-done | bytes 5242896 | tf_op jit(solution)/shard_map/all_gather | solution.py:65
  316.6 3.3 %convert_reduce_fusion = f32[128,2560]{1,0:T(8,128)S(1)} fusion(bf16[8,128,2560]{2,1,0:T(8,128)(2,1)} %all-gather.9.cloned.1.call-done), kind=kLoop, calls=%fused_computation.5 | loop fusion | flops 4915200 | bytes 6553600 | tf_op jit(solution)/shard_map/reduce_sum | solution.py:65
  320.4 1.3 fusion.7
  (82 shorter events, 6.5 us)
Async XLA Ops:
  7.2 8.2 %copy-start.1 = (bf16[1,128,2560]{2,1,0:T(8,128)(2,1)S(1)}, bf16[1,128,2560]{2,1,0:T(8,128)(2,1)}, u32[]{:S(2)}) copy-start(bf16[1,128,2560]{2,1,0:T(8,128)(2,1)} %param.8) | copy-start | bytes 1966084
  7.2 132.7 %all-gather.7.cloned.1.call-start = ((), (), s32[]{:S(2)}) async-start(), calls=%async_computation.2 | async-start | bytes 5898240 | tf_op jit(solution)/shard_map/all_gather | solution.py:61
  9.3 1.4 copy-start.24
  11.7 4.1 %copy-start.21 = (f32[2560]{0:T(1024)S(1)}, f32[2560]{0:T(1024)}, u32[]{:S(2)}) copy-start(f32[2560]{0:T(1024)} %param.12) | copy-start | bytes 30724
  16.1 3.5 %copy-start = (bf16[1,128,2560]{2,1,0:T(8,128)(2,1)S(1)}, bf16[1,128,2560]{2,1,0:T(8,128)(2,1)}, u32[]{:S(2)}) copy-start(bf16[1,128,2560]{2,1,0:T(8,128)(2,1)} %param.9) | copy-start | bytes 1966084
  55.7 1.8 copy-start.6
  144.2 1.6 copy-start.7
  144.2 3.3 %copy-start.11 = (bf16[1,256,1,2560]{3,2,1,0:T(2,128)(2,1)S(1)}, bf16[1,256,1,2560]{3,2,1,0:T(2,128)(2,1)}, u32[]{:S(2)}) copy-start(bf16[1,256,1,2560]{3,2,1,0:T(2,128)(2,1)} %get-tuple-element.40) | copy-start | bytes 3932164
  145.6 2.8 copy-start.9
  147.5 1.7 copy-start.15
  148.4 1.9 copy-start.19
  152.7 69.3 %all-to-all-start.1 = ((bf16[32,16,2560]{2,1,0:T(8,128)(2,1)}), bf16[32,16,2560]{2,1,0:T(8,128)(2,1)S(1)}, u32[]{:S(2)}, u32[]{:S(2)}) async-start(bf16[32,16,2560]{2,1,0:T(8,128)(2,1)} %bitcast.263), calls=%async_computation.1 | async-start | bytes 5242880 | tf_op jit(solution)/shard_map/all_to_all | solution.py:163
  160.3 156.3 %all-gather.9.cloned.1.call-start = ((), (), s32[]{:S(2)}) async-start(), calls=%async_computation.3 | async-start | bytes 5898240 | tf_op jit(solution)/shard_map/all_gather | solution.py:65
  168.2 2.4 copy-start.16
  168.2 2.4 copy-start.18
  170.5 20.0 %copy-start.3 = (f32[20,128,128]{1,2,0:T(8,128)}, f32[20,128,128]{1,2,0:T(8,128)S(1)}, u32[]{:S(2)}) copy-start(f32[20,128,128]{1,2,0:T(8,128)S(1)} %get-tuple-element.46) | copy-start | bytes 3932164
  190.5 0.6 copy-start.22
  190.5 0.6 copy-start.23
  190.5 1.1 copy-start.14
  191.6 1.4 copy-start.12
  232.5 2.8 copy-start.4
  232.5 2.9 copy-start.17
  235.3 4.5 %copy-start.13 = (bf16[20,128,128]{1,2,0:T(8,128)(2,1)S(1)}, bf16[20,128,128]{1,2,0:T(8,128)(2,1)}, u32[]{:S(2)}) copy-start(bf16[20,128,128]{1,2,0:T(8,128)(2,1)} %copy-done.12) | copy-start | bytes 1966084
  237.5 2.3 copy-start.5
  241.3 4.6 %copy-start.8 = (bf16[32,16,2560]{2,1,0:T(8,128)(2,1)S(1)}, bf16[32,16,2560]{2,1,0:T(8,128)(2,1)}, u32[]{:S(2)}) copy-start(bf16[32,16,2560]{2,1,0:T(8,128)(2,1)} %copy-done.7) | copy-start | bytes 7864324
  245.8 1.7 copy-start.10
  245.9 1.8 copy-start.20
  253.0 66.9 %copy-start.2 = (bf16[1,128,2560]{2,1,0:T(8,128)(2,1)S(1)}, bf16[1,128,2560]{2,1,0:T(8,128)(2,1)}, u32[]{:S(2)}) copy-start(bf16[1,128,2560]{2,1,0:T(8,128)(2,1)} %param.8) | copy-start | bytes 1966084
Sparse Core Ops, SparseCore 0:
  57.6 82.2 all-gather.6
  235.4 81.1 all-gather.8

commit v2 on v1

v2 whole, which is shorter than its diff:
```python
import math

import jax
import jax.numpy as jnp
from jax import lax
from jax.experimental import pallas as pl
from jax.experimental.pallas import tpu as pltpu
from jax.sharding import Mesh
from jax.sharding import PartitionSpec as P

HEADS = 20
HEAD = 128
D = 2560
HALF = 1280
TOKENS = 128
KEYS = 128
UNITS = 256
EXPERTS = 32
CTX_COUNT = 8
ROWS = 256
SLOTS = 512
CHUNK = 640
CTX = ("ctx_0", "ctx_1")
EPSILON = 1e-05
SCALE = HEAD**-0.5
BF16 = jnp.bfloat16
F32 = jnp.float32
VMEM_LIMIT = 56 * 2**20

VMEM = pl.BlockSpec(memory_space=pltpu.VMEM)
SMEM = pl.BlockSpec(memory_space=pltpu.SMEM)


def call(kernel, ins, outs, scratch=(), flops=0, moved=0):
    return pl.pallas_call(
        kernel,
        in_specs=ins,
        out_specs=[VMEM] * len(outs),
        out_shape=outs,
        scratch_shapes=list(scratch),
        compiler_params=pltpu.CompilerParams(vmem_limit_bytes=VMEM_LIMIT),
        cost_estimate=pl.CostEstimate(flops=flops, bytes_accessed=moved, transcendentals=0),
    )


def shape(dims, dtype=BF16):
    return jax.ShapeDtypeStruct(dims, dtype)


def dot(a, b, dims=((1,), (0,))):
    return lax.dot_general(a, b, (dims, ((), ())), preferred_element_type=F32)


def iota(dims, axis):
    return lax.broadcasted_iota(jnp.int32, dims, axis)


def one(mask):
    return jnp.where(mask, 1.0, 0.0).astype(BF16)


def route_kernel(c_ref, states, grads, gain, ids, gates, normed_out, send, even, odd):
    c = c_ref[0]
    x = states[...].astype(F32)
    inverse = lax.rsqrt(jnp.mean(x * x, axis=-1, keepdims=True) + EPSILON)
    normed_out[...] = (x * inverse * gain[...]).astype(BF16)
    expert = iota((ROWS, TOKENS), 0) // 8
    i = iota((ROWS, TOKENS), 0) % 8
    first = ids[0:1, :] == expert
    second = ids[1:2, :] == expert
    named = first | second
    before = one(iota((TOKENS, TOKENS), 0) < iota((TOKENS, TOKENS), 1))
    slot = dot(one(named), before).astype(jnp.int32)
    slot = jnp.where(named, slot, -1)
    even[...] = one(slot == 2 * i)
    odd[...] = one(slot == 2 * i + 1)
    mine = slot == 2 * c + i % 2
    gate = jnp.where(first, gates[0:1, :], 0.0) + jnp.where(second, gates[1:2, :], 0.0)
    gate = jnp.sum(jnp.where(mine, gate, 0.0), axis=1, keepdims=True)
    low = i < 4
    is_row = (i // 2) % 2 == 0
    row_low = one(mine & low & is_row)
    row_high = one(mine & (~low) & is_row)
    grad_low = one(mine & low & (~is_row))
    grad_high = one(mine & (~low) & (~is_row))
    rows = dot(row_low, normed_out[:, :HALF]) + dot(row_high, normed_out[:, HALF:])
    douts = dot(grad_low, grads[:, :HALF]) + dot(grad_high, grads[:, HALF:])
    send[...] = (rows + gate * douts).astype(BF16)


def scores_kernel(normed, grads, keys, values, weights_out, slopes_out, stats):
    for h in range(HEADS):
        at = slice(h * HEAD, (h + 1) * HEAD)
        s = dot(keys[:, at], normed[:, at], ((1,), (1,))) * SCALE
        peak = jnp.max(s, axis=0, keepdims=True)
        w = jnp.exp(s - peak)
        slopes = dot(values[:, at], grads[:, at], ((1,), (1,)))
        weights_out[h] = w
        slopes_out[h] = slopes
        stats[h : h + 1, :] = peak
        stats[24 + h : 25 + h, :] = jnp.sum(w, axis=0, keepdims=True)
        stats[48 + h : 49 + h, :] = jnp.sum(w * slopes, axis=0, keepdims=True)
    for part in range(3):
        at = 24 * part + HEADS
        stats[at : at + 4, :] = jnp.zeros((4, TOKENS), F32)


def merged(stats):
    peak = stats[0][:24]
    for one_side in stats[1:]:
        peak = jnp.maximum(peak, one_side[:24])
    total = inner = 0.0
    for one_side in stats:
        factor = jnp.exp(one_side[:24] - peak)
        total = total + one_side[24:48] * factor
        inner = inner + one_side[48:] * factor
    return jnp.concatenate([peak, total, inner], axis=0)


def pack(out, rows, left, right, tail_left, tail_right):
    lane = iota(tail_left(0).shape, 1)
    for f in range(CTX_COUNT):
        out[f, rows, 0:256] = left(f).astype(BF16)
        out[f, rows, 256:512] = right(f).astype(BF16)
    for g in range(CTX_COUNT // 2):
        a, b = tail_left(g), tail_right(g)
        out[2 * g, rows, 512:640] = jnp.where(lane < 64, a, pltpu.roll(b, 64, 1)).astype(BF16)
        out[2 * g + 1, rows, 512:640] = jnp.where(lane < 64, pltpu.roll(a, 64, 1), b).astype(BF16)


def score_grad_kernel(
    normed, grads, keys, weights, slopes, local, near, far, keys_grad, values_grad, query_pack, query
):
    peak = jnp.maximum(near[0:24, :], far[0:24, :])
    near_factor = jnp.exp(near[0:24, :] - peak)
    far_factor = jnp.exp(far[0:24, :] - peak)
    total = near[24:48, :] * near_factor + far[24:48, :] * far_factor
    inner = near[48:72, :] * near_factor + far[48:72, :] * far_factor
    total = jnp.where(iota((24, TOKENS), 0) < HEADS, total, 1.0)
    factor = jnp.exp(local[0:24, :] - peak) / total
    delta = inner / total
    for h in range(HEADS):
        at = slice(h * HEAD, (h + 1) * HEAD)
        probs = weights[h] * factor[h : h + 1, :]
        score_grad = (probs * (slopes[h] - delta[h : h + 1, :])).astype(BF16)
        values_grad[:, at] = dot(probs.astype(BF16), grads[:, at]).astype(BF16)
        keys_grad[:, at] = (dot(score_grad, normed[:, at]) * SCALE).astype(BF16)
        query[:, at] = dot(score_grad, keys[:, at], ((0,), (0,))) * SCALE
    pack(
        query_pack,
        slice(0, 64),
        lambda f: query[0:64, 256 * f : 256 * f + 256],
        lambda f: query[64:128, 256 * f : 256 * f + 256],
        lambda g: query[0:64, 2048 + 128 * g : 2176 + 128 * g],
        lambda g: query[64:128, 2048 + 128 * g : 2176 + 128 * g],
    )


def expert_kernel(at_ref, *refs):
    shards, (w_in, w_out, query_pack), (sums, rows, douts, act, pre_grad) = refs[:10], refs[10:13], refs[13:]
    to, source = iota((ROWS, ROWS), 0), iota((ROWS, ROWS), 1)
    order = one(source == 8 * (to % 32) + to // 32)
    whole, pieces = shards[:6], shards[6:]
    blocks = [lambda s=s: s[...] for s in whole]
    blocks += [
        lambda k=k: jnp.concatenate([pieces[k][...], pieces[k + 1][...]], axis=0) for k in (0, 2)
    ]
    for k, block in enumerate(blocks):
        c = at_ref[k]
        sorted_rows = dot(order, block()).astype(BF16)
        for q in range(2):
            where = pl.ds(pl.multiple_of(256 * q + 32 * c, 32), 32)
            for half in range(2):
                lanes = slice(HALF * half, HALF * half + HALF)
                first = 128 * half + 32 * q
                rows[where, lanes] = sorted_rows[first : first + 32, :]
                douts[where, lanes] = sorted_rows[first + 64 : first + 96, :]
    v = dot(rows[...], w_in[...], ((1,), (1,)))
    act_grad = dot(douts[...], w_out[...], ((1,), (1,)))
    root = math.sqrt(2 / math.pi)
    square = v * v
    t = jnp.tanh(root * (v + 0.044715 * (square * v)))
    act[...] = (0.5 * v * (1.0 + t)).astype(BF16)
    slope = 0.5 * (1.0 + t) + 0.5 * v * (1.0 - t * t) * (root * (1.0 + 3 * 0.044715 * square))
    pre_grad[...] = (act_grad * slope).astype(BF16)
    tails = dot(pre_grad[...], w_in[:, 2048:2560])
    chunks = [dot(pre_grad[...], w_in[:, 256 * f : 256 * f + 256]) for f in range(CTX_COUNT)]
    pack(
        sums,
        slice(0, 256),
        lambda f: chunks[f][0:256],
        lambda f: chunks[f][256:512],
        lambda g: tails[0:256, 128 * g : 128 * g + 128],
        lambda g: tails[256:512, 128 * g : 128 * g + 128],
    )
    sums[:, 256:320, :] = query_pack[...]


def weights_kernel(rows, douts, act, pre_grad, grad_in, grad_out):
    grad_in[...] = dot(pre_grad[...], rows[...], ((0,), (0,))).astype(BF16)
    grad_out[...] = dot(act[...], douts[...], ((0,), (0,))).astype(BF16)


def total_kernel(parts, back, query):
    total = parts[0].astype(F32)
    for k in range(1, CTX_COUNT):
        total = total + parts[k].astype(F32)
    to, source = iota((ROWS, ROWS), 0), iota((ROWS, ROWS), 1)
    order = one(source == 32 * (to % 8) + to // 8)
    back[...] = dot(order, total[0:256].astype(BF16)).astype(BF16)
    query[...] = total[256:320]


def tokens_kernel(returned, even, odd, query, out):
    a = dot(even[...], returned[...], ((0,), (0,)))
    b = dot(odd[...], returned[...], ((0,), (0,)))
    wide = a[:, 0:256] + b[:, 256:512]
    tail = a[:, 512:640] + pltpu.roll(b[:, 512:640], 64, 1)
    lane = iota((64, 128), 1)
    tail = jnp.where(lane < 64, tail[0:64], pltpu.roll(tail[64:128], 64, 1))
    out[:, 0:256] = (wide[0:64] + query[:, 0:256]).astype(BF16)
    out[:, 256:512] = (wide[64:128] + query[:, 256:512]).astype(BF16)
    out[:, 512:640] = (tail + query[:, 512:640]).astype(BF16)


def norm_grad_kernel(packs, states, grads, gain, out, total):
    for f in range(CTX_COUNT):
        at = slice(256 * f, 256 * f + 256)
        total[0:64, at] = packs[f, :, 0:256].astype(F32)
        total[64:128, at] = packs[f, :, 256:512].astype(F32)
    lane = iota((64, 128), 1)
    for g in range(CTX_COUNT // 2):
        at = slice(2048 + 128 * g, 2176 + 128 * g)
        a = packs[2 * g, :, 512:640].astype(F32)
        b = packs[2 * g + 1, :, 512:640].astype(F32)
        total[0:64, at] = jnp.where(lane < 64, a, pltpu.roll(b, 64, 1))
        total[64:128, at] = jnp.where(lane < 64, pltpu.roll(a, 64, 1), b)
    x = states[...].astype(F32)
    inverse = lax.rsqrt(jnp.mean(x * x, axis=-1, keepdims=True) + EPSILON)
    unit = x * inverse
    g = total[...] * gain[...]
    g = g - unit * jnp.mean(g * unit, axis=-1, keepdims=True)
    out[...] = (grads[...].astype(F32) + inverse * g).astype(BF16)


def moved_by(array, axis, step):
    count = lax.axis_size(axis)
    return lax.ppermute(array, axis, [(k, (k + step) % count) for k in range(count)])


def on_device(
    states, out_grad, doc_keys, doc_values, norm_gain, expert_ids, gate_values, expert_weights
):
    states, grads, keys, values = states[0], out_grad[0], doc_keys[0], doc_values[0]
    gain = norm_gain.reshape(1, D)
    y, x = lax.axis_index("ctx_0"), lax.axis_index("ctx_1")
    here = (2 * y + x).astype(jnp.int32)
    normed, send, even, odd = call(
        route_kernel,
        [SMEM] + [VMEM] * 5,
        [shape((TOKENS, D)), shape((ROWS, HALF)), shape((ROWS, TOKENS)), shape((ROWS, TOKENS))],
        flops=2 * 4 * ROWS * TOKENS * HALF,
        moved=3 * 2**20,
    )(here.reshape(1), states, grads, gain, expert_ids[0].T, gate_values[0].T)
    own = lax.all_to_all(
        send.reshape(EXPERTS, 8, HALF), "exp", split_axis=0, concat_axis=0, tiled=True
    ).reshape(ROWS, HALF)

    weights, slopes, stats = call(
        scores_kernel,
        [VMEM] * 4,
        [shape((HEADS, KEYS, TOKENS), F32), shape((HEADS, KEYS, TOKENS), F32), shape((72, TOKENS), F32)],
        flops=2 * 2 * KEYS * TOKENS * D,
        moved=5 * 2**20,
    )(normed, grads, keys, values)
    near = merged([stats] + [moved_by(stats, "ctx_0", k) for k in (1, 2, 3)])
    far = moved_by(near, "ctx_1", 1)
    keys_grad, values_grad, query_pack = call(
        score_grad_kernel,
        [VMEM] * 8,
        [shape((KEYS, D)), shape((KEYS, D)), shape((CTX_COUNT, 64, CHUNK))],
        [pltpu.VMEM((TOKENS, D), F32)],
        flops=3 * 2 * KEYS * TOKENS * D,
        moved=6 * 2**20,
    )(normed, grads, keys, weights, slopes, stats, near, far)

    up, down = moved_by(own, "ctx_0", 1), moved_by(own, "ctx_0", 3)
    partner = moved_by(own, "ctx_1", 1)
    across = [moved_by(up[:128], "ctx_0", 1), moved_by(down[128:], "ctx_0", 3)]
    partner_up, partner_down = moved_by(partner, "ctx_0", 1), moved_by(partner, "ctx_0", 3)
    partner_across = [
        moved_by(partner_up[:128], "ctx_0", 1),
        moved_by(partner_down[128:], "ctx_0", 3),
    ]
    shards = [own, up, down, partner, partner_up, partner_down, *across, *partner_across]
    places = [(0, 0), (-1, 0), (1, 0), (0, 1), (-1, 1), (1, 1), (2, 0), (2, 1)]
    at = jnp.stack([2 * ((y + a + 4) % 4) + (x + b) % 2 for a, b in places]).astype(jnp.int32)
    w_in, w_out = expert_weights[0, :, 0, :], expert_weights[0, :, 1, :]
    sums, rows, douts, act, pre_grad = call(
        expert_kernel,
        [SMEM] + [VMEM] * 13,
        [
            shape((CTX_COUNT, 320, CHUNK)),
            shape((SLOTS, D)),
            shape((SLOTS, D)),
            shape((SLOTS, UNITS)),
            shape((SLOTS, UNITS)),
        ],
        flops=2 * 3 * SLOTS * UNITS * D,
        moved=16 * 2**20,
    )(at, *shards, w_in, w_out, query_pack)
    parts = lax.all_to_all(sums, CTX, split_axis=0, concat_axis=0, tiled=True)
    grad_in, grad_out = call(
        weights_kernel,
        [VMEM] * 4,
        [shape((UNITS, D)), shape((UNITS, D))],
        flops=2 * 2 * SLOTS * UNITS * D,
        moved=8 * 2**20,
    )(rows, douts, act, pre_grad)
    weights_grad = jnp.stack([grad_in, grad_out], axis=1)[None]
    back, query = call(
        total_kernel,
        [VMEM],
        [shape((ROWS, CHUNK)), shape((64, CHUNK), F32)],
        moved=4 * 2**20,
    )(parts)
    returned = lax.all_to_all(
        back.reshape(EXPERTS, 8, CHUNK), "exp", split_axis=0, concat_axis=0, tiled=True
    ).reshape(ROWS, CHUNK)
    [total] = call(tokens_kernel, [VMEM] * 4, [shape((64, CHUNK))], moved=2**20)(
        returned, even, odd, query
    )
    packs = lax.all_gather(lax.all_gather(total, "ctx_1"), "ctx_0").reshape(CTX_COUNT, 64, CHUNK)
    [states_grad] = call(
        norm_grad_kernel,
        [VMEM] * 4,
        [shape((TOKENS, D))],
        [pltpu.VMEM((TOKENS, D), F32)],
        moved=3 * 2**20,
    )(packs, states, grads, gain)
    return states_grad[None], keys_grad[None], values_grad[None], weights_grad


def solution(mesh):
    finer = Mesh(mesh.devices.reshape(4, 2, mesh.shape["exp"]), (*CTX, "exp"))
    return jax.shard_map(
        on_device,
        mesh=finer,
        in_specs=(
            P("exp", None, None),
            P("exp", None, None),
            P("exp", CTX, None),
            P("exp", CTX, None),
            P(),
            P("exp", None, None),
            P("exp", None, None),
            P("exp", CTX, None, None),
        ),
        out_specs=(
            P("exp", None, None),
            P("exp", CTX, None),
            P("exp", CTX, None),
            P("exp", CTX, None, None),
        ),
        check_vma=False,
    )
```

time: 330 us -> 195 us (0.59)
  waiting for transfers between devices: 166 us -> 18.9 us
  blocking collectives: 49.4 us -> 94.4 us
  local copies, waits for them, and re-layouts: 57.7 us -> 16.5 us
  Pallas kernels: 0 us -> 35.1 us
  starting transfers between devices: 7.72 us -> 26.6 us
  other arithmetic: 19.5 us -> 2 us
  matrix products: 14 us -> 0 us
  between operations: 14.5 us -> 0.86 us
    all_gather x2 -> x0, waiting for transfers between devices: 141 us -> none  [the longest x1 77.3 us: side_by_side(): lax.all_gather(both, axis, axis=dim, tiled=True)]
    all_to_all x1 -> x2, blocking collectives: 30 us -> 73.8 us  [the longest x1 43.5 us: on_device(): parts = lax.all_to_all(sums, CTX, split_axis=0, concat_axis=0, tiled=True)]
    pallas_call x0 -> x8, Pallas kernels: none -> 35.1 us  [the longest x1 9.45 us: on_device(): call(expert_kernel, [SMEM] + [VMEM] * 13, [shape((CTX_COUNT, 320, CHUNK))...]
    all_to_all x1, waiting for transfers between devices: 24.9 us -> 2.18 us  [on_device(): lax.all_to_all(back.reshape(EXPERTS, 8, CHUNK), 'exp', split_axis=0, conc...]
    ppermute x0 -> x13, starting transfers between devices: none -> 22.4 us  [moved_by(): lax.ppermute(array, axis, [(k, (k + step) % count) for k in range(count)])]
    unnamed x60 -> x27, local copies, waits for them, and re-layouts: 23 us -> 5.57 us
    ppermute x0 -> x13, waiting for transfers between devices: none -> 16.8 us  [moved_by(): lax.ppermute(array, axis, [(k, (k + step) % count) for k in range(count)])]
    dot_general x10 -> x0, matrix products: 14 us -> none  [the longest x1 2.36 us: on_device(): jnp.einsum('qhd,khd->hqk', queries, key_heads, preferred_element_type=jnp...]
  transfers between devices with their start and end apart: 3 -> 14, of which waited for: 3 -> 5; matrix products, arithmetic and copies ran while one was open for 12% -> 8% of each run, Pallas kernels for 0% -> 7%
where the time goes in v2:
time: 195 us; the launch traced here: 194 us
  blocking collectives  94.4 us (48%)
  Pallas kernels  35.1 us (18%)
  starting transfers between devices  26.6 us (14%)
  waiting for transfers between devices  18.9 us (10%)
  local copies, waits for them, and re-layouts  16.5 us (8%)
  other arithmetic  2 us (1%)
    all_to_all x1, blocking collectives, on_device(): parts = lax.all_to_all(sums, CTX, split_axis=0, concat_axis=0, tiled=True)  43.5 us
    all_to_all x1, blocking collectives, on_device(): lax.all_to_all(send.reshape(EXPERTS, 8, HALF), 'exp', split_axis=0, conca...  30.2 us
    ppermute x13, starting transfers between devices, moved_by(): lax.ppermute(array, axis, [(k, (k + step) % count) for k in range(count)])  22.4 us
    ppermute x13, waiting for transfers between devices, moved_by(): lax.ppermute(array, axis, [(k, (k + step) % count) for k in range(count)])  16.8 us
    all_gather x1, blocking collectives, on_device(): lax.all_gather(lax.all_gather(total, 'ctx_1'), 'ctx_0')  13.8 us
    pallas_call x1, Pallas kernels, on_device(): call(expert_kernel, [SMEM] + [VMEM] * 13, [shape((CTX_COUNT, 320, CHUNK))...  9.45 us
    all_gather x1, blocking collectives, on_device(): lax.all_gather(total, 'ctx_1')  6.82 us
    unnamed x27, local copies, waits for them, and re-layouts  5.57 us
  transfers between devices with their start and end apart: 14, of which 5 were waited for; matrix products, arithmetic and copies ran while one was open for 8% of the time, Pallas kernels for 7%

profile of v2, /device:TPU:32, one launch (start us, length us, event | category | flops | bytes accessed | tf_op | source)
XLA Modules:
  0.0 194.4 jit_solution(18272495482426933710)
XLA Ops:
  0.6 1.3 reshape.30.gain
  1.9 3.5 %shard_map.111 = (bf16[128,2560]{1,0:T(8,128)(2,1)}, bf16[256,1280]{1,0:T(8,128)(2,1)}, bf16[256,128]{1,0:T(8,128)(2,1)}, bf16[256,128]{1,0:T(8,128)(2,1)}) custom-call(s32[1]{0:T(128)} %bitcast.8.c_ref, bf16[128,2560]{1,0:T(8,128)(2,1)} %bitcast.43, bf16[128,2560]{1,0:T(8,128)(2,1)} %bitcast.35, f32[1,2560]{1,0:T(1,128)} %reshape.30.gain, ...), custom_call_target="tpu_custom_call" | custom-call | flops 335544320 | bytes 3145728 | tf_op jit(solution)/shard_map/pallas_call | solution.py:258
  5.5 30.2 %all_to_all.15 = bf16[32,8,1280]{2,1,0:T(8,128)(2,1)S(1)} all-to-all(bf16[32,8,1280]{2,1,0:T(8,128)(2,1)} %bitcast.51), channel_id=1, replica_groups=mesh['ctx_0'=4,'ctx_1'=2,'exp'=32] {'exp'}, dimensions={0} | all-to-all | bytes 1310720 | tf_op jit(solution)/shard_map/all_to_all | solution.py:265
  35.7 2.7 %collective-permute-start.2 = (bf16[256,1280]{1,0:T(8,128)(2,1)S(1)}, bf16[256,1280]{1,0:T(8,128)(2,1)S(1)}, u32[]{:S(2)}, u32[]{:S(2)}) collective-permute-start(bf16[256,1280]{1,0:T(8,128)(2,1)S(1)} %bitcast.39), channel_id=1, source_target_pairs={{0,32},{32,0},{1,33},{33,1},{2,34},{34,2},{3,35},{35,3},{4,36},{36... | collective-permute-start | bytes 1966088 | tf_op jit(solution)/shard_map/ppermute | solution.py:248
  38.4 4.2 %shard_map.112 = (f32[20,128,128]{2,1,0:T(8,128)}, f32[20,128,128]{2,1,0:T(8,128)}, f32[72,128]{1,0:T(8,128)}) custom-call(bf16[128,2560]{1,0:T(8,128)(2,1)} %get-tuple-element.24.normed, bf16[128,2560]{1,0:T(8,128)(2,1)} %bitcast.36, bf16[128,2560]{1,0:T(8,128)(2,1)} %bitcast.45, bf16[128,2560]{1,0:T(8,128)(2,1)} %bitcast.50), custom_call_target="tpu_custom_call" | custom-call | flops 167772160 | bytes 5242880 | tf_op jit(solution)/shard_map/pallas_call | solution.py:269
  42.6 3.0 %collective-permute-start.11 = (f32[72,128]{1,0:T(8,128)}, f32[72,128]{1,0:T(8,128)S(1)}, u32[]{:S(2)}, u32[]{:S(2)}) collective-permute-start(f32[72,128]{1,0:T(8,128)} %get-tuple-element.27.local), channel_id=1, source_target_pairs={{0,192},{64,0},{128,64},{192,128},{1,193},{65,1},{129,65},{193,129... | collective-permute-start | bytes 110600 | tf_op jit(solution)/shard_map/ppermute | solution.py:248
  45.6 0.6 collective-permute-start.10
  46.3 1.0 collective-permute-start.9
  47.2 2.3 %collective-permute-start.1 = (bf16[256,1280]{1,0:T(8,128)(2,1)S(1)}, bf16[256,1280]{1,0:T(8,128)(2,1)S(1)}, u32[]{:S(2)}, u32[]{:S(2)}) collective-permute-start(bf16[256,1280]{1,0:T(8,128)(2,1)S(1)} %bitcast.40), channel_id=1, source_target_pairs={{0,192},{64,0},{128,64},{192,128},{1,193},{65,1},{129,65},{193,129... | collective-permute-start | bytes 1966088 | tf_op jit(solution)/shard_map/ppermute | solution.py:248
  49.5 0.0 collective-permute-done.11
  49.5 0.0 collective-permute-start
  49.5 3.3 %collective-permute-done.2.refs_3_ = bf16[256,1280]{1,0:T(8,128)(2,1)S(1)} collective-permute-done((bf16[256,1280]{1,0:T(8,128)(2,1)S(1)}, bf16[256,1280]{1,0:T(8,128)(2,1)S(1)}, u32[]{:S(2)}, u32[]{:S(2)}) %collective-permute-start.2) | collective-permute-done | bytes 655392 | tf_op jit(solution)/shard_map/ppermute | solution.py:248
  52.8 3.0 %collective-permute-start.4 = (bf16[256,1280]{1,0:T(8,128)(2,1)S(1)}, bf16[256,1280]{1,0:T(8,128)(2,1)S(1)}, u32[]{:S(2)}, u32[]{:S(2)}) collective-permute-start(bf16[256,1280]{1,0:T(8,128)(2,1)S(1)} %collective-permute-done.2.refs_3_), channel_id=1, source_target_pairs={{0,192},{64,0},{128,64},{192,128},{1,193},{65,1},{129,65},{193,129... | collective-permute-start | bytes 1966088 | tf_op jit(solution)/shard_map/ppermute | solution.py:248
  55.9 0.0 collective-permute-done.10
  55.9 0.0 collective-permute-start.3
  55.9 3.7 %fusion.6 = (bf16[1,256,1,2560]{3,2,1,0:T(2,128)(2,1)S(1)}, bf16[1,256,1,2560]{3,2,1,0:T(2,128)(2,1)S(1)}) fusion(bf16[1,256,2,2560]{3,2,1,0:T(2,128)(2,1)S(1)} %copy-done), kind=kLoop, calls=%fused_computation.21 | loop fusion | bytes 5242880 | tf_op jit(solution)/shard_map/slice | solution.py:298
  59.6 0.0 collective-permute-done.9
  59.7 2.8 %collective-permute-start.12 = (f32[72,128]{1,0:T(8,128)S(1)}, f32[72,128]{1,0:T(8,128)S(1)}, u32[]{:S(2)}, u32[]{:S(2)}) collective-permute-start(f32[72,128]{1,0:T(8,128)S(1)} %pad_maximum_fusion.near), channel_id=1, source_target_pairs={{0,32},{32,0},{1,33},{33,1},{2,34},{34,2},{3,35},{35,3},{4,36},{36... | collective-permute-start | bytes 110600 | tf_op jit(solution)/shard_map/ppermute | solution.py:248
  62.5 2.4 %collective-permute-done.1.refs_2_ = bf16[256,1280]{1,0:T(8,128)(2,1)S(1)} collective-permute-done((bf16[256,1280]{1,0:T(8,128)(2,1)S(1)}, bf16[256,1280]{1,0:T(8,128)(2,1)S(1)}, u32[]{:S(2)}, u32[]{:S(2)}) %collective-permute-start.1) | collective-permute-done | bytes 655392 | tf_op jit(solution)/shard_map/ppermute | solution.py:248
  64.9 0.8 slice.77
  65.7 3.5 %collective-permute-start.6 = (bf16[128,1280]{1,0:T(8,128)(2,1)}, bf16[128,1280]{1,0:T(8,128)(2,1)}, u32[]{:S(2)}, u32[]{:S(2)}) collective-permute-start(bf16[128,1280]{1,0:T(8,128)(2,1)} %slice.77), channel_id=1, source_target_pairs={{0,192},{64,0},{128,64},{192,128},{1,193},{65,1},{129,65},{193,129... | collective-permute-start | bytes 983048 | tf_op jit(solution)/shard_map/ppermute | solution.py:248
  69.2 0.0 collective-permute-done.refs_1_
  69.2 0.8 slice.76
  70.0 0.0 collective-permute-start.5
  70.0 9.0 %collective-permute-done.4.refs_5_ = bf16[256,1280]{1,0:T(8,128)(2,1)S(1)} collective-permute-done((bf16[256,1280]{1,0:T(8,128)(2,1)S(1)}, bf16[256,1280]{1,0:T(8,128)(2,1)S(1)}, u32[]{:S(2)}, u32[]{:S(2)}) %collective-permute-start.4) | collective-permute-done | bytes 655392 | tf_op jit(solution)/shard_map/ppermute | solution.py:248
  79.0 0.8 slice.79
  79.8 3.5 %collective-permute-start.8 = (bf16[128,1280]{1,0:T(8,128)(2,1)}, bf16[128,1280]{1,0:T(8,128)(2,1)S(1)}, u32[]{:S(2)}, u32[]{:S(2)}) collective-permute-start(bf16[128,1280]{1,0:T(8,128)(2,1)} %slice.79), channel_id=1, source_target_pairs={{0,192},{64,0},{128,64},{192,128},{1,193},{65,1},{129,65},{193,129... | collective-permute-start | bytes 983048 | tf_op jit(solution)/shard_map/ppermute | solution.py:248
  83.2 0.8 slice.78
  84.1 0.0 collective-permute-start.7
  84.1 2.0 %copy_bitcast_fusion = (bf16[256,2560]{1,0:T(8,128)(2,1)}, bf16[256,2560]{1,0:T(8,128)(2,1)}) fusion(bf16[1,256,1,2560]{3,2,1,0:T(2,128)(2,1)S(1)} %get-tuple-element.52, bf16[1,256,1,2560]{3,2,1,0:T(2,128)(2,1)S(1)} %get-tuple-element.53), kind=kLoop, calls=%fused_computation.1 | loop fusion | bytes 5242880 | tf_op jit(solution)/shard_map/squeeze | solution.py:298
  86.2 0.7 stack.44.at_ref
  86.9 0.6 copy-done.12
  87.5 4.4 %shard_map.113 = (bf16[128,2560]{1,0:T(8,128)(2,1)}, bf16[128,2560]{1,0:T(8,128)(2,1)}, bf16[8,64,640]{2,1,0:T(8,128)(2,1)}) custom-call(bf16[128,2560]{1,0:T(8,128)(2,1)} %get-tuple-element.24.normed, bf16[128,2560]{1,0:T(8,128)(2,1)} %bitcast.37, bf16[128,2560]{1,0:T(8,128)(2,1)} %bitcast.46, f32[20,128,128]{2,1,0:T(8,128)} %get-tuple-element.25.weights, ...), custom_call_target="tpu_custom_call" | custom-call | flops 251658240 | bytes 6291456 | tf_op jit(solution)/shard_map/pallas_call | solution.py:278
  91.8 0.0 copy-start.8
  91.9 2.1 %collective-permute-done.7.refs_8_ = bf16[128,1280]{1,0:T(8,128)(2,1)} collective-permute-done((bf16[128,1280]{1,0:T(8,128)(2,1)}, bf16[128,1280]{1,0:T(8,128)(2,1)}, u32[]{:S(2)}, u32[]{:S(2)}) %collective-permute-start.7) | collective-permute-done | bytes 327712 | tf_op jit(solution)/shard_map/ppermute | solution.py:248
  93.9 9.5 %shard_map.114 = (bf16[8,320,640]{2,1,0:T(8,128)(2,1)}, bf16[512,2560]{1,0:T(8,128)(2,1)}, bf16[512,2560]{1,0:T(8,128)(2,1)}, bf16[512,256]{1,0:T(8,128)(2,1)}, bf16[512,256]{1,0:T(8,128)(2,1)}) custom-call(s32[8]{0:T(128)} %stack.44.at_ref, bf16[256,1280]{1,0:T(8,128)(2,1)} %bitcast.42, bf16[256,1280]{1,0:T(8,128)(2,1)} %copy-done.3, ...), custom_call_target="tpu_custom_call" | custom-call | flops 2013265920 | bytes 16777216 | tf_op jit(solution)/shard_map/pallas_call | solution.py:299
  103.4 43.5 %all_to_all.16.parts = bf16[8,320,640]{2,1,0:T(8,128)(2,1)} all-to-all(bf16[8,320,640]{2,1,0:T(8,128)(2,1)} %get-tuple-element.29), channel_id=1, replica_groups=mesh['ctx_0'=4,'ctx_1'=2,'exp'=32] {'ctx_0','ctx_1'}, dimensions={0} | all-to-all | bytes 6553600 | tf_op jit(solution)/shard_map/all_to_all | solution.py:312
  146.9 3.3 %shard_map.115 = (bf16[256,640]{1,0:T(8,128)(2,1)}, f32[64,640]{1,0:T(8,128)}) custom-call(bf16[8,320,640]{2,1,0:T(8,128)(2,1)} %all_to_all.16.parts), custom_call_target="tpu_custom_call" | custom-call | bytes 4194304 | tf_op jit(solution)/shard_map/pallas_call | solution.py:321
  150.2 4.2 %all-to-all-start.2 = ((bf16[32,8,640]{2,1,0:T(8,128)(2,1)}), bf16[32,8,640]{2,1,0:T(8,128)(2,1)S(1)}, u32[]{:S(2)}, u32[]{:S(2)}) async-start(bf16[32,8,640]{2,1,0:T(8,128)(2,1)} %bitcast.54), calls=%async_computation.2 | async-start | bytes 655360 | tf_op jit(solution)/shard_map/all_to_all | solution.py:327
  154.4 5.2 %shard_map.118 = (bf16[256,2560]{1,0:T(8,128)(2,1)}, bf16[256,2560]{1,0:T(8,128)(2,1)}) custom-call(bf16[512,2560]{1,0:T(8,128)(2,1)} %get-tuple-element.36.rows, bf16[512,2560]{1,0:T(8,128)(2,1)} %get-tuple-element.37.douts, bf16[512,256]{1,0:T(8,128)(2,1)} %get-tuple-element.38.act, bf16[512,256]{1,0:T(8,128)(2,1)} %get-tuple-element.39.pre_grad), custom_call_target="tpu_custom_call" | custom-call | flops 1342177280 | bytes 8388608 | tf_op jit(solution)/shard_map/pallas_call | solution.py:313
  159.7 2.0 %maximum_bitcast_fusion = bf16[1,256,2,2560]{3,1,2,0:T(8,128)(2,1)S(1)} fusion(bf16[256,1,2560]{2,0,1:T(8,128)(2,1)} %bitcast.48, bf16[256,1,2560]{2,0,1:T(8,128)(2,1)} %bitcast.47), kind=kLoop, calls=%fused_computation | loop fusion | flops 1310720 | bytes 5242880 | tf_op jit(solution)/shard_map/broadcast_in_dim | solution.py:320
  161.6 4.2 %copy.17 = bf16[1,256,2,2560]{3,2,1,0:T(2,128)(2,1)} copy(bf16[1,256,2,2560]{3,1,2,0:T(8,128)(2,1)S(1)} %maximum_bitcast_fusion) | data formatting | bytes 5242880
  165.8 2.2 %all-to-all-done.2 = bf16[32,8,640]{2,1,0:T(8,128)(2,1)S(1)} async-done(((bf16[32,8,640]{2,1,0:T(8,128)(2,1)}), bf16[32,8,640]{2,1,0:T(8,128)(2,1)S(1)}, u32[]{:S(2)}, u32[]{:S(2)}) %all-to-all-start.2) | async-done | bytes 327712 | tf_op jit(solution)/shard_map/all_to_all | solution.py:327
  168.0 0.7 copy-done.6
  168.7 2.1 %shard_map.116 = bf16[64,640]{1,0:T(8,128)(2,1)} custom-call(bf16[256,640]{1,0:T(8,128)(2,1)} %bitcast.49, bf16[256,128]{1,0:T(8,128)(2,1)} %get-tuple-element.31.even, bf16[256,128]{1,0:T(8,128)(2,1)} %get-tuple-element.32.odd, f32[64,640]{1,0:T(8,128)} %get-tuple-element.33.query), custom_call_target="tpu_custom_call" | custom-call | bytes 1048576 | tf_op jit(solution)/shard_map/pallas_call | solution.py:330
  170.8 6.8 %all-gather = bf16[128,640]{1,0:T(8,128)(2,1)S(1)} all-gather(bf16[64,640]{1,0:T(8,128)(2,1)} %shard_map.116), channel_id=2, replica_groups=mesh['ctx_0'=4,'ctx_1'=2,'exp'=32] {'ctx_1'}, dimensions={0}, use_global_device_ids=true | all-gather | bytes 245760 | tf_op jit(solution)/shard_map/all_gather | solution.py:333
  177.6 13.8 %all-gather.1.packs = bf16[8,64,640]{2,1,0:T(8,128)(2,1)} all-gather(bf16[2,64,640]{2,1,0:T(8,128)(2,1)S(1)} %bitcast.53), channel_id=3, replica_groups=mesh['ctx_0'=4,'ctx_1'=2,'exp'=32] {'ctx_0'}, dimensions={0}, use_global_device_ids=true | all-gather | bytes 819200 | tf_op jit(solution)/shard_map/all_gather | solution.py:333
  191.4 3.0 %shard_map.117 = bf16[128,2560]{1,0:T(8,128)(2,1)} custom-call(bf16[8,64,640]{2,1,0:T(8,128)(2,1)} %all-gather.1.packs, bf16[128,2560]{1,0:T(8,128)(2,1)} %bitcast.44, bf16[128,2560]{1,0:T(8,128)(2,1)} %bitcast.38, f32[1,2560]{1,0:T(1,128)} %reshape.30.gain), custom_call_target="tpu_custom_call" | custom-call | bytes 3145728 | tf_op jit(solution)/shard_map/pallas_call | solution.py:334
  (31 shorter events, 0.1 us)
Async XLA Ops:
  1.9 53.9 %copy-start = (bf16[1,256,2,2560]{3,2,1,0:T(2,128)(2,1)S(1)}, bf16[1,256,2,2560]{3,2,1,0:T(2,128)(2,1)}, u32[]{:S(2)}) copy-start(bf16[1,256,2,2560]{3,2,1,0:T(2,128)(2,1)} %param.15) | copy-start | bytes 7864324
  35.7 23.9 %copy-start.1 = (bf16[32,8,1280]{2,1,0:T(8,128)(2,1)}, bf16[32,8,1280]{2,1,0:T(8,128)(2,1)S(1)}, u32[]{:S(2)}) copy-start(bf16[32,8,1280]{2,1,0:T(8,128)(2,1)S(1)} %all_to_all.15) | copy-start | bytes 1966084
  35.7 17.2 %collective-permute-start.2 = (bf16[256,1280]{1,0:T(8,128)(2,1)S(1)}, bf16[256,1280]{1,0:T(8,128)(2,1)S(1)}, u32[]{:S(2)}, u32[]{:S(2)}) collective-permute-start(bf16[256,1280]{1,0:T(8,128)(2,1)S(1)} %bitcast.39), channel_id=1, source_target_pairs={{0,32},{32,0},{1,33},{33,1},{2,34},{34,2},{3,35},{35,3},{4,36},{36... | collective-permute-start | bytes 1966088 | tf_op jit(solution)/shard_map/ppermute | solution.py:248
  42.6 17.0 %copy-start.10 = (f32[72,128]{1,0:T(8,128)S(1)}, f32[72,128]{1,0:T(8,128)}, u32[]{:S(2)}) copy-start(f32[72,128]{1,0:T(8,128)} %get-tuple-element.27.local) | copy-start | bytes 110596
  42.6 6.9 %collective-permute-start.11 = (f32[72,128]{1,0:T(8,128)}, f32[72,128]{1,0:T(8,128)S(1)}, u32[]{:S(2)}, u32[]{:S(2)}) collective-permute-start(f32[72,128]{1,0:T(8,128)} %get-tuple-element.27.local), channel_id=1, source_target_pairs={{0,192},{64,0},{128,64},{192,128},{1,193},{65,1},{129,65},{193,129... | collective-permute-start | bytes 110600 | tf_op jit(solution)/shard_map/ppermute | solution.py:248
  45.6 10.2 %collective-permute-start.10 = (f32[72,128]{1,0:T(8,128)}, f32[72,128]{1,0:T(8,128)S(1)}, u32[]{:S(2)}, u32[]{:S(2)}) collective-permute-start(f32[72,128]{1,0:T(8,128)} %get-tuple-element.27.local), channel_id=1, source_target_pairs={{0,128},{64,192},{128,0},{192,64},{1,129},{65,193},{129,1},{193,65... | collective-permute-start | bytes 110600 | tf_op jit(solution)/shard_map/ppermute | solution.py:248
  46.3 13.4 %collective-permute-start.9 = (f32[72,128]{1,0:T(8,128)}, f32[72,128]{1,0:T(8,128)S(1)}, u32[]{:S(2)}, u32[]{:S(2)}) collective-permute-start(f32[72,128]{1,0:T(8,128)} %get-tuple-element.27.local), channel_id=1, source_target_pairs={{0,64},{64,128},{128,192},{192,0},{1,65},{65,129},{129,193},{193,1... | collective-permute-start | bytes 110600 | tf_op jit(solution)/shard_map/ppermute | solution.py:248
  47.2 17.7 %collective-permute-start.1 = (bf16[256,1280]{1,0:T(8,128)(2,1)S(1)}, bf16[256,1280]{1,0:T(8,128)(2,1)S(1)}, u32[]{:S(2)}, u32[]{:S(2)}) collective-permute-start(bf16[256,1280]{1,0:T(8,128)(2,1)S(1)} %bitcast.40), channel_id=1, source_target_pairs={{0,192},{64,0},{128,64},{192,128},{1,193},{65,1},{129,65},{193,129... | collective-permute-start | bytes 1966088 | tf_op jit(solution)/shard_map/ppermute | solution.py:248
  49.5 19.7 %collective-permute-start = (bf16[256,1280]{1,0:T(8,128)(2,1)S(1)}, bf16[256,1280]{1,0:T(8,128)(2,1)S(1)}, u32[]{:S(2)}, u32[]{:S(2)}) collective-permute-start(bf16[256,1280]{1,0:T(8,128)(2,1)S(1)} %bitcast.41), channel_id=1, source_target_pairs={{0,64},{64,128},{128,192},{192,0},{1,65},{65,129},{129,193},{193,1... | collective-permute-start | bytes 1966088 | tf_op jit(solution)/shard_map/ppermute | solution.py:248
  52.8 6.8 %copy-start.7 = (bf16[256,1280]{1,0:T(8,128)(2,1)}, bf16[256,1280]{1,0:T(8,128)(2,1)S(1)}, u32[]{:S(2)}) copy-start(bf16[256,1280]{1,0:T(8,128)(2,1)S(1)} %collective-permute-done.2.refs_3_) | copy-start | bytes 1966084
  52.8 26.1 %collective-permute-start.4 = (bf16[256,1280]{1,0:T(8,128)(2,1)S(1)}, bf16[256,1280]{1,0:T(8,128)(2,1)S(1)}, u32[]{:S(2)}, u32[]{:S(2)}) collective-permute-start(bf16[256,1280]{1,0:T(8,128)(2,1)S(1)} %collective-permute-done.2.refs_3_), channel_id=1, source_target_pairs={{0,192},{64,0},{128,64},{192,128},{1,193},{65,1},{129,65},{193,129... | collective-permute-start | bytes 1966088 | tf_op jit(solution)/shard_map/ppermute | solution.py:248
  55.9 27.4 %collective-permute-start.3 = (bf16[256,1280]{1,0:T(8,128)(2,1)S(1)}, bf16[256,1280]{1,0:T(8,128)(2,1)S(1)}, u32[]{:S(2)}, u32[]{:S(2)}) collective-permute-start(bf16[256,1280]{1,0:T(8,128)(2,1)S(1)} %collective-permute-done.2.refs_3_), channel_id=1, source_target_pairs={{0,64},{64,128},{128,192},{192,0},{1,65},{65,129},{129,193},{193,1... | collective-permute-start | bytes 1966088 | tf_op jit(solution)/shard_map/ppermute | solution.py:248
  59.7 26.4 %copy-start.11 = (f32[72,128]{1,0:T(8,128)}, f32[72,128]{1,0:T(8,128)S(1)}, u32[]{:S(2)}) copy-start(f32[72,128]{1,0:T(8,128)S(1)} %pad_maximum_fusion.near) | copy-start | bytes 110596
  59.7 27.2 %collective-permute-start.12 = (f32[72,128]{1,0:T(8,128)S(1)}, f32[72,128]{1,0:T(8,128)S(1)}, u32[]{:S(2)}, u32[]{:S(2)}) collective-permute-start(f32[72,128]{1,0:T(8,128)S(1)} %pad_maximum_fusion.near), channel_id=1, source_target_pairs={{0,32},{32,0},{1,33},{33,1},{2,34},{34,2},{3,35},{35,3},{4,36},{36... | collective-permute-start | bytes 110600 | tf_op jit(solution)/shard_map/ppermute | solution.py:248
  64.9 21.2 %copy-start.2 = (bf16[256,1280]{1,0:T(8,128)(2,1)}, bf16[256,1280]{1,0:T(8,128)(2,1)S(1)}, u32[]{:S(2)}) copy-start(bf16[256,1280]{1,0:T(8,128)(2,1)S(1)} %collective-permute-done.1.refs_2_) | copy-start | bytes 1966084
  65.7 26.1 %collective-permute-start.6 = (bf16[128,1280]{1,0:T(8,128)(2,1)}, bf16[128,1280]{1,0:T(8,128)(2,1)}, u32[]{:S(2)}, u32[]{:S(2)}) collective-permute-start(bf16[128,1280]{1,0:T(8,128)(2,1)} %slice.77), channel_id=1, source_target_pairs={{0,192},{64,0},{128,64},{192,128},{1,193},{65,1},{129,65},{193,129... | collective-permute-start | bytes 983048 | tf_op jit(solution)/shard_map/ppermute | solution.py:248
  69.2 16.9 %copy-start.3 = (bf16[256,1280]{1,0:T(8,128)(2,1)}, bf16[256,1280]{1,0:T(8,128)(2,1)S(1)}, u32[]{:S(2)}) copy-start(bf16[256,1280]{1,0:T(8,128)(2,1)S(1)} %collective-permute-done.refs_1_) | copy-start | bytes 1966084
  70.0 21.9 %collective-permute-start.5 = (bf16[128,1280]{1,0:T(8,128)(2,1)}, bf16[128,1280]{1,0:T(8,128)(2,1)S(1)}, u32[]{:S(2)}, u32[]{:S(2)}) collective-permute-start(bf16[128,1280]{1,0:T(8,128)(2,1)} %slice.76), channel_id=1, source_target_pairs={{0,64},{64,128},{128,192},{192,0},{1,65},{65,129},{129,193},{193,1... | collective-permute-start | bytes 983048 | tf_op jit(solution)/shard_map/ppermute | solution.py:248
  79.0 7.2 %copy-start.4 = (bf16[256,1280]{1,0:T(8,128)(2,1)}, bf16[256,1280]{1,0:T(8,128)(2,1)S(1)}, u32[]{:S(2)}) copy-start(bf16[256,1280]{1,0:T(8,128)(2,1)S(1)} %collective-permute-done.4.refs_5_) | copy-start | bytes 1966084
  79.8 12.1 %collective-permute-start.8 = (bf16[128,1280]{1,0:T(8,128)(2,1)}, bf16[128,1280]{1,0:T(8,128)(2,1)S(1)}, u32[]{:S(2)}, u32[]{:S(2)}) collective-permute-start(bf16[128,1280]{1,0:T(8,128)(2,1)} %slice.79), channel_id=1, source_target_pairs={{0,192},{64,0},{128,64},{192,128},{1,193},{65,1},{129,65},{193,129... | collective-permute-start | bytes 983048 | tf_op jit(solution)/shard_map/ppermute | solution.py:248
  83.2 2.9 %copy-start.5 = (bf16[256,1280]{1,0:T(8,128)(2,1)}, bf16[256,1280]{1,0:T(8,128)(2,1)S(1)}, u32[]{:S(2)}) copy-start(bf16[256,1280]{1,0:T(8,128)(2,1)S(1)} %collective-permute-done.3.refs_4_) | copy-start | bytes 1966084
  84.1 9.9 %collective-permute-start.7 = (bf16[128,1280]{1,0:T(8,128)(2,1)}, bf16[128,1280]{1,0:T(8,128)(2,1)}, u32[]{:S(2)}, u32[]{:S(2)}) collective-permute-start(bf16[128,1280]{1,0:T(8,128)(2,1)} %slice.78), channel_id=1, source_target_pairs={{0,64},{64,128},{128,192},{192,0},{1,65},{65,129},{129,193},{193,1... | collective-permute-start | bytes 983048 | tf_op jit(solution)/shard_map/ppermute | solution.py:248
  86.9 0.6 copy-start.12
  91.8 2.1 %copy-start.8 = (bf16[128,1280]{1,0:T(8,128)(2,1)}, bf16[128,1280]{1,0:T(8,128)(2,1)S(1)}, u32[]{:S(2)}) copy-start(bf16[128,1280]{1,0:T(8,128)(2,1)S(1)} %collective-permute-done.5.refs_6_) | copy-start | bytes 983044
  91.9 2.1 %copy-start.9 = (bf16[128,1280]{1,0:T(8,128)(2,1)}, bf16[128,1280]{1,0:T(8,128)(2,1)S(1)}, u32[]{:S(2)}) copy-start(bf16[128,1280]{1,0:T(8,128)(2,1)S(1)} %collective-permute-done.8.refs_9_) | copy-start | bytes 983044
  150.2 17.8 %all-to-all-start.2 = ((bf16[32,8,640]{2,1,0:T(8,128)(2,1)}), bf16[32,8,640]{2,1,0:T(8,128)(2,1)S(1)}, u32[]{:S(2)}, u32[]{:S(2)}) async-start(bf16[32,8,640]{2,1,0:T(8,128)(2,1)} %bitcast.54), calls=%async_computation.2 | async-start | bytes 655360 | tf_op jit(solution)/shard_map/all_to_all | solution.py:327
  168.0 0.7 copy-start.6

commit v3 on v2

--- a/solution.py
+++ b/solution.py
@@ -25,17 +25,18 @@
 SCALE = HEAD**-0.5
 BF16 = jnp.bfloat16
 F32 = jnp.float32
-VMEM_LIMIT = 56 * 2**20
+VMEM_LIMIT = 40 * 2**20
 
 VMEM = pl.BlockSpec(memory_space=pltpu.VMEM)
 SMEM = pl.BlockSpec(memory_space=pltpu.SMEM)
-
-
-def call(kernel, ins, outs, scratch=(), flops=0, moved=0):
+ANY = pl.BlockSpec(memory_space=pl.ANY)
+
+
+def call(kernel, ins, outs, scratch=(), flops=0, moved=0, places=None):
     return pl.pallas_call(
         kernel,
         in_specs=ins,
-        out_specs=[VMEM] * len(outs),
+        out_specs=places or [VMEM] * len(outs),
         out_shape=outs,
         scratch_shapes=list(scratch),
         compiler_params=pltpu.CompilerParams(vmem_limit_bytes=VMEM_LIMIT),
@@ -63,7 +64,7 @@
     c = c_ref[0]
     x = states[...].astype(F32)
     inverse = lax.rsqrt(jnp.mean(x * x, axis=-1, keepdims=True) + EPSILON)
-    normed_out[...] = (x * inverse * gain[...]).astype(BF16)
+    normed_out[...] = (x * inverse * gain[...].reshape(1, D)).astype(BF16)
     expert = iota((ROWS, TOKENS), 0) // 8
     i = iota((ROWS, TOKENS), 0) % 8
     first = ids[0:1, :] == expert
@@ -157,17 +158,42 @@
 
 
 def expert_kernel(at_ref, *refs):
-    shards, (w_in, w_out, query_pack), (sums, rows, douts, act, pre_grad) = refs[:10], refs[10:13], refs[13:]
+    given, results, held = refs[:13], refs[13:18], refs[18:]
+    shards, w_in, w_out = held[:8], held[8], held[9]
+    sums, rows, douts, act, pre_grad, arrived, left = held[10:]
+    landing = [
+        *shards[:6],
+        shards[6].at[0:128],
+        shards[6].at[128:256],
+        shards[7].at[0:128],
+        shards[7].at[128:256],
+        w_in,
+        w_out,
+    ]
+    loads = [
+        pltpu.make_async_copy(given[k], landing[k], arrived.at[k]) for k in range(len(landing))
+    ]
+    for load in loads:
+        load.start()
+    stores = [
+        pltpu.make_async_copy(given[12], results[0].at[:, 256:320, :], left.at[0]),
+        *(
+            pltpu.make_async_copy(held[11 + k], results[1 + k], left.at[1 + k])
+            for k in range(4)
+        ),
+        *(
+            pltpu.make_async_copy(sums.at[f], results[0].at[f, 0:256, :], left.at[5 + f])
+            for f in range(CTX_COUNT)
+        ),
+    ]
+    stores[0].start()
     to, source = iota((ROWS, ROWS), 0), iota((ROWS, ROWS), 1)
     order = one(source == 8 * (to % 32) + to // 32)
-    whole, pieces = shards[:6], shards[6:]
-    blocks = [lambda s=s: s[...] for s in whole]
-    blocks += [
-        lambda k=k: jnp.concatenate([pieces[k][...], pieces[k + 1][...]], axis=0) for k in (0, 2)
-    ]
-    for k, block in enumerate(blocks):
+    for k, shard in enumerate(shards):
+        for load in loads[k : k + 1] if k < 6 else loads[2 * k - 6 : 2 * k - 4]:
+            load.wait()
         c = at_ref[k]
-        sorted_rows = dot(order, block()).astype(BF16)
+        sorted_rows = dot(order, shard[...]).astype(BF16)
         for q in range(2):
             where = pl.ds(pl.multiple_of(256 * q + 32 * c, 32), 32)
             for half in range(2):
@@ -175,7 +201,11 @@
                 first = 128 * half + 32 * q
                 rows[where, lanes] = sorted_rows[first : first + 32, :]
                 douts[where, lanes] = sorted_rows[first + 64 : first + 96, :]
+    stores[1].start()
+    stores[2].start()
+    loads[10].wait()
     v = dot(rows[...], w_in[...], ((1,), (1,)))
+    loads[11].wait()
     act_grad = dot(douts[...], w_out[...], ((1,), (1,)))
     root = math.sqrt(2 / math.pi)
     square = v * v
@@ -183,17 +213,24 @@
     act[...] = (0.5 * v * (1.0 + t)).astype(BF16)
     slope = 0.5 * (1.0 + t) + 0.5 * v * (1.0 - t * t) * (root * (1.0 + 3 * 0.044715 * square))
     pre_grad[...] = (act_grad * slope).astype(BF16)
+    stores[3].start()
+    stores[4].start()
     tails = dot(pre_grad[...], w_in[:, 2048:2560])
-    chunks = [dot(pre_grad[...], w_in[:, 256 * f : 256 * f + 256]) for f in range(CTX_COUNT)]
-    pack(
-        sums,
-        slice(0, 256),
-        lambda f: chunks[f][0:256],
-        lambda f: chunks[f][256:512],
-        lambda g: tails[0:256, 128 * g : 128 * g + 128],
-        lambda g: tails[256:512, 128 * g : 128 * g + 128],
-    )
-    sums[:, 256:320, :] = query_pack[...]
+    lane = iota((256, 128), 1)
+    for f in range(CTX_COUNT):
+        part = dot(pre_grad[...], w_in[:, 256 * f : 256 * f + 256])
+        sums[f, :, 0:256] = part[0:256].astype(BF16)
+        sums[f, :, 256:512] = part[256:512].astype(BF16)
+        tile = slice(128 * (f // 2), 128 * (f // 2) + 128)
+        a, b = tails[0:256, tile], tails[256:512, tile]
+        if f % 2 == 0:
+            tail = jnp.where(lane < 64, a, pltpu.roll(b, 64, 1))
+        else:
+            tail = jnp.where(lane < 64, pltpu.roll(a, 64, 1), b)
+        sums[f, :, 512:640] = tail.astype(BF16)
+        stores[5 + f].start()
+    for store in stores:
+        store.wait()
 
 
 def weights_kernel(rows, douts, act, pre_grad, grad_in, grad_out):
@@ -201,10 +238,22 @@
     grad_out[...] = dot(act[...], douts[...], ((0,), (0,))).astype(BF16)
 
 
-def total_kernel(parts, back, query):
-    total = parts[0].astype(F32)
-    for k in range(1, CTX_COUNT):
-        total = total + parts[k].astype(F32)
+def total_kernel(given, back, query, parts, arrived):
+    loads = [
+        pltpu.make_async_copy(given.at[k], parts.at[k], arrived.at[k]) for k in range(CTX_COUNT)
+    ]
+    for load in loads:
+        load.start()
+    for load in loads[:4]:
+        load.wait()
+    total = (parts[0].astype(F32) + parts[1].astype(F32)) + (
+        parts[2].astype(F32) + parts[3].astype(F32)
+    )
+    for load in loads[4:]:
+        load.wait()
+    total = total + (parts[4].astype(F32) + parts[5].astype(F32)) + (
+        parts[6].astype(F32) + parts[7].astype(F32)
+    )
     to, source = iota((ROWS, ROWS), 0), iota((ROWS, ROWS), 1)
     order = one(source == 32 * (to % 8) + to // 8)
     back[...] = dot(order, total[0:256].astype(BF16)).astype(BF16)
@@ -223,22 +272,26 @@
     out[:, 512:640] = (tail + query[:, 512:640]).astype(BF16)
 
 
-def norm_grad_kernel(packs, states, grads, gain, out, total):
-    for f in range(CTX_COUNT):
-        at = slice(256 * f, 256 * f + 256)
-        total[0:64, at] = packs[f, :, 0:256].astype(F32)
-        total[64:128, at] = packs[f, :, 256:512].astype(F32)
+def norm_grad_kernel(place, *refs):
+    packs, (states, grads, gain, out, total) = refs[:CTX_COUNT], refs[CTX_COUNT:]
+    y, column = place[0], place[1]
     lane = iota((64, 128), 1)
-    for g in range(CTX_COUNT // 2):
-        at = slice(2048 + 128 * g, 2176 + 128 * g)
-        a = packs[2 * g, :, 512:640].astype(F32)
-        b = packs[2 * g + 1, :, 512:640].astype(F32)
+    for k in range(4):
+        row = (y + k) % 4
+        for pack, side in ((packs[2 * k], column), (packs[2 * k + 1], 1 - column)):
+            at = pl.ds(pl.multiple_of(256 * (2 * row + side), 256), 256)
+            total[0:64, at] = pack[:, 0:256].astype(F32)
+            total[64:128, at] = pack[:, 256:512].astype(F32)
+        at = pl.ds(pl.multiple_of(2048 + 128 * row, 128), 128)
+        near = packs[2 * k][:, 512:640].astype(F32)
+        far = packs[2 * k + 1][:, 512:640].astype(F32)
+        a, b = jnp.where(column == 0, near, far), jnp.where(column == 0, far, near)
         total[0:64, at] = jnp.where(lane < 64, a, pltpu.roll(b, 64, 1))
         total[64:128, at] = jnp.where(lane < 64, pltpu.roll(a, 64, 1), b)
     x = states[...].astype(F32)
     inverse = lax.rsqrt(jnp.mean(x * x, axis=-1, keepdims=True) + EPSILON)
     unit = x * inverse
-    g = total[...] * gain[...]
+    g = total[...] * gain[...].reshape(1, D)
     g = g - unit * jnp.mean(g * unit, axis=-1, keepdims=True)
     out[...] = (grads[...].astype(F32) + inverse * g).astype(BF16)
 
@@ -252,7 +305,6 @@
     states, out_grad, doc_keys, doc_values, norm_gain, expert_ids, gate_values, expert_weights
 ):
     states, grads, keys, values = states[0], out_grad[0], doc_keys[0], doc_values[0]
-    gain = norm_gain.reshape(1, D)
     y, x = lax.axis_index("ctx_0"), lax.axis_index("ctx_1")
     here = (2 * y + x).astype(jnp.int32)
     normed, send, even, odd = call(
@@ -261,7 +313,7 @@
         [shape((TOKENS, D)), shape((ROWS, HALF)), shape((ROWS, TOKENS)), shape((ROWS, TOKENS))],
         flops=2 * 4 * ROWS * TOKENS * HALF,
         moved=3 * 2**20,
-    )(here.reshape(1), states, grads, gain, expert_ids[0].T, gate_values[0].T)
+    )(here.reshape(1), states, grads, norm_gain, expert_ids[0].T, gate_values[0].T)
     own = lax.all_to_all(
         send.reshape(EXPERTS, 8, HALF), "exp", split_axis=0, concat_axis=0, tiled=True
     ).reshape(ROWS, HALF)
@@ -288,17 +340,14 @@
     partner = moved_by(own, "ctx_1", 1)
     across = [moved_by(up[:128], "ctx_0", 1), moved_by(down[128:], "ctx_0", 3)]
     partner_up, partner_down = moved_by(partner, "ctx_0", 1), moved_by(partner, "ctx_0", 3)
-    partner_across = [
-        moved_by(partner_up[:128], "ctx_0", 1),
-        moved_by(partner_down[128:], "ctx_0", 3),
-    ]
+    partner_across = [moved_by(piece, "ctx_1", 1) for piece in across]
     shards = [own, up, down, partner, partner_up, partner_down, *across, *partner_across]
     places = [(0, 0), (-1, 0), (1, 0), (0, 1), (-1, 1), (1, 1), (2, 0), (2, 1)]
     at = jnp.stack([2 * ((y + a + 4) % 4) + (x + b) % 2 for a, b in places]).astype(jnp.int32)
     w_in, w_out = expert_weights[0, :, 0, :], expert_weights[0, :, 1, :]
     sums, rows, douts, act, pre_grad = call(
         expert_kernel,
-        [SMEM] + [VMEM] * 13,
+        [SMEM] + [ANY] * 13,
         [
             shape((CTX_COUNT, 320, CHUNK)),
             shape((SLOTS, D)),
@@ -306,10 +355,31 @@
             shape((SLOTS, UNITS)),
             shape((SLOTS, UNITS)),
         ],
+        [
+            *[pltpu.VMEM((ROWS, HALF), BF16)] * 8,
+            *[pltpu.VMEM((UNITS, D), BF16)] * 2,
+            pltpu.VMEM((CTX_COUNT, ROWS, CHUNK), BF16),
+            *[pltpu.VMEM((SLOTS, D), BF16)] * 2,
+            *[pltpu.VMEM((SLOTS, UNITS), BF16)] * 2,
+            pltpu.SemaphoreType.DMA((12,)),
+            pltpu.SemaphoreType.DMA((13,)),
+        ],
+        places=[ANY] * 5,
         flops=2 * 3 * SLOTS * UNITS * D,
         moved=16 * 2**20,
     )(at, *shards, w_in, w_out, query_pack)
     parts = lax.all_to_all(sums, CTX, split_axis=0, concat_axis=0, tiled=True)
+    back, query = call(
+        total_kernel,
+        [ANY],
+        [shape((ROWS, CHUNK)), shape((64, CHUNK), F32)],
+        [pltpu.VMEM((CTX_COUNT, 320, CHUNK), BF16), pltpu.SemaphoreType.DMA((CTX_COUNT,))],
+        moved=4 * 2**20,
+    )(parts)
+    rows, back = lax.optimization_barrier((rows, back))
+    returned = lax.all_to_all(
+        back.reshape(EXPERTS, 8, CHUNK), "exp", split_axis=0, concat_axis=0, tiled=True
+    ).reshape(ROWS, CHUNK)
     grad_in, grad_out = call(
         weights_kernel,
         [VMEM] * 4,
@@ -318,26 +388,23 @@
         moved=8 * 2**20,
     )(rows, douts, act, pre_grad)
     weights_grad = jnp.stack([grad_in, grad_out], axis=1)[None]
-    back, query = call(
-        total_kernel,
-        [VMEM],
-        [shape((ROWS, CHUNK)), shape((64, CHUNK), F32)],
-        moved=4 * 2**20,
-    )(parts)
-    returned = lax.all_to_all(
-        back.reshape(EXPERTS, 8, CHUNK), "exp", split_axis=0, concat_axis=0, tiled=True
-    ).reshape(ROWS, CHUNK)
+    returned, weights_grad = lax.optimization_barrier((returned, weights_grad))
     [total] = call(tokens_kernel, [VMEM] * 4, [shape((64, CHUNK))], moved=2**20)(
         returned, even, odd, query
     )
-    packs = lax.all_gather(lax.all_gather(total, "ctx_1"), "ctx_0").reshape(CTX_COUNT, 64, CHUNK)
+    packs = [total]
+    for k in range(1, CTX_COUNT):
+        pairs = [
+            (2 * i + j, 2 * ((i - k // 2) % 4) + (j + k) % 2) for i in range(4) for j in range(2)
+        ]
+        packs.append(lax.ppermute(total, CTX, pairs))
     [states_grad] = call(
         norm_grad_kernel,
-        [VMEM] * 4,
+        [SMEM] + [VMEM] * 11,
         [shape((TOKENS, D))],
         [pltpu.VMEM((TOKENS, D), F32)],
         moved=3 * 2**20,
-    )(packs, states, grads, gain)
+    )(jnp.stack([y, x]).astype(jnp.int32), *packs, states, grads, norm_gain)
     return states_grad[None], keys_grad[None], values_grad[None], weights_grad
 
 

time: 195 us -> 184 us (0.944)
  blocking collectives: 94.4 us -> 41.9 us
  starting transfers between devices: 26.6 us -> 49.8 us
  waiting for transfers between devices: 18.9 us -> 35.9 us
  local copies, waits for them, and re-layouts: 16.5 us -> 31 us
  Pallas kernels: 35.1 us -> 21.6 us
    all_to_all x1 -> x0, blocking collectives: 30.2 us -> none  [on_device(): lax.all_to_all(send.reshape(EXPERTS, 8, HALF), 'exp', split_axis=0, conca...]
    all_gather x2 -> x0, blocking collectives: 20.6 us -> none  [the longest x1 13.8 us: on_device(): lax.all_gather(lax.all_gather(total, 'ctx_1'), 'ctx_0')]
    unnamed x27 -> x69, local copies, waits for them, and re-layouts: 5.57 us -> 23.8 us
    ppermute x0 -> x7, starting transfers between devices: none -> 14.2 us  [on_device(): packs.append(lax.ppermute(total, CTX, pairs))]
    all_to_all x0 -> x1, waiting for transfers between devices: none -> 12.7 us  [on_device(): lax.all_to_all(send.reshape(EXPERTS, 8, HALF), 'exp', split_axis=0, conca...]
    all_to_all x0 -> x1, starting transfers between devices: none -> 9.65 us  [on_device(): lax.all_to_all(send.reshape(EXPERTS, 8, HALF), 'exp', split_axis=0, conca...]
    ppermute x13, starting transfers between devices: 22.4 us -> 18.3 us  [moved_by(): lax.ppermute(array, axis, [(k, (k + step) % count) for k in range(count)])]
    pallas_call x1, Pallas kernels: 5.22 us -> 1.54 us  [on_device(): call(weights_kernel, [VMEM] * 4, [shape((UNITS, D)), shape((UNITS, D))],...]
  transfers between devices with their start and end apart: 14 -> 22, of which waited for: 5 -> 7; matrix products, arithmetic and copies ran while one was open for 8% -> 8% of each run, Pallas kernels for 7% -> 2%
where the time goes in v3:
time: 184 us; the launch traced here: 183 us
  starting transfers between devices  49.8 us (27%)
  blocking collectives  41.9 us (23%)
  waiting for transfers between devices  35.9 us (20%)
  local copies, waits for them, and re-layouts  31 us (17%)
  Pallas kernels  21.6 us (12%)
    all_to_all x1, blocking collectives, on_device(): parts = lax.all_to_all(sums, CTX, split_axis=0, concat_axis=0, tiled=True)  41.9 us
    unnamed x69, local copies, waits for them, and re-layouts  23.8 us
    ppermute x13, starting transfers between devices, moved_by(): lax.ppermute(array, axis, [(k, (k + step) % count) for k in range(count)])  18.3 us
    ppermute x13, waiting for transfers between devices, moved_by(): lax.ppermute(array, axis, [(k, (k + step) % count) for k in range(count)])  17.4 us
    ppermute x7, starting transfers between devices, on_device(): packs.append(lax.ppermute(total, CTX, pairs))  14.2 us
    all_to_all x1, waiting for transfers between devices, on_device(): lax.all_to_all(send.reshape(EXPERTS, 8, HALF), 'exp', split_axis=0, conca...  12.7 us
    pallas_call x1, Pallas kernels, on_device(): call(expert_kernel, [SMEM] + [ANY] * 13, [shape((CTX_COUNT, 320, CHUNK)),...  10.1 us
    all_to_all x1, starting transfers between devices, on_device(): lax.all_to_all(send.reshape(EXPERTS, 8, HALF), 'exp', split_axis=0, conca...  9.65 us
  transfers between devices with their start and end apart: 22, of which 7 were waited for; matrix products, arithmetic and copies ran while one was open for 8% of the time, Pallas kernels for 2%

profile of v3, /device:TPU:32, one launch (start us, length us, event | category | flops | bytes accessed | tf_op | source)
XLA Modules:
  0.0 183.1 jit_solution(9598844515402014710)
XLA Ops:
  0.7 1.1 copy-done
  1.7 1.1 copy-done.8
  2.8 0.7 copy-done.30
  3.5 0.7 copy-done.32
  4.2 0.7 copy-done.33
  4.9 1.2 shard_map.111
  6.1 0.8 copy-done.23
  6.9 0.6 copy-done.26
  8.2 9.7 %all-to-all-start = ((bf16[32,8,1280]{2,1,0:T(8,128)(2,1)}), bf16[32,8,1280]{2,1,0:T(8,128)(2,1)S(1)}, u32[]{:S(2)}, u32[]{:S(2)}) async-start(bf16[32,8,1280]{2,1,0:T(8,128)(2,1)} %bitcast.52), calls=%async_computation | async-start | bytes 1310720 | tf_op jit(solution)/shard_map/all_to_all | solution.py:317
  17.9 1.1 shard_map.112
  19.0 1.0 copy-done.18
  20.0 1.1 copy-done.20
  21.1 3.0 %collective-permute-start.11 = (f32[72,128]{1,0:T(8,128)S(1)}, f32[72,128]{1,0:T(8,128)S(1)}, u32[]{:S(2)}, u32[]{:S(2)}) collective-permute-start(f32[72,128]{1,0:T(8,128)S(1)} %get-tuple-element.31.local), channel_id=1, source_target_pairs={{0,192},{64,0},{128,64},{192,128},{1,193},{65,1},{129,65},{193,129... | collective-permute-start | bytes 110600 | tf_op jit(solution)/shard_map/ppermute | solution.py:301
  24.8 1.0 collective-permute-start.9
  25.7 12.7 %all-to-all-done = bf16[32,8,1280]{2,1,0:T(8,128)(2,1)S(1)} async-done(((bf16[32,8,1280]{2,1,0:T(8,128)(2,1)}), bf16[32,8,1280]{2,1,0:T(8,128)(2,1)S(1)}, u32[]{:S(2)}, u32[]{:S(2)}) %all-to-all-start) | async-done | bytes 655392 | tf_op jit(solution)/shard_map/all_to_all | solution.py:317
  38.4 2.7 %collective-permute-start.2 = (bf16[256,1280]{1,0:T(8,128)(2,1)S(1)}, bf16[256,1280]{1,0:T(8,128)(2,1)}, u32[]{:S(2)}, u32[]{:S(2)}) collective-permute-start(bf16[256,1280]{1,0:T(8,128)(2,1)S(1)} %bitcast.40), channel_id=1, source_target_pairs={{0,32},{32,0},{1,33},{33,1},{2,34},{34,2},{3,35},{35,3},{4,36},{36... | collective-permute-start | bytes 1966088 | tf_op jit(solution)/shard_map/ppermute | solution.py:301
  41.2 3.0 %collective-permute-start.1 = (bf16[256,1280]{1,0:T(8,128)(2,1)S(1)}, bf16[256,1280]{1,0:T(8,128)(2,1)S(1)}, u32[]{:S(2)}, u32[]{:S(2)}) collective-permute-start(bf16[256,1280]{1,0:T(8,128)(2,1)S(1)} %bitcast.41), channel_id=1, source_target_pairs={{0,192},{64,0},{128,64},{192,128},{1,193},{65,1},{129,65},{193,129... | collective-permute-start | bytes 1966088 | tf_op jit(solution)/shard_map/ppermute | solution.py:301
  44.2 6.5 %fusion.6 = (bf16[1,256,1,2560]{3,2,1,0:T(2,128)(2,1)S(1)}, bf16[1,256,1,2560]{3,2,1,0:T(2,128)(2,1)S(1)}) fusion(bf16[1,256,2,2560]{3,2,1,0:T(2,128)(2,1)} %param.15), kind=kLoop, calls=%fused_computation.22 | loop fusion | bytes 5242880 | tf_op jit(solution)/shard_map/slice | solution.py:347
  50.8 6.3 %collective-permute-done.1.refs_2_ = bf16[256,1280]{1,0:T(8,128)(2,1)S(1)} collective-permute-done((bf16[256,1280]{1,0:T(8,128)(2,1)S(1)}, bf16[256,1280]{1,0:T(8,128)(2,1)S(1)}, u32[]{:S(2)}, u32[]{:S(2)}) %collective-permute-start.1) | collective-permute-done | bytes 655392 | tf_op jit(solution)/shard_map/ppermute | solution.py:301
  57.1 3.8 %collective-permute-start.6 = (bf16[128,1280]{1,0:T(8,128)(2,1)S(1)}, bf16[128,1280]{1,0:T(8,128)(2,1)}, u32[]{:S(2)}, u32[]{:S(2)}) collective-permute-start(bf16[128,1280]{1,0:T(8,128)(2,1)S(1)} %slice.69), channel_id=1, source_target_pairs={{0,192},{64,0},{128,64},{192,128},{1,193},{65,1},{129,65},{193,129... | collective-permute-start | bytes 983048 | tf_op jit(solution)/shard_map/ppermute | solution.py:301
  61.0 0.9 collective-permute-start.12
  61.9 3.2 %collective-permute-start.4 = (bf16[256,1280]{1,0:T(8,128)(2,1)}, bf16[256,1280]{1,0:T(8,128)(2,1)}, u32[]{:S(2)}, u32[]{:S(2)}) collective-permute-start(bf16[256,1280]{1,0:T(8,128)(2,1)} %collective-permute-done.2.refs_3_), channel_id=1, source_target_pairs={{0,192},{64,0},{128,64},{192,128},{1,193},{65,1},{129,65},{193,129... | collective-permute-start | bytes 1966088 | tf_op jit(solution)/shard_map/ppermute | solution.py:301
  65.1 3.9 %collective-permute-done.6.refs_7_ = bf16[128,1280]{1,0:T(8,128)(2,1)} collective-permute-done((bf16[128,1280]{1,0:T(8,128)(2,1)S(1)}, bf16[128,1280]{1,0:T(8,128)(2,1)}, u32[]{:S(2)}, u32[]{:S(2)}) %collective-permute-start.6) | collective-permute-done | bytes 327712 | tf_op jit(solution)/shard_map/ppermute | solution.py:301
  69.0 3.9 %collective-permute-done.5.refs_6_ = bf16[128,1280]{1,0:T(8,128)(2,1)} collective-permute-done((bf16[128,1280]{1,0:T(8,128)(2,1)S(1)}, bf16[128,1280]{1,0:T(8,128)(2,1)}, u32[]{:S(2)}, u32[]{:S(2)}) %collective-permute-start.5) | collective-permute-done | bytes 327712 | tf_op jit(solution)/shard_map/ppermute | solution.py:301
  73.7 1.1 copy-done.11
  74.8 1.1 copy-done.13
  75.9 1.3 copy-done.19
  77.2 1.3 copy-done.21
  78.5 1.8 shard_map.113
  80.3 1.5 collective-permute-done.7.refs_8_
  81.8 1.7 collective-permute-done.3.refs_4_
  83.6 10.1 %shard_map.114 = (bf16[8,320,640]{2,1,0:T(8,128)(2,1)}, bf16[512,2560]{1,0:T(8,128)(2,1)S(1)}, bf16[512,2560]{1,0:T(8,128)(2,1)S(1)}, bf16[512,256]{1,0:T(8,128)(2,1)S(1)}, bf16[512,256]{1,0:T(8,128)(2,1)S(1)}) custom-call(s32[8]{0:T(128)S(1)} %stack.56.at_ref, bf16[256,1280]{1,0:T(8,128)(2,1)S(1)} %bitcast.43, bf16[256,1280]{1,0:T(8,128)(2,1)S(1)} %copy-done.17, ...), custom_call_target="tpu_custom_call" | custom-call | flops 2013265920 | bytes 16777216 | tf_op jit(solution)/shard_map/pallas_call | solution.py:348
  93.8 41.9 %all_to_all.15.given = bf16[8,320,640]{2,1,0:T(8,128)(2,1)S(1)} all-to-all(bf16[8,320,640]{2,1,0:T(8,128)(2,1)} %get-tuple-element.34), channel_id=1, replica_groups=mesh['ctx_0'=4,'ctx_1'=2,'exp'=32] {'ctx_0','ctx_1'}, dimensions={0} | all-to-all | bytes 6553600 | tf_op jit(solution)/shard_map/all_to_all | solution.py:371
  135.7 3.3 %shard_map.115 = (bf16[256,640]{1,0:T(8,128)(2,1)}, f32[64,640]{1,0:T(8,128)S(1)}) custom-call(bf16[8,320,640]{2,1,0:T(8,128)(2,1)S(1)} %all_to_all.15.given), custom_call_target="tpu_custom_call" | custom-call | bytes 4194304 | tf_op jit(solution)/shard_map/pallas_call | solution.py:372
  139.0 7.6 %all-to-all-start.2 = ((bf16[32,8,640]{2,1,0:T(8,128)(2,1)}), bf16[32,8,640]{2,1,0:T(8,128)(2,1)S(1)}, u32[]{:S(2)}, u32[]{:S(2)}) async-start(bf16[32,8,640]{2,1,0:T(8,128)(2,1)} %bitcast.23), calls=%async_computation.2 | async-start | bytes 655360 | tf_op jit(solution)/shard_map/all_to_all | solution.py:380
  146.7 1.7 copy-done.5
  148.4 1.7 copy-done.7
  150.1 0.9 copy-done.25
  151.1 1.5 shard_map.116
  152.6 1.7 maximum_bitcast_fusion
  154.3 5.8 %all-to-all-done.2 = bf16[32,8,640]{2,1,0:T(8,128)(2,1)S(1)} async-done(((bf16[32,8,640]{2,1,0:T(8,128)(2,1)}), bf16[32,8,640]{2,1,0:T(8,128)(2,1)S(1)}, u32[]{:S(2)}, u32[]{:S(2)}) %all-to-all-start.2) | async-done | bytes 327712 | tf_op jit(solution)/shard_map/all_to_all | solution.py:380
  160.6 0.8 collective-permute-start.19
  161.6 6.1 %collective-permute-start.17 = (bf16[64,640]{1,0:T(8,128)(2,1)S(1)}, bf16[64,640]{1,0:T(8,128)(2,1)S(1)}, u32[]{:S(2)}, u32[]{:S(2)}) collective-permute-start(bf16[64,640]{1,0:T(8,128)(2,1)S(1)} %shard_map.117.refs_0_), channel_id=1, source_target_pairs={{0,160},{32,128},{64,224},{96,192},{128,32},{160,0},{192,96},{224,... | collective-permute-start | bytes 245768 | tf_op jit(solution)/shard_map/ppermute | solution.py:400
  167.8 2.8 %collective-permute-start.15 = (bf16[64,640]{1,0:T(8,128)(2,1)S(1)}, bf16[64,640]{1,0:T(8,128)(2,1)S(1)}, u32[]{:S(2)}, u32[]{:S(2)}) collective-permute-start(bf16[64,640]{1,0:T(8,128)(2,1)S(1)} %shard_map.117.refs_0_), channel_id=1, source_target_pairs={{0,224},{32,192},{64,32},{96,0},{128,96},{160,64},{192,160},{224,1... | collective-permute-start | bytes 245768 | tf_op jit(solution)/shard_map/ppermute | solution.py:400
  170.6 1.5 collective-permute-start.14
  172.0 2.8 %collective-permute-start.13 = (bf16[64,640]{1,0:T(8,128)(2,1)S(1)}, bf16[64,640]{1,0:T(8,128)(2,1)S(1)}, u32[]{:S(2)}, u32[]{:S(2)}) collective-permute-start(bf16[64,640]{1,0:T(8,128)(2,1)S(1)} %shard_map.117.refs_0_), channel_id=1, source_target_pairs={{0,32},{32,0},{64,96},{96,64},{128,160},{160,128},{192,224},{224,1... | collective-permute-start | bytes 245768 | tf_op jit(solution)/shard_map/ppermute | solution.py:400
  174.9 6.0 %copy.14 = bf16[1,256,2,2560]{3,2,1,0:T(2,128)(2,1)} copy(bf16[1,256,2,2560]{3,1,2,0:T(8,128)(2,1)} %maximum_bitcast_fusion) | data formatting | bytes 5242880
  181.0 2.2 %shard_map.118 = bf16[128,2560]{1,0:T(8,128)(2,1)} custom-call(s32[2]{0:T(128)S(1)} %pad_add_fusion.place, bf16[64,640]{1,0:T(8,128)(2,1)S(1)} %shard_map.117.refs_0_, bf16[64,640]{1,0:T(8,128)(2,1)S(1)} %collective-permute-done.13.refs_1_, bf16[64,640]{1,0:T(8,128)(2,1)S(1)} %collective-permute-done.14.refs_2_, ...), custom_call_target="tpu_custom_call" | custom-call | bytes 3145728 | tf_op jit(solution)/shard_map/pallas_call | solution.py:401
  (84 shorter events, 2.9 us)
Async XLA Ops:
  0.6 1.1 copy-start
  1.7 1.1 copy-start.8
  4.9 13.0 %copy-start.1 = (bf16[1,128,2560]{2,1,0:T(8,128)(2,1)S(1)}, bf16[1,128,2560]{2,1,0:T(8,128)(2,1)}, u32[]{:S(2)}) copy-start(bf16[1,128,2560]{2,1,0:T(8,128)(2,1)} %param.9) | copy-start | bytes 1966084
  4.9 13.0 %copy-start.10 = (bf16[1,128,2560]{2,1,0:T(8,128)(2,1)S(1)}, bf16[1,128,2560]{2,1,0:T(8,128)(2,1)}, u32[]{:S(2)}) copy-start(bf16[1,128,2560]{2,1,0:T(8,128)(2,1)} %param.10) | copy-start | bytes 1966084
  4.9 13.0 %copy-start.22 = (bf16[1,128,2560]{2,1,0:T(8,128)(2,1)S(1)}, bf16[1,128,2560]{2,1,0:T(8,128)(2,1)}, u32[]{:S(2)}) copy-start(bf16[1,128,2560]{2,1,0:T(8,128)(2,1)} %param.11) | copy-start | bytes 1966084
  8.2 42.5 %copy-start.12 = (bf16[128,2560]{1,0:T(8,128)(2,1)}, bf16[128,2560]{1,0:T(8,128)(2,1)S(1)}, u32[]{:S(2)}) copy-start(bf16[128,2560]{1,0:T(8,128)(2,1)S(1)} %get-tuple-element.28.normed) | copy-start | bytes 1966084
  8.2 30.2 %all-to-all-start = ((bf16[32,8,1280]{2,1,0:T(8,128)(2,1)}), bf16[32,8,1280]{2,1,0:T(8,128)(2,1)S(1)}, u32[]{:S(2)}, u32[]{:S(2)}) async-start(bf16[32,8,1280]{2,1,0:T(8,128)(2,1)} %bitcast.52), calls=%async_computation | async-start | bytes 1310720 | tf_op jit(solution)/shard_map/all_to_all | solution.py:317
  20.0 1.1 copy-start.20
  21.1 23.1 %collective-permute-start.11 = (f32[72,128]{1,0:T(8,128)S(1)}, f32[72,128]{1,0:T(8,128)S(1)}, u32[]{:S(2)}, u32[]{:S(2)}) collective-permute-start(f32[72,128]{1,0:T(8,128)S(1)} %get-tuple-element.31.local), channel_id=1, source_target_pairs={{0,192},{64,0},{128,64},{192,128},{1,193},{65,1},{129,65},{193,129... | collective-permute-start | bytes 110600 | tf_op jit(solution)/shard_map/ppermute | solution.py:301
  24.1 26.6 %collective-permute-start.10 = (f32[72,128]{1,0:T(8,128)S(1)}, f32[72,128]{1,0:T(8,128)S(1)}, u32[]{:S(2)}, u32[]{:S(2)}) collective-permute-start(f32[72,128]{1,0:T(8,128)S(1)} %get-tuple-element.31.local), channel_id=1, source_target_pairs={{0,128},{64,192},{128,0},{192,64},{1,129},{65,193},{129,1},{193,65... | collective-permute-start | bytes 110600 | tf_op jit(solution)/shard_map/ppermute | solution.py:301
  24.8 26.0 %collective-permute-start.9 = (f32[72,128]{1,0:T(8,128)S(1)}, f32[72,128]{1,0:T(8,128)S(1)}, u32[]{:S(2)}, u32[]{:S(2)}) collective-permute-start(f32[72,128]{1,0:T(8,128)S(1)} %get-tuple-element.31.local), channel_id=1, source_target_pairs={{0,64},{64,128},{128,192},{192,0},{1,65},{65,129},{129,193},{193,1... | collective-permute-start | bytes 110600 | tf_op jit(solution)/shard_map/ppermute | solution.py:301
  38.4 12.3 %copy-start.2 = (bf16[32,8,1280]{2,1,0:T(8,128)(2,1)}, bf16[32,8,1280]{2,1,0:T(8,128)(2,1)S(1)}, u32[]{:S(2)}) copy-start(bf16[32,8,1280]{2,1,0:T(8,128)(2,1)S(1)} %all-to-all-done) | copy-start | bytes 1966084
  38.4 23.5 %collective-permute-start.2 = (bf16[256,1280]{1,0:T(8,128)(2,1)S(1)}, bf16[256,1280]{1,0:T(8,128)(2,1)}, u32[]{:S(2)}, u32[]{:S(2)}) collective-permute-start(bf16[256,1280]{1,0:T(8,128)(2,1)S(1)} %bitcast.40), channel_id=1, source_target_pairs={{0,32},{32,0},{1,33},{33,1},{2,34},{34,2},{3,35},{35,3},{4,36},{36... | collective-permute-start | bytes 1966088 | tf_op jit(solution)/shard_map/ppermute | solution.py:301
  41.2 15.9 %collective-permute-start.1 = (bf16[256,1280]{1,0:T(8,128)(2,1)S(1)}, bf16[256,1280]{1,0:T(8,128)(2,1)S(1)}, u32[]{:S(2)}, u32[]{:S(2)}) collective-permute-start(bf16[256,1280]{1,0:T(8,128)(2,1)S(1)} %bitcast.41), channel_id=1, source_target_pairs={{0,192},{64,0},{128,64},{192,128},{1,193},{65,1},{129,65},{193,129... | collective-permute-start | bytes 1966088 | tf_op jit(solution)/shard_map/ppermute | solution.py:301
  44.2 16.7 %collective-permute-start = (bf16[256,1280]{1,0:T(8,128)(2,1)S(1)}, bf16[256,1280]{1,0:T(8,128)(2,1)S(1)}, u32[]{:S(2)}, u32[]{:S(2)}) collective-permute-start(bf16[256,1280]{1,0:T(8,128)(2,1)S(1)} %bitcast.42), channel_id=1, source_target_pairs={{0,64},{64,128},{128,192},{192,0},{1,65},{65,129},{129,193},{193,1... | collective-permute-start | bytes 1966088 | tf_op jit(solution)/shard_map/ppermute | solution.py:301
  57.1 15.9 %copy-start.14 = (bf16[256,1280]{1,0:T(8,128)(2,1)}, bf16[256,1280]{1,0:T(8,128)(2,1)S(1)}, u32[]{:S(2)}) copy-start(bf16[256,1280]{1,0:T(8,128)(2,1)S(1)} %collective-permute-done.1.refs_2_) | copy-start | bytes 1966084
  57.1 11.9 %collective-permute-start.6 = (bf16[128,1280]{1,0:T(8,128)(2,1)S(1)}, bf16[128,1280]{1,0:T(8,128)(2,1)}, u32[]{:S(2)}, u32[]{:S(2)}) collective-permute-start(bf16[128,1280]{1,0:T(8,128)(2,1)S(1)} %slice.69), channel_id=1, source_target_pairs={{0,192},{64,0},{128,64},{192,128},{1,193},{65,1},{129,65},{193,129... | collective-permute-start | bytes 983048 | tf_op jit(solution)/shard_map/ppermute | solution.py:301
  60.9 12.1 %copy-start.16 = (bf16[256,1280]{1,0:T(8,128)(2,1)}, bf16[256,1280]{1,0:T(8,128)(2,1)S(1)}, u32[]{:S(2)}) copy-start(bf16[256,1280]{1,0:T(8,128)(2,1)S(1)} %collective-permute-done.refs_1_) | copy-start | bytes 1966084
  60.9 12.0 %collective-permute-start.5 = (bf16[128,1280]{1,0:T(8,128)(2,1)S(1)}, bf16[128,1280]{1,0:T(8,128)(2,1)}, u32[]{:S(2)}, u32[]{:S(2)}) collective-permute-start(bf16[128,1280]{1,0:T(8,128)(2,1)S(1)} %slice.68), channel_id=1, source_target_pairs={{0,64},{64,128},{128,192},{192,0},{1,65},{65,129},{129,193},{193,1... | collective-permute-start | bytes 983048 | tf_op jit(solution)/shard_map/ppermute | solution.py:301
  61.0 12.6 %collective-permute-start.12 = (f32[72,128]{1,0:T(8,128)S(1)}, f32[72,128]{1,0:T(8,128)S(1)}, u32[]{:S(2)}, u32[]{:S(2)}) collective-permute-start(f32[72,128]{1,0:T(8,128)S(1)} %pad_maximum_fusion.near), channel_id=1, source_target_pairs={{0,32},{32,0},{1,33},{33,1},{2,34},{34,2},{3,35},{35,3},{4,36},{36... | collective-permute-start | bytes 110600 | tf_op jit(solution)/shard_map/ppermute | solution.py:301
  61.9 19.9 %collective-permute-start.4 = (bf16[256,1280]{1,0:T(8,128)(2,1)}, bf16[256,1280]{1,0:T(8,128)(2,1)}, u32[]{:S(2)}, u32[]{:S(2)}) collective-permute-start(bf16[256,1280]{1,0:T(8,128)(2,1)} %collective-permute-done.2.refs_3_), channel_id=1, source_target_pairs={{0,192},{64,0},{128,64},{192,128},{1,193},{65,1},{129,65},{193,129... | collective-permute-start | bytes 1966088 | tf_op jit(solution)/shard_map/ppermute | solution.py:301
  65.1 18.4 %collective-permute-start.3 = (bf16[256,1280]{1,0:T(8,128)(2,1)}, bf16[256,1280]{1,0:T(8,128)(2,1)}, u32[]{:S(2)}, u32[]{:S(2)}) collective-permute-start(bf16[256,1280]{1,0:T(8,128)(2,1)} %collective-permute-done.2.refs_3_), channel_id=1, source_target_pairs={{0,64},{64,128},{128,192},{192,0},{1,65},{65,129},{129,193},{193,1... | collective-permute-start | bytes 1966088 | tf_op jit(solution)/shard_map/ppermute | solution.py:301
  69.0 11.3 %collective-permute-start.8 = (bf16[128,1280]{1,0:T(8,128)(2,1)}, bf16[128,1280]{1,0:T(8,128)(2,1)}, u32[]{:S(2)}, u32[]{:S(2)}) collective-permute-start(bf16[128,1280]{1,0:T(8,128)(2,1)} %collective-permute-done.6.refs_7_), channel_id=1, source_target_pairs={{0,32},{32,0},{1,33},{33,1},{2,34},{34,2},{3,35},{35,3},{4,36},{36... | collective-permute-start | bytes 983048 | tf_op jit(solution)/shard_map/ppermute | solution.py:301
  72.9 8.9 %collective-permute-start.7 = (bf16[128,1280]{1,0:T(8,128)(2,1)}, bf16[128,1280]{1,0:T(8,128)(2,1)}, u32[]{:S(2)}, u32[]{:S(2)}) collective-permute-start(bf16[128,1280]{1,0:T(8,128)(2,1)} %collective-permute-done.5.refs_6_), channel_id=1, source_target_pairs={{0,32},{32,0},{1,33},{33,1},{2,34},{34,2},{3,35},{35,3},{4,36},{36... | collective-permute-start | bytes 983048 | tf_op jit(solution)/shard_map/ppermute | solution.py:301
  73.6 9.9 %copy-start.3 = (bf16[32,8,1280]{2,1,0:T(8,128)(2,1)S(1)}, bf16[32,8,1280]{2,1,0:T(8,128)(2,1)}, u32[]{:S(2)}) copy-start(bf16[32,8,1280]{2,1,0:T(8,128)(2,1)} %copy-done.2) | copy-start | bytes 1966084
  73.6 1.2 copy-start.11
  74.8 1.1 copy-start.13
  75.9 1.3 copy-start.19
  77.2 1.3 copy-start.21
  78.5 5.0 %copy-start.15 = (bf16[256,1280]{1,0:T(8,128)(2,1)S(1)}, bf16[256,1280]{1,0:T(8,128)(2,1)}, u32[]{:S(2)}) copy-start(bf16[256,1280]{1,0:T(8,128)(2,1)} %copy-done.14) | copy-start | bytes 1966084
  78.5 5.0 %copy-start.17 = (bf16[256,1280]{1,0:T(8,128)(2,1)S(1)}, bf16[256,1280]{1,0:T(8,128)(2,1)}, u32[]{:S(2)}) copy-start(bf16[256,1280]{1,0:T(8,128)(2,1)} %copy-done.16) | copy-start | bytes 1966084
  93.7 42.0 %copy-start.4 = (bf16[512,2560]{1,0:T(8,128)(2,1)}, bf16[512,2560]{1,0:T(8,128)(2,1)S(1)}, u32[]{:S(2)}) copy-start(bf16[512,2560]{1,0:T(8,128)(2,1)S(1)} %get-tuple-element.37.rows) | copy-start | bytes 7864324
  93.7 41.9 %copy-start.6 = (bf16[512,2560]{1,0:T(8,128)(2,1)}, bf16[512,2560]{1,0:T(8,128)(2,1)S(1)}, u32[]{:S(2)}) copy-start(bf16[512,2560]{1,0:T(8,128)(2,1)S(1)} %get-tuple-element.38.douts) | copy-start | bytes 7864324
  93.8 41.9 %copy-start.24 = (bf16[512,256]{1,0:T(8,128)(2,1)}, bf16[512,256]{1,0:T(8,128)(2,1)S(1)}, u32[]{:S(2)}) copy-start(bf16[512,256]{1,0:T(8,128)(2,1)S(1)} %get-tuple-element.40.pre_grad) | copy-start | bytes 786436
  139.0 21.2 %all-to-all-start.2 = ((bf16[32,8,640]{2,1,0:T(8,128)(2,1)}), bf16[32,8,640]{2,1,0:T(8,128)(2,1)S(1)}, u32[]{:S(2)}, u32[]{:S(2)}) async-start(bf16[32,8,640]{2,1,0:T(8,128)(2,1)} %bitcast.23), calls=%async_computation.2 | async-start | bytes 655360 | tf_op jit(solution)/shard_map/all_to_all | solution.py:380
  146.6 1.7 copy-start.5
  148.4 1.7 copy-start.7
  152.6 7.6 %copy-start.27 = (bf16[256,128]{1,0:T(8,128)(2,1)S(1)}, bf16[256,128]{1,0:T(8,128)(2,1)}, u32[]{:S(2)}) copy-start(bf16[256,128]{1,0:T(8,128)(2,1)} %copy-done.26) | copy-start | bytes 196612
  152.6 7.6 %copy-start.29 = (bf16[256,128]{1,0:T(8,128)(2,1)S(1)}, bf16[256,128]{1,0:T(8,128)(2,1)}, u32[]{:S(2)}) copy-start(bf16[256,128]{1,0:T(8,128)(2,1)} %copy-done.28) | copy-start | bytes 196612
  160.6 10.0 %collective-permute-start.19 = (bf16[64,640]{1,0:T(8,128)(2,1)S(1)}, bf16[64,640]{1,0:T(8,128)(2,1)S(1)}, u32[]{:S(2)}, u32[]{:S(2)}) collective-permute-start(bf16[64,640]{1,0:T(8,128)(2,1)S(1)} %shard_map.117.refs_0_), channel_id=1, source_target_pairs={{0,96},{32,64},{64,160},{96,128},{128,224},{160,192},{192,32},{224... | collective-permute-start | bytes 245768 | tf_op jit(solution)/shard_map/ppermute | solution.py:400
  161.4 10.6 %collective-permute-start.18 = (bf16[64,640]{1,0:T(8,128)(2,1)S(1)}, bf16[64,640]{1,0:T(8,128)(2,1)S(1)}, u32[]{:S(2)}, u32[]{:S(2)}) collective-permute-start(bf16[64,640]{1,0:T(8,128)(2,1)S(1)} %shard_map.117.refs_0_), channel_id=1, source_target_pairs={{0,64},{32,96},{64,128},{96,160},{128,192},{160,224},{192,0},{224,... | collective-permute-start | bytes 245768 | tf_op jit(solution)/shard_map/ppermute | solution.py:400
  161.6 19.3 %collective-permute-start.17 = (bf16[64,640]{1,0:T(8,128)(2,1)S(1)}, bf16[64,640]{1,0:T(8,128)(2,1)S(1)}, u32[]{:S(2)}, u32[]{:S(2)}) collective-permute-start(bf16[64,640]{1,0:T(8,128)(2,1)S(1)} %shard_map.117.refs_0_), channel_id=1, source_target_pairs={{0,160},{32,128},{64,224},{96,192},{128,32},{160,0},{192,96},{224,... | collective-permute-start | bytes 245768 | tf_op jit(solution)/shard_map/ppermute | solution.py:400
  167.8 13.1 %collective-permute-start.16 = (bf16[64,640]{1,0:T(8,128)(2,1)S(1)}, bf16[64,640]{1,0:T(8,128)(2,1)S(1)}, u32[]{:S(2)}, u32[]{:S(2)}) collective-permute-start(bf16[64,640]{1,0:T(8,128)(2,1)S(1)} %shard_map.117.refs_0_), channel_id=1, source_target_pairs={{0,128},{32,160},{64,192},{96,224},{128,0},{160,32},{192,64},{224,... | collective-permute-start | bytes 245768 | tf_op jit(solution)/shard_map/ppermute | solution.py:400
  167.8 13.1 %collective-permute-start.15 = (bf16[64,640]{1,0:T(8,128)(2,1)S(1)}, bf16[64,640]{1,0:T(8,128)(2,1)S(1)}, u32[]{:S(2)}, u32[]{:S(2)}) collective-permute-start(bf16[64,640]{1,0:T(8,128)(2,1)S(1)} %shard_map.117.refs_0_), channel_id=1, source_target_pairs={{0,224},{32,192},{64,32},{96,0},{128,96},{160,64},{192,160},{224,1... | collective-permute-start | bytes 245768 | tf_op jit(solution)/shard_map/ppermute | solution.py:400
  170.6 10.3 %collective-permute-start.14 = (bf16[64,640]{1,0:T(8,128)(2,1)S(1)}, bf16[64,640]{1,0:T(8,128)(2,1)S(1)}, u32[]{:S(2)}, u32[]{:S(2)}) collective-permute-start(bf16[64,640]{1,0:T(8,128)(2,1)S(1)} %shard_map.117.refs_0_), channel_id=1, source_target_pairs={{0,192},{32,224},{64,0},{96,32},{128,64},{160,96},{192,128},{224,1... | collective-permute-start | bytes 245768 | tf_op jit(solution)/shard_map/ppermute | solution.py:400
  172.0 8.9 %collective-permute-start.13 = (bf16[64,640]{1,0:T(8,128)(2,1)S(1)}, bf16[64,640]{1,0:T(8,128)(2,1)S(1)}, u32[]{:S(2)}, u32[]{:S(2)}) collective-permute-start(bf16[64,640]{1,0:T(8,128)(2,1)S(1)} %shard_map.117.refs_0_), channel_id=1, source_target_pairs={{0,32},{32,0},{64,96},{96,64},{128,160},{160,128},{192,224},{224,1... | collective-permute-start | bytes 245768 | tf_op jit(solution)/shard_map/ppermute | solution.py:400
  174.9 6.0 %copy-start.9 = (bf16[1,128,2560]{2,1,0:T(8,128)(2,1)S(1)}, bf16[1,128,2560]{2,1,0:T(8,128)(2,1)}, u32[]{:S(2)}) copy-start(bf16[1,128,2560]{2,1,0:T(8,128)(2,1)} %param.8) | copy-start | bytes 1966084
  174.9 6.0 %copy-start.31 = (f32[2560]{0:T(1024)S(1)}, f32[2560]{0:T(1024)}, u32[]{:S(2)}) copy-start(f32[2560]{0:T(1024)} %refs_10_.1) | copy-start | bytes 30724
  (8 other events, 6.2 us)

commit v4 on v2

v4 whole, which is shorter than its diff:
```python
import math

import jax
import jax.numpy as jnp
from jax import lax
from jax.experimental import pallas as pl
from jax.experimental.pallas import tpu as pltpu
from jax.sharding import Mesh
from jax.sharding import PartitionSpec as P

HEADS = 20
HEAD = 128
D = 2560
HALF = 1280
TOKENS = 128
KEYS = 128
UNITS = 256
EXPERTS = 32
ROWS_OF_CTX = 4
ROWS = 256
SLOTS = 256
CHUNK = 640
CTX = ("ctx_0", "ctx_1")
EPSILON = 1e-05
SCALE = HEAD**-0.5
BF16 = jnp.bfloat16
F32 = jnp.float32
VMEM_LIMIT = 40 * 2**20
VMEM_ALL = 60 * 2**20

VMEM = pl.BlockSpec(memory_space=pltpu.VMEM)
SMEM = pl.BlockSpec(memory_space=pltpu.SMEM)
ANY = pl.BlockSpec(memory_space=pl.ANY)


def call(kernel, ins, outs, scratch=(), flops=0, moved=0, places=None, limit=VMEM_LIMIT):
    return pl.pallas_call(
        kernel,
        in_specs=ins,
        out_specs=places or [VMEM] * len(outs),
        out_shape=outs,
        scratch_shapes=list(scratch),
        compiler_params=pltpu.CompilerParams(vmem_limit_bytes=limit),
        cost_estimate=pl.CostEstimate(flops=flops, bytes_accessed=moved, transcendentals=0),
    )


def shape(dims, dtype=BF16):
    return jax.ShapeDtypeStruct(dims, dtype)


def dot(a, b, dims=((1,), (0,))):
    return lax.dot_general(a, b, (dims, ((), ())), preferred_element_type=F32)


def iota(dims, axis):
    return lax.broadcasted_iota(jnp.int32, dims, axis)


def one(mask):
    return jnp.where(mask, 1.0, 0.0).astype(BF16)


def route_kernel(place, states, grads, gain, ids, gates, normed_out, send, table):
    y, x = place[0], place[1]
    inputs = states[...].astype(F32)
    inverse = lax.rsqrt(jnp.mean(inputs * inputs, axis=-1, keepdims=True) + EPSILON)
    normed_out[...] = (inputs * inverse * gain[...].reshape(1, D)).astype(BF16)
    expert = iota((ROWS, TOKENS), 0) // 8
    i = iota((ROWS, TOKENS), 0) % 8
    first = ids[0:1, :] == expert
    second = ids[1:2, :] == expert
    named = first | second
    before = one(iota((TOKENS, TOKENS), 0) < iota((TOKENS, TOKENS), 1))
    slot = dot(one(named), before).astype(jnp.int32)
    slot = jnp.where(named, slot, -1)
    table[...] = one(slot == 8 * x + i)
    mine = slot == 8 * x + 2 * y + i % 2
    gate = jnp.where(first, gates[0:1, :], 0.0) + jnp.where(second, gates[1:2, :], 0.0)
    gate = jnp.sum(jnp.where(mine, gate, 0.0), axis=1, keepdims=True)
    low = i < 4
    is_row = (i // 2) % 2 == 0
    row_low = one(mine & low & is_row)
    row_high = one(mine & (~low) & is_row)
    grad_low = one(mine & low & (~is_row))
    grad_high = one(mine & (~low) & (~is_row))
    rows = dot(row_low, normed_out[:, :HALF]) + dot(row_high, normed_out[:, HALF:])
    douts = dot(grad_low, grads[:, :HALF]) + dot(grad_high, grads[:, HALF:])
    send[...] = (rows + gate * douts).astype(BF16)


def scores_kernel(normed, grads, keys, values, weights_out, slopes_out, stats):
    for h in range(HEADS):
        at = slice(h * HEAD, (h + 1) * HEAD)
        s = dot(keys[:, at], normed[:, at], ((1,), (1,))) * SCALE
        peak = jnp.max(s, axis=0, keepdims=True)
        w = jnp.exp(s - peak)
        slopes = dot(values[:, at], grads[:, at], ((1,), (1,)))
        weights_out[h] = w
        slopes_out[h] = slopes
        stats[h : h + 1, :] = peak
        stats[24 + h : 25 + h, :] = jnp.sum(w, axis=0, keepdims=True)
        stats[48 + h : 49 + h, :] = jnp.sum(w * slopes, axis=0, keepdims=True)
    for part in range(3):
        at = 24 * part + HEADS
        stats[at : at + 4, :] = jnp.zeros((4, TOKENS), F32)


def merged(stats):
    peak = stats[0][:24]
    for one_side in stats[1:]:
        peak = jnp.maximum(peak, one_side[:24])
    total = inner = 0.0
    for one_side in stats:
        factor = jnp.exp(one_side[:24] - peak)
        total = total + one_side[24:48] * factor
        inner = inner + one_side[48:] * factor
    return jnp.concatenate([peak, total, inner], axis=0)


def score_grad_kernel(
    normed, grads, keys, weights, slopes, local, near, far, keys_grad, values_grad, query
):
    peak = jnp.maximum(near[0:24, :], far[0:24, :])
    near_factor = jnp.exp(near[0:24, :] - peak)
    far_factor = jnp.exp(far[0:24, :] - peak)
    total = near[24:48, :] * near_factor + far[24:48, :] * far_factor
    inner = near[48:72, :] * near_factor + far[48:72, :] * far_factor
    total = jnp.where(iota((24, TOKENS), 0) < HEADS, total, 1.0)
    factor = jnp.exp(local[0:24, :] - peak) / total
    delta = inner / total
    for h in range(HEADS):
        at = slice(h * HEAD, (h + 1) * HEAD)
        probs = weights[h] * factor[h : h + 1, :]
        score_grad = (probs * (slopes[h] - delta[h : h + 1, :])).astype(BF16)
        values_grad[:, at] = dot(probs.astype(BF16), grads[:, at]).astype(BF16)
        keys_grad[:, at] = (dot(score_grad, normed[:, at]) * SCALE).astype(BF16)
        query[h // 5, :, (h % 5) * HEAD : (h % 5 + 1) * HEAD] = (
            dot(score_grad, keys[:, at], ((0,), (0,))) * SCALE
        ).astype(BF16)


def expert_kernel(place, *refs):
    given, results, held = refs[:8], refs[8:14], refs[14:]
    shards, weights, sums = held[:4], held[4:6], held[6:10]
    inputs, spread, arrived, left = held[10:]
    y = place[0]
    landing = [*shards[:3], shards[3].at[0:128], shards[3].at[128:256], *weights]
    loads = [pltpu.make_async_copy(given[k], landing[k], arrived.at[k]) for k in range(7)]
    for load in loads:
        load.start()
    stores = [
        pltpu.make_async_copy(inputs, results[4], left.at[0]),
        pltpu.make_async_copy(spread, results[5], left.at[1]),
        *(
            pltpu.make_async_copy(sums[k], results[k].at[0:SLOTS, :], left.at[2 + k])
            for k in range(4)
        ),
        *(
            pltpu.make_async_copy(
                given[7].at[(y + k) % 4], results[k].at[SLOTS : SLOTS + TOKENS, :], left.at[6 + k]
            )
            for k in range(4)
        ),
    ]
    for store in stores[6:]:
        store.start()
    to, source = iota((ROWS, ROWS), 0), iota((ROWS, ROWS), 1)
    order = one(source == 8 * (to % 32) + to // 32)
    for k, step in enumerate((0, -1, 1, 2)):
        for load in loads[k : k + 1] if k < 3 else loads[3:5]:
            load.wait()
        row = (y + step + 4) % 4
        sorted_rows = dot(order, shards[k][...]).astype(BF16)
        for kind in range(2):
            for half in range(2):
                first = 128 * half + 64 * kind
                where = pl.ds(pl.multiple_of(SLOTS * kind + 64 * row, 64), 64)
                inputs[where, HALF * half : HALF * half + HALF] = sorted_rows[first : first + 64, :]
    stores[0].start()
    root = math.sqrt(2 / math.pi)
    even = iota((SLOTS, 2 * UNITS), 1) % 2 == 0
    for g in range(2):
        loads[5 + g].wait()
        v = dot(inputs[0:SLOTS, :], weights[g][...], ((1,), (1,)))
        act_grad = dot(inputs[SLOTS:, :], weights[g][...], ((1,), (1,)))
        act_grad = pltpu.roll(act_grad, 2 * UNITS - 1, 1)
        square = v * v
        t = jnp.tanh(root * (v + 0.044715 * (square * v)))
        act = 0.5 * v * (1.0 + t)
        slope = 0.5 * (1.0 + t) + 0.5 * v * (1.0 - t * t) * (root * (1.0 + 3 * 0.044715 * square))
        at = slice(2 * UNITS * g, 2 * UNITS * g + 2 * UNITS)
        spread[0:SLOTS, at] = jnp.where(even, act_grad * slope, 0.0).astype(BF16)
        spread[SLOTS:, at] = jnp.where(even, 0.0, pltpu.roll(act, 1, 1)).astype(BF16)
    stores[1].start()
    for k in (1, 3, 2, 0):
        lanes = pl.ds(pl.multiple_of(CHUNK * ((y + k) % 4), 128), CHUNK)
        part = dot(spread[0:SLOTS, 0 : 2 * UNITS], weights[0][:, lanes])
        part = part + dot(spread[0:SLOTS, 2 * UNITS :], weights[1][:, lanes])
        sums[k][...] = part.astype(BF16)
        stores[2 + k].start()
    for store in stores:
        store.wait()


def far_weights_kernel(inputs, spread, out):
    out[...] = dot(spread[:, 2 * UNITS :], inputs[...], ((0,), (0,))).astype(BF16)


def own_weights_kernel(inputs, spread, out):
    out[...] = dot(spread[:, : 2 * UNITS], inputs[...], ((0,), (0,)))


def add_kernel(own, far, out):
    out[...] = (own[...] + far[...].astype(F32)).astype(BF16)


def total_kernel(*refs):
    given, back, query, parts, arrived = refs[:4], *refs[4:]
    loads = [
        pltpu.make_async_copy(given[k], parts.at[k], arrived.at[k]) for k in range(ROWS_OF_CTX)
    ]
    for load in loads:
        load.start()
    for load in loads:
        load.wait()
    total = (parts[0].astype(F32) + parts[1].astype(F32)) + (
        parts[2].astype(F32) + parts[3].astype(F32)
    )
    to, source = iota((ROWS, ROWS), 0), iota((ROWS, ROWS), 1)
    order = one(source == 32 * (to % 8) + to // 8)
    back[...] = dot(order, total[0:SLOTS].astype(BF16)).astype(BF16)
    query[...] = total[SLOTS:]


def tokens_kernel(returned, table, query, out):
    out[...] = (dot(table[...], returned[...], ((0,), (0,))) + query[...]).astype(BF16)


def norm_grad_kernel(place, *refs):
    chunks, (states, grads, gain, out, total) = refs[:ROWS_OF_CTX], refs[ROWS_OF_CTX:]
    for k in range(ROWS_OF_CTX):
        lanes = pl.ds(pl.multiple_of(CHUNK * ((place[0] + k) % 4), 128), CHUNK)
        total[:, lanes] = chunks[k][...].astype(F32)
    inputs = states[...].astype(F32)
    inverse = lax.rsqrt(jnp.mean(inputs * inputs, axis=-1, keepdims=True) + EPSILON)
    unit = inputs * inverse
    g = total[...] * gain[...].reshape(1, D)
    g = g - unit * jnp.mean(g * unit, axis=-1, keepdims=True)
    out[...] = (grads[...].astype(F32) + inverse * g).astype(BF16)


def moved_by(array, axis, step):
    count = lax.axis_size(axis)
    return lax.ppermute(array, axis, [(k, (k + step) % count) for k in range(count)])


def on_device(
    states, out_grad, doc_keys, doc_values, norm_gain, expert_ids, gate_values, expert_weights
):
    states, grads, keys, values = states[0], out_grad[0], doc_keys[0], doc_values[0]
    y, x = lax.axis_index("ctx_0"), lax.axis_index("ctx_1")
    place = jnp.stack([y, x]).astype(jnp.int32)
    far_experts = moved_by(expert_weights, "ctx_1", 1).reshape(2 * UNITS, D)
    own_experts = expert_weights.reshape(2 * UNITS, D)
    normed, send, table = call(
        route_kernel,
        [SMEM] + [VMEM] * 5,
        [shape((TOKENS, D)), shape((ROWS, HALF)), shape((ROWS, TOKENS))],
        flops=2 * 4 * ROWS * TOKENS * HALF,
        moved=3 * 2**20,
        limit=VMEM_ALL,
    )(place, states, grads, norm_gain, expert_ids[0].T, gate_values[0].T)
    own = lax.all_to_all(
        send.reshape(EXPERTS, 8, HALF), "exp", split_axis=0, concat_axis=0, tiled=True
    ).reshape(ROWS, HALF)

    weights, slopes, stats = call(
        scores_kernel,
        [VMEM] * 4,
        [shape((HEADS, KEYS, TOKENS), F32), shape((HEADS, KEYS, TOKENS), F32), shape((72, TOKENS), F32)],
        flops=2 * 2 * KEYS * TOKENS * D,
        moved=5 * 2**20,
    )(normed, grads, keys, values)
    near = merged([stats] + [moved_by(stats, "ctx_0", k) for k in (1, 2, 3)])
    far = moved_by(near, "ctx_1", 1)
    keys_grad, values_grad, query_parts = call(
        score_grad_kernel,
        [VMEM] * 8,
        [shape((KEYS, D)), shape((KEYS, D)), shape((ROWS_OF_CTX, TOKENS, CHUNK))],
        flops=3 * 2 * KEYS * TOKENS * D,
        moved=6 * 2**20,
    )(normed, grads, keys, weights, slopes, stats, near, far)

    up, down = moved_by(own, "ctx_0", 1), moved_by(own, "ctx_0", 3)
    across = [moved_by(up[:128], "ctx_0", 1), moved_by(down[128:], "ctx_0", 3)]
    *sums, inputs, spread = call(
        expert_kernel,
        [SMEM] + [ANY] * 8,
        [
            *[shape((SLOTS + TOKENS, CHUNK))] * 4,
            shape((2 * SLOTS, D)),
            shape((2 * SLOTS, 4 * UNITS)),
        ],
        [
            *[pltpu.VMEM((ROWS, HALF), BF16)] * 4,
            *[pltpu.VMEM((2 * UNITS, D), BF16)] * 2,
            *[pltpu.VMEM((SLOTS, CHUNK), BF16)] * 4,
            pltpu.VMEM((2 * SLOTS, D), BF16),
            pltpu.VMEM((2 * SLOTS, 4 * UNITS), BF16),
            pltpu.SemaphoreType.DMA((7,)),
            pltpu.SemaphoreType.DMA((10,)),
        ],
        places=[ANY] * 6,
        flops=2 * 6 * SLOTS * 2 * UNITS * D,
        moved=16 * 2**20,
    )(place, own, up, down, *across, own_experts, far_experts, query_parts)

    parts = [sums[0]] + [moved_by(sums[k], "ctx_0", k) for k in (1, 2, 3)]
    [far_grad] = call(
        far_weights_kernel,
        [VMEM] * 2,
        [shape((2 * UNITS, D))],
        flops=2 * 2 * SLOTS * 2 * UNITS * D,
        moved=6 * 2**20,
    )(inputs, spread)
    far_grad = moved_by(far_grad, "ctx_1", 1)
    [own_grad] = call(
        own_weights_kernel,
        [VMEM] * 2,
        [shape((2 * UNITS, D), F32)],
        flops=2 * 2 * SLOTS * 2 * UNITS * D,
        moved=8 * 2**20,
    )(inputs, spread)
    back, query = call(
        total_kernel,
        [ANY] * 4,
        [shape((ROWS, CHUNK)), shape((TOKENS, CHUNK), F32)],
        [pltpu.VMEM((ROWS_OF_CTX, SLOTS + TOKENS, CHUNK), BF16), pltpu.SemaphoreType.DMA((4,))],
        moved=3 * 2**20,
    )(*parts)
    returned = lax.all_to_all(
        back.reshape(EXPERTS, 8, CHUNK), "exp", split_axis=0, concat_axis=0, tiled=True
    ).reshape(ROWS, CHUNK)
    [partial] = call(tokens_kernel, [VMEM] * 3, [shape((TOKENS, CHUNK))], moved=2**20)(
        returned, table, query
    )
    partner = moved_by(partial, "ctx_1", 1)
    chunk = (partial.astype(F32) + partner.astype(F32)).astype(BF16)
    chunks = [chunk] + [moved_by(chunk, "ctx_0", 4 - k) for k in (1, 2, 3)]
    [states_grad] = call(
        norm_grad_kernel,
        [SMEM] + [VMEM] * 7,
        [shape((TOKENS, D))],
        [pltpu.VMEM((TOKENS, D), F32)],
        moved=3 * 2**20,
    )(place, *chunks, states, grads, norm_gain)
    [weights_grad] = call(add_kernel, [VMEM] * 2, [shape((2 * UNITS, D))], moved=10 * 2**20)(
        own_grad, far_grad
    )
    weights_grad = weights_grad.reshape(1, UNITS, 2, D)
    return states_grad[None], keys_grad[None], values_grad[None], weights_grad


def solution(mesh):
    finer = Mesh(mesh.devices.reshape(4, 2, mesh.shape["exp"]), (*CTX, "exp"))
    return jax.shard_map(
        on_device,
        mesh=finer,
        in_specs=(
            P("exp", None, None),
            P("exp", None, None),
            P("exp", CTX, None),
            P("exp", CTX, None),
            P(),
            P("exp", None, None),
            P("exp", None, None),
            P("exp", CTX, None, None),
        ),
        out_specs=(
            P("exp", None, None),
            P("exp", CTX, None),
            P("exp", CTX, None),
            P("exp", CTX, None, None),
        ),
        check_vma=False,
    )
```

time: 195 us -> 224 us (1.15)
  waiting for transfers between devices: 18.9 us -> 44 us
  local copies, waits for them, and re-layouts: 16.5 us -> 31.7 us
  Pallas kernels: 35.1 us -> 24.9 us
    all_to_all x1, blocking collectives: 30.2 us -> 60.5 us  [on_device(): lax.all_to_all(send.reshape(EXPERTS, 8, HALF), 'exp', split_axis=0, conca...]
    ppermute x13 -> x17, waiting for transfers between devices: 16.8 us -> 44 us  [moved_by(): lax.ppermute(array, axis, [(k, (k + step) % count) for k in range(count)])]
    all_gather x2 -> x0, blocking collectives: 20.6 us -> none  [the longest x1 13.8 us: on_device(): lax.all_gather(lax.all_gather(total, 'ctx_1'), 'ctx_0')]
    reshape x1 -> x3, local copies, waits for them, and re-layouts: 1.31 us -> 14.6 us  [the longest x1 6.66 us: on_device(): far_experts = moved_by(expert_weights, 'ctx_1', 1).reshape(2 * UNITS, D)]
    unnamed x27 -> x46, local copies, waits for them, and re-layouts: 5.57 us -> 15.6 us
    all_to_all x1, blocking collectives: 43.5 us -> 34.2 us  [on_device(): lax.all_to_all(back.reshape(EXPERTS, 8, CHUNK), 'exp', split_axis=0, conc...]
    slice x3 -> x0, local copies, waits for them, and re-layouts: 5.36 us -> none  [the longest x1 3.71 us: on_device(): w_in, w_out = (expert_weights[0, :, 0, :], expert_weights[0, :, 1, :])]
    pallas_call x5 -> x7, Pallas kernels: 23 us -> 18.7 us  [the longest x1 10.8 us: on_device(): call(expert_kernel, [SMEM] + [ANY] * 8, [*[shape((SLOTS + TOKENS, CHUNK))...]
  transfers between devices with their start and end apart: 14 -> 17, of which waited for: 5 -> 8; matrix products, arithmetic and copies ran while one was open for 8% -> 6% of each run, Pallas kernels for 7% -> 5%
where the time goes in v4:
time: 224 us; the launch traced here: 223 us
  blocking collectives  94.7 us (42%)
  waiting for transfers between devices  44 us (20%)
  local copies, waits for them, and re-layouts  31.7 us (14%)
  starting transfers between devices  26.1 us (12%)
  Pallas kernels  24.9 us (11%)
    all_to_all x1, blocking collectives, on_device(): lax.all_to_all(send.reshape(EXPERTS, 8, HALF), 'exp', split_axis=0, conca...  60.5 us
    ppermute x17, waiting for transfers between devices, moved_by(): lax.ppermute(array, axis, [(k, (k + step) % count) for k in range(count)])  44 us
    all_to_all x1, blocking collectives, on_device(): lax.all_to_all(back.reshape(EXPERTS, 8, CHUNK), 'exp', split_axis=0, conc...  34.2 us
    ppermute x17, starting transfers between devices, moved_by(): lax.ppermute(array, axis, [(k, (k + step) % count) for k in range(count)])  26.1 us
    unnamed x46, local copies, waits for them, and re-layouts  15.6 us
    pallas_call x1, Pallas kernels, on_device(): call(expert_kernel, [SMEM] + [ANY] * 8, [*[shape((SLOTS + TOKENS, CHUNK))...  10.8 us
    reshape x1, local copies, waits for them, and re-layouts, on_device(): far_experts = moved_by(expert_weights, 'ctx_1', 1).reshape(2 * UNITS, D)  6.66 us
    reshape x1, local copies, waits for them, and re-layouts, on_device(): own_experts = expert_weights.reshape(2 * UNITS, D)  5.49 us
  transfers between devices with their start and end apart: 17, of which 8 were waited for; matrix products, arithmetic and copies ran while one was open for 6% of the time, Pallas kernels for 5%

profile of v4, /device:TPU:32, one launch (start us, length us, event | category | flops | bytes accessed | tf_op | source)
XLA Modules:
  0.0 222.9 jit_solution(9566806023985113197)
XLA Ops:
  0.7 3.1 %collective-permute-start.4 = (bf16[1,256,2,2560]{3,2,1,0:T(2,128)(2,1)}, bf16[1,256,2,2560]{3,2,1,0:T(2,128)(2,1)}, u32[]{:S(2)}, u32[]{:S(2)}) collective-permute-start(bf16[1,256,2,2560]{3,2,1,0:T(2,128)(2,1)} %param.15), channel_id=1, source_target_pairs={{0,32},{32,0},{1,33},{33,1},{2,34},{34,2},{3,35},{35,3},{4,36},{36... | collective-permute-start | bytes 7864328 | tf_op jit(solution)/shard_map/ppermute | solution.py:255
  3.8 0.6 pad_add_fusion.place
  4.4 3.3 %shard_map.111 = (bf16[128,2560]{1,0:T(8,128)(2,1)}, bf16[256,1280]{1,0:T(8,128)(2,1)}, bf16[256,128]{1,0:T(8,128)(2,1)}) custom-call(s32[2]{0:T(128)} %pad_add_fusion.place, bf16[128,2560]{1,0:T(8,128)(2,1)} %bitcast.23, bf16[128,2560]{1,0:T(8,128)(2,1)} %bitcast.19, f32[2560]{0:T(1024)} %refs_6_.1, s32[2,128]{1,0:T(2,128)} %bitcast.35, f32[2,128]{1,0:T(2,128)} %bitcast.36), custom_call_target="tpu_custom_call" | custom-call | flops 335544320 | bytes 3145728 | tf_op jit(solution)/shard_map/pallas_call | solution.py:266
  7.7 60.5 %all_to_all.10 = bf16[32,8,1280]{2,1,0:T(8,128)(2,1)S(1)} all-to-all(bf16[32,8,1280]{2,1,0:T(8,128)(2,1)} %bitcast.33), channel_id=1, replica_groups=mesh['ctx_0'=4,'ctx_1'=2,'exp'=32] {'exp'}, dimensions={0} | all-to-all | bytes 1310720 | tf_op jit(solution)/shard_map/all_to_all | solution.py:274
  68.2 3.0 %collective-permute-start.1 = (bf16[256,1280]{1,0:T(8,128)(2,1)S(1)}, bf16[256,1280]{1,0:T(8,128)(2,1)S(1)}, u32[]{:S(2)}, u32[]{:S(2)}) collective-permute-start(bf16[256,1280]{1,0:T(8,128)(2,1)S(1)} %bitcast.29), channel_id=1, source_target_pairs={{0,192},{64,0},{128,64},{192,128},{1,193},{65,1},{129,65},{193,129... | collective-permute-start | bytes 1966088 | tf_op jit(solution)/shard_map/ppermute | solution.py:255
  71.2 1.1 copy-done.5
  72.3 1.1 shard_map.112
  73.4 1.1 copy-done.9
  74.5 3.2 %collective-permute-start.7 = (f32[72,128]{1,0:T(8,128)S(1)}, f32[72,128]{1,0:T(8,128)S(1)}, u32[]{:S(2)}, u32[]{:S(2)}) collective-permute-start(f32[72,128]{1,0:T(8,128)S(1)} %get-tuple-element.25.local), channel_id=1, source_target_pairs={{0,192},{64,0},{128,64},{192,128},{1,193},{65,1},{129,65},{193,129... | collective-permute-start | bytes 110600 | tf_op jit(solution)/shard_map/ppermute | solution.py:255
  77.7 8.9 %collective-permute-done.7 = f32[72,128]{1,0:T(8,128)S(1)} collective-permute-done((f32[72,128]{1,0:T(8,128)S(1)}, f32[72,128]{1,0:T(8,128)S(1)}, u32[]{:S(2)}, u32[]{:S(2)}) %collective-permute-start.7) | collective-permute-done | bytes 36896 | tf_op jit(solution)/shard_map/ppermute | solution.py:255
  86.6 0.5 collective-permute-start.5
  87.2 1.1 collective-permute-done.6
  88.3 3.9 %collective-permute-done.5 = f32[72,128]{1,0:T(8,128)S(1)} collective-permute-done((f32[72,128]{1,0:T(8,128)S(1)}, f32[72,128]{1,0:T(8,128)S(1)}, u32[]{:S(2)}, u32[]{:S(2)}) %collective-permute-start.5) | collective-permute-done | bytes 36896 | tf_op jit(solution)/shard_map/ppermute | solution.py:255
  92.3 0.7 slice.61
  93.0 0.9 copy-done.14
  93.9 2.0 collective-permute-start.3
  95.9 0.7 slice.60
  96.7 0.8 copy-done.16
  97.6 2.6 %collective-permute-start.8 = (f32[72,128]{1,0:T(8,128)S(1)}, f32[72,128]{1,0:T(8,128)S(1)}, u32[]{:S(2)}, u32[]{:S(2)}) collective-permute-start(f32[72,128]{1,0:T(8,128)S(1)} %pad_maximum_fusion.near), channel_id=1, source_target_pairs={{0,32},{32,0},{1,33},{33,1},{2,34},{34,2},{3,35},{35,3},{4,36},{36... | collective-permute-start | bytes 110600 | tf_op jit(solution)/shard_map/ppermute | solution.py:255
  100.2 5.5 %reshape.31.refs_5_ = bf16[512,2560]{1,0:T(8,128)(2,1)S(1)} reshape(bf16[1,256,2,2560]{3,2,1,0:T(2,128)(2,1)} %param.15) | data formatting | bytes 5242880 | tf_op jit(solution)/shard_map/reshape | solution.py:265
  105.7 1.1 copy-done.4
  106.8 1.1 copy-done.6
  107.9 1.3 copy-done.8
  109.2 1.3 copy-done.10
  110.5 1.8 shard_map.113
  112.3 0.8 copy-done.21
  113.1 6.7 %reshape.32.refs_6_ = bf16[512,2560]{1,0:T(8,128)(2,1)} reshape(bf16[1,256,2,2560]{3,2,1,0:T(2,128)(2,1)} %collective-permute-done.4) | data formatting | bytes 5242880 | tf_op jit(solution)/shard_map/reshape | solution.py:264
  119.8 1.7 copy-done.1
  121.5 1.1 copy-done.13
  122.6 1.1 copy-done.15
  123.7 1.1 copy-done.17
  124.8 1.1 copy-done.22
  125.9 10.8 %shard_map.114 = (bf16[384,640]{1,0:T(8,128)(2,1)S(1)}, bf16[384,640]{1,0:T(8,128)(2,1)S(1)}, bf16[384,640]{1,0:T(8,128)(2,1)S(1)}, bf16[384,640]{1,0:T(8,128)(2...) custom-call(s32[2]{0:T(128)S(1)} %copy-done.20, bf16[256,1280]{1,0:T(8,128)(2,1)S(1)} %bitcast.31, ...), custom_call_target="tpu_custom_call" | custom-call | flops 4026531840 | bytes 16777216 | tf_op jit(solution)/shard_map/pallas_call | solution.py:297
  136.7 1.6 shard_map.119
  138.3 1.3 collective-permute-start.16
  139.6 4.7 %collective-permute-start.10 = (bf16[384,640]{1,0:T(8,128)(2,1)S(1)}, bf16[384,640]{1,0:T(8,128)(2,1)S(1)}, u32[]{:S(2)}, u32[]{:S(2)}) collective-permute-start(bf16[384,640]{1,0:T(8,128)(2,1)S(1)} %get-tuple-element.29), channel_id=1, source_target_pairs={{0,128},{64,192},{128,0},{192,64},{1,129},{65,193},{129,1},{193,65... | collective-permute-start | bytes 1474568 | tf_op jit(solution)/shard_map/ppermute | solution.py:255
  144.3 9.8 %collective-permute-done.9.refs_1_ = bf16[384,640]{1,0:T(8,128)(2,1)S(1)} collective-permute-done((bf16[384,640]{1,0:T(8,128)(2,1)S(1)}, bf16[384,640]{1,0:T(8,128)(2,1)S(1)}, u32[]{:S(2)}, u32[]{:S(2)}) %collective-permute-start.9) | collective-permute-done | bytes 491552 | tf_op jit(solution)/shard_map/ppermute | solution.py:255
  154.1 8.4 %collective-permute-done.10.refs_2_ = bf16[384,640]{1,0:T(8,128)(2,1)S(1)} collective-permute-done((bf16[384,640]{1,0:T(8,128)(2,1)S(1)}, bf16[384,640]{1,0:T(8,128)(2,1)S(1)}, u32[]{:S(2)}, u32[]{:S(2)}) %collective-permute-start.10) | collective-permute-done | bytes 491552 | tf_op jit(solution)/shard_map/ppermute | solution.py:255
  162.5 1.8 shard_map.115
  164.3 34.2 %all_to_all.11 = bf16[32,8,640]{2,1,0:T(8,128)(2,1)S(1)} all-to-all(bf16[32,8,640]{2,1,0:T(8,128)(2,1)S(1)} %bitcast.32), channel_id=1, replica_groups=mesh['ctx_0'=4,'ctx_1'=2,'exp'=32] {'exp'}, dimensions={0} | all-to-all | bytes 655360 | tf_op jit(solution)/shard_map/all_to_all | solution.py:342
  198.7 1.1 collective-permute-start.12
  199.9 6.6 %collective-permute-done.12 = bf16[128,640]{1,0:T(8,128)(2,1)S(1)} collective-permute-done((bf16[128,640]{1,0:T(8,128)(2,1)S(1)}, bf16[128,640]{1,0:T(8,128)(2,1)S(1)}, u32[]{:S(2)}, u32[]{:S(2)}) %collective-permute-start.12) | collective-permute-done | bytes 163872 | tf_op jit(solution)/shard_map/ppermute | solution.py:255
  206.9 4.1 %collective-permute-start.14 = (bf16[128,640]{1,0:T(8,128)(2,1)S(1)}, bf16[128,640]{1,0:T(8,128)(2,1)S(1)}, u32[]{:S(2)}, u32[]{:S(2)}) collective-permute-start(bf16[128,640]{1,0:T(8,128)(2,1)S(1)} %add_convert_fusion.refs_0_), channel_id=1, source_target_pairs={{0,128},{64,192},{128,0},{192,64},{1,129},{65,193},{129,1},{193,65... | collective-permute-start | bytes 491528 | tf_op jit(solution)/shard_map/ppermute | solution.py:255
  211.0 1.6 shard_map.118.own
  212.6 1.3 collective-permute-done.15.refs_3_
  213.9 3.9 %collective-permute-done.14.refs_2_ = bf16[128,640]{1,0:T(8,128)(2,1)S(1)} collective-permute-done((bf16[128,640]{1,0:T(8,128)(2,1)S(1)}, bf16[128,640]{1,0:T(8,128)(2,1)S(1)}, u32[]{:S(2)}, u32[]{:S(2)}) %collective-permute-start.14) | collective-permute-done | bytes 163872 | tf_op jit(solution)/shard_map/ppermute | solution.py:255
  217.8 2.3 %shard_map.117 = bf16[128,2560]{1,0:T(8,128)(2,1)} custom-call(s32[2]{0:T(128)S(1)} %copy-done.20, bf16[128,640]{1,0:T(8,128)(2,1)S(1)} %add_convert_fusion.refs_0_, bf16[128,640]{1,0:T(8,128)(2,1)S(1)} %collective-permute-done.13.refs_1_, bf16[128,640]{1,0:T(8,128)(2,1)S(1)} %collective-permute-done.14.refs_2_, ...), custom_call_target="tpu_custom_call" | custom-call | bytes 3145728 | tf_op jit(solution)/shard_map/pallas_call | solution.py:351
  220.5 2.4 %reshape.35 = bf16[1,256,2,2560]{3,2,1,0:T(2,128)(2,1)} reshape(bf16[512,2560]{1,0:T(8,128)(2,1)S(1)} %shard_map.120) | data formatting | bytes 5242880 | tf_op jit(solution)/shard_map/reshape | solution.py:361
  (54 shorter events, 1.2 us)
Async XLA Ops:
  0.6 70.6 %copy-start = (bf16[1,128,2560]{2,1,0:T(8,128)(2,1)S(1)}, bf16[1,128,2560]{2,1,0:T(8,128)(2,1)}, u32[]{:S(2)}) copy-start(bf16[1,128,2560]{2,1,0:T(8,128)(2,1)} %param.9) | copy-start | bytes 1966084
  0.6 70.6 %copy-start.11 = (bf16[1,128,2560]{2,1,0:T(8,128)(2,1)S(1)}, bf16[1,128,2560]{2,1,0:T(8,128)(2,1)}, u32[]{:S(2)}) copy-start(bf16[1,128,2560]{2,1,0:T(8,128)(2,1)} %param.11) | copy-start | bytes 1966084
  0.7 70.6 %copy-start.3 = (bf16[1,128,2560]{2,1,0:T(8,128)(2,1)S(1)}, bf16[1,128,2560]{2,1,0:T(8,128)(2,1)}, u32[]{:S(2)}) copy-start(bf16[1,128,2560]{2,1,0:T(8,128)(2,1)} %param.10) | copy-start | bytes 1966084
  0.7 112.5 %collective-permute-start.4 = (bf16[1,256,2,2560]{3,2,1,0:T(2,128)(2,1)}, bf16[1,256,2,2560]{3,2,1,0:T(2,128)(2,1)}, u32[]{:S(2)}, u32[]{:S(2)}) collective-permute-start(bf16[1,256,2,2560]{3,2,1,0:T(2,128)(2,1)} %param.15), channel_id=1, source_target_pairs={{0,32},{32,0},{1,33},{33,1},{2,34},{34,2},{3,35},{35,3},{4,36},{36... | collective-permute-start | bytes 7864328 | tf_op jit(solution)/shard_map/ppermute | solution.py:255
  68.2 29.4 %copy-start.12 = (bf16[32,8,1280]{2,1,0:T(8,128)(2,1)}, bf16[32,8,1280]{2,1,0:T(8,128)(2,1)S(1)}, u32[]{:S(2)}) copy-start(bf16[32,8,1280]{2,1,0:T(8,128)(2,1)S(1)} %all_to_all.10) | copy-start | bytes 1966084
  68.2 24.1 %collective-permute-start.1 = (bf16[256,1280]{1,0:T(8,128)(2,1)S(1)}, bf16[256,1280]{1,0:T(8,128)(2,1)S(1)}, u32[]{:S(2)}, u32[]{:S(2)}) collective-permute-start(bf16[256,1280]{1,0:T(8,128)(2,1)S(1)} %bitcast.29), channel_id=1, source_target_pairs={{0,192},{64,0},{128,64},{192,128},{1,193},{65,1},{129,65},{193,129... | collective-permute-start | bytes 1966088 | tf_op jit(solution)/shard_map/ppermute | solution.py:255
  71.2 24.7 %collective-permute-start = (bf16[256,1280]{1,0:T(8,128)(2,1)S(1)}, bf16[256,1280]{1,0:T(8,128)(2,1)S(1)}, u32[]{:S(2)}, u32[]{:S(2)}) collective-permute-start(bf16[256,1280]{1,0:T(8,128)(2,1)S(1)} %bitcast.30), channel_id=1, source_target_pairs={{0,64},{64,128},{128,192},{192,0},{1,65},{65,129},{129,193},{193,1... | collective-permute-start | bytes 1966088 | tf_op jit(solution)/shard_map/ppermute | solution.py:255
  71.2 1.1 copy-start.5
  73.4 1.1 copy-start.9
  74.5 23.1 %copy-start.7 = (f32[20,128,128]{2,1,0:T(8,128)}, f32[20,128,128]{2,1,0:T(8,128)S(1)}, u32[]{:S(2)}) copy-start(f32[20,128,128]{2,1,0:T(8,128)S(1)} %get-tuple-element.23.weights) | copy-start | bytes 3932164
  74.5 12.2 %collective-permute-start.7 = (f32[72,128]{1,0:T(8,128)S(1)}, f32[72,128]{1,0:T(8,128)S(1)}, u32[]{:S(2)}, u32[]{:S(2)}) collective-permute-start(f32[72,128]{1,0:T(8,128)S(1)} %get-tuple-element.25.local), channel_id=1, source_target_pairs={{0,192},{64,0},{128,64},{192,128},{1,193},{65,1},{129,65},{193,129... | collective-permute-start | bytes 110600 | tf_op jit(solution)/shard_map/ppermute | solution.py:255
  77.7 10.6 %collective-permute-start.6 = (f32[72,128]{1,0:T(8,128)S(1)}, f32[72,128]{1,0:T(8,128)S(1)}, u32[]{:S(2)}, u32[]{:S(2)}) collective-permute-start(f32[72,128]{1,0:T(8,128)S(1)} %get-tuple-element.25.local), channel_id=1, source_target_pairs={{0,128},{64,192},{128,0},{192,64},{1,129},{65,193},{129,1},{193,65... | collective-permute-start | bytes 110600 | tf_op jit(solution)/shard_map/ppermute | solution.py:255
  86.6 5.6 %collective-permute-start.5 = (f32[72,128]{1,0:T(8,128)S(1)}, f32[72,128]{1,0:T(8,128)S(1)}, u32[]{:S(2)}, u32[]{:S(2)}) collective-permute-start(f32[72,128]{1,0:T(8,128)S(1)} %get-tuple-element.25.local), channel_id=1, source_target_pairs={{0,64},{64,128},{128,192},{192,0},{1,65},{65,129},{129,193},{193,1... | collective-permute-start | bytes 110600 | tf_op jit(solution)/shard_map/ppermute | solution.py:255
  93.0 0.9 copy-start.14
  93.9 25.9 %collective-permute-start.3 = (bf16[128,1280]{1,0:T(8,128)(2,1)}, bf16[128,1280]{1,0:T(8,128)(2,1)}, u32[]{:S(2)}, u32[]{:S(2)}) collective-permute-start(bf16[128,1280]{1,0:T(8,128)(2,1)} %slice.61), channel_id=1, source_target_pairs={{0,192},{64,0},{128,64},{192,128},{1,193},{65,1},{129,65},{193,129... | collective-permute-start | bytes 983048 | tf_op jit(solution)/shard_map/ppermute | solution.py:255
  96.7 0.8 copy-start.16
  97.5 22.3 %collective-permute-start.2 = (bf16[128,1280]{1,0:T(8,128)(2,1)}, bf16[128,1280]{1,0:T(8,128)(2,1)}, u32[]{:S(2)}, u32[]{:S(2)}) collective-permute-start(bf16[128,1280]{1,0:T(8,128)(2,1)} %slice.60), channel_id=1, source_target_pairs={{0,64},{64,128},{128,192},{192,0},{1,65},{65,129},{129,193},{193,1... | collective-permute-start | bytes 983048 | tf_op jit(solution)/shard_map/ppermute | solution.py:255
  97.6 8.1 %collective-permute-start.8 = (f32[72,128]{1,0:T(8,128)S(1)}, f32[72,128]{1,0:T(8,128)S(1)}, u32[]{:S(2)}, u32[]{:S(2)}) collective-permute-start(f32[72,128]{1,0:T(8,128)S(1)} %pad_maximum_fusion.near), channel_id=1, source_target_pairs={{0,32},{32,0},{1,33},{33,1},{2,34},{34,2},{3,35},{35,3},{4,36},{36... | collective-permute-start | bytes 110600 | tf_op jit(solution)/shard_map/ppermute | solution.py:255
  105.7 1.1 copy-start.4
  106.8 1.1 copy-start.6
  107.9 1.3 copy-start.8
  109.2 1.3 copy-start.10
  112.3 0.8 copy-start.21
  113.1 6.7 %copy-start.20 = (s32[2]{0:T(128)S(1)}, s32[2]{0:T(128)}, u32[]{:S(2)}) copy-start(s32[2]{0:T(128)} %pad_add_fusion.place) | copy-start | bytes 28
  119.8 1.7 copy-start.1
  121.5 1.1 copy-start.13
  122.6 1.1 copy-start.15
  123.7 1.1 copy-start.17
  124.8 1.1 copy-start.22
  138.3 60.2 %copy-start.18 = (bf16[256,128]{1,0:T(8,128)(2,1)S(1)}, bf16[256,128]{1,0:T(8,128)(2,1)}, u32[]{:S(2)}) copy-start(bf16[256,128]{1,0:T(8,128)(2,1)} %get-tuple-element.32.table) | copy-start | bytes 196612
  138.3 81.7 %collective-permute-start.16 = (bf16[512,2560]{1,0:T(8,128)(2,1)S(1)}, bf16[512,2560]{1,0:T(8,128)(2,1)S(1)}, u32[]{:S(2)}, u32[]{:S(2)}) collective-permute-start(bf16[512,2560]{1,0:T(8,128)(2,1)S(1)} %shard_map.119), channel_id=1, source_target_pairs={{0,32},{32,0},{1,33},{33,1},{2,34},{34,2},{3,35},{35,3},{4,36},{36... | collective-permute-start | bytes 7864328 | tf_op jit(solution)/shard_map/ppermute | solution.py:255
  139.6 14.5 %collective-permute-start.9 = (bf16[384,640]{1,0:T(8,128)(2,1)S(1)}, bf16[384,640]{1,0:T(8,128)(2,1)S(1)}, u32[]{:S(2)}, u32[]{:S(2)}) collective-permute-start(bf16[384,640]{1,0:T(8,128)(2,1)S(1)} %get-tuple-element.28), channel_id=1, source_target_pairs={{0,64},{64,128},{128,192},{192,0},{1,65},{65,129},{129,193},{193,1... | collective-permute-start | bytes 1474568 | tf_op jit(solution)/shard_map/ppermute | solution.py:255
  139.6 22.8 %collective-permute-start.10 = (bf16[384,640]{1,0:T(8,128)(2,1)S(1)}, bf16[384,640]{1,0:T(8,128)(2,1)S(1)}, u32[]{:S(2)}, u32[]{:S(2)}) collective-permute-start(bf16[384,640]{1,0:T(8,128)(2,1)S(1)} %get-tuple-element.29), channel_id=1, source_target_pairs={{0,128},{64,192},{128,0},{192,64},{1,129},{65,193},{129,1},{193,65... | collective-permute-start | bytes 1474568 | tf_op jit(solution)/shard_map/ppermute | solution.py:255
  144.3 18.2 %collective-permute-start.11 = (bf16[384,640]{1,0:T(8,128)(2,1)S(1)}, bf16[384,640]{1,0:T(8,128)(2,1)S(1)}, u32[]{:S(2)}, u32[]{:S(2)}) collective-permute-start(bf16[384,640]{1,0:T(8,128)(2,1)S(1)} %get-tuple-element.30), channel_id=1, source_target_pairs={{0,192},{64,0},{128,64},{192,128},{1,193},{65,1},{129,65},{193,129... | collective-permute-start | bytes 1474568 | tf_op jit(solution)/shard_map/ppermute | solution.py:255
  198.7 7.7 %collective-permute-start.12 = (bf16[128,640]{1,0:T(8,128)(2,1)S(1)}, bf16[128,640]{1,0:T(8,128)(2,1)S(1)}, u32[]{:S(2)}, u32[]{:S(2)}) collective-permute-start(bf16[128,640]{1,0:T(8,128)(2,1)S(1)} %shard_map.116), channel_id=1, source_target_pairs={{0,32},{32,0},{1,33},{33,1},{2,34},{34,2},{3,35},{35,3},{4,36},{36... | collective-permute-start | bytes 491528 | tf_op jit(solution)/shard_map/ppermute | solution.py:255
  206.5 11.3 %copy-start.2 = (bf16[1,128,2560]{2,1,0:T(8,128)(2,1)S(1)}, bf16[1,128,2560]{2,1,0:T(8,128)(2,1)}, u32[]{:S(2)}) copy-start(bf16[1,128,2560]{2,1,0:T(8,128)(2,1)} %param.8) | copy-start | bytes 1966084
  206.5 11.3 %copy-start.19 = (f32[2560]{0:T(1024)S(1)}, f32[2560]{0:T(1024)}, u32[]{:S(2)}) copy-start(f32[2560]{0:T(1024)} %refs_6_.1) | copy-start | bytes 30724
  206.5 7.4 %collective-permute-start.15 = (bf16[128,640]{1,0:T(8,128)(2,1)S(1)}, bf16[128,640]{1,0:T(8,128)(2,1)S(1)}, u32[]{:S(2)}, u32[]{:S(2)}) collective-permute-start(bf16[128,640]{1,0:T(8,128)(2,1)S(1)} %add_convert_fusion.refs_0_), channel_id=1, source_target_pairs={{0,64},{64,128},{128,192},{192,0},{1,65},{65,129},{129,193},{193,1... | collective-permute-start | bytes 491528 | tf_op jit(solution)/shard_map/ppermute | solution.py:255
  206.9 10.9 %collective-permute-start.14 = (bf16[128,640]{1,0:T(8,128)(2,1)S(1)}, bf16[128,640]{1,0:T(8,128)(2,1)S(1)}, u32[]{:S(2)}, u32[]{:S(2)}) collective-permute-start(bf16[128,640]{1,0:T(8,128)(2,1)S(1)} %add_convert_fusion.refs_0_), channel_id=1, source_target_pairs={{0,128},{64,192},{128,0},{192,64},{1,129},{65,193},{129,1},{193,65... | collective-permute-start | bytes 491528 | tf_op jit(solution)/shard_map/ppermute | solution.py:255
  211.0 6.7 %collective-permute-start.13 = (bf16[128,640]{1,0:T(8,128)(2,1)S(1)}, bf16[128,640]{1,0:T(8,128)(2,1)S(1)}, u32[]{:S(2)}, u32[]{:S(2)}) collective-permute-start(bf16[128,640]{1,0:T(8,128)(2,1)S(1)} %add_convert_fusion.refs_0_), channel_id=1, source_target_pairs={{0,192},{64,0},{128,64},{192,128},{1,193},{65,1},{129,65},{193,129... | collective-permute-start | bytes 491528 | tf_op jit(solution)/shard_map/ppermute | solution.py:255

commit v5 on v2

--- a/solution.py
+++ b/solution.py
@@ -18,27 +18,28 @@
 EXPERTS = 32
 CTX_COUNT = 8
 ROWS = 256
-SLOTS = 512
+SLOTS = 256
 CHUNK = 640
 CTX = ("ctx_0", "ctx_1")
 EPSILON = 1e-05
 SCALE = HEAD**-0.5
 BF16 = jnp.bfloat16
 F32 = jnp.float32
-VMEM_LIMIT = 56 * 2**20
+VMEM_LIMIT = 24 * 2**20
+VMEM_ALL = 60 * 2**20
 
 VMEM = pl.BlockSpec(memory_space=pltpu.VMEM)
 SMEM = pl.BlockSpec(memory_space=pltpu.SMEM)
 
 
-def call(kernel, ins, outs, scratch=(), flops=0, moved=0):
+def call(kernel, ins, outs, scratch=(), flops=0, moved=0, limit=VMEM_LIMIT):
     return pl.pallas_call(
         kernel,
         in_specs=ins,
         out_specs=[VMEM] * len(outs),
         out_shape=outs,
         scratch_shapes=list(scratch),
-        compiler_params=pltpu.CompilerParams(vmem_limit_bytes=VMEM_LIMIT),
+        compiler_params=pltpu.CompilerParams(vmem_limit_bytes=limit),
         cost_estimate=pl.CostEstimate(flops=flops, bytes_accessed=moved, transcendentals=0),
     )
 
@@ -63,7 +64,7 @@
     c = c_ref[0]
     x = states[...].astype(F32)
     inverse = lax.rsqrt(jnp.mean(x * x, axis=-1, keepdims=True) + EPSILON)
-    normed_out[...] = (x * inverse * gain[...]).astype(BF16)
+    normed_out[...] = (x * inverse * gain[...].reshape(1, D)).astype(BF16)
     expert = iota((ROWS, TOKENS), 0) // 8
     i = iota((ROWS, TOKENS), 0) % 8
     first = ids[0:1, :] == expert
@@ -156,20 +157,13 @@
     )
 
 
-def expert_kernel(at_ref, *refs):
-    shards, (w_in, w_out, query_pack), (sums, rows, douts, act, pre_grad) = refs[:10], refs[10:13], refs[13:]
+def experts_of(blocks, w_in, w_out, rows, douts, act, pre_grad, put):
     to, source = iota((ROWS, ROWS), 0), iota((ROWS, ROWS), 1)
     order = one(source == 8 * (to % 32) + to // 32)
-    whole, pieces = shards[:6], shards[6:]
-    blocks = [lambda s=s: s[...] for s in whole]
-    blocks += [
-        lambda k=k: jnp.concatenate([pieces[k][...], pieces[k + 1][...]], axis=0) for k in (0, 2)
-    ]
     for k, block in enumerate(blocks):
-        c = at_ref[k]
         sorted_rows = dot(order, block()).astype(BF16)
         for q in range(2):
-            where = pl.ds(pl.multiple_of(256 * q + 32 * c, 32), 32)
+            where = slice(128 * q + 32 * k, 128 * q + 32 * k + 32)
             for half in range(2):
                 lanes = slice(HALF * half, HALF * half + HALF)
                 first = 128 * half + 32 * q
@@ -184,21 +178,59 @@
     slope = 0.5 * (1.0 + t) + 0.5 * v * (1.0 - t * t) * (root * (1.0 + 3 * 0.044715 * square))
     pre_grad[...] = (act_grad * slope).astype(BF16)
     tails = dot(pre_grad[...], w_in[:, 2048:2560])
-    chunks = [dot(pre_grad[...], w_in[:, 256 * f : 256 * f + 256]) for f in range(CTX_COUNT)]
-    pack(
-        sums,
-        slice(0, 256),
-        lambda f: chunks[f][0:256],
-        lambda f: chunks[f][256:512],
-        lambda g: tails[0:256, 128 * g : 128 * g + 128],
-        lambda g: tails[256:512, 128 * g : 128 * g + 128],
-    )
-    sums[:, 256:320, :] = query_pack[...]
-
-
-def weights_kernel(rows, douts, act, pre_grad, grad_in, grad_out):
-    grad_in[...] = dot(pre_grad[...], rows[...], ((0,), (0,))).astype(BF16)
-    grad_out[...] = dot(act[...], douts[...], ((0,), (0,))).astype(BF16)
+    lane = iota((128, 128), 1)
+    for f in range(CTX_COUNT):
+        part = dot(pre_grad[...], w_in[:, 256 * f : 256 * f + 256])
+        put(f, slice(0, 256), part[0:128].astype(BF16))
+        put(f, slice(256, 512), part[128:256].astype(BF16))
+        tile = slice(128 * (f // 2), 128 * (f // 2) + 128)
+        a, b = tails[0:128, tile], tails[128:256, tile]
+        if f % 2 == 0:
+            tail = jnp.where(lane < 64, a, pltpu.roll(b, 64, 1))
+        else:
+            tail = jnp.where(lane < 64, pltpu.roll(a, 64, 1), b)
+        put(f, slice(512, 640), tail.astype(BF16))
+
+
+def early_kernel(own, up, down, partner, w_in, w_out, sums, rows, douts, act, pre_grad):
+    def put(f, lanes, value):
+        sums[f, :, lanes] = value
+
+    blocks = [lambda s=s: s[...] for s in (own, up, down, partner)]
+    experts_of(blocks, w_in, w_out, rows, douts, act, pre_grad, put)
+
+
+def late_kernel(at_ref, *refs):
+    shards, (w_in, w_out, early, query_pack) = refs[:6], refs[6:10]
+    sums, rows, douts, act, pre_grad = refs[10:]
+    where = [pl.ds(pl.multiple_of(32 * at_ref[k], 32), 32) for k in range(CTX_COUNT)]
+
+    def put(f, lanes, value):
+        for k in range(4):
+            sums[f, where[4 + k], lanes] = value[32 * k : 32 * k + 32]
+
+    blocks = [lambda s=s: s[...] for s in shards[:2]]
+    blocks += [
+        lambda k=k: jnp.concatenate([shards[k][...], shards[k + 1][...]], axis=0) for k in (2, 4)
+    ]
+    experts_of(blocks, w_in, w_out, rows, douts, act, pre_grad, put)
+    for f in range(CTX_COUNT):
+        for k in range(4):
+            sums[f, where[k], :] = early[f, 32 * k : 32 * k + 32, :]
+        sums[f, 256:320, :] = query_pack[f]
+
+
+def weights_kernel(*refs):
+    (early, late), out = (refs[:4], refs[4:8]), refs[8]
+    unit, column = iota((UNITS, 2 * UNITS), 0), iota((UNITS, 2 * UNITS), 1)
+    even, odd = one(column == 2 * unit), one(column == 2 * unit + 1)
+    terms = []
+    for rows, douts, act, pre_grad in (early, late):
+        terms.append((dot(pre_grad[...], even).astype(BF16), rows))
+        terms.append((dot(act[...], odd).astype(BF16), douts))
+    for n in range(D // 512):
+        lanes = slice(512 * n, 512 * n + 512)
+        out[:, lanes] = sum(dot(a, b[:, lanes], ((0,), (0,))) for a, b in terms).astype(BF16)
 
 
 def total_kernel(parts, back, query):
@@ -218,9 +250,13 @@
     tail = a[:, 512:640] + pltpu.roll(b[:, 512:640], 64, 1)
     lane = iota((64, 128), 1)
     tail = jnp.where(lane < 64, tail[0:64], pltpu.roll(tail[64:128], 64, 1))
-    out[:, 0:256] = (wide[0:64] + query[:, 0:256]).astype(BF16)
-    out[:, 256:512] = (wide[64:128] + query[:, 256:512]).astype(BF16)
-    out[:, 512:640] = (tail + query[:, 512:640]).astype(BF16)
+    left = (wide[0:64] + query[:, 0:256]).astype(BF16)
+    right = (wide[64:128] + query[:, 256:512]).astype(BF16)
+    tail = (tail + query[:, 512:640]).astype(BF16)
+    for f in range(CTX_COUNT):
+        out[f, :, 0:256] = left
+        out[f, :, 256:512] = right
+        out[f, :, 512:640] = tail
 
 
 def norm_grad_kernel(packs, states, grads, gain, out, total):
@@ -238,7 +274,7 @@
     x = states[...].astype(F32)
     inverse = lax.rsqrt(jnp.mean(x * x, axis=-1, keepdims=True) + EPSILON)
     unit = x * inverse
-    g = total[...] * gain[...]
+    g = total[...] * gain[...].reshape(1, D)
     g = g - unit * jnp.mean(g * unit, axis=-1, keepdims=True)
     out[...] = (grads[...].astype(F32) + inverse * g).astype(BF16)
 
@@ -252,7 +288,6 @@
     states, out_grad, doc_keys, doc_values, norm_gain, expert_ids, gate_values, expert_weights
 ):
     states, grads, keys, values = states[0], out_grad[0], doc_keys[0], doc_values[0]
-    gain = norm_gain.reshape(1, D)
     y, x = lax.axis_index("ctx_0"), lax.axis_index("ctx_1")
     here = (2 * y + x).astype(jnp.int32)
     normed, send, even, odd = call(
@@ -261,7 +296,8 @@
         [shape((TOKENS, D)), shape((ROWS, HALF)), shape((ROWS, TOKENS)), shape((ROWS, TOKENS))],
         flops=2 * 4 * ROWS * TOKENS * HALF,
         moved=3 * 2**20,
-    )(here.reshape(1), states, grads, gain, expert_ids[0].T, gate_values[0].T)
+        limit=VMEM_ALL,
+    )(here.reshape(1), states, grads, norm_gain, expert_ids[0].T, gate_values[0].T)
     own = lax.all_to_all(
         send.reshape(EXPERTS, 8, HALF), "exp", split_axis=0, concat_axis=0, tiled=True
     ).reshape(ROWS, HALF)
@@ -282,62 +318,64 @@
         [pltpu.VMEM((TOKENS, D), F32)],
         flops=3 * 2 * KEYS * TOKENS * D,
         moved=6 * 2**20,
+        limit=VMEM_ALL,
     )(normed, grads, keys, weights, slopes, stats, near, far)
 
     up, down = moved_by(own, "ctx_0", 1), moved_by(own, "ctx_0", 3)
     partner = moved_by(own, "ctx_1", 1)
     across = [moved_by(up[:128], "ctx_0", 1), moved_by(down[128:], "ctx_0", 3)]
     partner_up, partner_down = moved_by(partner, "ctx_0", 1), moved_by(partner, "ctx_0", 3)
-    partner_across = [
-        moved_by(partner_up[:128], "ctx_0", 1),
-        moved_by(partner_down[128:], "ctx_0", 3),
-    ]
-    shards = [own, up, down, partner, partner_up, partner_down, *across, *partner_across]
+    partner_across = [moved_by(piece, "ctx_1", 1) for piece in across]
     places = [(0, 0), (-1, 0), (1, 0), (0, 1), (-1, 1), (1, 1), (2, 0), (2, 1)]
     at = jnp.stack([2 * ((y + a + 4) % 4) + (x + b) % 2 for a, b in places]).astype(jnp.int32)
     w_in, w_out = expert_weights[0, :, 0, :], expert_weights[0, :, 1, :]
-    sums, rows, douts, act, pre_grad = call(
-        expert_kernel,
-        [SMEM] + [VMEM] * 13,
-        [
-            shape((CTX_COUNT, 320, CHUNK)),
-            shape((SLOTS, D)),
-            shape((SLOTS, D)),
-            shape((SLOTS, UNITS)),
-            shape((SLOTS, UNITS)),
-        ],
+    kept = [shape((SLOTS, D))] * 2 + [shape((SLOTS, UNITS))] * 2
+    early_sums, *early = call(
+        early_kernel,
+        [VMEM] * 6,
+        [shape((CTX_COUNT, SLOTS // 2, CHUNK)), *kept],
         flops=2 * 3 * SLOTS * UNITS * D,
-        moved=16 * 2**20,
-    )(at, *shards, w_in, w_out, query_pack)
+        moved=8 * 2**20,
+    )(own, up, down, partner, w_in, w_out)
+    sums, *late = call(
+        late_kernel,
+        [SMEM] + [VMEM] * 10,
+        [shape((CTX_COUNT, 320, CHUNK)), *kept],
+        flops=2 * 3 * SLOTS * UNITS * D,
+        moved=12 * 2**20,
+    )(at, partner_up, partner_down, *across, *partner_across, w_in, w_out, early_sums, query_pack)
     parts = lax.all_to_all(sums, CTX, split_axis=0, concat_axis=0, tiled=True)
-    grad_in, grad_out = call(
-        weights_kernel,
-        [VMEM] * 4,
-        [shape((UNITS, D)), shape((UNITS, D))],
-        flops=2 * 2 * SLOTS * UNITS * D,
-        moved=8 * 2**20,
-    )(rows, douts, act, pre_grad)
-    weights_grad = jnp.stack([grad_in, grad_out], axis=1)[None]
     back, query = call(
         total_kernel,
         [VMEM],
         [shape((ROWS, CHUNK)), shape((64, CHUNK), F32)],
         moved=4 * 2**20,
     )(parts)
+    late[3], back = lax.optimization_barrier((late[3], back))
     returned = lax.all_to_all(
         back.reshape(EXPERTS, 8, CHUNK), "exp", split_axis=0, concat_axis=0, tiled=True
     ).reshape(ROWS, CHUNK)
-    [total] = call(tokens_kernel, [VMEM] * 4, [shape((64, CHUNK))], moved=2**20)(
+    [weights_grad] = call(
+        weights_kernel,
+        [VMEM] * 8,
+        [shape((2 * UNITS, D))],
+        flops=2 * 4 * SLOTS * UNITS * D,
+        moved=8 * 2**20,
+        limit=VMEM_ALL,
+    )(*early, *late)
+    weights_grad = weights_grad.reshape(1, UNITS, 2, D)
+    returned, weights_grad = lax.optimization_barrier((returned, weights_grad))
+    [total] = call(tokens_kernel, [VMEM] * 4, [shape((CTX_COUNT, 64, CHUNK))], moved=2**20)(
         returned, even, odd, query
     )
-    packs = lax.all_gather(lax.all_gather(total, "ctx_1"), "ctx_0").reshape(CTX_COUNT, 64, CHUNK)
+    packs = lax.all_to_all(total, CTX, split_axis=0, concat_axis=0, tiled=True)
     [states_grad] = call(
         norm_grad_kernel,
         [VMEM] * 4,
         [shape((TOKENS, D))],
         [pltpu.VMEM((TOKENS, D), F32)],
         moved=3 * 2**20,
-    )(packs, states, grads, gain)
+    )(packs, states, grads, norm_gain)
     return states_grad[None], keys_grad[None], values_grad[None], weights_grad
 
 

time: 195 us -> 170 us (0.87)
  blocking collectives: 94.4 us -> 55 us
  starting transfers between devices: 26.6 us -> 45.6 us
  Pallas kernels: 35.1 us -> 26.8 us
  local copies, waits for them, and re-layouts: 16.5 us -> 23.9 us
  waiting for transfers between devices: 18.9 us -> 16 us
  other arithmetic: 2 us -> 0.05 us
    all_gather x2 -> x0, blocking collectives: 20.6 us -> none  [the longest x1 13.8 us: on_device(): lax.all_gather(lax.all_gather(total, 'ctx_1'), 'ctx_0')]
    all_to_all x1, blocking collectives: 30.2 us -> 16.1 us  [on_device(): packs = lax.all_to_all(total, CTX, split_axis=0, concat_axis=0, tiled=True)]
    ppermute x13, waiting for transfers between devices: 16.8 us -> 4.47 us  [moved_by(): lax.ppermute(array, axis, [(k, (k + step) % count) for k in range(count)])]
    all_to_all x0 -> x1, waiting for transfers between devices: none -> 11.6 us  [on_device(): lax.all_to_all(send.reshape(EXPERTS, 8, HALF), 'exp', split_axis=0, conca...]
    all_to_all x0 -> x1, starting transfers between devices: none -> 9.66 us  [on_device(): lax.all_to_all(send.reshape(EXPERTS, 8, HALF), 'exp', split_axis=0, conca...]
    ppermute x13, starting transfers between devices: 22.4 us -> 28.2 us  [moved_by(): lax.ppermute(array, axis, [(k, (k + step) % count) for k in range(count)])]
    reshape x1, local copies, waits for them, and re-layouts: 1.31 us -> 6.55 us  [on_device(): weights_grad = weights_grad.reshape(1, UNITS, 2, D)]
    unnamed x27 -> x58, local copies, waits for them, and re-layouts: 5.57 us -> 10.2 us
  transfers between devices with their start and end apart: 14 -> 15, of which waited for: 5 -> 3; matrix products, arithmetic and copies ran while one was open for 8% -> 8% of each run, Pallas kernels for 7% -> 9%
where the time goes in v5:
time: 170 us; the launch traced here: 168 us
  blocking collectives  55 us (32%)
  starting transfers between devices  45.6 us (27%)
  Pallas kernels  26.8 us (16%)
  local copies, waits for them, and re-layouts  23.9 us (14%)
  waiting for transfers between devices  16 us (9%)
    all_to_all x1, blocking collectives, on_device(): parts = lax.all_to_all(sums, CTX, split_axis=0, concat_axis=0, tiled=True)  38.9 us
    ppermute x13, starting transfers between devices, moved_by(): lax.ppermute(array, axis, [(k, (k + step) % count) for k in range(count)])  28.2 us
    all_to_all x1, blocking collectives, on_device(): packs = lax.all_to_all(total, CTX, split_axis=0, concat_axis=0, tiled=True)  16.1 us
    all_to_all x1, waiting for transfers between devices, on_device(): lax.all_to_all(send.reshape(EXPERTS, 8, HALF), 'exp', split_axis=0, conca...  11.6 us
    unnamed x58, local copies, waits for them, and re-layouts  10.2 us
    all_to_all x1, starting transfers between devices, on_device(): lax.all_to_all(send.reshape(EXPERTS, 8, HALF), 'exp', split_axis=0, conca...  9.66 us
    all_to_all x1, starting transfers between devices, on_device(): lax.all_to_all(back.reshape(EXPERTS, 8, CHUNK), 'exp', split_axis=0, conc...  7.74 us
    pallas_call x1, Pallas kernels, on_device(): call(weights_kernel, [VMEM] * 8, [shape((2 * UNITS, D))], flops=2 * 4 * S...  7.33 us
  transfers between devices with their start and end apart: 15, of which 3 were waited for; matrix products, arithmetic and copies ran while one was open for 8% of the time, Pallas kernels for 9%

profile of v5, /device:TPU:32, one launch (start us, length us, event | category | flops | bytes accessed | tf_op | source)
XLA Modules:
  0.0 168.5 jit_solution(1664560335684229782)
XLA Ops:
  0.6 0.0 copy-start
  0.7 0.0 copy-start.5
  0.7 3.5 %shard_map.111 = (bf16[128,2560]{1,0:T(8,128)(2,1)}, bf16[256,1280]{1,0:T(8,128)(2,1)}, bf16[256,128]{1,0:T(8,128)(2,1)}, bf16[256,128]{1,0:T(8,128)(2,1)}) custom-call(s32[1]{0:T(128)} %bitcast.8.c_ref, bf16[128,2560]{1,0:T(8,128)(2,1)} %bitcast.34, bf16[128,2560]{1,0:T(8,128)(2,1)} %bitcast.30, f32[2560]{0:T(1024)} %gain.3, s32[2,128]{1,0:T(2,128)} %bitcast.46, ...), custom_call_target="tpu_custom_call" | custom-call | flops 335544320 | bytes 3145728 | tf_op jit(solution)/shard_map/pallas_call | solution.py:293
  4.2 9.7 %all-to-all-start = ((bf16[32,8,1280]{2,1,0:T(8,128)(2,1)}), bf16[32,8,1280]{2,1,0:T(8,128)(2,1)S(1)}, u32[]{:S(2)}, u32[]{:S(2)}) async-start(bf16[32,8,1280]{2,1,0:T(8,128)(2,1)} %bitcast.45), calls=%async_computation | async-start | bytes 1310720 | tf_op jit(solution)/shard_map/all_to_all | solution.py:301
  13.9 0.0 copy-start.6
  13.9 1.1 copy-done.6
  15.0 1.1 shard_map.113
  16.0 1.0 copy-done.11
  17.1 1.1 copy-done.12
  18.2 3.0 %collective-permute-start.11 = (f32[72,128]{1,0:T(8,128)S(1)}, f32[72,128]{1,0:T(8,128)S(1)}, u32[]{:S(2)}, u32[]{:S(2)}) collective-permute-start(f32[72,128]{1,0:T(8,128)S(1)} %get-tuple-element.35.local), channel_id=1, source_target_pairs={{0,192},{64,0},{128,64},{192,128},{1,193},{65,1},{129,65},{193,129... | collective-permute-start | bytes 110600 | tf_op jit(solution)/shard_map/ppermute | solution.py:284
  21.2 0.6 collective-permute-start.10
  21.9 1.0 collective-permute-start.9
  22.8 11.6 %all-to-all-done = bf16[32,8,1280]{2,1,0:T(8,128)(2,1)S(1)} async-done(((bf16[32,8,1280]{2,1,0:T(8,128)(2,1)}), bf16[32,8,1280]{2,1,0:T(8,128)(2,1)S(1)}, u32[]{:S(2)}, u32[]{:S(2)}) %all-to-all-start) | async-done | bytes 655392 | tf_op jit(solution)/shard_map/all_to_all | solution.py:301
  34.4 3.0 %collective-permute-start.5 = (bf16[256,1280]{1,0:T(8,128)(2,1)S(1)}, bf16[256,1280]{1,0:T(8,128)(2,1)S(1)}, u32[]{:S(2)}, u32[]{:S(2)}) collective-permute-start(bf16[256,1280]{1,0:T(8,128)(2,1)S(1)} %bitcast.36), channel_id=1, source_target_pairs={{0,192},{64,0},{128,64},{192,128},{1,193},{65,1},{129,65},{193,129... | collective-permute-start | bytes 1966088 | tf_op jit(solution)/shard_map/ppermute | solution.py:284
  37.4 2.7 %collective-permute-start = (bf16[256,1280]{1,0:T(8,128)(2,1)S(1)}, bf16[256,1280]{1,0:T(8,128)(2,1)}, u32[]{:S(2)}, u32[]{:S(2)}) collective-permute-start(bf16[256,1280]{1,0:T(8,128)(2,1)S(1)} %bitcast.38), channel_id=1, source_target_pairs={{0,32},{32,0},{1,33},{33,1},{2,34},{34,2},{3,35},{35,3},{4,36},{36... | collective-permute-start | bytes 1966088 | tf_op jit(solution)/shard_map/ppermute | solution.py:284
  40.2 6.5 %fusion.6 = (bf16[1,256,1,2560]{3,2,1,0:T(2,128)(2,1)S(1)}, bf16[1,256,1,2560]{3,2,1,0:T(2,128)(2,1)S(1)}) fusion(bf16[1,256,2,2560]{3,2,1,0:T(2,128)(2,1)} %param.15), kind=kLoop, calls=%fused_computation.20 | loop fusion | bytes 5242880 | tf_op jit(solution)/shard_map/slice | solution.py:331
  46.7 3.9 %collective-permute-done.5.down = bf16[256,1280]{1,0:T(8,128)(2,1)S(1)} collective-permute-done((bf16[256,1280]{1,0:T(8,128)(2,1)S(1)}, bf16[256,1280]{1,0:T(8,128)(2,1)S(1)}, u32[]{:S(2)}, u32[]{:S(2)}) %collective-permute-start.5) | collective-permute-done | bytes 655392 | tf_op jit(solution)/shard_map/ppermute | solution.py:284
  50.6 3.8 %collective-permute-start.6 = (bf16[128,1280]{1,0:T(8,128)(2,1)S(1)}, bf16[128,1280]{1,0:T(8,128)(2,1)}, u32[]{:S(2)}, u32[]{:S(2)}) collective-permute-start(bf16[128,1280]{1,0:T(8,128)(2,1)S(1)} %slice.69), channel_id=1, source_target_pairs={{0,192},{64,0},{128,64},{192,128},{1,193},{65,1},{129,65},{193,129... | collective-permute-start | bytes 983048 | tf_op jit(solution)/shard_map/ppermute | solution.py:284
  54.4 0.1 collective-permute-start.4
  54.6 2.8 %collective-permute-start.12 = (f32[72,128]{1,0:T(8,128)S(1)}, f32[72,128]{1,0:T(8,128)S(1)}, u32[]{:S(2)}, u32[]{:S(2)}) collective-permute-start(f32[72,128]{1,0:T(8,128)S(1)} %pad_maximum_fusion.near), channel_id=1, source_target_pairs={{0,32},{32,0},{1,33},{33,1},{2,34},{34,2},{3,35},{35,3},{4,36},{36... | collective-permute-start | bytes 110600 | tf_op jit(solution)/shard_map/ppermute | solution.py:284
  57.4 3.2 %collective-permute-start.2 = (bf16[256,1280]{1,0:T(8,128)(2,1)}, bf16[256,1280]{1,0:T(8,128)(2,1)}, u32[]{:S(2)}, u32[]{:S(2)}) collective-permute-start(bf16[256,1280]{1,0:T(8,128)(2,1)} %collective-permute-done.partner), channel_id=1, source_target_pairs={{0,192},{64,0},{128,64},{192,128},{1,193},{65,1},{129,65},{193,129... | collective-permute-start | bytes 1966088 | tf_op jit(solution)/shard_map/ppermute | solution.py:284
  60.6 0.6 collective-permute-done.6.refs_3_
  61.2 4.1 %collective-permute-start.8 = (bf16[128,1280]{1,0:T(8,128)(2,1)}, bf16[128,1280]{1,0:T(8,128)(2,1)}, u32[]{:S(2)}, u32[]{:S(2)}) collective-permute-start(bf16[128,1280]{1,0:T(8,128)(2,1)} %collective-permute-done.6.refs_3_), channel_id=1, source_target_pairs={{0,32},{32,0},{1,33},{33,1},{2,34},{34,2},{3,35},{35,3},{4,36},{36... | collective-permute-start | bytes 983048 | tf_op jit(solution)/shard_map/ppermute | solution.py:284
  65.3 3.9 %collective-permute-start.7 = (bf16[128,1280]{1,0:T(8,128)(2,1)}, bf16[128,1280]{1,0:T(8,128)(2,1)}, u32[]{:S(2)}, u32[]{:S(2)}) collective-permute-start(bf16[128,1280]{1,0:T(8,128)(2,1)} %collective-permute-done.4.refs_2_), channel_id=1, source_target_pairs={{0,32},{32,0},{1,33},{33,1},{2,34},{34,2},{3,35},{35,3},{4,36},{36... | collective-permute-start | bytes 983048 | tf_op jit(solution)/shard_map/ppermute | solution.py:284
  69.2 0.5 copy_bitcast_fusion
  69.8 0.1 stack.35.at_ref
  69.9 0.6 copy-done.28
  70.5 4.3 %shard_map.114 = (bf16[128,2560]{1,0:T(8,128)(2,1)}, bf16[128,2560]{1,0:T(8,128)(2,1)}, bf16[8,64,640]{2,1,0:T(8,128)(2,1)}) custom-call(bf16[128,2560]{1,0:T(8,128)(2,1)} %get-tuple-element.32.normed, bf16[128,2560]{1,0:T(8,128)(2,1)} %bitcast.31, bf16[128,2560]{1,0:T(8,128)(2,1)} %bitcast.40, f32[20,128,128]{2,1,0:T(8,128)} %copy-done.11, ...), custom_call_target="tpu_custom_call" | custom-call | flops 251658240 | bytes 6291456 | tf_op jit(solution)/shard_map/pallas_call | solution.py:314
  74.9 1.1 copy-done.8
  75.9 1.1 copy-done.10
  77.0 3.2 %shard_map.112 = (bf16[8,128,640]{2,1,0:T(8,128)(2,1)S(1)}, bf16[256,2560]{1,0:T(8,128)(2,1)S(1)}, bf16[256,2560]{1,0:T(8,128)(2,1)S(1)}, bf16[256,256]{1,0:T(8,128)(2,1)S(1)}, bf16[256,256]{1,0:T(8,128)(2,1)S(1)}) custom-call(bf16[256,1280]{1,0:T(8,128)(2,1)S(1)} %bitcast.39, bf16[256,1280]{1,0:T(8,128)(2,1)S(1)} %copy-done.10, ...), custom_call_target="tpu_custom_call" | custom-call | flops 1006632960 | bytes 8388608 | tf_op jit(solution)/shard_map/pallas_call | solution.py:333
  80.3 0.0 copy-start.13
  80.3 1.0 copy-done.13
  81.3 1.1 copy-done.14
  82.4 0.6 copy-done.20
  83.1 0.7 copy-done.21
  83.8 4.0 %shard_map.115 = (bf16[8,320,640]{2,1,0:T(8,128)(2,1)S(1)}, bf16[256,2560]{1,0:T(8,128)(2,1)S(1)}, bf16[256,2560]{1,0:T(8,128)(2,1)S(1)}, bf16[256,256]{1,0:T(8,128)(2,1)S(1)}, bf16[256,256]{1,0:T(8,128)(2,1)S(1)}) custom-call(s32[8]{0:T(128)S(1)} %stack.35.at_ref, bf16[256,1280]{1,0:T(8,128)(2,1)} %collective-permute-done.1.refs_0_, ...), custom_call_target="tpu_custom_call" | custom-call | flops 1006632960 | bytes 12582912 | tf_op jit(solution)/shard_map/pallas_call | solution.py:340
  87.8 0.6 copy-done.23
  88.4 38.9 %all_to_all.20.parts = bf16[8,320,640]{2,1,0:T(8,128)(2,1)S(1)} all-to-all(bf16[8,320,640]{2,1,0:T(8,128)(2,1)S(1)} %get-tuple-element.38), channel_id=1, replica_groups=mesh['ctx_0'=4,'ctx_1'=2,'exp'=32] {'ctx_0','ctx_1'}, dimensions={0} | all-to-all | bytes 6553600 | tf_op jit(solution)/shard_map/all_to_all | solution.py:347
  127.4 1.4 shard_map.116
  128.8 7.7 %all-to-all-start.2 = ((bf16[32,8,640]{2,1,0:T(8,128)(2,1)}), bf16[32,8,640]{2,1,0:T(8,128)(2,1)S(1)}, u32[]{:S(2)}, u32[]{:S(2)}) async-start(bf16[32,8,640]{2,1,0:T(8,128)(2,1)} %bitcast.21), calls=%async_computation.2 | async-start | bytes 655360 | tf_op jit(solution)/shard_map/all_to_all | solution.py:355
  136.5 7.3 %shard_map.117 = bf16[512,2560]{1,0:T(8,128)(2,1)} custom-call(bf16[256,2560]{1,0:T(8,128)(2,1)} %copy-done.13, bf16[256,2560]{1,0:T(8,128)(2,1)} %copy-done.14, bf16[256,256]{1,0:T(8,128)(2,1)} %copy-done.20, bf16[256,256]{1,0:T(8,128)(2,1)} %copy-done.21, bf16[256,2560]{1,0:T(8,128)(2,1)} %copy-done.15, bf16[256,2560]{1,0:T(8,128)(2,1)} %copy-done.16, ...), custom_call_target="tpu_custom_call" | custom-call | flops 1342177280 | bytes 8388608 | tf_op jit(solution)/shard_map/pallas_call | solution.py:358
  143.8 0.0 copy-start.2
  143.9 0.0 copy-start.26
  143.9 6.6 %reshape.31 = bf16[1,256,2,2560]{3,2,1,0:T(2,128)(2,1)} reshape(bf16[512,2560]{1,0:T(8,128)(2,1)} %shard_map.117) | data formatting | bytes 5242880 | tf_op jit(solution)/shard_map/reshape | solution.py:366
  150.4 0.4 shard_map.118
  150.8 16.1 %all_to_all.21.packs = bf16[8,64,640]{2,1,0:T(8,128)(2,1)S(1)} all-to-all(bf16[8,64,640]{2,1,0:T(8,128)(2,1)S(1)} %shard_map.118), channel_id=1, replica_groups=mesh['ctx_0'=4,'ctx_1'=2,'exp'=32] {'ctx_0','ctx_1'}, dimensions={0} | all-to-all | bytes 1310720 | tf_op jit(solution)/shard_map/all_to_all | solution.py:371
  166.9 1.5 shard_map.119
  (60 shorter events, 0.2 us)
Async XLA Ops:
  0.6 13.2 %copy-start = (bf16[1,128,2560]{2,1,0:T(8,128)(2,1)S(1)}, bf16[1,128,2560]{2,1,0:T(8,128)(2,1)}, u32[]{:S(2)}) copy-start(bf16[1,128,2560]{2,1,0:T(8,128)(2,1)} %param.9) | copy-start | bytes 1966084
  0.6 13.2 %copy-start.18 = (bf16[1,128,2560]{2,1,0:T(8,128)(2,1)S(1)}, bf16[1,128,2560]{2,1,0:T(8,128)(2,1)}, u32[]{:S(2)}) copy-start(bf16[1,128,2560]{2,1,0:T(8,128)(2,1)} %param.11) | copy-start | bytes 1966084
  0.7 13.2 %copy-start.5 = (bf16[1,128,2560]{2,1,0:T(8,128)(2,1)S(1)}, bf16[1,128,2560]{2,1,0:T(8,128)(2,1)}, u32[]{:S(2)}) copy-start(bf16[1,128,2560]{2,1,0:T(8,128)(2,1)} %param.10) | copy-start | bytes 1966084
  4.2 30.2 %all-to-all-start = ((bf16[32,8,1280]{2,1,0:T(8,128)(2,1)}), bf16[32,8,1280]{2,1,0:T(8,128)(2,1)S(1)}, u32[]{:S(2)}, u32[]{:S(2)}) async-start(bf16[32,8,1280]{2,1,0:T(8,128)(2,1)} %bitcast.45), calls=%async_computation | async-start | bytes 1310720 | tf_op jit(solution)/shard_map/all_to_all | solution.py:301
  13.9 1.1 copy-start.6
  16.0 1.1 copy-start.11
  17.1 1.1 copy-start.12
  18.2 36.3 %copy-start.19 = (f32[72,128]{1,0:T(8,128)}, f32[72,128]{1,0:T(8,128)S(1)}, u32[]{:S(2)}) copy-start(f32[72,128]{1,0:T(8,128)S(1)} %get-tuple-element.35.local) | copy-start | bytes 110596
  18.2 19.2 %collective-permute-start.11 = (f32[72,128]{1,0:T(8,128)S(1)}, f32[72,128]{1,0:T(8,128)S(1)}, u32[]{:S(2)}, u32[]{:S(2)}) collective-permute-start(f32[72,128]{1,0:T(8,128)S(1)} %get-tuple-element.35.local), channel_id=1, source_target_pairs={{0,192},{64,0},{128,64},{192,128},{1,193},{65,1},{129,65},{193,129... | collective-permute-start | bytes 110600 | tf_op jit(solution)/shard_map/ppermute | solution.py:284
  21.2 25.4 %collective-permute-start.10 = (f32[72,128]{1,0:T(8,128)S(1)}, f32[72,128]{1,0:T(8,128)S(1)}, u32[]{:S(2)}, u32[]{:S(2)}) collective-permute-start(f32[72,128]{1,0:T(8,128)S(1)} %get-tuple-element.35.local), channel_id=1, source_target_pairs={{0,128},{64,192},{128,0},{192,64},{1,129},{65,193},{129,1},{193,65... | collective-permute-start | bytes 110600 | tf_op jit(solution)/shard_map/ppermute | solution.py:284
  21.9 24.8 %collective-permute-start.9 = (f32[72,128]{1,0:T(8,128)S(1)}, f32[72,128]{1,0:T(8,128)S(1)}, u32[]{:S(2)}, u32[]{:S(2)}) collective-permute-start(f32[72,128]{1,0:T(8,128)S(1)} %get-tuple-element.35.local), channel_id=1, source_target_pairs={{0,64},{64,128},{128,192},{192,0},{1,65},{65,129},{129,193},{193,1... | collective-permute-start | bytes 110600 | tf_op jit(solution)/shard_map/ppermute | solution.py:284
  34.4 12.3 %copy-start.3 = (bf16[32,8,1280]{2,1,0:T(8,128)(2,1)}, bf16[32,8,1280]{2,1,0:T(8,128)(2,1)S(1)}, u32[]{:S(2)}) copy-start(bf16[32,8,1280]{2,1,0:T(8,128)(2,1)S(1)} %all-to-all-done) | copy-start | bytes 1966084
  34.4 16.2 %collective-permute-start.5 = (bf16[256,1280]{1,0:T(8,128)(2,1)S(1)}, bf16[256,1280]{1,0:T(8,128)(2,1)S(1)}, u32[]{:S(2)}, u32[]{:S(2)}) collective-permute-start(bf16[256,1280]{1,0:T(8,128)(2,1)S(1)} %bitcast.36), channel_id=1, source_target_pairs={{0,192},{64,0},{128,64},{192,128},{1,193},{65,1},{129,65},{193,129... | collective-permute-start | bytes 1966088 | tf_op jit(solution)/shard_map/ppermute | solution.py:284
  37.4 17.0 %collective-permute-start.3 = (bf16[256,1280]{1,0:T(8,128)(2,1)S(1)}, bf16[256,1280]{1,0:T(8,128)(2,1)S(1)}, u32[]{:S(2)}, u32[]{:S(2)}) collective-permute-start(bf16[256,1280]{1,0:T(8,128)(2,1)S(1)} %bitcast.37), channel_id=1, source_target_pairs={{0,64},{64,128},{128,192},{192,0},{1,65},{65,129},{129,193},{193,1... | collective-permute-start | bytes 1966088 | tf_op jit(solution)/shard_map/ppermute | solution.py:284
  37.4 20.0 %collective-permute-start = (bf16[256,1280]{1,0:T(8,128)(2,1)S(1)}, bf16[256,1280]{1,0:T(8,128)(2,1)}, u32[]{:S(2)}, u32[]{:S(2)}) collective-permute-start(bf16[256,1280]{1,0:T(8,128)(2,1)S(1)} %bitcast.38), channel_id=1, source_target_pairs={{0,32},{32,0},{1,33},{33,1},{2,34},{34,2},{3,35},{35,3},{4,36},{36... | collective-permute-start | bytes 1966088 | tf_op jit(solution)/shard_map/ppermute | solution.py:284
  50.6 18.6 %copy-start.7 = (bf16[256,1280]{1,0:T(8,128)(2,1)}, bf16[256,1280]{1,0:T(8,128)(2,1)S(1)}, u32[]{:S(2)}) copy-start(bf16[256,1280]{1,0:T(8,128)(2,1)S(1)} %collective-permute-done.5.down) | copy-start | bytes 1966084
  50.6 10.6 %collective-permute-start.6 = (bf16[128,1280]{1,0:T(8,128)(2,1)S(1)}, bf16[128,1280]{1,0:T(8,128)(2,1)}, u32[]{:S(2)}, u32[]{:S(2)}) collective-permute-start(bf16[128,1280]{1,0:T(8,128)(2,1)S(1)} %slice.69), channel_id=1, source_target_pairs={{0,192},{64,0},{128,64},{192,128},{1,193},{65,1},{129,65},{193,129... | collective-permute-start | bytes 983048 | tf_op jit(solution)/shard_map/ppermute | solution.py:284
  54.4 14.8 %copy-start.9 = (bf16[256,1280]{1,0:T(8,128)(2,1)}, bf16[256,1280]{1,0:T(8,128)(2,1)S(1)}, u32[]{:S(2)}) copy-start(bf16[256,1280]{1,0:T(8,128)(2,1)S(1)} %collective-permute-done.3.up) | copy-start | bytes 1966084
  54.4 10.9 %collective-permute-start.4 = (bf16[128,1280]{1,0:T(8,128)(2,1)S(1)}, bf16[128,1280]{1,0:T(8,128)(2,1)}, u32[]{:S(2)}, u32[]{:S(2)}) collective-permute-start(bf16[128,1280]{1,0:T(8,128)(2,1)S(1)} %slice.68), channel_id=1, source_target_pairs={{0,64},{64,128},{128,192},{192,0},{1,65},{65,129},{129,193},{193,1... | collective-permute-start | bytes 983048 | tf_op jit(solution)/shard_map/ppermute | solution.py:284
  54.6 15.2 %copy-start.27 = (f32[72,128]{1,0:T(8,128)}, f32[72,128]{1,0:T(8,128)S(1)}, u32[]{:S(2)}) copy-start(f32[72,128]{1,0:T(8,128)S(1)} %pad_maximum_fusion.near) | copy-start | bytes 110596
  54.6 15.3 %collective-permute-start.12 = (f32[72,128]{1,0:T(8,128)S(1)}, f32[72,128]{1,0:T(8,128)S(1)}, u32[]{:S(2)}, u32[]{:S(2)}) collective-permute-start(f32[72,128]{1,0:T(8,128)S(1)} %pad_maximum_fusion.near), channel_id=1, source_target_pairs={{0,32},{32,0},{1,33},{33,1},{2,34},{34,2},{3,35},{35,3},{4,36},{36... | collective-permute-start | bytes 110600 | tf_op jit(solution)/shard_map/ppermute | solution.py:284
  57.4 26.4 %collective-permute-start.2 = (bf16[256,1280]{1,0:T(8,128)(2,1)}, bf16[256,1280]{1,0:T(8,128)(2,1)}, u32[]{:S(2)}, u32[]{:S(2)}) collective-permute-start(bf16[256,1280]{1,0:T(8,128)(2,1)} %collective-permute-done.partner), channel_id=1, source_target_pairs={{0,192},{64,0},{128,64},{192,128},{1,193},{65,1},{129,65},{193,129... | collective-permute-start | bytes 1966088 | tf_op jit(solution)/shard_map/ppermute | solution.py:284
  60.6 23.1 %collective-permute-start.1 = (bf16[256,1280]{1,0:T(8,128)(2,1)}, bf16[256,1280]{1,0:T(8,128)(2,1)}, u32[]{:S(2)}, u32[]{:S(2)}) collective-permute-start(bf16[256,1280]{1,0:T(8,128)(2,1)} %collective-permute-done.partner), channel_id=1, source_target_pairs={{0,64},{64,128},{128,192},{192,0},{1,65},{65,129},{129,193},{193,1... | collective-permute-start | bytes 1966088 | tf_op jit(solution)/shard_map/ppermute | solution.py:284
  61.2 22.5 %collective-permute-start.8 = (bf16[128,1280]{1,0:T(8,128)(2,1)}, bf16[128,1280]{1,0:T(8,128)(2,1)}, u32[]{:S(2)}, u32[]{:S(2)}) collective-permute-start(bf16[128,1280]{1,0:T(8,128)(2,1)} %collective-permute-done.6.refs_3_), channel_id=1, source_target_pairs={{0,32},{32,0},{1,33},{33,1},{2,34},{34,2},{3,35},{35,3},{4,36},{36... | collective-permute-start | bytes 983048 | tf_op jit(solution)/shard_map/ppermute | solution.py:284
  65.3 18.5 %collective-permute-start.7 = (bf16[128,1280]{1,0:T(8,128)(2,1)}, bf16[128,1280]{1,0:T(8,128)(2,1)}, u32[]{:S(2)}, u32[]{:S(2)}) collective-permute-start(bf16[128,1280]{1,0:T(8,128)(2,1)} %collective-permute-done.4.refs_2_), channel_id=1, source_target_pairs={{0,32},{32,0},{1,33},{33,1},{2,34},{34,2},{3,35},{35,3},{4,36},{36... | collective-permute-start | bytes 983048 | tf_op jit(solution)/shard_map/ppermute | solution.py:284
  69.8 5.1 %copy-start.4 = (bf16[32,8,1280]{2,1,0:T(8,128)(2,1)S(1)}, bf16[32,8,1280]{2,1,0:T(8,128)(2,1)}, u32[]{:S(2)}) copy-start(bf16[32,8,1280]{2,1,0:T(8,128)(2,1)} %copy-done.3) | copy-start | bytes 1966084
  69.9 0.6 copy-start.28
  74.9 1.1 copy-start.8
  75.9 1.1 copy-start.10
  77.0 6.7 %copy-start.17 = (bf16[8,64,640]{2,1,0:T(8,128)(2,1)S(1)}, bf16[8,64,640]{2,1,0:T(8,128)(2,1)}, u32[]{:S(2)}) copy-start(bf16[8,64,640]{2,1,0:T(8,128)(2,1)} %get-tuple-element.36.refs_9_) | copy-start | bytes 1966084
  80.3 1.1 copy-start.13
  81.3 1.1 copy-start.14
  82.4 0.6 copy-start.20
  83.1 0.7 copy-start.21
  87.8 0.7 copy-start.23
  88.4 39.0 %copy-start.15 = (bf16[256,2560]{1,0:T(8,128)(2,1)}, bf16[256,2560]{1,0:T(8,128)(2,1)S(1)}, u32[]{:S(2)}) copy-start(bf16[256,2560]{1,0:T(8,128)(2,1)S(1)} %get-tuple-element.45.refs_4_) | copy-start | bytes 3932164
  88.4 39.0 %copy-start.16 = (bf16[256,2560]{1,0:T(8,128)(2,1)}, bf16[256,2560]{1,0:T(8,128)(2,1)S(1)}, u32[]{:S(2)}) copy-start(bf16[256,2560]{1,0:T(8,128)(2,1)S(1)} %get-tuple-element.46.refs_5_) | copy-start | bytes 3932164
  88.4 39.0 %copy-start.22 = (bf16[256,256]{1,0:T(8,128)(2,1)}, bf16[256,256]{1,0:T(8,128)(2,1)S(1)}, u32[]{:S(2)}) copy-start(bf16[256,256]{1,0:T(8,128)(2,1)S(1)} %get-tuple-element.47.refs_6_) | copy-start | bytes 393220
  128.8 21.7 %all-to-all-start.2 = ((bf16[32,8,640]{2,1,0:T(8,128)(2,1)}), bf16[32,8,640]{2,1,0:T(8,128)(2,1)S(1)}, u32[]{:S(2)}, u32[]{:S(2)}) async-start(bf16[32,8,640]{2,1,0:T(8,128)(2,1)} %bitcast.21), calls=%async_computation.2 | async-start | bytes 655360 | tf_op jit(solution)/shard_map/all_to_all | solution.py:355
  143.8 6.6 %copy-start.24 = (bf16[256,128]{1,0:T(8,128)(2,1)S(1)}, bf16[256,128]{1,0:T(8,128)(2,1)}, u32[]{:S(2)}) copy-start(bf16[256,128]{1,0:T(8,128)(2,1)} %get-tuple-element.50.even) | copy-start | bytes 196612
  143.8 6.6 %copy-start.25 = (bf16[256,128]{1,0:T(8,128)(2,1)S(1)}, bf16[256,128]{1,0:T(8,128)(2,1)}, u32[]{:S(2)}) copy-start(bf16[256,128]{1,0:T(8,128)(2,1)} %get-tuple-element.51.odd) | copy-start | bytes 196612
  143.8 23.1 %copy-start.1 = (bf16[1,128,2560]{2,1,0:T(8,128)(2,1)S(1)}, bf16[1,128,2560]{2,1,0:T(8,128)(2,1)}, u32[]{:S(2)}) copy-start(bf16[1,128,2560]{2,1,0:T(8,128)(2,1)} %param.9) | copy-start | bytes 1966084
  143.8 23.1 %copy-start.2 = (bf16[1,128,2560]{2,1,0:T(8,128)(2,1)S(1)}, bf16[1,128,2560]{2,1,0:T(8,128)(2,1)}, u32[]{:S(2)}) copy-start(bf16[1,128,2560]{2,1,0:T(8,128)(2,1)} %param.8) | copy-start | bytes 1966084
  143.9 23.1 %copy-start.26 = (f32[2560]{0:T(1024)S(1)}, f32[2560]{0:T(1024)}, u32[]{:S(2)}) copy-start(f32[2560]{0:T(1024)} %gain.3) | copy-start | bytes 30724

commit v6 on v5

--- a/solution.py
+++ b/solution.py
@@ -30,13 +30,14 @@
 
 VMEM = pl.BlockSpec(memory_space=pltpu.VMEM)
 SMEM = pl.BlockSpec(memory_space=pltpu.SMEM)
-
-
-def call(kernel, ins, outs, scratch=(), flops=0, moved=0, limit=VMEM_LIMIT):
+ANY = pl.BlockSpec(memory_space=pl.ANY)
+
+
+def call(kernel, ins, outs, scratch=(), flops=0, moved=0, places=None, limit=VMEM_LIMIT):
     return pl.pallas_call(
         kernel,
         in_specs=ins,
-        out_specs=[VMEM] * len(outs),
+        out_specs=places or [VMEM] * len(outs),
         out_shape=outs,
         scratch_shapes=list(scratch),
         compiler_params=pltpu.CompilerParams(vmem_limit_bytes=limit),
@@ -60,8 +61,8 @@
     return jnp.where(mask, 1.0, 0.0).astype(BF16)
 
 
-def route_kernel(c_ref, states, grads, gain, ids, gates, normed_out, send, even, odd):
-    c = c_ref[0]
+def route_kernel(place, states, grads, gain, ids, gates, normed_out, send, even, odd):
+    c = 2 * place[0] + place[1]
     x = states[...].astype(F32)
     inverse = lax.rsqrt(jnp.mean(x * x, axis=-1, keepdims=True) + EPSILON)
     normed_out[...] = (x * inverse * gain[...].reshape(1, D)).astype(BF16)
@@ -118,19 +119,8 @@
     return jnp.concatenate([peak, total, inner], axis=0)
 
 
-def pack(out, rows, left, right, tail_left, tail_right):
-    lane = iota(tail_left(0).shape, 1)
-    for f in range(CTX_COUNT):
-        out[f, rows, 0:256] = left(f).astype(BF16)
-        out[f, rows, 256:512] = right(f).astype(BF16)
-    for g in range(CTX_COUNT // 2):
-        a, b = tail_left(g), tail_right(g)
-        out[2 * g, rows, 512:640] = jnp.where(lane < 64, a, pltpu.roll(b, 64, 1)).astype(BF16)
-        out[2 * g + 1, rows, 512:640] = jnp.where(lane < 64, pltpu.roll(a, 64, 1), b).astype(BF16)
-
-
 def score_grad_kernel(
-    normed, grads, keys, weights, slopes, local, near, far, keys_grad, values_grad, query_pack, query
+    place, normed, grads, keys, weights, slopes, local, near, far, keys_grad, values_grad, query_pack, query
 ):
     peak = jnp.maximum(near[0:24, :], far[0:24, :])
     near_factor = jnp.exp(near[0:24, :] - peak)
@@ -147,17 +137,27 @@
         values_grad[:, at] = dot(probs.astype(BF16), grads[:, at]).astype(BF16)
         keys_grad[:, at] = (dot(score_grad, normed[:, at]) * SCALE).astype(BF16)
         query[:, at] = dot(score_grad, keys[:, at], ((0,), (0,))) * SCALE
-    pack(
-        query_pack,
-        slice(0, 64),
-        lambda f: query[0:64, 256 * f : 256 * f + 256],
-        lambda f: query[64:128, 256 * f : 256 * f + 256],
-        lambda g: query[0:64, 2048 + 128 * g : 2176 + 128 * g],
-        lambda g: query[64:128, 2048 + 128 * g : 2176 + 128 * g],
-    )
-
-
-def experts_of(blocks, w_in, w_out, rows, douts, act, pre_grad, put):
+    lane = iota((64, 128), 1)
+    for f in range(CTX_COUNT):
+        column, row = (f + place[1] + 1) % 2, (f // 2 - place[0] + 4) % 4
+        at = slice(256 * f, 256 * f + 256)
+        query_pack[column, row, :, 0:256] = query[0:64, at].astype(BF16)
+        query_pack[column, row, :, 256:512] = query[64:128, at].astype(BF16)
+        tile = slice(2048 + 128 * (f // 2), 2176 + 128 * (f // 2))
+        a, b = query[0:64, tile], query[64:128, tile]
+        if f % 2 == 0:
+            tail = jnp.where(lane < 64, a, pltpu.roll(b, 64, 1))
+        else:
+            tail = jnp.where(lane < 64, pltpu.roll(a, 64, 1), b)
+        query_pack[column, row, :, 512:640] = tail.astype(BF16)
+
+
+def join_kernel(query_pack, far, *outs):
+    for k in range(4):
+        outs[k][...] = (query_pack[1, k].astype(F32) + far[k].astype(F32)).astype(BF16)
+
+
+def experts_of(blocks, w_in, w_out, rows, douts, act, pre_grad, put, after=lambda step: None):
     to, source = iota((ROWS, ROWS), 0), iota((ROWS, ROWS), 1)
     order = one(source == 8 * (to % 32) + to // 32)
     for k, block in enumerate(blocks):
@@ -169,6 +169,7 @@
                 first = 128 * half + 32 * q
                 rows[where, lanes] = sorted_rows[first : first + 32, :]
                 douts[where, lanes] = sorted_rows[first + 64 : first + 96, :]
+    after("rows")
     v = dot(rows[...], w_in[...], ((1,), (1,)))
     act_grad = dot(douts[...], w_out[...], ((1,), (1,)))
     root = math.sqrt(2 / math.pi)
@@ -177,6 +178,7 @@
     act[...] = (0.5 * v * (1.0 + t)).astype(BF16)
     slope = 0.5 * (1.0 + t) + 0.5 * v * (1.0 - t * t) * (root * (1.0 + 3 * 0.044715 * square))
     pre_grad[...] = (act_grad * slope).astype(BF16)
+    after("units")
     tails = dot(pre_grad[...], w_in[:, 2048:2560])
     lane = iota((128, 128), 1)
     for f in range(CTX_COUNT):
@@ -190,6 +192,7 @@
         else:
             tail = jnp.where(lane < 64, pltpu.roll(a, 64, 1), b)
         put(f, slice(512, 640), tail.astype(BF16))
+        after(f)
 
 
 def early_kernel(own, up, down, partner, w_in, w_out, sums, rows, douts, act, pre_grad):
@@ -201,31 +204,76 @@
 
 
 def late_kernel(at_ref, *refs):
-    shards, (w_in, w_out, early, query_pack) = refs[:6], refs[6:10]
-    sums, rows, douts, act, pre_grad = refs[10:]
+    given, results, held = refs[:9], refs[9:14], refs[14:]
+    shards, (w_in, w_out), sums, kept = held[:4], held[4:6], held[6], held[7:11]
+    arrived, left = held[11:]
     where = [pl.ds(pl.multiple_of(32 * at_ref[k], 32), 32) for k in range(CTX_COUNT)]
+    landing = [
+        *shards[:2],
+        *(shards[k].at[128 * j : 128 * j + 128] for k in (2, 3) for j in range(2)),
+        w_in,
+        w_out,
+    ]
+    loads = [pltpu.make_async_copy(given[k], landing[k], arrived.at[k]) for k in range(8)]
+    for load in loads:
+        load.start()
+    stores = [pltpu.make_async_copy(kept[k], results[1 + k], left.at[k]) for k in range(4)]
+    stores += [
+        pltpu.make_async_copy(
+            given[8].at[:, 32 * k : 32 * k + 32, :], results[0].at[:, where[k], :], left.at[4 + k]
+        )
+        for k in range(4)
+    ]
+    for store in stores[4:]:
+        store.start()
+    for k in range(4):
+        stores += [
+            pltpu.make_async_copy(
+                sums.at[f, 32 * k : 32 * k + 32, :],
+                results[0].at[f, where[4 + k], :],
+                left.at[8 + CTX_COUNT * k + f],
+            )
+            for f in range(CTX_COUNT)
+        ]
+
+    def block(k):
+        for load in loads[k : k + 1] if k < 2 else loads[2 * k - 2 : 2 * k]:
+            load.wait()
+        return shards[k][...]
 
     def put(f, lanes, value):
-        for k in range(4):
-            sums[f, where[4 + k], lanes] = value[32 * k : 32 * k + 32]
-
-    blocks = [lambda s=s: s[...] for s in shards[:2]]
-    blocks += [
-        lambda k=k: jnp.concatenate([shards[k][...], shards[k + 1][...]], axis=0) for k in (2, 4)
-    ]
-    experts_of(blocks, w_in, w_out, rows, douts, act, pre_grad, put)
-    for f in range(CTX_COUNT):
-        for k in range(4):
-            sums[f, where[k], :] = early[f, 32 * k : 32 * k + 32, :]
-        sums[f, 256:320, :] = query_pack[f]
+        sums[f, :, lanes] = value
+
+    def after(step):
+        if step == "rows":
+            stores[0].start()
+            stores[1].start()
+            loads[6].wait()
+            loads[7].wait()
+        elif step == "units":
+            stores[2].start()
+            stores[3].start()
+        else:
+            for k in range(4):
+                stores[8 + CTX_COUNT * k + step].start()
+
+    blocks = [lambda k=k: block(k) for k in range(4)]
+    experts_of(blocks, w_in, w_out, *kept, put, after)
+    for store in stores:
+        store.wait()
 
 
 def weights_kernel(*refs):
-    (early, late), out = (refs[:4], refs[4:8]), refs[8]
+    given, out, held, arrived = refs[:8], refs[8], refs[9:17], refs[17]
+    loads = [pltpu.make_async_copy(given[k], held[k], arrived.at[k]) for k in range(8)]
+    for load in loads:
+        load.start()
     unit, column = iota((UNITS, 2 * UNITS), 0), iota((UNITS, 2 * UNITS), 1)
     even, odd = one(column == 2 * unit), one(column == 2 * unit + 1)
+    for load in loads:
+        load.wait()
     terms = []
-    for rows, douts, act, pre_grad in (early, late):
+    for rows, douts, act, pre_grad in (held[:4], held[4:]):
         terms.append((dot(pre_grad[...], even).astype(BF16), rows))
         terms.append((dot(act[...], odd).astype(BF16), douts))
     for n in range(D // 512):
@@ -233,17 +281,19 @@
         out[:, lanes] = sum(dot(a, b[:, lanes], ((0,), (0,))) for a, b in terms).astype(BF16)
 
 
-def total_kernel(parts, back, query):
+def total_kernel(parts, back):
     total = parts[0].astype(F32)
     for k in range(1, CTX_COUNT):
         total = total + parts[k].astype(F32)
     to, source = iota((ROWS, ROWS), 0), iota((ROWS, ROWS), 1)
     order = one(source == 32 * (to % 8) + to // 8)
-    back[...] = dot(order, total[0:256].astype(BF16)).astype(BF16)
-    query[...] = total[256:320]
-
-
-def tokens_kernel(returned, even, odd, query, out):
+    back[...] = dot(order, total.astype(BF16)).astype(BF16)
+
+
+def tokens_kernel(returned, even, odd, own, below, across, above, out):
+    query = (own[...].astype(F32) + across[...].astype(F32)) + (
+        below[...].astype(F32) + above[...].astype(F32)
+    )
     a = dot(even[...], returned[...], ((0,), (0,)))
     b = dot(odd[...], returned[...], ((0,), (0,)))
     wide = a[:, 0:256] + b[:, 256:512]
@@ -289,7 +339,7 @@
 ):
     states, grads, keys, values = states[0], out_grad[0], doc_keys[0], doc_values[0]
     y, x = lax.axis_index("ctx_0"), lax.axis_index("ctx_1")
-    here = (2 * y + x).astype(jnp.int32)
+    place = jnp.stack([y, x]).astype(jnp.int32)
     normed, send, even, odd = call(
         route_kernel,
         [SMEM] + [VMEM] * 5,
@@ -297,7 +347,7 @@
         flops=2 * 4 * ROWS * TOKENS * HALF,
         moved=3 * 2**20,
         limit=VMEM_ALL,
-    )(here.reshape(1), states, grads, norm_gain, expert_ids[0].T, gate_values[0].T)
+    )(place, states, grads, norm_gain, expert_ids[0].T, gate_values[0].T)
     own = lax.all_to_all(
         send.reshape(EXPERTS, 8, HALF), "exp", split_axis=0, concat_axis=0, tiled=True
     ).reshape(ROWS, HALF)
@@ -313,22 +363,26 @@
     far = moved_by(near, "ctx_1", 1)
     keys_grad, values_grad, query_pack = call(
         score_grad_kernel,
-        [VMEM] * 8,
-        [shape((KEYS, D)), shape((KEYS, D)), shape((CTX_COUNT, 64, CHUNK))],
+        [SMEM] + [VMEM] * 8,
+        [shape((KEYS, D)), shape((KEYS, D)), shape((2, 4, 64, CHUNK))],
         [pltpu.VMEM((TOKENS, D), F32)],
         flops=3 * 2 * KEYS * TOKENS * D,
         moved=6 * 2**20,
         limit=VMEM_ALL,
-    )(normed, grads, keys, weights, slopes, stats, near, far)
+    )(place, normed, grads, keys, weights, slopes, stats, near, far)
+
 
     up, down = moved_by(own, "ctx_0", 1), moved_by(own, "ctx_0", 3)
     partner = moved_by(own, "ctx_1", 1)
+    up, down, partner, query_pack = lax.optimization_barrier((up, down, partner, query_pack))
     across = [moved_by(up[:128], "ctx_0", 1), moved_by(down[128:], "ctx_0", 3)]
+    far_query = moved_by(query_pack[0], "ctx_1", 1)
+    *across, expert_weights = lax.optimization_barrier((*across, expert_weights))
     partner_up, partner_down = moved_by(partner, "ctx_0", 1), moved_by(partner, "ctx_0", 3)
     partner_across = [moved_by(piece, "ctx_1", 1) for piece in across]
+    w_in, w_out = expert_weights[0, :, 0, :], expert_weights[0, :, 1, :]
     places = [(0, 0), (-1, 0), (1, 0), (0, 1), (-1, 1), (1, 1), (2, 0), (2, 1)]
     at = jnp.stack([2 * ((y + a + 4) % 4) + (x + b) % 2 for a, b in places]).astype(jnp.int32)
-    w_in, w_out = expert_weights[0, :, 0, :], expert_weights[0, :, 1, :]
     kept = [shape((SLOTS, D))] * 2 + [shape((SLOTS, UNITS))] * 2
     early_sums, *early = call(
         early_kernel,
@@ -336,37 +390,47 @@
         [shape((CTX_COUNT, SLOTS // 2, CHUNK)), *kept],
         flops=2 * 3 * SLOTS * UNITS * D,
         moved=8 * 2**20,
+        limit=VMEM_ALL,
     )(own, up, down, partner, w_in, w_out)
     sums, *late = call(
         late_kernel,
-        [SMEM] + [VMEM] * 10,
-        [shape((CTX_COUNT, 320, CHUNK)), *kept],
+        [SMEM] + [ANY] * 9,
+        [shape((CTX_COUNT, ROWS, CHUNK)), *kept],
+        [
+            *[pltpu.VMEM((ROWS, HALF), BF16)] * 4,
+            *[pltpu.VMEM((UNITS, D), BF16)] * 2,
+            pltpu.VMEM((CTX_COUNT, SLOTS // 2, CHUNK), BF16),
+            *[pltpu.VMEM(k.shape, BF16) for k in kept],
+            pltpu.SemaphoreType.DMA((8,)),
+            pltpu.SemaphoreType.DMA((8 + 4 * CTX_COUNT,)),
+        ],
         flops=2 * 3 * SLOTS * UNITS * D,
         moved=12 * 2**20,
-    )(at, partner_up, partner_down, *across, *partner_across, w_in, w_out, early_sums, query_pack)
+        places=[ANY] * 5,
+        limit=VMEM_ALL,
+    )(at, partner_up, partner_down, *across, *partner_across, w_in, w_out, early_sums)
+    sums, far_query = lax.optimization_barrier((sums, far_query))
     parts = lax.all_to_all(sums, CTX, split_axis=0, concat_axis=0, tiled=True)
-    back, query = call(
-        total_kernel,
-        [VMEM],
-        [shape((ROWS, CHUNK)), shape((64, CHUNK), F32)],
-        moved=4 * 2**20,
-    )(parts)
-    late[3], back = lax.optimization_barrier((late[3], back))
-    returned = lax.all_to_all(
-        back.reshape(EXPERTS, 8, CHUNK), "exp", split_axis=0, concat_axis=0, tiled=True
-    ).reshape(ROWS, CHUNK)
     [weights_grad] = call(
         weights_kernel,
-        [VMEM] * 8,
+        [ANY] * 8,
         [shape((2 * UNITS, D))],
+        [pltpu.VMEM(k.shape, BF16) for k in (*kept, *kept)] + [pltpu.SemaphoreType.DMA((8,))],
         flops=2 * 4 * SLOTS * UNITS * D,
         moved=8 * 2**20,
         limit=VMEM_ALL,
     )(*early, *late)
     weights_grad = weights_grad.reshape(1, UNITS, 2, D)
-    returned, weights_grad = lax.optimization_barrier((returned, weights_grad))
-    [total] = call(tokens_kernel, [VMEM] * 4, [shape((CTX_COUNT, 64, CHUNK))], moved=2**20)(
-        returned, even, odd, query
+    parts, weights_grad = lax.optimization_barrier((parts, weights_grad))
+    [back] = call(total_kernel, [VMEM], [shape((ROWS, CHUNK))], moved=3 * 2**20)(parts)
+    back, far_query = lax.optimization_barrier((back, far_query))
+    returned = lax.all_to_all(
+        back.reshape(EXPERTS, 8, CHUNK), "exp", split_axis=0, concat_axis=0, tiled=True
+    ).reshape(ROWS, CHUNK)
+    queries = call(join_kernel, [VMEM] * 2, [shape((64, CHUNK))] * 4, moved=2**20)(query_pack, far_query)
+    queries = [queries[0]] + [moved_by(queries[k], "ctx_0", k) for k in (1, 2, 3)]
+    [total] = call(tokens_kernel, [VMEM] * 7, [shape((CTX_COUNT, 64, CHUNK))], moved=2**20)(
+        returned, even, odd, *queries
     )
     packs = lax.all_to_all(total, CTX, split_axis=0, concat_axis=0, tiled=True)
     [states_grad] = call(

time: 170 us -> 212 us (1.25)
  waiting for transfers between devices: 16 us -> 58.5 us
  blocking collectives: 55 us -> 14.9 us
  Pallas kernels: 26.8 us -> 66.6 us
  starting transfers between devices: 45.6 us -> 50.5 us
  local copies, waits for them, and re-layouts: 23.9 us -> 19.2 us
    all_to_all x1 -> x0, blocking collectives: 38.9 us -> none  [on_device(): parts = lax.all_to_all(sums, CTX, split_axis=0, concat_axis=0, tiled=True)]
    pallas_call x5 -> x6, Pallas kernels: 17.4 us -> 54.8 us  [the longest x1 42 us: on_device(): call(late_kernel, [SMEM] + [ANY] * 9, [shape((CTX_COUNT, ROWS, CHUNK)), *...]
    ppermute x13 -> x17, waiting for transfers between devices: 4.47 us -> 26.6 us  [moved_by(): lax.ppermute(array, axis, [(k, (k + step) % count) for k in range(count)])]
    all_to_all x0 -> x1, waiting for transfers between devices: none -> 16 us  [on_device(): parts = lax.all_to_all(sums, CTX, split_axis=0, concat_axis=0, tiled=True)]
    slice x1 -> x0, local copies, waits for them, and re-layouts: 6.5 us -> none  [on_device(): w_in, w_out = (expert_weights[0, :, 0, :], expert_weights[0, :, 1, :])]
    all_to_all x0 -> x1, starting transfers between devices: none -> 4.99 us  [on_device(): parts = lax.all_to_all(sums, CTX, split_axis=0, concat_axis=0, tiled=True)]
    all_to_all x1, waiting for transfers between devices: 0.01 us -> 4.37 us  [on_device(): lax.all_to_all(back.reshape(EXPERTS, 8, CHUNK), 'exp', split_axis=0, conc...]
    unnamed x58 -> x42, local copies, waits for them, and re-layouts: 10.2 us -> 5.92 us
  transfers between devices with their start and end apart: 15 -> 20, of which waited for: 3 -> 8; matrix products, arithmetic and copies ran while one was open for 8% -> 5% of each run, Pallas kernels for 9% -> 29%
where the time goes in v6:
time: 212 us; the launch traced here: 211 us
  Pallas kernels  66.6 us (31%)
  waiting for transfers between devices  58.5 us (28%)
  starting transfers between devices  50.5 us (24%)
  local copies, waits for them, and re-layouts  19.2 us (9%)
  blocking collectives  14.9 us (7%)
    pallas_call x1, Pallas kernels, on_device(): call(late_kernel, [SMEM] + [ANY] * 9, [shape((CTX_COUNT, ROWS, CHUNK)), *...  42 us
    ppermute x17, starting transfers between devices, moved_by(): lax.ppermute(array, axis, [(k, (k + step) % count) for k in range(count)])  27.8 us
    ppermute x17, waiting for transfers between devices, moved_by(): lax.ppermute(array, axis, [(k, (k + step) % count) for k in range(count)])  26.6 us
    all_to_all x1, waiting for transfers between devices, on_device(): parts = lax.all_to_all(sums, CTX, split_axis=0, concat_axis=0, tiled=True)  16 us
    all_to_all x1, blocking collectives, on_device(): packs = lax.all_to_all(total, CTX, split_axis=0, concat_axis=0, tiled=True)  14.9 us
    all_to_all x1, waiting for transfers between devices, on_device(): lax.all_to_all(send.reshape(EXPERTS, 8, HALF), 'exp', split_axis=0, conca...  11.5 us
    all_to_all x1, starting transfers between devices, on_device(): lax.all_to_all(send.reshape(EXPERTS, 8, HALF), 'exp', split_axis=0, conca...  9.83 us
    all_to_all x1, starting transfers between devices, on_device(): lax.all_to_all(back.reshape(EXPERTS, 8, CHUNK), 'exp', split_axis=0, conc...  7.81 us
  transfers between devices with their start and end apart: 20, of which 8 were waited for; matrix products, arithmetic and copies ran while one was open for 5% of the time, Pallas kernels for 29%

profile of v6, /device:TPU:32, one launch (start us, length us, event | category | flops | bytes accessed | tf_op | source)
XLA Modules:
  0.0 211.3 jit_solution(14295534448757774808)
XLA Ops:
  0.6 0.6 pad_add_fusion.place
  1.3 3.5 %shard_map.111 = (bf16[128,2560]{1,0:T(8,128)(2,1)}, bf16[256,1280]{1,0:T(8,128)(2,1)}, bf16[256,128]{1,0:T(8,128)(2,1)}, bf16[256,128]{1,0:T(8,128)(2,1)}) custom-call(s32[2]{0:T(128)} %pad_add_fusion.place, bf16[128,2560]{1,0:T(8,128)(2,1)} %bitcast.37, bf16[128,2560]{1,0:T(8,128)(2,1)} %bitcast.33, f32[2560]{0:T(1024)} %gain.3, s32[2,128]{1,0:T(2,128)} %bitcast.46, ...), custom_call_target="tpu_custom_call" | custom-call | flops 335544320 | bytes 3145728 | tf_op jit(solution)/shard_map/pallas_call | solution.py:343
  4.8 9.8 %all-to-all-start = ((bf16[32,8,1280]{2,1,0:T(8,128)(2,1)}), bf16[32,8,1280]{2,1,0:T(8,128)(2,1)}, u32[]{:S(2)}, u32[]{:S(2)}) async-start(bf16[32,8,1280]{2,1,0:T(8,128)(2,1)} %bitcast.45), calls=%async_computation | async-start | bytes 1310720 | tf_op jit(solution)/shard_map/all_to_all | solution.py:351
  14.7 1.1 shard_map.112
  15.8 1.0 copy-done.6
  16.8 1.1 copy-done.7
  17.9 1.6 collective-permute-start.3
  19.5 2.9 %collective-permute-start.4 = (f32[72,128]{1,0:T(8,128)S(1)}, f32[72,128]{1,0:T(8,128)S(1)}, u32[]{:S(2)}, u32[]{:S(2)}) collective-permute-start(f32[72,128]{1,0:T(8,128)S(1)} %get-tuple-element.45.local), channel_id=1, source_target_pairs={{0,128},{64,192},{128,0},{192,64},{1,129},{65,193},{129,1},{193,65... | collective-permute-start | bytes 110600 | tf_op jit(solution)/shard_map/ppermute | solution.py:334
  22.4 1.3 collective-permute-start.5
  23.7 11.5 %all-to-all-done = bf16[32,8,1280]{2,1,0:T(8,128)(2,1)} async-done(((bf16[32,8,1280]{2,1,0:T(8,128)(2,1)}), bf16[32,8,1280]{2,1,0:T(8,128)(2,1)}, u32[]{:S(2)}, u32[]{:S(2)}) %all-to-all-start) | async-done | bytes 655392 | tf_op jit(solution)/shard_map/all_to_all | solution.py:351
  35.3 1.6 collective-permute-start
  36.8 1.7 collective-permute-start.1
  38.5 2.7 %collective-permute-start.2 = (bf16[256,1280]{1,0:T(8,128)(2,1)}, bf16[256,1280]{1,0:T(8,128)(2,1)}, u32[]{:S(2)}, u32[]{:S(2)}) collective-permute-start(bf16[256,1280]{1,0:T(8,128)(2,1)} %bitcast.17.own), channel_id=1, source_target_pairs={{0,32},{32,0},{1,33},{33,1},{2,34},{34,2},{3,35},{35,3},{4,36},{36... | collective-permute-start | bytes 1966088 | tf_op jit(solution)/shard_map/ppermute | solution.py:334
  41.3 0.9 collective-permute-start.6
  42.2 14.0 %collective-permute-done.6.far = f32[72,128]{1,0:T(8,128)S(1)} collective-permute-done((f32[72,128]{1,0:T(8,128)S(1)}, f32[72,128]{1,0:T(8,128)S(1)}, u32[]{:S(2)}, u32[]{:S(2)}) %collective-permute-start.6) | collective-permute-done | bytes 36896 | tf_op jit(solution)/shard_map/ppermute | solution.py:334
  56.2 0.6 copy-done.20
  56.8 4.5 %shard_map.113 = (bf16[128,2560]{1,0:T(8,128)(2,1)}, bf16[128,2560]{1,0:T(8,128)(2,1)}, bf16[2,4,64,640]{3,2,1,0:T(8,128)(2,1)}) custom-call(s32[2]{0:T(128)} %pad_add_fusion.place, bf16[128,2560]{1,0:T(8,128)(2,1)} %get-tuple-element.42.normed, bf16[128,2560]{1,0:T(8,128)(2,1)} %bitcast.34, bf16[128,2560]{1,0:T(8,128)(2,1)} %bitcast.39, ...), custom_call_target="tpu_custom_call" | custom-call | flops 251658240 | bytes 6291456 | tf_op jit(solution)/shard_map/pallas_call | solution.py:364
  61.3 1.8 slice.68
  63.0 1.7 collective-permute-start.10
  64.8 1.7 slice.67
  66.8 0.6 stack.44.at_ref
  67.7 2.9 %collective-permute-start.8 = (bf16[256,1280]{1,0:T(8,128)(2,1)}, bf16[256,1280]{1,0:T(8,128)(2,1)}, u32[]{:S(2)}, u32[]{:S(2)}) collective-permute-start(bf16[256,1280]{1,0:T(8,128)(2,1)} %collective-permute-done.2.partner), channel_id=1, source_target_pairs={{0,192},{64,0},{128,64},{192,128},{1,193},{65,1},{129,65},{193,129... | collective-permute-start | bytes 1966088 | tf_op jit(solution)/shard_map/ppermute | solution.py:334
  70.7 0.8 slice_bitcast_fusion.2
  71.4 2.7 %collective-permute-start.13 = (bf16[4,64,640]{2,1,0:T(8,128)(2,1)}, bf16[4,64,640]{2,1,0:T(8,128)(2,1)S(1)}, u32[]{:S(2)}, u32[]{:S(2)}) collective-permute-start(bf16[4,64,640]{2,1,0:T(8,128)(2,1)} %slice_bitcast_fusion.2), channel_id=1, source_target_pairs={{0,32},{32,0},{1,33},{33,1},{2,34},{34,2},{3,35},{35,3},{4,36},{36... | collective-permute-start | bytes 983048 | tf_op jit(solution)/shard_map/ppermute | solution.py:334
  74.2 4.5 %collective-permute-done.9.refs_2_ = bf16[128,1280]{1,0:T(8,128)(2,1)} collective-permute-done((bf16[128,1280]{1,0:T(8,128)(2,1)}, bf16[128,1280]{1,0:T(8,128)(2,1)}, u32[]{:S(2)}, u32[]{:S(2)}) %collective-permute-start.9) | collective-permute-done | bytes 327712 | tf_op jit(solution)/shard_map/ppermute | solution.py:334
  78.9 2.8 %collective-permute-start.11 = (bf16[128,1280]{1,0:T(8,128)(2,1)}, bf16[128,1280]{1,0:T(8,128)(2,1)S(1)}, u32[]{:S(2)}, u32[]{:S(2)}) collective-permute-start(bf16[128,1280]{1,0:T(8,128)(2,1)} %collective-permute-done.9.refs_2_), channel_id=1, source_target_pairs={{0,32},{32,0},{1,33},{33,1},{2,34},{34,2},{3,35},{35,3},{4,36},{36... | collective-permute-start | bytes 983048 | tf_op jit(solution)/shard_map/ppermute | solution.py:334
  81.8 0.8 collective-permute-start.12
  82.6 1.7 slice_bitcast_fusion
  84.2 5.7 %shard_map.114 = (bf16[8,128,640]{2,1,0:T(8,128)(2,1)}, bf16[256,2560]{1,0:T(8,128)(2,1)}, bf16[256,2560]{1,0:T(8,128)(2,1)}, bf16[256,256]{1,0:T(8,128)(2,1)}, bf16[256,256]{1,0:T(8,128)(2,1)}) custom-call(bf16[256,1280]{1,0:T(8,128)(2,1)} %bitcast.17.own, bf16[256,1280]{1,0:T(8,128)(2,1)} %collective-permute-done.up, ...), custom_call_target="tpu_custom_call" | custom-call | flops 1006632960 | bytes 8388608 | tf_op jit(solution)/shard_map/pallas_call | solution.py:387
  90.0 3.5 %collective-permute-done.12.refs_5_ = bf16[128,1280]{1,0:T(8,128)(2,1)S(1)} collective-permute-done((bf16[128,1280]{1,0:T(8,128)(2,1)}, bf16[128,1280]{1,0:T(8,128)(2,1)S(1)}, u32[]{:S(2)}, u32[]{:S(2)}) %collective-permute-start.12) | collective-permute-done | bytes 327712 | tf_op jit(solution)/shard_map/ppermute | solution.py:334
  93.5 0.7 copy-done.18
  94.2 42.0 %shard_map.115 = (bf16[8,256,640]{2,1,0:T(8,128)(2,1)}, bf16[256,2560]{1,0:T(8,128)(2,1)}, bf16[256,2560]{1,0:T(8,128)(2,1)}, bf16[256,256]{1,0:T(8,128)(2,1)}, bf16[256,256]{1,0:T(8,128)(2,1)}) custom-call(s32[8]{0:T(128)} %stack.44.at_ref, bf16[256,1280]{1,0:T(8,128)(2,1)} %collective-permute-done.7.refs_0_, ...), custom_call_target="tpu_custom_call" | custom-call | flops 1006632960 | bytes 12582912 | tf_op jit(solution)/shard_map/pallas_call | solution.py:395
  136.2 0.7 copy-done.10
  136.9 5.0 %all-to-all-start.1 = ((bf16[8,256,640]{2,1,0:T(8,128)(2,1)}), bf16[8,256,640]{2,1,0:T(8,128)(2,1)S(1)}, u32[]{:S(2)}, u32[]{:S(2)}) async-start(bf16[8,256,640]{2,1,0:T(8,128)(2,1)} %get-tuple-element.56), calls=%async_computation.1 | async-start | bytes 5242880 | tf_op jit(solution)/shard_map/all_to_all | solution.py:413
  141.9 7.4 %shard_map.116 = bf16[512,2560]{1,0:T(8,128)(2,1)} custom-call(bf16[256,2560]{1,0:T(8,128)(2,1)} %get-tuple-element.57.refs_0_, bf16[256,2560]{1,0:T(8,128)(2,1)} %get-tuple-element.58.refs_1_, bf16[256,256]{1,0:T(8,128)(2,1)} %get-tuple-element.59.refs_2_, bf16[256,256]{1,0:T(8,128)(2,1)} %get-tuple-element.60.refs_3_, ...), custom_call_target="tpu_custom_call" | custom-call | flops 1342177280 | bytes 8388608 | tf_op jit(solution)/shard_map/pallas_call | solution.py:414
  149.3 6.4 %reshape.25 = bf16[1,256,2,2560]{3,2,1,0:T(2,128)(2,1)} reshape(bf16[512,2560]{1,0:T(8,128)(2,1)} %shard_map.116) | data formatting | bytes 5242880 | tf_op jit(solution)/shard_map/reshape | solution.py:423
  155.7 16.0 %all-to-all-done.1.parts = bf16[8,256,640]{2,1,0:T(8,128)(2,1)S(1)} async-done(((bf16[8,256,640]{2,1,0:T(8,128)(2,1)}), bf16[8,256,640]{2,1,0:T(8,128)(2,1)S(1)}, u32[]{:S(2)}, u32[]{:S(2)}) %all-to-all-start.1) | async-done | bytes 2621472 | tf_op jit(solution)/shard_map/all_to_all | solution.py:413
  171.8 0.6 shard_map.117
  172.4 0.7 copy-done.8
  173.1 7.8 %all-to-all-start.2 = ((bf16[32,8,640]{2,1,0:T(8,128)(2,1)}), bf16[32,8,640]{2,1,0:T(8,128)(2,1)S(1)}, u32[]{:S(2)}, u32[]{:S(2)}) async-start(bf16[32,8,640]{2,1,0:T(8,128)(2,1)} %bitcast.42), calls=%async_computation.2 | async-start | bytes 655360 | tf_op jit(solution)/shard_map/all_to_all | solution.py:427
  180.9 1.0 copy-done.11
  182.1 2.3 %collective-permute-start.15 = (bf16[64,640]{1,0:T(8,128)(2,1)S(1)}, bf16[64,640]{1,0:T(8,128)(2,1)S(1)}, u32[]{:S(2)}, u32[]{:S(2)}) collective-permute-start(bf16[64,640]{1,0:T(8,128)(2,1)S(1)} %get-tuple-element.73), channel_id=1, source_target_pairs={{0,128},{64,192},{128,0},{192,64},{1,129},{65,193},{129,1},{193,65... | collective-permute-start | bytes 245768 | tf_op jit(solution)/shard_map/ppermute | solution.py:334
  184.4 1.2 collective-permute-start.16
  185.5 4.0 %collective-permute-done.14.below = bf16[64,640]{1,0:T(8,128)(2,1)S(1)} collective-permute-done((bf16[64,640]{1,0:T(8,128)(2,1)S(1)}, bf16[64,640]{1,0:T(8,128)(2,1)S(1)}, u32[]{:S(2)}, u32[]{:S(2)}) %collective-permute-start.14) | collective-permute-done | bytes 81952 | tf_op jit(solution)/shard_map/ppermute | solution.py:334
  189.5 0.6 collective-permute-done.16.above
  190.1 4.4 %all-to-all-done.2 = bf16[32,8,640]{2,1,0:T(8,128)(2,1)S(1)} async-done(((bf16[32,8,640]{2,1,0:T(8,128)(2,1)}), bf16[32,8,640]{2,1,0:T(8,128)(2,1)S(1)}, u32[]{:S(2)}, u32[]{:S(2)}) %all-to-all-start.2) | async-done | bytes 327712 | tf_op jit(solution)/shard_map/all_to_all | solution.py:427
  194.9 14.9 %all_to_all.20.packs = bf16[8,64,640]{2,1,0:T(8,128)(2,1)S(1)} all-to-all(bf16[8,64,640]{2,1,0:T(8,128)(2,1)S(1)} %shard_map.119), channel_id=1, replica_groups=mesh['ctx_0'=4,'ctx_1'=2,'exp'=32] {'ctx_0','ctx_1'}, dimensions={0} | all-to-all | bytes 1310720 | tf_op jit(solution)/shard_map/all_to_all | solution.py:435
  209.8 1.5 shard_map.120
  (56 shorter events, 1.6 us)
Async XLA Ops:
  1.3 13.3 %copy-start = (bf16[1,128,2560]{2,1,0:T(8,128)(2,1)S(1)}, bf16[1,128,2560]{2,1,0:T(8,128)(2,1)}, u32[]{:S(2)}) copy-start(bf16[1,128,2560]{2,1,0:T(8,128)(2,1)} %param.9) | copy-start | bytes 1966084
  1.3 13.4 %copy-start.3 = (bf16[1,128,2560]{2,1,0:T(8,128)(2,1)S(1)}, bf16[1,128,2560]{2,1,0:T(8,128)(2,1)}, u32[]{:S(2)}) copy-start(bf16[1,128,2560]{2,1,0:T(8,128)(2,1)} %param.10) | copy-start | bytes 1966084
  1.3 13.4 %copy-start.9 = (bf16[1,128,2560]{2,1,0:T(8,128)(2,1)S(1)}, bf16[1,128,2560]{2,1,0:T(8,128)(2,1)}, u32[]{:S(2)}) copy-start(bf16[1,128,2560]{2,1,0:T(8,128)(2,1)} %param.11) | copy-start | bytes 1966084
  4.8 9.9 %copy-start.4 = (bf16[128,2560]{1,0:T(8,128)(2,1)S(1)}, bf16[128,2560]{1,0:T(8,128)(2,1)}, u32[]{:S(2)}) copy-start(bf16[128,2560]{1,0:T(8,128)(2,1)} %get-tuple-element.42.normed) | copy-start | bytes 1966084
  4.8 30.5 %all-to-all-start = ((bf16[32,8,1280]{2,1,0:T(8,128)(2,1)}), bf16[32,8,1280]{2,1,0:T(8,128)(2,1)}, u32[]{:S(2)}, u32[]{:S(2)}) async-start(bf16[32,8,1280]{2,1,0:T(8,128)(2,1)} %bitcast.45), calls=%async_computation | async-start | bytes 1310720 | tf_op jit(solution)/shard_map/all_to_all | solution.py:351
  15.7 1.1 copy-start.6
  16.8 1.1 copy-start.7
  17.9 38.2 %copy-start.12 = (f32[72,128]{1,0:T(8,128)}, f32[72,128]{1,0:T(8,128)S(1)}, u32[]{:S(2)}) copy-start(f32[72,128]{1,0:T(8,128)S(1)} %get-tuple-element.45.local) | copy-start | bytes 110596
  17.9 20.6 %collective-permute-start.3 = (f32[72,128]{1,0:T(8,128)S(1)}, f32[72,128]{1,0:T(8,128)S(1)}, u32[]{:S(2)}, u32[]{:S(2)}) collective-permute-start(f32[72,128]{1,0:T(8,128)S(1)} %get-tuple-element.45.local), channel_id=1, source_target_pairs={{0,64},{64,128},{128,192},{192,0},{1,65},{65,129},{129,193},{193,1... | collective-permute-start | bytes 110600 | tf_op jit(solution)/shard_map/ppermute | solution.py:334
  19.5 21.7 %collective-permute-start.4 = (f32[72,128]{1,0:T(8,128)S(1)}, f32[72,128]{1,0:T(8,128)S(1)}, u32[]{:S(2)}, u32[]{:S(2)}) collective-permute-start(f32[72,128]{1,0:T(8,128)S(1)} %get-tuple-element.45.local), channel_id=1, source_target_pairs={{0,128},{64,192},{128,0},{192,64},{1,129},{65,193},{129,1},{193,65... | collective-permute-start | bytes 110600 | tf_op jit(solution)/shard_map/ppermute | solution.py:334
  22.4 18.8 %collective-permute-start.5 = (f32[72,128]{1,0:T(8,128)S(1)}, f32[72,128]{1,0:T(8,128)S(1)}, u32[]{:S(2)}, u32[]{:S(2)}) collective-permute-start(f32[72,128]{1,0:T(8,128)S(1)} %get-tuple-element.45.local), channel_id=1, source_target_pairs={{0,192},{64,0},{128,64},{192,128},{1,193},{65,1},{129,65},{193,129... | collective-permute-start | bytes 110600 | tf_op jit(solution)/shard_map/ppermute | solution.py:334
  35.3 26.0 %collective-permute-start = (bf16[256,1280]{1,0:T(8,128)(2,1)}, bf16[256,1280]{1,0:T(8,128)(2,1)}, u32[]{:S(2)}, u32[]{:S(2)}) collective-permute-start(bf16[256,1280]{1,0:T(8,128)(2,1)} %bitcast.17.own), channel_id=1, source_target_pairs={{0,64},{64,128},{128,192},{192,0},{1,65},{65,129},{129,193},{193,1... | collective-permute-start | bytes 1966088 | tf_op jit(solution)/shard_map/ppermute | solution.py:334
  36.8 24.4 %collective-permute-start.1 = (bf16[256,1280]{1,0:T(8,128)(2,1)}, bf16[256,1280]{1,0:T(8,128)(2,1)}, u32[]{:S(2)}, u32[]{:S(2)}) collective-permute-start(bf16[256,1280]{1,0:T(8,128)(2,1)} %bitcast.17.own), channel_id=1, source_target_pairs={{0,192},{64,0},{128,64},{192,128},{1,193},{65,1},{129,65},{193,129... | collective-permute-start | bytes 1966088 | tf_op jit(solution)/shard_map/ppermute | solution.py:334
  38.5 22.8 %collective-permute-start.2 = (bf16[256,1280]{1,0:T(8,128)(2,1)}, bf16[256,1280]{1,0:T(8,128)(2,1)}, u32[]{:S(2)}, u32[]{:S(2)}) collective-permute-start(bf16[256,1280]{1,0:T(8,128)(2,1)} %bitcast.17.own), channel_id=1, source_target_pairs={{0,32},{32,0},{1,33},{33,1},{2,34},{34,2},{3,35},{35,3},{4,36},{36... | collective-permute-start | bytes 1966088 | tf_op jit(solution)/shard_map/ppermute | solution.py:334
  41.3 14.9 %copy-start.19 = (f32[72,128]{1,0:T(8,128)}, f32[72,128]{1,0:T(8,128)S(1)}, u32[]{:S(2)}) copy-start(f32[72,128]{1,0:T(8,128)S(1)} %pad_maximum_fusion.near) | copy-start | bytes 110596
  41.3 14.8 %collective-permute-start.6 = (f32[72,128]{1,0:T(8,128)S(1)}, f32[72,128]{1,0:T(8,128)S(1)}, u32[]{:S(2)}, u32[]{:S(2)}) collective-permute-start(f32[72,128]{1,0:T(8,128)S(1)} %pad_maximum_fusion.near), channel_id=1, source_target_pairs={{0,32},{32,0},{1,33},{33,1},{2,34},{34,2},{3,35},{35,3},{4,36},{36... | collective-permute-start | bytes 110600 | tf_op jit(solution)/shard_map/ppermute | solution.py:334
  56.1 0.6 copy-start.20
  56.8 21.9 %copy-start.16 = (bf16[1,256,2,2560]{3,2,1,0:T(2,128)(2,1)S(1)}, bf16[1,256,2,2560]{3,2,1,0:T(2,128)(2,1)}, u32[]{:S(2)}) copy-start(bf16[1,256,2,2560]{3,2,1,0:T(2,128)(2,1)} %param.15) | copy-start | bytes 7864324
  61.2 9.4 %copy-start.5 = (bf16[2,4,64,640]{3,2,1,0:T(8,128)(2,1)S(1)}, bf16[2,4,64,640]{3,2,1,0:T(8,128)(2,1)}, u32[]{:S(2)}) copy-start(bf16[2,4,64,640]{3,2,1,0:T(8,128)(2,1)} %get-tuple-element.55.query_pack) | copy-start | bytes 1966084
  63.0 11.1 %collective-permute-start.10 = (bf16[128,1280]{1,0:T(8,128)(2,1)}, bf16[128,1280]{1,0:T(8,128)(2,1)}, u32[]{:S(2)}, u32[]{:S(2)}) collective-permute-start(bf16[128,1280]{1,0:T(8,128)(2,1)} %slice.68), channel_id=1, source_target_pairs={{0,192},{64,0},{128,64},{192,128},{1,193},{65,1},{129,65},{193,129... | collective-permute-start | bytes 983048 | tf_op jit(solution)/shard_map/ppermute | solution.py:334
  66.5 12.2 %collective-permute-start.9 = (bf16[128,1280]{1,0:T(8,128)(2,1)}, bf16[128,1280]{1,0:T(8,128)(2,1)}, u32[]{:S(2)}, u32[]{:S(2)}) collective-permute-start(bf16[128,1280]{1,0:T(8,128)(2,1)} %slice.67), channel_id=1, source_target_pairs={{0,64},{64,128},{128,192},{192,0},{1,65},{65,129},{129,193},{193,1... | collective-permute-start | bytes 983048 | tf_op jit(solution)/shard_map/ppermute | solution.py:334
  67.4 26.1 %collective-permute-start.7 = (bf16[256,1280]{1,0:T(8,128)(2,1)}, bf16[256,1280]{1,0:T(8,128)(2,1)}, u32[]{:S(2)}, u32[]{:S(2)}) collective-permute-start(bf16[256,1280]{1,0:T(8,128)(2,1)} %collective-permute-done.2.partner), channel_id=1, source_target_pairs={{0,64},{64,128},{128,192},{192,0},{1,65},{65,129},{129,193},{193,1... | collective-permute-start | bytes 1966088 | tf_op jit(solution)/shard_map/ppermute | solution.py:334
  67.7 25.8 %collective-permute-start.8 = (bf16[256,1280]{1,0:T(8,128)(2,1)}, bf16[256,1280]{1,0:T(8,128)(2,1)}, u32[]{:S(2)}, u32[]{:S(2)}) collective-permute-start(bf16[256,1280]{1,0:T(8,128)(2,1)} %collective-permute-done.2.partner), channel_id=1, source_target_pairs={{0,192},{64,0},{128,64},{192,128},{1,193},{65,1},{129,65},{193,129... | collective-permute-start | bytes 1966088 | tf_op jit(solution)/shard_map/ppermute | solution.py:334
  71.4 64.8 %collective-permute-start.13 = (bf16[4,64,640]{2,1,0:T(8,128)(2,1)}, bf16[4,64,640]{2,1,0:T(8,128)(2,1)S(1)}, u32[]{:S(2)}, u32[]{:S(2)}) collective-permute-start(bf16[4,64,640]{2,1,0:T(8,128)(2,1)} %slice_bitcast_fusion.2), channel_id=1, source_target_pairs={{0,32},{32,0},{1,33},{33,1},{2,34},{34,2},{3,35},{35,3},{4,36},{36... | collective-permute-start | bytes 983048 | tf_op jit(solution)/shard_map/ppermute | solution.py:334
  78.9 11.1 %collective-permute-start.11 = (bf16[128,1280]{1,0:T(8,128)(2,1)}, bf16[128,1280]{1,0:T(8,128)(2,1)S(1)}, u32[]{:S(2)}, u32[]{:S(2)}) collective-permute-start(bf16[128,1280]{1,0:T(8,128)(2,1)} %collective-permute-done.9.refs_2_), channel_id=1, source_target_pairs={{0,32},{32,0},{1,33},{33,1},{2,34},{34,2},{3,35},{35,3},{4,36},{36... | collective-permute-start | bytes 983048 | tf_op jit(solution)/shard_map/ppermute | solution.py:334
  81.8 11.8 %collective-permute-start.12 = (bf16[128,1280]{1,0:T(8,128)(2,1)}, bf16[128,1280]{1,0:T(8,128)(2,1)S(1)}, u32[]{:S(2)}, u32[]{:S(2)}) collective-permute-start(bf16[128,1280]{1,0:T(8,128)(2,1)} %collective-permute-done.10.refs_3_), channel_id=1, source_target_pairs={{0,32},{32,0},{1,33},{33,1},{2,34},{34,2},{3,35},{35,3},{4,36},{36... | collective-permute-start | bytes 983048 | tf_op jit(solution)/shard_map/ppermute | solution.py:334
  90.0 3.5 %copy-start.17 = (bf16[128,1280]{1,0:T(8,128)(2,1)}, bf16[128,1280]{1,0:T(8,128)(2,1)S(1)}, u32[]{:S(2)}) copy-start(bf16[128,1280]{1,0:T(8,128)(2,1)S(1)} %collective-permute-done.11.refs_4_) | copy-start | bytes 983044
  93.5 0.7 copy-start.18
  136.2 0.7 copy-start.10
  136.9 34.8 %all-to-all-start.1 = ((bf16[8,256,640]{2,1,0:T(8,128)(2,1)}), bf16[8,256,640]{2,1,0:T(8,128)(2,1)S(1)}, u32[]{:S(2)}, u32[]{:S(2)}) async-start(bf16[8,256,640]{2,1,0:T(8,128)(2,1)} %get-tuple-element.56), calls=%async_computation.1 | async-start | bytes 5242880 | tf_op jit(solution)/shard_map/all_to_all | solution.py:413
  172.4 0.7 copy-start.8
  173.1 21.4 %copy-start.13 = (bf16[256,128]{1,0:T(8,128)(2,1)S(1)}, bf16[256,128]{1,0:T(8,128)(2,1)}, u32[]{:S(2)}) copy-start(bf16[256,128]{1,0:T(8,128)(2,1)} %get-tuple-element.68.even) | copy-start | bytes 196612
  173.1 21.4 %copy-start.14 = (bf16[256,128]{1,0:T(8,128)(2,1)S(1)}, bf16[256,128]{1,0:T(8,128)(2,1)}, u32[]{:S(2)}) copy-start(bf16[256,128]{1,0:T(8,128)(2,1)} %get-tuple-element.69.odd) | copy-start | bytes 196612
  173.1 21.4 %all-to-all-start.2 = ((bf16[32,8,640]{2,1,0:T(8,128)(2,1)}), bf16[32,8,640]{2,1,0:T(8,128)(2,1)S(1)}, u32[]{:S(2)}, u32[]{:S(2)}) async-start(bf16[32,8,640]{2,1,0:T(8,128)(2,1)} %bitcast.42), calls=%async_computation.2 | async-start | bytes 655360 | tf_op jit(solution)/shard_map/all_to_all | solution.py:427
  180.9 1.0 copy-start.11
  182.0 7.5 %collective-permute-start.14 = (bf16[64,640]{1,0:T(8,128)(2,1)S(1)}, bf16[64,640]{1,0:T(8,128)(2,1)S(1)}, u32[]{:S(2)}, u32[]{:S(2)}) collective-permute-start(bf16[64,640]{1,0:T(8,128)(2,1)S(1)} %get-tuple-element.72), channel_id=1, source_target_pairs={{0,64},{64,128},{128,192},{192,0},{1,65},{65,129},{129,193},{193,1... | collective-permute-start | bytes 245768 | tf_op jit(solution)/shard_map/ppermute | solution.py:334
  182.1 7.5 %collective-permute-start.15 = (bf16[64,640]{1,0:T(8,128)(2,1)S(1)}, bf16[64,640]{1,0:T(8,128)(2,1)S(1)}, u32[]{:S(2)}, u32[]{:S(2)}) collective-permute-start(bf16[64,640]{1,0:T(8,128)(2,1)S(1)} %get-tuple-element.73), channel_id=1, source_target_pairs={{0,128},{64,192},{128,0},{192,64},{1,129},{65,193},{129,1},{193,65... | collective-permute-start | bytes 245768 | tf_op jit(solution)/shard_map/ppermute | solution.py:334
  184.4 5.7 %collective-permute-start.16 = (bf16[64,640]{1,0:T(8,128)(2,1)S(1)}, bf16[64,640]{1,0:T(8,128)(2,1)S(1)}, u32[]{:S(2)}, u32[]{:S(2)}) collective-permute-start(bf16[64,640]{1,0:T(8,128)(2,1)S(1)} %get-tuple-element.74), channel_id=1, source_target_pairs={{0,192},{64,0},{128,64},{192,128},{1,193},{65,1},{129,65},{193,129... | collective-permute-start | bytes 245768 | tf_op jit(solution)/shard_map/ppermute | solution.py:334
  194.5 15.3 %copy-start.1 = (bf16[1,128,2560]{2,1,0:T(8,128)(2,1)S(1)}, bf16[1,128,2560]{2,1,0:T(8,128)(2,1)}, u32[]{:S(2)}) copy-start(bf16[1,128,2560]{2,1,0:T(8,128)(2,1)} %param.9) | copy-start | bytes 1966084
  194.5 15.3 %copy-start.2 = (bf16[1,128,2560]{2,1,0:T(8,128)(2,1)S(1)}, bf16[1,128,2560]{2,1,0:T(8,128)(2,1)}, u32[]{:S(2)}) copy-start(bf16[1,128,2560]{2,1,0:T(8,128)(2,1)} %param.8) | copy-start | bytes 1966084
  194.5 15.3 %copy-start.15 = (f32[2560]{0:T(1024)S(1)}, f32[2560]{0:T(1024)}, u32[]{:S(2)}) copy-start(f32[2560]{0:T(1024)} %gain.3) | copy-start | bytes 30724

commit v7 on v6

--- a/solution.py
+++ b/solution.py
@@ -62,7 +62,7 @@
 
 
 def route_kernel(place, states, grads, gain, ids, gates, normed_out, send, even, odd):
-    c = 2 * place[0] + place[1]
+    c = place[0]
     x = states[...].astype(F32)
     inverse = lax.rsqrt(jnp.mean(x * x, axis=-1, keepdims=True) + EPSILON)
     normed_out[...] = (x * inverse * gain[...].reshape(1, D)).astype(BF16)
@@ -139,7 +139,7 @@
         query[:, at] = dot(score_grad, keys[:, at], ((0,), (0,))) * SCALE
     lane = iota((64, 128), 1)
     for f in range(CTX_COUNT):
-        column, row = (f + place[1] + 1) % 2, (f // 2 - place[0] + 4) % 4
+        column, row = (f + place[0] + 1) % 2, (f // 2 - place[0] // 2 + 4) % 4
         at = slice(256 * f, 256 * f + 256)
         query_pack[column, row, :, 0:256] = query[0:64, at].astype(BF16)
         query_pack[column, row, :, 256:512] = query[64:128, at].astype(BF16)
@@ -217,24 +217,19 @@
     loads = [pltpu.make_async_copy(given[k], landing[k], arrived.at[k]) for k in range(8)]
     for load in loads:
         load.start()
-    stores = [pltpu.make_async_copy(kept[k], results[1 + k], left.at[k]) for k in range(4)]
-    stores += [
+    early = [
         pltpu.make_async_copy(
-            given[8].at[:, 32 * k : 32 * k + 32, :], results[0].at[:, where[k], :], left.at[4 + k]
+            given[8].at[:, 32 * k : 32 * k + 32, :], sums.at[:, where[k], :], arrived.at[8 + k]
         )
         for k in range(4)
     ]
-    for store in stores[4:]:
-        store.start()
-    for k in range(4):
-        stores += [
-            pltpu.make_async_copy(
-                sums.at[f, 32 * k : 32 * k + 32, :],
-                results[0].at[f, where[4 + k], :],
-                left.at[8 + CTX_COUNT * k + f],
-            )
-            for f in range(CTX_COUNT)
-        ]
+    for load in early:
+        load.start()
+    stores = [pltpu.make_async_copy(kept[k], results[1 + k], left.at[k]) for k in range(4)]
+    stores += [
+        pltpu.make_async_copy(sums.at[f], results[0].at[f], left.at[4 + f])
+        for f in range(CTX_COUNT)
+    ]
 
     def block(k):
         for load in loads[k : k + 1] if k < 2 else loads[2 * k - 2 : 2 * k]:
@@ -242,7 +237,8 @@
         return shards[k][...]
 
     def put(f, lanes, value):
-        sums[f, :, lanes] = value
+        for k in range(4):
+            sums[f, where[4 + k], lanes] = value[32 * k : 32 * k + 32]
 
     def after(step):
         if step == "rows":
@@ -253,9 +249,10 @@
         elif step == "units":
             stores[2].start()
             stores[3].start()
+            for load in early:
+                load.wait()
         else:
-            for k in range(4):
-                stores[8 + CTX_COUNT * k + step].start()
+            stores[4 + step].start()
 
     blocks = [lambda k=k: block(k) for k in range(4)]
     experts_of(blocks, w_in, w_out, *kept, put, after)
@@ -339,7 +336,7 @@
 ):
     states, grads, keys, values = states[0], out_grad[0], doc_keys[0], doc_values[0]
     y, x = lax.axis_index("ctx_0"), lax.axis_index("ctx_1")
-    place = jnp.stack([y, x]).astype(jnp.int32)
+    place = (2 * y + x).astype(jnp.int32).reshape(1)
     normed, send, even, odd = call(
         route_kernel,
         [SMEM] + [VMEM] * 5,
@@ -361,6 +358,42 @@
     )(normed, grads, keys, values)
     near = merged([stats] + [moved_by(stats, "ctx_0", k) for k in (1, 2, 3)])
     far = moved_by(near, "ctx_1", 1)
+    up, down = moved_by(own, "ctx_0", 1), moved_by(own, "ctx_0", 3)
+    partner = moved_by(own, "ctx_1", 1)
+    across = [moved_by(up[:128], "ctx_0", 1), moved_by(down[128:], "ctx_0", 3)]
+    partner_up, partner_down = moved_by(partner, "ctx_0", 1), moved_by(partner, "ctx_0", 3)
+    partner_across = [moved_by(piece, "ctx_1", 1) for piece in across]
+    w_in, w_out = expert_weights[0, :, 0, :], expert_weights[0, :, 1, :]
+    places = [(0, 0), (-1, 0), (1, 0), (0, 1), (-1, 1), (1, 1), (2, 0), (2, 1)]
+    at = jnp.stack([2 * ((y + a + 4) % 4) + (x + b) % 2 for a, b in places]).astype(jnp.int32)
+    kept = [shape((SLOTS, D))] * 2 + [shape((SLOTS, UNITS))] * 2
+    ready, far = lax.optimization_barrier((partner, far))
+    early_sums, *early = call(
+        early_kernel,
+        [VMEM] * 6,
+        [shape((CTX_COUNT, SLOTS // 2, CHUNK)), *kept],
+        flops=2 * 3 * SLOTS * UNITS * D,
+        moved=8 * 2**20,
+        limit=VMEM_ALL,
+    )(own, up, down, ready, w_in, w_out)
+    sums, *late = call(
+        late_kernel,
+        [SMEM] + [ANY] * 9,
+        [shape((CTX_COUNT, ROWS, CHUNK)), *kept],
+        [
+            *[pltpu.VMEM((ROWS, HALF), BF16)] * 4,
+            *[pltpu.VMEM((UNITS, D), BF16)] * 2,
+            pltpu.VMEM((CTX_COUNT, ROWS, CHUNK), BF16),
+            *[pltpu.VMEM(k.shape, BF16) for k in kept],
+            pltpu.SemaphoreType.DMA((12,)),
+            pltpu.SemaphoreType.DMA((4 + CTX_COUNT,)),
+        ],
+        flops=2 * 3 * SLOTS * UNITS * D,
+        moved=12 * 2**20,
+        places=[ANY] * 5,
+        limit=VMEM_ALL,
+    )(at, partner_up, partner_down, *across, *partner_across, w_in, w_out, early_sums)
+    parts = lax.all_to_all(sums, CTX, split_axis=0, concat_axis=0, tiled=True)
     keys_grad, values_grad, query_pack = call(
         score_grad_kernel,
         [SMEM] + [VMEM] * 8,
@@ -370,47 +403,6 @@
         moved=6 * 2**20,
         limit=VMEM_ALL,
     )(place, normed, grads, keys, weights, slopes, stats, near, far)
-
-
-    up, down = moved_by(own, "ctx_0", 1), moved_by(own, "ctx_0", 3)
-    partner = moved_by(own, "ctx_1", 1)
-    up, down, partner, query_pack = lax.optimization_barrier((up, down, partner, query_pack))
-    across = [moved_by(up[:128], "ctx_0", 1), moved_by(down[128:], "ctx_0", 3)]
-    far_query = moved_by(query_pack[0], "ctx_1", 1)
-    *across, expert_weights = lax.optimization_barrier((*across, expert_weights))
-    partner_up, partner_down = moved_by(partner, "ctx_0", 1), moved_by(partner, "ctx_0", 3)
-    partner_across = [moved_by(piece, "ctx_1", 1) for piece in across]
-    w_in, w_out = expert_weights[0, :, 0, :], expert_weights[0, :, 1, :]
-    places = [(0, 0), (-1, 0), (1, 0), (0, 1), (-1, 1), (1, 1), (2, 0), (2, 1)]
-    at = jnp.stack([2 * ((y + a + 4) % 4) + (x + b) % 2 for a, b in places]).astype(jnp.int32)
-    kept = [shape((SLOTS, D))] * 2 + [shape((SLOTS, UNITS))] * 2
-    early_sums, *early = call(
-        early_kernel,
-        [VMEM] * 6,
-        [shape((CTX_COUNT, SLOTS // 2, CHUNK)), *kept],
-        flops=2 * 3 * SLOTS * UNITS * D,
-        moved=8 * 2**20,
-        limit=VMEM_ALL,
-    )(own, up, down, partner, w_in, w_out)
-    sums, *late = call(
-        late_kernel,
-        [SMEM] + [ANY] * 9,
-        [shape((CTX_COUNT, ROWS, CHUNK)), *kept],
-        [
-            *[pltpu.VMEM((ROWS, HALF), BF16)] * 4,
-            *[pltpu.VMEM((UNITS, D), BF16)] * 2,
-            pltpu.VMEM((CTX_COUNT, SLOTS // 2, CHUNK), BF16),
-            *[pltpu.VMEM(k.shape, BF16) for k in kept],
-            pltpu.SemaphoreType.DMA((8,)),
-            pltpu.SemaphoreType.DMA((8 + 4 * CTX_COUNT,)),
-        ],
-        flops=2 * 3 * SLOTS * UNITS * D,
-        moved=12 * 2**20,
-        places=[ANY] * 5,
-        limit=VMEM_ALL,
-    )(at, partner_up, partner_down, *across, *partner_across, w_in, w_out, early_sums)
-    sums, far_query = lax.optimization_barrier((sums, far_query))
-    parts = lax.all_to_all(sums, CTX, split_axis=0, concat_axis=0, tiled=True)
     [weights_grad] = call(
         weights_kernel,
         [ANY] * 8,
@@ -421,6 +413,7 @@
         limit=VMEM_ALL,
     )(*early, *late)
     weights_grad = weights_grad.reshape(1, UNITS, 2, D)
+    far_query = moved_by(query_pack[0], "ctx_1", 1)
     parts, weights_grad = lax.optimization_barrier((parts, weights_grad))
     [back] = call(total_kernel, [VMEM], [shape((ROWS, CHUNK))], moved=3 * 2**20)(parts)
     back, far_query = lax.optimization_barrier((back, far_query))

time: 212 us -> 167 us (0.79)
  Pallas kernels: 66.6 us -> 31.8 us
  waiting for transfers between devices: 58.5 us -> 35 us
  starting transfers between devices: 50.5 us -> 60.5 us
  local copies, waits for them, and re-layouts: 19.2 us -> 21.4 us
    pallas_call x1, Pallas kernels: 42 us -> 6.25 us  [on_device(): call(late_kernel, [SMEM] + [ANY] * 9, [shape((CTX_COUNT, ROWS, CHUNK)), *...]
    ppermute x17, waiting for transfers between devices: 26.6 us -> 7.95 us  [moved_by(): lax.ppermute(array, axis, [(k, (k + step) % count) for k in range(count)])]
    ppermute x17, starting transfers between devices: 27.8 us -> 37.4 us  [moved_by(): lax.ppermute(array, axis, [(k, (k + step) % count) for k in range(count)])]
    slice x0 -> x1, local copies, waits for them, and re-layouts: none -> 6.48 us  [on_device(): w_in, w_out = (expert_weights[0, :, 0, :], expert_weights[0, :, 1, :])]
    all_to_all x1, waiting for transfers between devices: 16 us -> 10.6 us  [on_device(): parts = lax.all_to_all(sums, CTX, split_axis=0, concat_axis=0, tiled=True)]
    slice x2, local copies, waits for them, and re-layouts: 3.5 us -> 0.04 us  [on_device(): across = [moved_by(up[:128], 'ctx_0', 1), moved_by(down[128:], 'ctx_0', 3)]]
  transfers between devices with their start and end apart: 20 -> 20, of which waited for: 8 -> 9; matrix products, arithmetic and copies ran while one was open for 5% -> 11% of each run, Pallas kernels for 29% -> 12%
where the time goes in v7:
time: 167 us; the launch traced here: 166 us
  starting transfers between devices  60.5 us (36%)
  waiting for transfers between devices  35 us (21%)
  Pallas kernels  31.8 us (19%)
  local copies, waits for them, and re-layouts  21.4 us (13%)
  blocking collectives  16.2 us (10%)
    ppermute x17, starting transfers between devices, moved_by(): lax.ppermute(array, axis, [(k, (k + step) % count) for k in range(count)])  37.4 us
    all_to_all x1, blocking collectives, on_device(): packs = lax.all_to_all(total, CTX, split_axis=0, concat_axis=0, tiled=True)  16.2 us
    all_to_all x1, waiting for transfers between devices, on_device(): lax.all_to_all(send.reshape(EXPERTS, 8, HALF), 'exp', split_axis=0, conca...  12.7 us
    all_to_all x1, waiting for transfers between devices, on_device(): parts = lax.all_to_all(sums, CTX, split_axis=0, concat_axis=0, tiled=True)  10.6 us
    all_to_all x1, starting transfers between devices, on_device(): lax.all_to_all(send.reshape(EXPERTS, 8, HALF), 'exp', split_axis=0, conca...  9.7 us
    all_to_all x1, starting transfers between devices, on_device(): lax.all_to_all(back.reshape(EXPERTS, 8, CHUNK), 'exp', split_axis=0, conc...  8.7 us
    ppermute x17, waiting for transfers between devices, moved_by(): lax.ppermute(array, axis, [(k, (k + step) % count) for k in range(count)])  7.95 us
    pallas_call x1, Pallas kernels, on_device(): call(weights_kernel, [ANY] * 8, [shape((2 * UNITS, D))], [pltpu.VMEM(k.sh...  7.36 us
  transfers between devices with their start and end apart: 20, of which 9 were waited for; matrix products, arithmetic and copies ran while one was open for 11% of the time, Pallas kernels for 12%

profile of v7, /device:TPU:32, one launch (start us, length us, event | category | flops | bytes accessed | tf_op | source)
XLA Modules:
  0.0 165.9 jit_solution(14422903357550113775)
XLA Ops:
  0.7 3.5 %shard_map.111 = (bf16[128,2560]{1,0:T(8,128)(2,1)}, bf16[256,1280]{1,0:T(8,128)(2,1)}, bf16[256,128]{1,0:T(8,128)(2,1)}, bf16[256,128]{1,0:T(8,128)(2,1)}) custom-call(s32[1]{0:T(128)} %bitcast.8.place, bf16[128,2560]{1,0:T(8,128)(2,1)} %bitcast.36, bf16[128,2560]{1,0:T(8,128)(2,1)} %bitcast.32, f32[2560]{0:T(1024)} %gain.3, s32[2,128]{1,0:T(2,128)} %bitcast.45, ...), custom_call_target="tpu_custom_call" | custom-call | flops 335544320 | bytes 3145728 | tf_op jit(solution)/shard_map/pallas_call | solution.py:340
  4.2 9.7 %all-to-all-start = ((bf16[32,8,1280]{2,1,0:T(8,128)(2,1)}), bf16[32,8,1280]{2,1,0:T(8,128)(2,1)}, u32[]{:S(2)}, u32[]{:S(2)}) async-start(bf16[32,8,1280]{2,1,0:T(8,128)(2,1)} %bitcast.44), calls=%async_computation | async-start | bytes 1310720 | tf_op jit(solution)/shard_map/all_to_all | solution.py:348
  13.9 1.1 copy-done.4
  15.0 1.1 shard_map.112
  16.1 1.1 copy-done.6
  17.2 3.0 %collective-permute-start.11 = (f32[72,128]{1,0:T(8,128)S(1)}, f32[72,128]{1,0:T(8,128)S(1)}, u32[]{:S(2)}, u32[]{:S(2)}) collective-permute-start(f32[72,128]{1,0:T(8,128)S(1)} %get-tuple-element.36.local), channel_id=1, source_target_pairs={{0,192},{64,0},{128,64},{192,128},{1,193},{65,1},{129,65},{193,129... | collective-permute-start | bytes 110600 | tf_op jit(solution)/shard_map/ppermute | solution.py:331
  20.2 0.6 collective-permute-start.10
  20.8 1.0 collective-permute-start.9
  21.8 12.7 %all-to-all-done = bf16[32,8,1280]{2,1,0:T(8,128)(2,1)} async-done(((bf16[32,8,1280]{2,1,0:T(8,128)(2,1)}), bf16[32,8,1280]{2,1,0:T(8,128)(2,1)}, u32[]{:S(2)}, u32[]{:S(2)}) %all-to-all-start) | async-done | bytes 655392 | tf_op jit(solution)/shard_map/all_to_all | solution.py:348
  34.5 3.0 %collective-permute-start.5 = (bf16[256,1280]{1,0:T(8,128)(2,1)}, bf16[256,1280]{1,0:T(8,128)(2,1)S(1)}, u32[]{:S(2)}, u32[]{:S(2)}) collective-permute-start(bf16[256,1280]{1,0:T(8,128)(2,1)} %bitcast.16.own), channel_id=1, source_target_pairs={{0,192},{64,0},{128,64},{192,128},{1,193},{65,1},{129,65},{193,129... | collective-permute-start | bytes 1966088 | tf_op jit(solution)/shard_map/ppermute | solution.py:331
  37.5 2.7 %collective-permute-start = (bf16[256,1280]{1,0:T(8,128)(2,1)}, bf16[256,1280]{1,0:T(8,128)(2,1)S(1)}, u32[]{:S(2)}, u32[]{:S(2)}) collective-permute-start(bf16[256,1280]{1,0:T(8,128)(2,1)} %bitcast.16.own), channel_id=1, source_target_pairs={{0,32},{32,0},{1,33},{33,1},{2,34},{34,2},{3,35},{35,3},{4,36},{36... | collective-permute-start | bytes 1966088 | tf_op jit(solution)/shard_map/ppermute | solution.py:331
  40.3 6.5 %fusion.6 = (bf16[1,256,1,2560]{3,2,1,0:T(2,128)(2,1)S(1)}, bf16[1,256,1,2560]{3,2,1,0:T(2,128)(2,1)S(1)}) fusion(bf16[1,256,2,2560]{3,2,1,0:T(2,128)(2,1)} %param.15), kind=kLoop, calls=%fused_computation.21 | loop fusion | bytes 5242880 | tf_op jit(solution)/shard_map/slice | solution.py:366
  46.8 4.2 %collective-permute-done.5.down = bf16[256,1280]{1,0:T(8,128)(2,1)S(1)} collective-permute-done((bf16[256,1280]{1,0:T(8,128)(2,1)}, bf16[256,1280]{1,0:T(8,128)(2,1)S(1)}, u32[]{:S(2)}, u32[]{:S(2)}) %collective-permute-start.5) | collective-permute-done | bytes 655392 | tf_op jit(solution)/shard_map/ppermute | solution.py:331
  51.0 3.7 %collective-permute-start.6 = (bf16[128,1280]{1,0:T(8,128)(2,1)S(1)}, bf16[128,1280]{1,0:T(8,128)(2,1)}, u32[]{:S(2)}, u32[]{:S(2)}) collective-permute-start(bf16[128,1280]{1,0:T(8,128)(2,1)S(1)} %slice.73), channel_id=1, source_target_pairs={{0,192},{64,0},{128,64},{192,128},{1,193},{65,1},{129,65},{193,129... | collective-permute-start | bytes 983048 | tf_op jit(solution)/shard_map/ppermute | solution.py:331
  54.7 0.1 collective-permute-start.4
  54.9 2.8 %collective-permute-start.12 = (f32[72,128]{1,0:T(8,128)S(1)}, f32[72,128]{1,0:T(8,128)S(1)}, u32[]{:S(2)}, u32[]{:S(2)}) collective-permute-start(f32[72,128]{1,0:T(8,128)S(1)} %pad_maximum_fusion.near), channel_id=1, source_target_pairs={{0,32},{32,0},{1,33},{33,1},{2,34},{34,2},{3,35},{35,3},{4,36},{36... | collective-permute-start | bytes 110600 | tf_op jit(solution)/shard_map/ppermute | solution.py:331
  57.7 3.2 %collective-permute-start.2 = (bf16[256,1280]{1,0:T(8,128)(2,1)S(1)}, bf16[256,1280]{1,0:T(8,128)(2,1)S(1)}, u32[]{:S(2)}, u32[]{:S(2)}) collective-permute-start(bf16[256,1280]{1,0:T(8,128)(2,1)S(1)} %collective-permute-done.partner), channel_id=1, source_target_pairs={{0,192},{64,0},{128,64},{192,128},{1,193},{65,1},{129,65},{193,129... | collective-permute-start | bytes 1966088 | tf_op jit(solution)/shard_map/ppermute | solution.py:331
  60.9 0.6 collective-permute-done.6.refs_3_
  61.5 4.1 %collective-permute-start.8 = (bf16[128,1280]{1,0:T(8,128)(2,1)}, bf16[128,1280]{1,0:T(8,128)(2,1)}, u32[]{:S(2)}, u32[]{:S(2)}) collective-permute-start(bf16[128,1280]{1,0:T(8,128)(2,1)} %collective-permute-done.6.refs_3_), channel_id=1, source_target_pairs={{0,32},{32,0},{1,33},{33,1},{2,34},{34,2},{3,35},{35,3},{4,36},{36... | collective-permute-start | bytes 983048 | tf_op jit(solution)/shard_map/ppermute | solution.py:331
  65.6 3.9 %collective-permute-start.7 = (bf16[128,1280]{1,0:T(8,128)(2,1)}, bf16[128,1280]{1,0:T(8,128)(2,1)}, u32[]{:S(2)}, u32[]{:S(2)}) collective-permute-start(bf16[128,1280]{1,0:T(8,128)(2,1)} %collective-permute-done.4.refs_2_), channel_id=1, source_target_pairs={{0,32},{32,0},{1,33},{33,1},{2,34},{34,2},{3,35},{35,3},{4,36},{36... | collective-permute-start | bytes 983048 | tf_op jit(solution)/shard_map/ppermute | solution.py:331
  69.5 2.1 %copy_bitcast_fusion = (bf16[256,2560]{1,0:T(8,128)(2,1)}, bf16[256,2560]{1,0:T(8,128)(2,1)}) fusion(bf16[1,256,1,2560]{3,2,1,0:T(2,128)(2,1)S(1)} %get-tuple-element.66, bf16[1,256,1,2560]{3,2,1,0:T(2,128)(2,1)S(1)} %get-tuple-element.67), kind=kLoop, calls=%fused_computation | loop fusion | bytes 5242880 | tf_op jit(solution)/shard_map/squeeze | solution.py:366
  71.7 0.7 stack.35.at_ref
  72.3 5.7 %shard_map.113 = (bf16[8,128,640]{2,1,0:T(8,128)(2,1)}, bf16[256,2560]{1,0:T(8,128)(2,1)}, bf16[256,2560]{1,0:T(8,128)(2,1)}, bf16[256,256]{1,0:T(8,128)(2,1)}, bf16[256,256]{1,0:T(8,128)(2,1)}) custom-call(bf16[256,1280]{1,0:T(8,128)(2,1)} %bitcast.16.own, bf16[256,1280]{1,0:T(8,128)(2,1)} %copy-done.15, bf16[256,1280]{1,0:T(8,128)(2,1)} %copy-done.14, ...), custom_call_target="tpu_custom_call" | custom-call | flops 1006632960 | bytes 8388608 | tf_op jit(solution)/shard_map/pallas_call | solution.py:371
  78.2 0.8 copy-done.17
  79.0 0.2 copy-done.18
  79.2 6.3 %shard_map.114 = (bf16[8,256,640]{2,1,0:T(8,128)(2,1)}, bf16[256,2560]{1,0:T(8,128)(2,1)}, bf16[256,2560]{1,0:T(8,128)(2,1)}, bf16[256,256]{1,0:T(8,128)(2,1)}, bf16[256,256]{1,0:T(8,128)(2,1)}) custom-call(s32[8]{0:T(128)} %stack.35.at_ref, bf16[256,1280]{1,0:T(8,128)(2,1)} %copy-done.18, bf16[256,1280]{1,0:T(8,128)(2,1)} %copy-done.17, ...), custom_call_target="tpu_custom_call" | custom-call | flops 1006632960 | bytes 12582912 | tf_op jit(solution)/shard_map/pallas_call | solution.py:379
  85.4 4.7 %all-to-all-start.1 = ((bf16[8,256,640]{2,1,0:T(8,128)(2,1)}), bf16[8,256,640]{2,1,0:T(8,128)(2,1)S(1)}, u32[]{:S(2)}, u32[]{:S(2)}) async-start(bf16[8,256,640]{2,1,0:T(8,128)(2,1)} %get-tuple-element.39), calls=%async_computation.1 | async-start | bytes 5242880 | tf_op jit(solution)/shard_map/all_to_all | solution.py:396
  90.1 4.3 %shard_map.117 = (bf16[128,2560]{1,0:T(8,128)(2,1)}, bf16[128,2560]{1,0:T(8,128)(2,1)}, bf16[2,4,64,640]{3,2,1,0:T(8,128)(2,1)}) custom-call(s32[1]{0:T(128)} %bitcast.8.place, bf16[128,2560]{1,0:T(8,128)(2,1)} %get-tuple-element.35.normed, bf16[128,2560]{1,0:T(8,128)(2,1)} %bitcast.33, bf16[128,2560]{1,0:T(8,128)(2,1)} %bitcast.38, ...), custom_call_target="tpu_custom_call" | custom-call | flops 251658240 | bytes 6291456 | tf_op jit(solution)/shard_map/pallas_call | solution.py:397
  94.4 1.8 %slice_bitcast_fusion = bf16[4,64,640]{2,1,0:T(8,128)(2,1)} fusion(bf16[2,4,64,640]{3,2,1,0:T(8,128)(2,1)} %get-tuple-element.52.query_pack), kind=kLoop, calls=%fused_computation.2 | loop fusion | bytes 655360 | tf_op jit(solution)/shard_map/squeeze | solution.py:416
  96.2 3.5 %collective-permute-start.13 = (bf16[4,64,640]{2,1,0:T(8,128)(2,1)}, bf16[4,64,640]{2,1,0:T(8,128)(2,1)}, u32[]{:S(2)}, u32[]{:S(2)}) collective-permute-start(bf16[4,64,640]{2,1,0:T(8,128)(2,1)} %slice_bitcast_fusion), channel_id=1, source_target_pairs={{0,32},{32,0},{1,33},{33,1},{2,34},{34,2},{3,35},{35,3},{4,36},{36... | collective-permute-start | bytes 983048 | tf_op jit(solution)/shard_map/ppermute | solution.py:331
  99.7 7.4 %shard_map.115 = bf16[512,2560]{1,0:T(8,128)(2,1)} custom-call(bf16[256,2560]{1,0:T(8,128)(2,1)} %get-tuple-element.40.refs_0_, bf16[256,2560]{1,0:T(8,128)(2,1)} %get-tuple-element.41.refs_1_, bf16[256,256]{1,0:T(8,128)(2,1)} %get-tuple-element.42.refs_2_, bf16[256,256]{1,0:T(8,128)(2,1)} %get-tuple-element.43.refs_3_, ...), custom_call_target="tpu_custom_call" | custom-call | flops 1342177280 | bytes 8388608 | tf_op jit(solution)/shard_map/pallas_call | solution.py:406
  107.1 6.4 %reshape.29 = bf16[1,256,2,2560]{3,2,1,0:T(2,128)(2,1)} reshape(bf16[512,2560]{1,0:T(8,128)(2,1)} %shard_map.115) | data formatting | bytes 5242880 | tf_op jit(solution)/shard_map/reshape | solution.py:415
  113.5 10.6 %all-to-all-done.1.parts = bf16[8,256,640]{2,1,0:T(8,128)(2,1)S(1)} async-done(((bf16[8,256,640]{2,1,0:T(8,128)(2,1)}), bf16[8,256,640]{2,1,0:T(8,128)(2,1)S(1)}, u32[]{:S(2)}, u32[]{:S(2)}) %all-to-all-start.1) | async-done | bytes 2621472 | tf_op jit(solution)/shard_map/all_to_all | solution.py:396
  124.1 0.6 shard_map.116
  124.7 0.7 copy-done.8
  125.4 0.2 collective-permute-done.13.far
  125.5 8.7 %all-to-all-start.2 = ((bf16[32,8,640]{2,1,0:T(8,128)(2,1)}), bf16[32,8,640]{2,1,0:T(8,128)(2,1)S(1)}, u32[]{:S(2)}, u32[]{:S(2)}) async-start(bf16[32,8,640]{2,1,0:T(8,128)(2,1)} %bitcast.41), calls=%async_computation.2 | async-start | bytes 655360 | tf_op jit(solution)/shard_map/all_to_all | solution.py:420
  134.3 1.1 shard_map.118
  135.3 1.6 collective-permute-start.14
  136.9 2.7 %collective-permute-start.15 = (bf16[64,640]{1,0:T(8,128)(2,1)S(1)}, bf16[64,640]{1,0:T(8,128)(2,1)S(1)}, u32[]{:S(2)}, u32[]{:S(2)}) collective-permute-start(bf16[64,640]{1,0:T(8,128)(2,1)S(1)} %get-tuple-element.59), channel_id=1, source_target_pairs={{0,128},{64,192},{128,0},{192,64},{1,129},{65,193},{129,1},{193,65... | collective-permute-start | bytes 245768 | tf_op jit(solution)/shard_map/ppermute | solution.py:331
  139.6 1.5 collective-permute-start.16
  141.1 0.3 collective-permute-done.14.below
  141.3 2.5 %collective-permute-done.15.across = bf16[64,640]{1,0:T(8,128)(2,1)S(1)} collective-permute-done((bf16[64,640]{1,0:T(8,128)(2,1)S(1)}, bf16[64,640]{1,0:T(8,128)(2,1)S(1)}, u32[]{:S(2)}, u32[]{:S(2)}) %collective-permute-start.15) | collective-permute-done | bytes 81952 | tf_op jit(solution)/shard_map/ppermute | solution.py:331
  143.9 0.2 collective-permute-done.16.above
  144.1 3.7 %all-to-all-done.2 = bf16[32,8,640]{2,1,0:T(8,128)(2,1)S(1)} async-done(((bf16[32,8,640]{2,1,0:T(8,128)(2,1)}), bf16[32,8,640]{2,1,0:T(8,128)(2,1)S(1)}, u32[]{:S(2)}, u32[]{:S(2)}) %all-to-all-start.2) | async-done | bytes 327712 | tf_op jit(solution)/shard_map/all_to_all | solution.py:420
  147.8 0.4 shard_map.119
  148.2 16.2 %all_to_all.20.packs = bf16[8,64,640]{2,1,0:T(8,128)(2,1)S(1)} all-to-all(bf16[8,64,640]{2,1,0:T(8,128)(2,1)S(1)} %shard_map.119), channel_id=1, replica_groups=mesh['ctx_0'=4,'ctx_1'=2,'exp'=32] {'ctx_0','ctx_1'}, dimensions={0} | all-to-all | bytes 1310720 | tf_op jit(solution)/shard_map/all_to_all | solution.py:428
  164.4 1.5 shard_map.120
  (55 shorter events, 0.2 us)
Async XLA Ops:
  0.6 13.3 %copy-start = (bf16[1,128,2560]{2,1,0:T(8,128)(2,1)S(1)}, bf16[1,128,2560]{2,1,0:T(8,128)(2,1)}, u32[]{:S(2)}) copy-start(bf16[1,128,2560]{2,1,0:T(8,128)(2,1)} %param.9) | copy-start | bytes 1966084
  0.6 13.3 %copy-start.9 = (bf16[1,128,2560]{2,1,0:T(8,128)(2,1)S(1)}, bf16[1,128,2560]{2,1,0:T(8,128)(2,1)}, u32[]{:S(2)}) copy-start(bf16[1,128,2560]{2,1,0:T(8,128)(2,1)} %param.11) | copy-start | bytes 1966084
  0.7 13.3 %copy-start.3 = (bf16[1,128,2560]{2,1,0:T(8,128)(2,1)S(1)}, bf16[1,128,2560]{2,1,0:T(8,128)(2,1)}, u32[]{:S(2)}) copy-start(bf16[1,128,2560]{2,1,0:T(8,128)(2,1)} %param.10) | copy-start | bytes 1966084
  4.2 30.3 %all-to-all-start = ((bf16[32,8,1280]{2,1,0:T(8,128)(2,1)}), bf16[32,8,1280]{2,1,0:T(8,128)(2,1)}, u32[]{:S(2)}, u32[]{:S(2)}) async-start(bf16[32,8,1280]{2,1,0:T(8,128)(2,1)} %bitcast.44), calls=%async_computation | async-start | bytes 1310720 | tf_op jit(solution)/shard_map/all_to_all | solution.py:348
  13.9 1.1 copy-start.4
  16.1 1.1 copy-start.6
  17.2 29.6 %copy-start.7 = (f32[20,128,128]{2,1,0:T(8,128)}, f32[20,128,128]{2,1,0:T(8,128)S(1)}, u32[]{:S(2)}) copy-start(f32[20,128,128]{2,1,0:T(8,128)S(1)} %get-tuple-element.50.slopes) | copy-start | bytes 3932164
  17.2 37.7 %copy-start.10 = (f32[72,128]{1,0:T(8,128)}, f32[72,128]{1,0:T(8,128)S(1)}, u32[]{:S(2)}) copy-start(f32[72,128]{1,0:T(8,128)S(1)} %get-tuple-element.36.local) | copy-start | bytes 110596
  17.2 20.4 %collective-permute-start.11 = (f32[72,128]{1,0:T(8,128)S(1)}, f32[72,128]{1,0:T(8,128)S(1)}, u32[]{:S(2)}, u32[]{:S(2)}) collective-permute-start(f32[72,128]{1,0:T(8,128)S(1)} %get-tuple-element.36.local), channel_id=1, source_target_pairs={{0,192},{64,0},{128,64},{192,128},{1,193},{65,1},{129,65},{193,129... | collective-permute-start | bytes 110600 | tf_op jit(solution)/shard_map/ppermute | solution.py:331
  20.2 26.6 %collective-permute-start.10 = (f32[72,128]{1,0:T(8,128)S(1)}, f32[72,128]{1,0:T(8,128)S(1)}, u32[]{:S(2)}, u32[]{:S(2)}) collective-permute-start(f32[72,128]{1,0:T(8,128)S(1)} %get-tuple-element.36.local), channel_id=1, source_target_pairs={{0,128},{64,192},{128,0},{192,64},{1,129},{65,193},{129,1},{193,65... | collective-permute-start | bytes 110600 | tf_op jit(solution)/shard_map/ppermute | solution.py:331
  20.8 26.0 %collective-permute-start.9 = (f32[72,128]{1,0:T(8,128)S(1)}, f32[72,128]{1,0:T(8,128)S(1)}, u32[]{:S(2)}, u32[]{:S(2)}) collective-permute-start(f32[72,128]{1,0:T(8,128)S(1)} %get-tuple-element.36.local), channel_id=1, source_target_pairs={{0,64},{64,128},{128,192},{192,0},{1,65},{65,129},{129,193},{193,1... | collective-permute-start | bytes 110600 | tf_op jit(solution)/shard_map/ppermute | solution.py:331
  34.5 16.5 %collective-permute-start.5 = (bf16[256,1280]{1,0:T(8,128)(2,1)}, bf16[256,1280]{1,0:T(8,128)(2,1)S(1)}, u32[]{:S(2)}, u32[]{:S(2)}) collective-permute-start(bf16[256,1280]{1,0:T(8,128)(2,1)} %bitcast.16.own), channel_id=1, source_target_pairs={{0,192},{64,0},{128,64},{192,128},{1,193},{65,1},{129,65},{193,129... | collective-permute-start | bytes 1966088 | tf_op jit(solution)/shard_map/ppermute | solution.py:331
  37.5 17.2 %collective-permute-start.3 = (bf16[256,1280]{1,0:T(8,128)(2,1)}, bf16[256,1280]{1,0:T(8,128)(2,1)S(1)}, u32[]{:S(2)}, u32[]{:S(2)}) collective-permute-start(bf16[256,1280]{1,0:T(8,128)(2,1)} %bitcast.16.own), channel_id=1, source_target_pairs={{0,64},{64,128},{128,192},{192,0},{1,65},{65,129},{129,193},{193,1... | collective-permute-start | bytes 1966088 | tf_op jit(solution)/shard_map/ppermute | solution.py:331
  37.5 20.2 %collective-permute-start = (bf16[256,1280]{1,0:T(8,128)(2,1)}, bf16[256,1280]{1,0:T(8,128)(2,1)S(1)}, u32[]{:S(2)}, u32[]{:S(2)}) collective-permute-start(bf16[256,1280]{1,0:T(8,128)(2,1)} %bitcast.16.own), channel_id=1, source_target_pairs={{0,32},{32,0},{1,33},{33,1},{2,34},{34,2},{3,35},{35,3},{4,36},{36... | collective-permute-start | bytes 1966088 | tf_op jit(solution)/shard_map/ppermute | solution.py:331
  51.0 20.6 %copy-start.14 = (bf16[256,1280]{1,0:T(8,128)(2,1)}, bf16[256,1280]{1,0:T(8,128)(2,1)S(1)}, u32[]{:S(2)}) copy-start(bf16[256,1280]{1,0:T(8,128)(2,1)S(1)} %collective-permute-done.5.down) | copy-start | bytes 1966084
  51.0 10.5 %collective-permute-start.6 = (bf16[128,1280]{1,0:T(8,128)(2,1)S(1)}, bf16[128,1280]{1,0:T(8,128)(2,1)}, u32[]{:S(2)}, u32[]{:S(2)}) collective-permute-start(bf16[128,1280]{1,0:T(8,128)(2,1)S(1)} %slice.73), channel_id=1, source_target_pairs={{0,192},{64,0},{128,64},{192,128},{1,193},{65,1},{129,65},{193,129... | collective-permute-start | bytes 983048 | tf_op jit(solution)/shard_map/ppermute | solution.py:331
  54.7 16.9 %copy-start.15 = (bf16[256,1280]{1,0:T(8,128)(2,1)}, bf16[256,1280]{1,0:T(8,128)(2,1)S(1)}, u32[]{:S(2)}) copy-start(bf16[256,1280]{1,0:T(8,128)(2,1)S(1)} %collective-permute-done.3.up) | copy-start | bytes 1966084
  54.7 10.9 %collective-permute-start.4 = (bf16[128,1280]{1,0:T(8,128)(2,1)S(1)}, bf16[128,1280]{1,0:T(8,128)(2,1)}, u32[]{:S(2)}, u32[]{:S(2)}) collective-permute-start(bf16[128,1280]{1,0:T(8,128)(2,1)S(1)} %slice.72), channel_id=1, source_target_pairs={{0,64},{64,128},{128,192},{192,0},{1,65},{65,129},{129,193},{193,1... | collective-permute-start | bytes 983048 | tf_op jit(solution)/shard_map/ppermute | solution.py:331
  54.9 16.7 %copy-start.19 = (f32[72,128]{1,0:T(8,128)}, f32[72,128]{1,0:T(8,128)S(1)}, u32[]{:S(2)}) copy-start(f32[72,128]{1,0:T(8,128)S(1)} %pad_maximum_fusion.near) | copy-start | bytes 110596
  54.9 17.5 %collective-permute-start.12 = (f32[72,128]{1,0:T(8,128)S(1)}, f32[72,128]{1,0:T(8,128)S(1)}, u32[]{:S(2)}, u32[]{:S(2)}) collective-permute-start(f32[72,128]{1,0:T(8,128)S(1)} %pad_maximum_fusion.near), channel_id=1, source_target_pairs={{0,32},{32,0},{1,33},{33,1},{2,34},{34,2},{3,35},{35,3},{4,36},{36... | collective-permute-start | bytes 110600 | tf_op jit(solution)/shard_map/ppermute | solution.py:331
  57.7 13.9 %copy-start.16 = (bf16[256,1280]{1,0:T(8,128)(2,1)}, bf16[256,1280]{1,0:T(8,128)(2,1)S(1)}, u32[]{:S(2)}) copy-start(bf16[256,1280]{1,0:T(8,128)(2,1)S(1)} %collective-permute-done.partner) | copy-start | bytes 1966084
  57.7 20.4 %collective-permute-start.2 = (bf16[256,1280]{1,0:T(8,128)(2,1)S(1)}, bf16[256,1280]{1,0:T(8,128)(2,1)S(1)}, u32[]{:S(2)}, u32[]{:S(2)}) collective-permute-start(bf16[256,1280]{1,0:T(8,128)(2,1)S(1)} %collective-permute-done.partner), channel_id=1, source_target_pairs={{0,192},{64,0},{128,64},{192,128},{1,193},{65,1},{129,65},{193,129... | collective-permute-start | bytes 1966088 | tf_op jit(solution)/shard_map/ppermute | solution.py:331
  60.9 17.2 %collective-permute-start.1 = (bf16[256,1280]{1,0:T(8,128)(2,1)S(1)}, bf16[256,1280]{1,0:T(8,128)(2,1)S(1)}, u32[]{:S(2)}, u32[]{:S(2)}) collective-permute-start(bf16[256,1280]{1,0:T(8,128)(2,1)S(1)} %collective-permute-done.partner), channel_id=1, source_target_pairs={{0,64},{64,128},{128,192},{192,0},{1,65},{65,129},{129,193},{193,1... | collective-permute-start | bytes 1966088 | tf_op jit(solution)/shard_map/ppermute | solution.py:331
  61.5 16.6 %collective-permute-start.8 = (bf16[128,1280]{1,0:T(8,128)(2,1)}, bf16[128,1280]{1,0:T(8,128)(2,1)}, u32[]{:S(2)}, u32[]{:S(2)}) collective-permute-start(bf16[128,1280]{1,0:T(8,128)(2,1)} %collective-permute-done.6.refs_3_), channel_id=1, source_target_pairs={{0,32},{32,0},{1,33},{33,1},{2,34},{34,2},{3,35},{35,3},{4,36},{36... | collective-permute-start | bytes 983048 | tf_op jit(solution)/shard_map/ppermute | solution.py:331
  65.6 12.5 %collective-permute-start.7 = (bf16[128,1280]{1,0:T(8,128)(2,1)}, bf16[128,1280]{1,0:T(8,128)(2,1)}, u32[]{:S(2)}, u32[]{:S(2)}) collective-permute-start(bf16[128,1280]{1,0:T(8,128)(2,1)} %collective-permute-done.4.refs_2_), channel_id=1, source_target_pairs={{0,32},{32,0},{1,33},{33,1},{2,34},{34,2},{3,35},{35,3},{4,36},{36... | collective-permute-start | bytes 983048 | tf_op jit(solution)/shard_map/ppermute | solution.py:331
  72.3 5.7 %copy-start.20 = (f32[72,128]{1,0:T(8,128)}, f32[72,128]{1,0:T(8,128)S(1)}, u32[]{:S(2)}) copy-start(f32[72,128]{1,0:T(8,128)S(1)} %collective-permute-done.12.far) | copy-start | bytes 110596
  78.1 0.8 copy-start.17
  78.1 1.0 copy-start.18
  85.4 38.6 %all-to-all-start.1 = ((bf16[8,256,640]{2,1,0:T(8,128)(2,1)}), bf16[8,256,640]{2,1,0:T(8,128)(2,1)S(1)}, u32[]{:S(2)}, u32[]{:S(2)}) async-start(bf16[8,256,640]{2,1,0:T(8,128)(2,1)} %get-tuple-element.39), calls=%async_computation.1 | async-start | bytes 5242880 | tf_op jit(solution)/shard_map/all_to_all | solution.py:396
  96.2 29.4 %collective-permute-start.13 = (bf16[4,64,640]{2,1,0:T(8,128)(2,1)}, bf16[4,64,640]{2,1,0:T(8,128)(2,1)}, u32[]{:S(2)}, u32[]{:S(2)}) collective-permute-start(bf16[4,64,640]{2,1,0:T(8,128)(2,1)} %slice_bitcast_fusion), channel_id=1, source_target_pairs={{0,32},{32,0},{1,33},{33,1},{2,34},{34,2},{3,35},{35,3},{4,36},{36... | collective-permute-start | bytes 983048 | tf_op jit(solution)/shard_map/ppermute | solution.py:331
  113.5 20.8 %copy-start.5 = (bf16[2,4,64,640]{3,2,1,0:T(8,128)(2,1)S(1)}, bf16[2,4,64,640]{3,2,1,0:T(8,128)(2,1)}, u32[]{:S(2)}) copy-start(bf16[2,4,64,640]{3,2,1,0:T(8,128)(2,1)} %get-tuple-element.52.query_pack) | copy-start | bytes 1966084
  113.5 34.3 %copy-start.11 = (bf16[256,128]{1,0:T(8,128)(2,1)S(1)}, bf16[256,128]{1,0:T(8,128)(2,1)}, u32[]{:S(2)}) copy-start(bf16[256,128]{1,0:T(8,128)(2,1)} %get-tuple-element.54.even) | copy-start | bytes 196612
  113.5 34.3 %copy-start.12 = (bf16[256,128]{1,0:T(8,128)(2,1)S(1)}, bf16[256,128]{1,0:T(8,128)(2,1)}, u32[]{:S(2)}) copy-start(bf16[256,128]{1,0:T(8,128)(2,1)} %get-tuple-element.55.odd) | copy-start | bytes 196612
  124.6 0.7 copy-start.8
  125.4 39.0 %copy-start.1 = (bf16[1,128,2560]{2,1,0:T(8,128)(2,1)S(1)}, bf16[1,128,2560]{2,1,0:T(8,128)(2,1)}, u32[]{:S(2)}) copy-start(bf16[1,128,2560]{2,1,0:T(8,128)(2,1)} %param.9) | copy-start | bytes 1966084
  125.4 39.0 %copy-start.2 = (bf16[1,128,2560]{2,1,0:T(8,128)(2,1)S(1)}, bf16[1,128,2560]{2,1,0:T(8,128)(2,1)}, u32[]{:S(2)}) copy-start(bf16[1,128,2560]{2,1,0:T(8,128)(2,1)} %param.8) | copy-start | bytes 1966084
  125.4 39.0 %copy-start.13 = (f32[2560]{0:T(1024)S(1)}, f32[2560]{0:T(1024)}, u32[]{:S(2)}) copy-start(f32[2560]{0:T(1024)} %gain.3) | copy-start | bytes 30724
  125.5 22.3 %all-to-all-start.2 = ((bf16[32,8,640]{2,1,0:T(8,128)(2,1)}), bf16[32,8,640]{2,1,0:T(8,128)(2,1)S(1)}, u32[]{:S(2)}, u32[]{:S(2)}) async-start(bf16[32,8,640]{2,1,0:T(8,128)(2,1)} %bitcast.41), calls=%async_computation.2 | async-start | bytes 655360 | tf_op jit(solution)/shard_map/all_to_all | solution.py:420
  135.3 6.0 %collective-permute-start.14 = (bf16[64,640]{1,0:T(8,128)(2,1)S(1)}, bf16[64,640]{1,0:T(8,128)(2,1)S(1)}, u32[]{:S(2)}, u32[]{:S(2)}) collective-permute-start(bf16[64,640]{1,0:T(8,128)(2,1)S(1)} %get-tuple-element.58), channel_id=1, source_target_pairs={{0,64},{64,128},{128,192},{192,0},{1,65},{65,129},{129,193},{193,1... | collective-permute-start | bytes 245768 | tf_op jit(solution)/shard_map/ppermute | solution.py:331
  136.9 6.9 %collective-permute-start.15 = (bf16[64,640]{1,0:T(8,128)(2,1)S(1)}, bf16[64,640]{1,0:T(8,128)(2,1)S(1)}, u32[]{:S(2)}, u32[]{:S(2)}) collective-permute-start(bf16[64,640]{1,0:T(8,128)(2,1)S(1)} %get-tuple-element.59), channel_id=1, source_target_pairs={{0,128},{64,192},{128,0},{192,64},{1,129},{65,193},{129,1},{193,65... | collective-permute-start | bytes 245768 | tf_op jit(solution)/shard_map/ppermute | solution.py:331
  139.6 4.4 %collective-permute-start.16 = (bf16[64,640]{1,0:T(8,128)(2,1)S(1)}, bf16[64,640]{1,0:T(8,128)(2,1)S(1)}, u32[]{:S(2)}, u32[]{:S(2)}) collective-permute-start(bf16[64,640]{1,0:T(8,128)(2,1)S(1)} %get-tuple-element.60), channel_id=1, source_target_pairs={{0,192},{64,0},{128,64},{192,128},{1,193},{65,1},{129,65},{193,129... | collective-permute-start | bytes 245768 | tf_op jit(solution)/shard_map/ppermute | solution.py:331

commit v8 on v7

--- a/solution.py
+++ b/solution.py
@@ -120,7 +120,20 @@
 
 
 def score_grad_kernel(
-    place, normed, grads, keys, weights, slopes, local, near, far, keys_grad, values_grad, query_pack, query
+    place,
+    normed,
+    grads,
+    keys,
+    weights,
+    slopes,
+    local,
+    near,
+    far,
+    keys_grad,
+    values_grad,
+    own_pack,
+    far_pack,
+    query,
 ):
     peak = jnp.maximum(near[0:24, :], far[0:24, :])
     near_factor = jnp.exp(near[0:24, :] - peak)
@@ -138,23 +151,25 @@
         keys_grad[:, at] = (dot(score_grad, normed[:, at]) * SCALE).astype(BF16)
         query[:, at] = dot(score_grad, keys[:, at], ((0,), (0,))) * SCALE
     lane = iota((64, 128), 1)
-    for f in range(CTX_COUNT):
-        column, row = (f + place[0] + 1) % 2, (f // 2 - place[0] // 2 + 4) % 4
-        at = slice(256 * f, 256 * f + 256)
-        query_pack[column, row, :, 0:256] = query[0:64, at].astype(BF16)
-        query_pack[column, row, :, 256:512] = query[64:128, at].astype(BF16)
-        tile = slice(2048 + 128 * (f // 2), 2176 + 128 * (f // 2))
+    first = place[0] % 2 == 0
+    for g in range(CTX_COUNT // 2):
+        row = (g - place[0] // 2 + 4) % 4
+        tile = slice(2048 + 128 * g, 2176 + 128 * g)
         a, b = query[0:64, tile], query[64:128, tile]
-        if f % 2 == 0:
-            tail = jnp.where(lane < 64, a, pltpu.roll(b, 64, 1))
-        else:
-            tail = jnp.where(lane < 64, pltpu.roll(a, 64, 1), b)
-        query_pack[column, row, :, 512:640] = tail.astype(BF16)
-
-
-def join_kernel(query_pack, far, *outs):
+        packs = []
+        for f, tail in (
+            (2 * g, jnp.where(lane < 64, a, pltpu.roll(b, 64, 1))),
+            (2 * g + 1, jnp.where(lane < 64, pltpu.roll(a, 64, 1), b)),
+        ):
+            at = slice(256 * f, 256 * f + 256)
+            packs.append(jnp.concatenate([query[0:64, at], query[64:128, at], tail], axis=1))
+        own_pack[row] = jnp.where(first, packs[0], packs[1]).astype(BF16)
+        far_pack[row] = jnp.where(first, packs[1], packs[0]).astype(BF16)
+
+
+def join_kernel(own, far, *outs):
     for k in range(4):
-        outs[k][...] = (query_pack[1, k].astype(F32) + far[k].astype(F32)).astype(BF16)
+        outs[k][...] = (own[k].astype(F32) + far[k].astype(F32)).astype(BF16)
 
 
 def experts_of(blocks, w_in, w_out, rows, douts, act, pre_grad, put, after=lambda step: None):
@@ -349,6 +364,10 @@
         send.reshape(EXPERTS, 8, HALF), "exp", split_axis=0, concat_axis=0, tiled=True
     ).reshape(ROWS, HALF)
 
+    normed, expert_weights = lax.optimization_barrier((normed, expert_weights))
+    w_in, w_out = expert_weights[0, :, 0, :], expert_weights[0, :, 1, :]
+    keys, w_in, w_out = lax.optimization_barrier((keys, w_in, w_out))
+
     weights, slopes, stats = call(
         scores_kernel,
         [VMEM] * 4,
@@ -357,17 +376,27 @@
         moved=5 * 2**20,
     )(normed, grads, keys, values)
     near = merged([stats] + [moved_by(stats, "ctx_0", k) for k in (1, 2, 3)])
+    own, near = lax.optimization_barrier((own, near))
     far = moved_by(near, "ctx_1", 1)
     up, down = moved_by(own, "ctx_0", 1), moved_by(own, "ctx_0", 3)
-    partner = moved_by(own, "ctx_1", 1)
+    after_far, far = lax.optimization_barrier((own, far))
+    partner = moved_by(after_far, "ctx_1", 1)
+    keys_grad, values_grad, own_pack, far_pack = call(
+        score_grad_kernel,
+        [SMEM] + [VMEM] * 8,
+        [shape((KEYS, D)), shape((KEYS, D)), *[shape((4, 64, CHUNK))] * 2],
+        [pltpu.VMEM((TOKENS, D), F32)],
+        flops=3 * 2 * KEYS * TOKENS * D,
+        moved=6 * 2**20,
+        limit=VMEM_ALL,
+    )(place, normed, grads, keys, weights, slopes, stats, near, far)
+    up, down, far_pack = lax.optimization_barrier((up, down, far_pack))
     across = [moved_by(up[:128], "ctx_0", 1), moved_by(down[128:], "ctx_0", 3)]
     partner_up, partner_down = moved_by(partner, "ctx_0", 1), moved_by(partner, "ctx_0", 3)
     partner_across = [moved_by(piece, "ctx_1", 1) for piece in across]
-    w_in, w_out = expert_weights[0, :, 0, :], expert_weights[0, :, 1, :]
     places = [(0, 0), (-1, 0), (1, 0), (0, 1), (-1, 1), (1, 1), (2, 0), (2, 1)]
     at = jnp.stack([2 * ((y + a + 4) % 4) + (x + b) % 2 for a, b in places]).astype(jnp.int32)
     kept = [shape((SLOTS, D))] * 2 + [shape((SLOTS, UNITS))] * 2
-    ready, far = lax.optimization_barrier((partner, far))
     early_sums, *early = call(
         early_kernel,
         [VMEM] * 6,
@@ -375,7 +404,9 @@
         flops=2 * 3 * SLOTS * UNITS * D,
         moved=8 * 2**20,
         limit=VMEM_ALL,
-    )(own, up, down, ready, w_in, w_out)
+    )(own, up, down, partner, w_in, w_out)
+    early_sums, far_pack = lax.optimization_barrier((early_sums, far_pack))
+    far_query = moved_by(far_pack, "ctx_1", 1)
     sums, *late = call(
         late_kernel,
         [SMEM] + [ANY] * 9,
@@ -393,16 +424,8 @@
         places=[ANY] * 5,
         limit=VMEM_ALL,
     )(at, partner_up, partner_down, *across, *partner_across, w_in, w_out, early_sums)
+    sums, far_query = lax.optimization_barrier((sums, far_query))
     parts = lax.all_to_all(sums, CTX, split_axis=0, concat_axis=0, tiled=True)
-    keys_grad, values_grad, query_pack = call(
-        score_grad_kernel,
-        [SMEM] + [VMEM] * 8,
-        [shape((KEYS, D)), shape((KEYS, D)), shape((2, 4, 64, CHUNK))],
-        [pltpu.VMEM((TOKENS, D), F32)],
-        flops=3 * 2 * KEYS * TOKENS * D,
-        moved=6 * 2**20,
-        limit=VMEM_ALL,
-    )(place, normed, grads, keys, weights, slopes, stats, near, far)
     [weights_grad] = call(
         weights_kernel,
         [ANY] * 8,
@@ -413,14 +436,13 @@
         limit=VMEM_ALL,
     )(*early, *late)
     weights_grad = weights_grad.reshape(1, UNITS, 2, D)
-    far_query = moved_by(query_pack[0], "ctx_1", 1)
     parts, weights_grad = lax.optimization_barrier((parts, weights_grad))
     [back] = call(total_kernel, [VMEM], [shape((ROWS, CHUNK))], moved=3 * 2**20)(parts)
     back, far_query = lax.optimization_barrier((back, far_query))
     returned = lax.all_to_all(
         back.reshape(EXPERTS, 8, CHUNK), "exp", split_axis=0, concat_axis=0, tiled=True
     ).reshape(ROWS, CHUNK)
-    queries = call(join_kernel, [VMEM] * 2, [shape((64, CHUNK))] * 4, moved=2**20)(query_pack, far_query)
+    queries = call(join_kernel, [VMEM] * 2, [shape((64, CHUNK))] * 4, moved=2**20)(own_pack, far_query)
     queries = [queries[0]] + [moved_by(queries[k], "ctx_0", k) for k in (1, 2, 3)]
     [total] = call(tokens_kernel, [VMEM] * 7, [shape((CTX_COUNT, 64, CHUNK))], moved=2**20)(
         returned, even, odd, *queries

time: 167 us -> 161 us (0.964)
  waiting for transfers between devices: 35 us -> 51.8 us
  starting transfers between devices: 60.5 us -> 46.2 us
  local copies, waits for them, and re-layouts: 21.4 us -> 14.8 us
    ppermute x17, waiting for transfers between devices: 7.95 us -> 29.7 us  [moved_by(): lax.ppermute(array, axis, [(k, (k + step) % count) for k in range(count)])]
    ppermute x17, starting transfers between devices: 37.4 us -> 25 us  [moved_by(): lax.ppermute(array, axis, [(k, (k + step) % count) for k in range(count)])]
    all_to_all x1, waiting for transfers between devices: 12.7 us -> 3.75 us  [on_device(): lax.all_to_all(send.reshape(EXPERTS, 8, HALF), 'exp', split_axis=0, conca...]
    slice x1 -> x0, local copies, waits for them, and re-layouts: 6.48 us -> none  [on_device(): w_in, w_out = (expert_weights[0, :, 0, :], expert_weights[0, :, 1, :])]
    all_to_all x1, waiting for transfers between devices: 10.6 us -> 13 us  [on_device(): parts = lax.all_to_all(sums, CTX, split_axis=0, concat_axis=0, tiled=True)]
    optimization_barrier x0 -> x1, local copies, waits for them, and re-layouts: none -> 2 us  [on_device(): normed, expert_weights = lax.optimization_barrier((normed, expert_weights))]
    squeeze x1 -> x0, local copies, waits for them, and re-layouts: 1.75 us -> none  [on_device(): far_query = moved_by(query_pack[0], 'ctx_1', 1)]
  transfers between devices with their start and end apart: 20 -> 20, of which waited for: 9 -> 13; matrix products, arithmetic and copies ran while one was open for 11% -> 7% of each run, Pallas kernels for 12% -> 16%
where the time goes in v8:
time: 161 us; the launch traced here: 160 us
  waiting for transfers between devices  51.8 us (32%)
  starting transfers between devices  46.2 us (29%)
  Pallas kernels  31.4 us (20%)
  blocking collectives  14.9 us (9%)
  local copies, waits for them, and re-layouts  14.8 us (9%)
    ppermute x17, waiting for transfers between devices, moved_by(): lax.ppermute(array, axis, [(k, (k + step) % count) for k in range(count)])  29.7 us
    ppermute x17, starting transfers between devices, moved_by(): lax.ppermute(array, axis, [(k, (k + step) % count) for k in range(count)])  25 us
    all_to_all x1, blocking collectives, on_device(): packs = lax.all_to_all(total, CTX, split_axis=0, concat_axis=0, tiled=True)  14.9 us
    all_to_all x1, waiting for transfers between devices, on_device(): parts = lax.all_to_all(sums, CTX, split_axis=0, concat_axis=0, tiled=True)  13 us
    all_to_all x1, starting transfers between devices, on_device(): lax.all_to_all(send.reshape(EXPERTS, 8, HALF), 'exp', split_axis=0, conca...  9.66 us
    all_to_all x1, starting transfers between devices, on_device(): lax.all_to_all(back.reshape(EXPERTS, 8, CHUNK), 'exp', split_axis=0, conc...  7.93 us
    pallas_call x1, Pallas kernels, on_device(): call(weights_kernel, [ANY] * 8, [shape((2 * UNITS, D))], [pltpu.VMEM(k.sh...  7.36 us
    reshape x1, local copies, waits for them, and re-layouts, on_device(): weights_grad = weights_grad.reshape(1, UNITS, 2, D)  6.45 us
  transfers between devices with their start and end apart: 20, of which 13 were waited for; matrix products, arithmetic and copies ran while one was open for 7% of the time, Pallas kernels for 16%

profile of v8, /device:TPU:32, one launch (start us, length us, event | category | flops | bytes accessed | tf_op | source)
XLA Modules:
  0.0 160.0 jit_solution(12606802341899627408)
XLA Ops:
  0.6 3.4 %shard_map.111 = (bf16[128,2560]{1,0:T(8,128)(2,1)}, bf16[256,1280]{1,0:T(8,128)(2,1)}, bf16[256,128]{1,0:T(8,128)(2,1)}, bf16[256,128]{1,0:T(8,128)(2,1)}) custom-call(s32[1]{0:T(128)} %bitcast.8.place, bf16[128,2560]{1,0:T(8,128)(2,1)} %bitcast.34, bf16[128,2560]{1,0:T(8,128)(2,1)} %bitcast.30, f32[2560]{0:T(1024)} %gain.3, s32[2,128]{1,0:T(2,128)} %bitcast.46, ...), custom_call_target="tpu_custom_call" | custom-call | flops 335544320 | bytes 3145728 | tf_op jit(solution)/shard_map/pallas_call | solution.py:355
  4.0 9.7 %all-to-all-start = ((bf16[32,8,1280]{2,1,0:T(8,128)(2,1)}), bf16[32,8,1280]{2,1,0:T(8,128)(2,1)S(1)}, u32[]{:S(2)}, u32[]{:S(2)}) async-start(bf16[32,8,1280]{2,1,0:T(8,128)(2,1)} %bitcast.45), calls=%async_computation | async-start | bytes 1310720 | tf_op jit(solution)/shard_map/all_to_all | solution.py:363
  13.7 2.0 %copy.12 = bf16[1,256,2,2560]{3,1,2,0:T(8,128)(2,1)S(1)} copy(bf16[1,256,2,2560]{3,2,1,0:T(2,128)(2,1)} %param.15) | data formatting | bytes 5242880 | tf_op jit(solution)/shard_map/optimization_barrier | solution.py:367
  15.7 1.7 %slice_bitcast_fusion = (bf16[256,2560]{1,0:T(8,128)(2,1)}, bf16[256,2560]{1,0:T(8,128)(2,1)}) fusion(bf16[1,256,2,2560]{3,1,2,0:T(8,128)(2,1)S(1)} %copy.12), kind=kLoop, calls=%fused_computation | loop fusion | bytes 5242880 | tf_op jit(solution)/shard_map/squeeze | solution.py:368
  17.4 0.7 copy-done.4
  18.3 1.1 shard_map.112
  19.4 1.1 copy-done.5
  20.5 1.0 copy-done.6
  21.5 3.0 %collective-permute-start.2 = (f32[72,128]{1,0:T(8,128)S(1)}, f32[72,128]{1,0:T(8,128)S(1)}, u32[]{:S(2)}, u32[]{:S(2)}) collective-permute-start(f32[72,128]{1,0:T(8,128)S(1)} %get-tuple-element.54.local), channel_id=1, source_target_pairs={{0,192},{64,0},{128,64},{192,128},{1,193},{65,1},{129,65},{193,129... | collective-permute-start | bytes 110600 | tf_op jit(solution)/shard_map/ppermute | solution.py:346
  24.6 0.6 collective-permute-start.1
  25.2 1.0 collective-permute-start
  26.4 3.6 %collective-permute-done.1 = f32[72,128]{1,0:T(8,128)S(1)} collective-permute-done((f32[72,128]{1,0:T(8,128)S(1)}, f32[72,128]{1,0:T(8,128)S(1)}, u32[]{:S(2)}, u32[]{:S(2)}) %collective-permute-start.1) | collective-permute-done | bytes 36896 | tf_op jit(solution)/shard_map/ppermute | solution.py:346
  30.0 0.4 collective-permute-done
  30.5 3.7 %all-to-all-done = bf16[32,8,1280]{2,1,0:T(8,128)(2,1)S(1)} async-done(((bf16[32,8,1280]{2,1,0:T(8,128)(2,1)}), bf16[32,8,1280]{2,1,0:T(8,128)(2,1)S(1)}, u32[]{:S(2)}, u32[]{:S(2)}) %all-to-all-start) | async-done | bytes 655392 | tf_op jit(solution)/shard_map/all_to_all | solution.py:363
  34.2 2.7 %collective-permute-start.3 = (f32[72,128]{1,0:T(8,128)S(1)}, f32[72,128]{1,0:T(8,128)S(1)}, u32[]{:S(2)}, u32[]{:S(2)}) collective-permute-start(f32[72,128]{1,0:T(8,128)S(1)} %pad_maximum_fusion.near), channel_id=1, source_target_pairs={{0,32},{32,0},{1,33},{33,1},{2,34},{34,2},{3,35},{35,3},{4,36},{36... | collective-permute-start | bytes 110600 | tf_op jit(solution)/shard_map/ppermute | solution.py:346
  37.0 3.0 %collective-permute-start.8 = (bf16[256,1280]{1,0:T(8,128)(2,1)S(1)}, bf16[256,1280]{1,0:T(8,128)(2,1)S(1)}, u32[]{:S(2)}, u32[]{:S(2)}) collective-permute-start(bf16[256,1280]{1,0:T(8,128)(2,1)S(1)} %bitcast.40), channel_id=1, source_target_pairs={{0,192},{64,0},{128,64},{192,128},{1,193},{65,1},{129,65},{193,129... | collective-permute-start | bytes 1966088 | tf_op jit(solution)/shard_map/ppermute | solution.py:346
  40.0 2.4 %collective-permute-start.4 = (bf16[256,1280]{1,0:T(8,128)(2,1)S(1)}, bf16[256,1280]{1,0:T(8,128)(2,1)S(1)}, u32[]{:S(2)}, u32[]{:S(2)}) collective-permute-start(bf16[256,1280]{1,0:T(8,128)(2,1)S(1)} %bitcast.42), channel_id=1, source_target_pairs={{0,32},{32,0},{1,33},{33,1},{2,34},{34,2},{3,35},{35,3},{4,36},{36... | collective-permute-start | bytes 1966088 | tf_op jit(solution)/shard_map/ppermute | solution.py:346
  42.4 4.3 %shard_map.113 = (bf16[128,2560]{1,0:T(8,128)(2,1)}, bf16[128,2560]{1,0:T(8,128)(2,1)}, bf16[4,64,640]{2,1,0:T(8,128)(2,1)}, bf16[4,64,640]{2,1,0:T(8,128)(2,1)}) custom-call(s32[1]{0:T(128)} %bitcast.8.place, bf16[128,2560]{1,0:T(8,128)(2,1)} %get-tuple-element.51.normed, bf16[128,2560]{1,0:T(8,128)(2,1)} %bitcast.31, bf16[128,2560]{1,0:T(8,128)(2,1)} %bitcast.36, ...), custom_call_target="tpu_custom_call" | custom-call | flops 251658240 | bytes 6291456 | tf_op jit(solution)/shard_map/pallas_call | solution.py:384
  46.8 6.1 %collective-permute-done.8.down = bf16[256,1280]{1,0:T(8,128)(2,1)S(1)} collective-permute-done((bf16[256,1280]{1,0:T(8,128)(2,1)S(1)}, bf16[256,1280]{1,0:T(8,128)(2,1)S(1)}, u32[]{:S(2)}, u32[]{:S(2)}) %collective-permute-start.8) | collective-permute-done | bytes 655392 | tf_op jit(solution)/shard_map/ppermute | solution.py:346
  52.9 3.4 %collective-permute-done.7.up = bf16[256,1280]{1,0:T(8,128)(2,1)S(1)} collective-permute-done((bf16[256,1280]{1,0:T(8,128)(2,1)S(1)}, bf16[256,1280]{1,0:T(8,128)(2,1)S(1)}, u32[]{:S(2)}, u32[]{:S(2)}) %collective-permute-start.7) | collective-permute-done | bytes 655392 | tf_op jit(solution)/shard_map/ppermute | solution.py:346
  56.3 0.4 collective-permute-start.10
  56.7 1.8 %collective-permute-start.9 = (bf16[128,1280]{1,0:T(8,128)(2,1)S(1)}, bf16[128,1280]{1,0:T(8,128)(2,1)}, u32[]{:S(2)}, u32[]{:S(2)}) collective-permute-start(bf16[128,1280]{1,0:T(8,128)(2,1)S(1)} %slice.66), channel_id=1, source_target_pairs={{0,64},{64,128},{128,192},{192,0},{1,65},{65,129},{129,193},{193,1... | collective-permute-start | bytes 983048 | tf_op jit(solution)/shard_map/ppermute | solution.py:346
  58.5 1.5 collective-permute-start.6
  60.0 0.5 collective-permute-start.5
  60.6 6.5 %collective-permute-done.10.refs_3_ = bf16[128,1280]{1,0:T(8,128)(2,1)S(1)} collective-permute-done((bf16[128,1280]{1,0:T(8,128)(2,1)S(1)}, bf16[128,1280]{1,0:T(8,128)(2,1)S(1)}, u32[]{:S(2)}, u32[]{:S(2)}) %collective-permute-start.10) | collective-permute-done | bytes 327712 | tf_op jit(solution)/shard_map/ppermute | solution.py:346
  67.0 0.8 collective-permute-start.12
  67.8 0.9 collective-permute-done.9.refs_2_
  68.7 1.8 %collective-permute-start.11 = (bf16[128,1280]{1,0:T(8,128)(2,1)}, bf16[128,1280]{1,0:T(8,128)(2,1)}, u32[]{:S(2)}, u32[]{:S(2)}) collective-permute-start(bf16[128,1280]{1,0:T(8,128)(2,1)} %collective-permute-done.9.refs_2_), channel_id=1, source_target_pairs={{0,32},{32,0},{1,33},{33,1},{2,34},{34,2},{3,35},{35,3},{4,36},{36... | collective-permute-start | bytes 983048 | tf_op jit(solution)/shard_map/ppermute | solution.py:346
  70.6 5.7 %shard_map.114 = (bf16[8,128,640]{2,1,0:T(8,128)(2,1)}, bf16[256,2560]{1,0:T(8,128)(2,1)}, bf16[256,2560]{1,0:T(8,128)(2,1)}, bf16[256,256]{1,0:T(8,128)(2,1)}, bf16[256,256]{1,0:T(8,128)(2,1)}) custom-call(bf16[256,1280]{1,0:T(8,128)(2,1)} %bitcast.43, bf16[256,1280]{1,0:T(8,128)(2,1)} %copy-done.15, bf16[256,1280]{1,0:T(8,128)(2,1)} %copy-done.14, ...), custom_call_target="tpu_custom_call" | custom-call | flops 1006632960 | bytes 8388608 | tf_op jit(solution)/shard_map/pallas_call | solution.py:400
  76.3 1.8 %collective-permute-start.13 = (bf16[4,64,640]{2,1,0:T(8,128)(2,1)}, bf16[4,64,640]{2,1,0:T(8,128)(2,1)S(1)}, u32[]{:S(2)}, u32[]{:S(2)}) collective-permute-start(bf16[4,64,640]{2,1,0:T(8,128)(2,1)} %get-tuple-element.70), channel_id=1, source_target_pairs={{0,32},{32,0},{1,33},{33,1},{2,34},{34,2},{3,35},{35,3},{4,36},{36... | collective-permute-start | bytes 983048 | tf_op jit(solution)/shard_map/ppermute | solution.py:346
  78.1 0.6 stack.35.at_ref
  78.7 4.0 %collective-permute-done.11.refs_4_ = bf16[128,1280]{1,0:T(8,128)(2,1)} collective-permute-done((bf16[128,1280]{1,0:T(8,128)(2,1)}, bf16[128,1280]{1,0:T(8,128)(2,1)}, u32[]{:S(2)}, u32[]{:S(2)}) %collective-permute-start.11) | collective-permute-done | bytes 327712 | tf_op jit(solution)/shard_map/ppermute | solution.py:346
  82.8 0.8 copy-done.17
  83.6 6.2 %shard_map.115 = (bf16[8,256,640]{2,1,0:T(8,128)(2,1)}, bf16[256,2560]{1,0:T(8,128)(2,1)}, bf16[256,2560]{1,0:T(8,128)(2,1)}, bf16[256,256]{1,0:T(8,128)(2,1)}, bf16[256,256]{1,0:T(8,128)(2,1)}) custom-call(s32[8]{0:T(128)} %stack.35.at_ref, bf16[256,1280]{1,0:T(8,128)(2,1)} %collective-permute-done.5.refs_0_, bf16[256,1280]{1,0:T(8,128)(2,1)} %copy-done.17, ...), custom_call_target="tpu_custom_call" | custom-call | flops 1006632960 | bytes 12582912 | tf_op jit(solution)/shard_map/pallas_call | solution.py:410
  89.8 3.6 %all-to-all-start.1 = ((bf16[8,256,640]{2,1,0:T(8,128)(2,1)}), bf16[8,256,640]{2,1,0:T(8,128)(2,1)S(1)}, u32[]{:S(2)}, u32[]{:S(2)}) async-start(bf16[8,256,640]{2,1,0:T(8,128)(2,1)} %get-tuple-element.71), calls=%async_computation.1 | async-start | bytes 5242880 | tf_op jit(solution)/shard_map/all_to_all | solution.py:428
  93.5 7.4 %shard_map.116 = bf16[512,2560]{1,0:T(8,128)(2,1)} custom-call(bf16[256,2560]{1,0:T(8,128)(2,1)} %get-tuple-element.72.refs_0_, bf16[256,2560]{1,0:T(8,128)(2,1)} %get-tuple-element.73.refs_1_, bf16[256,256]{1,0:T(8,128)(2,1)} %get-tuple-element.74.refs_2_, bf16[256,256]{1,0:T(8,128)(2,1)} %get-tuple-element.75.refs_3_, ...), custom_call_target="tpu_custom_call" | custom-call | flops 1342177280 | bytes 8388608 | tf_op jit(solution)/shard_map/pallas_call | solution.py:429
  100.9 6.4 %reshape.29 = bf16[1,256,2,2560]{3,2,1,0:T(2,128)(2,1)} reshape(bf16[512,2560]{1,0:T(8,128)(2,1)} %shard_map.116) | data formatting | bytes 5242880 | tf_op jit(solution)/shard_map/reshape | solution.py:438
  107.3 13.0 %all-to-all-done.1.parts = bf16[8,256,640]{2,1,0:T(8,128)(2,1)S(1)} async-done(((bf16[8,256,640]{2,1,0:T(8,128)(2,1)}), bf16[8,256,640]{2,1,0:T(8,128)(2,1)S(1)}, u32[]{:S(2)}, u32[]{:S(2)}) %all-to-all-start.1) | async-done | bytes 2621472 | tf_op jit(solution)/shard_map/all_to_all | solution.py:428
  120.3 1.3 shard_map.117
  121.6 7.9 %all-to-all-start.2 = ((bf16[32,8,640]{2,1,0:T(8,128)(2,1)}), bf16[32,8,640]{2,1,0:T(8,128)(2,1)S(1)}, u32[]{:S(2)}, u32[]{:S(2)}) async-start(bf16[32,8,640]{2,1,0:T(8,128)(2,1)} %bitcast.21), calls=%async_computation.2 | async-start | bytes 655360 | tf_op jit(solution)/shard_map/all_to_all | solution.py:442
  130.0 2.7 %collective-permute-start.15 = (bf16[64,640]{1,0:T(8,128)(2,1)S(1)}, bf16[64,640]{1,0:T(8,128)(2,1)S(1)}, u32[]{:S(2)}, u32[]{:S(2)}) collective-permute-start(bf16[64,640]{1,0:T(8,128)(2,1)S(1)} %get-tuple-element.89), channel_id=1, source_target_pairs={{0,128},{64,192},{128,0},{192,64},{1,129},{65,193},{129,1},{193,65... | collective-permute-start | bytes 245768 | tf_op jit(solution)/shard_map/ppermute | solution.py:346
  132.7 0.6 collective-permute-start.16
  133.3 3.9 %collective-permute-done.14.below = bf16[64,640]{1,0:T(8,128)(2,1)S(1)} collective-permute-done((bf16[64,640]{1,0:T(8,128)(2,1)S(1)}, bf16[64,640]{1,0:T(8,128)(2,1)S(1)}, u32[]{:S(2)}, u32[]{:S(2)}) %collective-permute-start.14) | collective-permute-done | bytes 81952 | tf_op jit(solution)/shard_map/ppermute | solution.py:346
  137.2 0.6 collective-permute-done.16.above
  137.8 5.3 %all-to-all-done.2 = bf16[32,8,640]{2,1,0:T(8,128)(2,1)S(1)} async-done(((bf16[32,8,640]{2,1,0:T(8,128)(2,1)}), bf16[32,8,640]{2,1,0:T(8,128)(2,1)S(1)}, u32[]{:S(2)}, u32[]{:S(2)}) %all-to-all-start.2) | async-done | bytes 327712 | tf_op jit(solution)/shard_map/all_to_all | solution.py:442
  143.1 0.4 shard_map.119
  143.5 14.9 %all_to_all.20.packs = bf16[8,64,640]{2,1,0:T(8,128)(2,1)S(1)} all-to-all(bf16[8,64,640]{2,1,0:T(8,128)(2,1)S(1)} %shard_map.119), channel_id=1, replica_groups=mesh['ctx_0'=4,'ctx_1'=2,'exp'=32] {'ctx_0','ctx_1'}, dimensions={0} | all-to-all | bytes 1310720 | tf_op jit(solution)/shard_map/all_to_all | solution.py:450
  158.5 1.5 shard_map.120
  (54 shorter events, 1.1 us)
Async XLA Ops:
  4.0 30.2 %all-to-all-start = ((bf16[32,8,1280]{2,1,0:T(8,128)(2,1)}), bf16[32,8,1280]{2,1,0:T(8,128)(2,1)S(1)}, u32[]{:S(2)}, u32[]{:S(2)}) async-start(bf16[32,8,1280]{2,1,0:T(8,128)(2,1)} %bitcast.45), calls=%async_computation | async-start | bytes 1310720 | tf_op jit(solution)/shard_map/all_to_all | solution.py:363
  15.7 1.7 %copy-start = (bf16[1,128,2560]{2,1,0:T(8,128)(2,1)S(1)}, bf16[1,128,2560]{2,1,0:T(8,128)(2,1)}, u32[]{:S(2)}) copy-start(bf16[1,128,2560]{2,1,0:T(8,128)(2,1)} %param.9) | copy-start | bytes 1966084
  15.7 1.7 %copy-start.3 = (bf16[1,128,2560]{2,1,0:T(8,128)(2,1)S(1)}, bf16[1,128,2560]{2,1,0:T(8,128)(2,1)}, u32[]{:S(2)}) copy-start(bf16[1,128,2560]{2,1,0:T(8,128)(2,1)} %param.10) | copy-start | bytes 1966084
  15.7 2.4 %copy-start.4 = (bf16[128,2560]{1,0:T(8,128)(2,1)S(1)}, bf16[128,2560]{1,0:T(8,128)(2,1)}, u32[]{:S(2)}) copy-start(bf16[128,2560]{1,0:T(8,128)(2,1)} %get-tuple-element.51.normed) | copy-start | bytes 1966084
  15.7 2.6 %copy-start.7 = (bf16[1,128,2560]{2,1,0:T(8,128)(2,1)S(1)}, bf16[1,128,2560]{2,1,0:T(8,128)(2,1)}, u32[]{:S(2)}) copy-start(bf16[1,128,2560]{2,1,0:T(8,128)(2,1)} %param.11) | copy-start | bytes 1966084
  19.4 1.1 copy-start.5
  20.5 1.1 copy-start.6
  21.5 20.9 %copy-start.9 = (f32[72,128]{1,0:T(8,128)}, f32[72,128]{1,0:T(8,128)S(1)}, u32[]{:S(2)}) copy-start(f32[72,128]{1,0:T(8,128)S(1)} %get-tuple-element.54.local) | copy-start | bytes 110596
  21.5 4.9 %collective-permute-start.2 = (f32[72,128]{1,0:T(8,128)S(1)}, f32[72,128]{1,0:T(8,128)S(1)}, u32[]{:S(2)}, u32[]{:S(2)}) collective-permute-start(f32[72,128]{1,0:T(8,128)S(1)} %get-tuple-element.54.local), channel_id=1, source_target_pairs={{0,192},{64,0},{128,64},{192,128},{1,193},{65,1},{129,65},{193,129... | collective-permute-start | bytes 110600 | tf_op jit(solution)/shard_map/ppermute | solution.py:346
  24.6 5.5 %collective-permute-start.1 = (f32[72,128]{1,0:T(8,128)S(1)}, f32[72,128]{1,0:T(8,128)S(1)}, u32[]{:S(2)}, u32[]{:S(2)}) collective-permute-start(f32[72,128]{1,0:T(8,128)S(1)} %get-tuple-element.54.local), channel_id=1, source_target_pairs={{0,128},{64,192},{128,0},{192,64},{1,129},{65,193},{129,1},{193,65... | collective-permute-start | bytes 110600 | tf_op jit(solution)/shard_map/ppermute | solution.py:346
  25.2 5.2 %collective-permute-start = (f32[72,128]{1,0:T(8,128)S(1)}, f32[72,128]{1,0:T(8,128)S(1)}, u32[]{:S(2)}, u32[]{:S(2)}) collective-permute-start(f32[72,128]{1,0:T(8,128)S(1)} %get-tuple-element.54.local), channel_id=1, source_target_pairs={{0,64},{64,128},{128,192},{192,0},{1,65},{65,129},{129,193},{193,1... | collective-permute-start | bytes 110600 | tf_op jit(solution)/shard_map/ppermute | solution.py:346
  30.5 12.0 %copy-start.19 = (f32[72,128]{1,0:T(8,128)}, f32[72,128]{1,0:T(8,128)S(1)}, u32[]{:S(2)}) copy-start(f32[72,128]{1,0:T(8,128)S(1)} %pad_maximum_fusion.near) | copy-start | bytes 110596
  34.2 12.5 %copy-start.13 = (bf16[32,8,1280]{2,1,0:T(8,128)(2,1)}, bf16[32,8,1280]{2,1,0:T(8,128)(2,1)S(1)}, u32[]{:S(2)}) copy-start(bf16[32,8,1280]{2,1,0:T(8,128)(2,1)S(1)} %all-to-all-done) | copy-start | bytes 1966084
  34.2 5.8 %collective-permute-start.3 = (f32[72,128]{1,0:T(8,128)S(1)}, f32[72,128]{1,0:T(8,128)S(1)}, u32[]{:S(2)}, u32[]{:S(2)}) collective-permute-start(f32[72,128]{1,0:T(8,128)S(1)} %pad_maximum_fusion.near), channel_id=1, source_target_pairs={{0,32},{32,0},{1,33},{33,1},{2,34},{34,2},{3,35},{35,3},{4,36},{36... | collective-permute-start | bytes 110600 | tf_op jit(solution)/shard_map/ppermute | solution.py:346
  37.0 15.9 %collective-permute-start.8 = (bf16[256,1280]{1,0:T(8,128)(2,1)S(1)}, bf16[256,1280]{1,0:T(8,128)(2,1)S(1)}, u32[]{:S(2)}, u32[]{:S(2)}) collective-permute-start(bf16[256,1280]{1,0:T(8,128)(2,1)S(1)} %bitcast.40), channel_id=1, source_target_pairs={{0,192},{64,0},{128,64},{192,128},{1,193},{65,1},{129,65},{193,129... | collective-permute-start | bytes 1966088 | tf_op jit(solution)/shard_map/ppermute | solution.py:346
  40.0 16.3 %collective-permute-start.7 = (bf16[256,1280]{1,0:T(8,128)(2,1)S(1)}, bf16[256,1280]{1,0:T(8,128)(2,1)S(1)}, u32[]{:S(2)}, u32[]{:S(2)}) collective-permute-start(bf16[256,1280]{1,0:T(8,128)(2,1)S(1)} %bitcast.41), channel_id=1, source_target_pairs={{0,64},{64,128},{128,192},{192,0},{1,65},{65,129},{129,193},{193,1... | collective-permute-start | bytes 1966088 | tf_op jit(solution)/shard_map/ppermute | solution.py:346
  40.0 2.4 %copy-start.20 = (f32[72,128]{1,0:T(8,128)}, f32[72,128]{1,0:T(8,128)S(1)}, u32[]{:S(2)}) copy-start(f32[72,128]{1,0:T(8,128)S(1)} %collective-permute-done.3.far) | copy-start | bytes 110596
  40.0 18.5 %collective-permute-start.4 = (bf16[256,1280]{1,0:T(8,128)(2,1)S(1)}, bf16[256,1280]{1,0:T(8,128)(2,1)S(1)}, u32[]{:S(2)}, u32[]{:S(2)}) collective-permute-start(bf16[256,1280]{1,0:T(8,128)(2,1)S(1)} %bitcast.42), channel_id=1, source_target_pairs={{0,32},{32,0},{1,33},{33,1},{2,34},{34,2},{3,35},{35,3},{4,36},{36... | collective-permute-start | bytes 1966088 | tf_op jit(solution)/shard_map/ppermute | solution.py:346
  52.9 17.7 %copy-start.14 = (bf16[256,1280]{1,0:T(8,128)(2,1)}, bf16[256,1280]{1,0:T(8,128)(2,1)S(1)}, u32[]{:S(2)}) copy-start(bf16[256,1280]{1,0:T(8,128)(2,1)S(1)} %collective-permute-done.8.down) | copy-start | bytes 1966084
  56.3 14.3 %copy-start.15 = (bf16[256,1280]{1,0:T(8,128)(2,1)}, bf16[256,1280]{1,0:T(8,128)(2,1)S(1)}, u32[]{:S(2)}) copy-start(bf16[256,1280]{1,0:T(8,128)(2,1)S(1)} %collective-permute-done.7.up) | copy-start | bytes 1966084
  56.3 10.7 %collective-permute-start.10 = (bf16[128,1280]{1,0:T(8,128)(2,1)S(1)}, bf16[128,1280]{1,0:T(8,128)(2,1)S(1)}, u32[]{:S(2)}, u32[]{:S(2)}) collective-permute-start(bf16[128,1280]{1,0:T(8,128)(2,1)S(1)} %slice.67), channel_id=1, source_target_pairs={{0,192},{64,0},{128,64},{192,128},{1,193},{65,1},{129,65},{193,129... | collective-permute-start | bytes 983048 | tf_op jit(solution)/shard_map/ppermute | solution.py:346
  56.7 12.0 %collective-permute-start.9 = (bf16[128,1280]{1,0:T(8,128)(2,1)S(1)}, bf16[128,1280]{1,0:T(8,128)(2,1)}, u32[]{:S(2)}, u32[]{:S(2)}) collective-permute-start(bf16[128,1280]{1,0:T(8,128)(2,1)S(1)} %slice.66), channel_id=1, source_target_pairs={{0,64},{64,128},{128,192},{192,0},{1,65},{65,129},{129,193},{193,1... | collective-permute-start | bytes 983048 | tf_op jit(solution)/shard_map/ppermute | solution.py:346
  58.5 12.1 %copy-start.16 = (bf16[256,1280]{1,0:T(8,128)(2,1)}, bf16[256,1280]{1,0:T(8,128)(2,1)S(1)}, u32[]{:S(2)}) copy-start(bf16[256,1280]{1,0:T(8,128)(2,1)S(1)} %collective-permute-done.4.partner) | copy-start | bytes 1966084
  58.5 24.2 %collective-permute-start.6 = (bf16[256,1280]{1,0:T(8,128)(2,1)S(1)}, bf16[256,1280]{1,0:T(8,128)(2,1)S(1)}, u32[]{:S(2)}, u32[]{:S(2)}) collective-permute-start(bf16[256,1280]{1,0:T(8,128)(2,1)S(1)} %collective-permute-done.4.partner), channel_id=1, source_target_pairs={{0,192},{64,0},{128,64},{192,128},{1,193},{65,1},{129,65},{193,129... | collective-permute-start | bytes 1966088 | tf_op jit(solution)/shard_map/ppermute | solution.py:346
  60.0 22.7 %collective-permute-start.5 = (bf16[256,1280]{1,0:T(8,128)(2,1)S(1)}, bf16[256,1280]{1,0:T(8,128)(2,1)}, u32[]{:S(2)}, u32[]{:S(2)}) collective-permute-start(bf16[256,1280]{1,0:T(8,128)(2,1)S(1)} %collective-permute-done.4.partner), channel_id=1, source_target_pairs={{0,64},{64,128},{128,192},{192,0},{1,65},{65,129},{129,193},{193,1... | collective-permute-start | bytes 1966088 | tf_op jit(solution)/shard_map/ppermute | solution.py:346
  67.0 9.3 %copy-start.18 = (bf16[128,1280]{1,0:T(8,128)(2,1)}, bf16[128,1280]{1,0:T(8,128)(2,1)S(1)}, u32[]{:S(2)}) copy-start(bf16[128,1280]{1,0:T(8,128)(2,1)S(1)} %collective-permute-done.10.refs_3_) | copy-start | bytes 983044
  67.0 11.7 %collective-permute-start.12 = (bf16[128,1280]{1,0:T(8,128)(2,1)S(1)}, bf16[128,1280]{1,0:T(8,128)(2,1)}, u32[]{:S(2)}, u32[]{:S(2)}) collective-permute-start(bf16[128,1280]{1,0:T(8,128)(2,1)S(1)} %collective-permute-done.10.refs_3_), channel_id=1, source_target_pairs={{0,32},{32,0},{1,33},{33,1},{2,34},{34,2},{3,35},{35,3},{4,36},{36... | collective-permute-start | bytes 983048 | tf_op jit(solution)/shard_map/ppermute | solution.py:346
  68.7 14.0 %collective-permute-start.11 = (bf16[128,1280]{1,0:T(8,128)(2,1)}, bf16[128,1280]{1,0:T(8,128)(2,1)}, u32[]{:S(2)}, u32[]{:S(2)}) collective-permute-start(bf16[128,1280]{1,0:T(8,128)(2,1)} %collective-permute-done.9.refs_2_), channel_id=1, source_target_pairs={{0,32},{32,0},{1,33},{33,1},{2,34},{34,2},{3,35},{35,3},{4,36},{36... | collective-permute-start | bytes 983048 | tf_op jit(solution)/shard_map/ppermute | solution.py:346
  76.3 13.5 %collective-permute-start.13 = (bf16[4,64,640]{2,1,0:T(8,128)(2,1)}, bf16[4,64,640]{2,1,0:T(8,128)(2,1)S(1)}, u32[]{:S(2)}, u32[]{:S(2)}) collective-permute-start(bf16[4,64,640]{2,1,0:T(8,128)(2,1)} %get-tuple-element.70), channel_id=1, source_target_pairs={{0,32},{32,0},{1,33},{33,1},{2,34},{34,2},{3,35},{35,3},{4,36},{36... | collective-permute-start | bytes 983048 | tf_op jit(solution)/shard_map/ppermute | solution.py:346
  82.8 0.8 copy-start.17
  89.8 30.5 %all-to-all-start.1 = ((bf16[8,256,640]{2,1,0:T(8,128)(2,1)}), bf16[8,256,640]{2,1,0:T(8,128)(2,1)S(1)}, u32[]{:S(2)}, u32[]{:S(2)}) async-start(bf16[8,256,640]{2,1,0:T(8,128)(2,1)} %get-tuple-element.71), calls=%async_computation.1 | async-start | bytes 5242880 | tf_op jit(solution)/shard_map/all_to_all | solution.py:428
  107.3 22.2 %copy-start.8 = (bf16[4,64,640]{2,1,0:T(8,128)(2,1)S(1)}, bf16[4,64,640]{2,1,0:T(8,128)(2,1)}, u32[]{:S(2)}) copy-start(bf16[4,64,640]{2,1,0:T(8,128)(2,1)} %get-tuple-element.85.own) | copy-start | bytes 983044
  121.6 21.5 %copy-start.10 = (bf16[256,128]{1,0:T(8,128)(2,1)S(1)}, bf16[256,128]{1,0:T(8,128)(2,1)}, u32[]{:S(2)}) copy-start(bf16[256,128]{1,0:T(8,128)(2,1)} %get-tuple-element.83.even) | copy-start | bytes 196612
  121.6 21.5 %copy-start.11 = (bf16[256,128]{1,0:T(8,128)(2,1)S(1)}, bf16[256,128]{1,0:T(8,128)(2,1)}, u32[]{:S(2)}) copy-start(bf16[256,128]{1,0:T(8,128)(2,1)} %get-tuple-element.84.odd) | copy-start | bytes 196612
  121.6 21.5 %all-to-all-start.2 = ((bf16[32,8,640]{2,1,0:T(8,128)(2,1)}), bf16[32,8,640]{2,1,0:T(8,128)(2,1)S(1)}, u32[]{:S(2)}, u32[]{:S(2)}) async-start(bf16[32,8,640]{2,1,0:T(8,128)(2,1)} %bitcast.21), calls=%async_computation.2 | async-start | bytes 655360 | tf_op jit(solution)/shard_map/all_to_all | solution.py:442
  129.7 7.5 %collective-permute-start.14 = (bf16[64,640]{1,0:T(8,128)(2,1)S(1)}, bf16[64,640]{1,0:T(8,128)(2,1)S(1)}, u32[]{:S(2)}, u32[]{:S(2)}) collective-permute-start(bf16[64,640]{1,0:T(8,128)(2,1)S(1)} %get-tuple-element.88), channel_id=1, source_target_pairs={{0,64},{64,128},{128,192},{192,0},{1,65},{65,129},{129,193},{193,1... | collective-permute-start | bytes 245768 | tf_op jit(solution)/shard_map/ppermute | solution.py:346
  130.0 7.2 %collective-permute-start.15 = (bf16[64,640]{1,0:T(8,128)(2,1)S(1)}, bf16[64,640]{1,0:T(8,128)(2,1)S(1)}, u32[]{:S(2)}, u32[]{:S(2)}) collective-permute-start(bf16[64,640]{1,0:T(8,128)(2,1)S(1)} %get-tuple-element.89), channel_id=1, source_target_pairs={{0,128},{64,192},{128,0},{192,64},{1,129},{65,193},{129,1},{193,65... | collective-permute-start | bytes 245768 | tf_op jit(solution)/shard_map/ppermute | solution.py:346
  132.7 5.1 %collective-permute-start.16 = (bf16[64,640]{1,0:T(8,128)(2,1)S(1)}, bf16[64,640]{1,0:T(8,128)(2,1)S(1)}, u32[]{:S(2)}, u32[]{:S(2)}) collective-permute-start(bf16[64,640]{1,0:T(8,128)(2,1)S(1)} %get-tuple-element.90), channel_id=1, source_target_pairs={{0,192},{64,0},{128,64},{192,128},{1,193},{65,1},{129,65},{193,129... | collective-permute-start | bytes 245768 | tf_op jit(solution)/shard_map/ppermute | solution.py:346
  143.1 15.3 %copy-start.1 = (bf16[1,128,2560]{2,1,0:T(8,128)(2,1)S(1)}, bf16[1,128,2560]{2,1,0:T(8,128)(2,1)}, u32[]{:S(2)}) copy-start(bf16[1,128,2560]{2,1,0:T(8,128)(2,1)} %param.9) | copy-start | bytes 1966084
  143.1 15.3 %copy-start.2 = (bf16[1,128,2560]{2,1,0:T(8,128)(2,1)S(1)}, bf16[1,128,2560]{2,1,0:T(8,128)(2,1)}, u32[]{:S(2)}) copy-start(bf16[1,128,2560]{2,1,0:T(8,128)(2,1)} %param.8) | copy-start | bytes 1966084
  143.1 15.3 %copy-start.12 = (f32[2560]{0:T(1024)S(1)}, f32[2560]{0:T(1024)}, u32[]{:S(2)}) copy-start(f32[2560]{0:T(1024)} %gain.3) | copy-start | bytes 30724

commit v9 on v8

--- a/solution.py
+++ b/solution.py
@@ -210,12 +210,19 @@
         after(f)
 
 
-def early_kernel(own, up, down, partner, w_in, w_out, sums, rows, douts, act, pre_grad):
+def early_kernel(*refs):
+    own, up, up_rest, down_rest, down, partner, w_in, w_out, sums = refs[:9]
+
     def put(f, lanes, value):
         sums[f, :, lanes] = value
 
-    blocks = [lambda s=s: s[...] for s in (own, up, down, partner)]
-    experts_of(blocks, w_in, w_out, rows, douts, act, pre_grad, put)
+    blocks = [
+        lambda: own[...],
+        lambda: jnp.concatenate([up[...], up_rest[...]], axis=0),
+        lambda: jnp.concatenate([down_rest[...], down[...]], axis=0),
+        lambda: partner[...],
+    ]
+    experts_of(blocks, w_in, w_out, *refs[9:], put)
 
 
 def late_kernel(at_ref, *refs):
@@ -376,11 +383,12 @@
         moved=5 * 2**20,
     )(normed, grads, keys, values)
     near = merged([stats] + [moved_by(stats, "ctx_0", k) for k in (1, 2, 3)])
-    own, near = lax.optimization_barrier((own, near))
     far = moved_by(near, "ctx_1", 1)
-    up, down = moved_by(own, "ctx_0", 1), moved_by(own, "ctx_0", 3)
-    after_far, far = lax.optimization_barrier((own, far))
-    partner = moved_by(after_far, "ctx_1", 1)
+    own, near, far = lax.optimization_barrier((own, near, far))
+    low, high = own[:128], own[128:]
+    up, down = moved_by(low, "ctx_0", 1), moved_by(high, "ctx_0", 3)
+    up_rest, down_rest = moved_by(high, "ctx_0", 1), moved_by(low, "ctx_0", 3)
+    partner = moved_by(own, "ctx_1", 1)
     keys_grad, values_grad, own_pack, far_pack = call(
         score_grad_kernel,
         [SMEM] + [VMEM] * 8,
@@ -391,7 +399,7 @@
         limit=VMEM_ALL,
     )(place, normed, grads, keys, weights, slopes, stats, near, far)
     up, down, far_pack = lax.optimization_barrier((up, down, far_pack))
-    across = [moved_by(up[:128], "ctx_0", 1), moved_by(down[128:], "ctx_0", 3)]
+    across = [moved_by(up, "ctx_0", 1), moved_by(down, "ctx_0", 3)]
     partner_up, partner_down = moved_by(partner, "ctx_0", 1), moved_by(partner, "ctx_0", 3)
     partner_across = [moved_by(piece, "ctx_1", 1) for piece in across]
     places = [(0, 0), (-1, 0), (1, 0), (0, 1), (-1, 1), (1, 1), (2, 0), (2, 1)]
@@ -399,12 +407,12 @@
     kept = [shape((SLOTS, D))] * 2 + [shape((SLOTS, UNITS))] * 2
     early_sums, *early = call(
         early_kernel,
-        [VMEM] * 6,
+        [VMEM] * 8,
         [shape((CTX_COUNT, SLOTS // 2, CHUNK)), *kept],
         flops=2 * 3 * SLOTS * UNITS * D,
         moved=8 * 2**20,
         limit=VMEM_ALL,
-    )(own, up, down, partner, w_in, w_out)
+    )(own, up, up_rest, down_rest, down, partner, w_in, w_out)
     early_sums, far_pack = lax.optimization_barrier((early_sums, far_pack))
     far_query = moved_by(far_pack, "ctx_1", 1)
     sums, *late = call(

time: 161 us -> 158 us (0.981)
  starting transfers between devices: 46.2 us -> 42 us
    ppermute x17 -> x19, waiting for transfers between devices: 29.7 us -> 34.2 us  [moved_by(): lax.ppermute(array, axis, [(k, (k + step) % count) for k in range(count)])]
    all_to_all x1, waiting for transfers between devices: 3.75 us -> 0.01 us  [on_device(): lax.all_to_all(send.reshape(EXPERTS, 8, HALF), 'exp', split_axis=0, conca...]
    all_to_all x1, starting transfers between devices: 7.93 us -> 4.91 us  [on_device(): lax.all_to_all(back.reshape(EXPERTS, 8, CHUNK), 'exp', split_axis=0, conc...]
    unnamed x42 -> x46, local copies, waits for them, and re-layouts: 3.96 us -> 5.53 us
    ppermute x17 -> x19, starting transfers between devices: 25 us -> 23.8 us  [moved_by(): lax.ppermute(array, axis, [(k, (k + step) % count) for k in range(count)])]
  transfers between devices with their start and end apart: 20 -> 22, of which waited for: 13 -> 14; matrix products, arithmetic and copies ran while one was open for 7% -> 7% of each run, Pallas kernels for 16% -> 16%
where the time goes in v9:
time: 158 us; the launch traced here: 157 us
  waiting for transfers between devices  51.5 us (33%)
  starting transfers between devices  42 us (27%)
  Pallas kernels  31.4 us (20%)
  local copies, waits for them, and re-layouts  16.4 us (10%)
  blocking collectives  15.3 us (10%)
    ppermute x19, waiting for transfers between devices, moved_by(): lax.ppermute(array, axis, [(k, (k + step) % count) for k in range(count)])  34.2 us
    ppermute x19, starting transfers between devices, moved_by(): lax.ppermute(array, axis, [(k, (k + step) % count) for k in range(count)])  23.8 us
    all_to_all x1, blocking collectives, on_device(): packs = lax.all_to_all(total, CTX, split_axis=0, concat_axis=0, tiled=True)  15.3 us
    all_to_all x1, waiting for transfers between devices, on_device(): parts = lax.all_to_all(sums, CTX, split_axis=0, concat_axis=0, tiled=True)  12 us
    all_to_all x1, starting transfers between devices, on_device(): lax.all_to_all(send.reshape(EXPERTS, 8, HALF), 'exp', split_axis=0, conca...  9.66 us
    pallas_call x1, Pallas kernels, on_device(): call(weights_kernel, [ANY] * 8, [shape((2 * UNITS, D))], [pltpu.VMEM(k.sh...  7.34 us
    reshape x1, local copies, waits for them, and re-layouts, on_device(): weights_grad = weights_grad.reshape(1, UNITS, 2, D)  6.45 us
    pallas_call x1, Pallas kernels, on_device(): call(late_kernel, [SMEM] + [ANY] * 9, [shape((CTX_COUNT, ROWS, CHUNK)), *...  6.23 us
  transfers between devices with their start and end apart: 22, of which 14 were waited for; matrix products, arithmetic and copies ran while one was open for 7% of the time, Pallas kernels for 16%

profile of v9, /device:TPU:32, one launch (start us, length us, event | category | flops | bytes accessed | tf_op | source)
XLA Modules:
  0.0 157.4 jit_solution(13739179956766079006)
XLA Ops:
  0.6 3.4 %shard_map.111 = (bf16[128,2560]{1,0:T(8,128)(2,1)}, bf16[256,1280]{1,0:T(8,128)(2,1)}, bf16[256,128]{1,0:T(8,128)(2,1)}, bf16[256,128]{1,0:T(8,128)(2,1)}) custom-call(s32[1]{0:T(128)} %bitcast.8.place, bf16[128,2560]{1,0:T(8,128)(2,1)} %bitcast.34, bf16[128,2560]{1,0:T(8,128)(2,1)} %bitcast.30, f32[2560]{0:T(1024)} %gain.3, s32[2,128]{1,0:T(2,128)} %bitcast.45, ...), custom_call_target="tpu_custom_call" | custom-call | flops 335544320 | bytes 3145728 | tf_op jit(solution)/shard_map/pallas_call | solution.py:362
  4.0 9.7 %all-to-all-start = ((bf16[32,8,1280]{2,1,0:T(8,128)(2,1)}), bf16[32,8,1280]{2,1,0:T(8,128)(2,1)S(1)}, u32[]{:S(2)}, u32[]{:S(2)}) async-start(bf16[32,8,1280]{2,1,0:T(8,128)(2,1)} %bitcast.44), calls=%async_computation | async-start | bytes 1310720 | tf_op jit(solution)/shard_map/all_to_all | solution.py:370
  13.7 2.0 %copy.12 = bf16[1,256,2,2560]{3,1,2,0:T(8,128)(2,1)S(1)} copy(bf16[1,256,2,2560]{3,2,1,0:T(2,128)(2,1)} %param.15) | data formatting | bytes 5242880 | tf_op jit(solution)/shard_map/optimization_barrier | solution.py:374
  15.7 1.7 %slice_bitcast_fusion = (bf16[256,2560]{1,0:T(8,128)(2,1)}, bf16[256,2560]{1,0:T(8,128)(2,1)}) fusion(bf16[1,256,2,2560]{3,1,2,0:T(8,128)(2,1)S(1)} %copy.12), kind=kLoop, calls=%fused_computation | loop fusion | bytes 5242880 | tf_op jit(solution)/shard_map/squeeze | solution.py:375
  17.4 0.6 copy-done.4
  18.3 1.1 shard_map.112
  19.4 1.1 copy-done.5
  20.5 1.1 copy-done.6
  21.6 3.0 %collective-permute-start.2 = (f32[72,128]{1,0:T(8,128)S(1)}, f32[72,128]{1,0:T(8,128)S(1)}, u32[]{:S(2)}, u32[]{:S(2)}) collective-permute-start(f32[72,128]{1,0:T(8,128)S(1)} %get-tuple-element.53.local), channel_id=1, source_target_pairs={{0,192},{64,0},{128,64},{192,128},{1,193},{65,1},{129,65},{193,129... | collective-permute-start | bytes 110600 | tf_op jit(solution)/shard_map/ppermute | solution.py:353
  24.6 0.6 collective-permute-start.1
  25.2 1.0 collective-permute-start
  26.4 3.6 %collective-permute-done.1 = f32[72,128]{1,0:T(8,128)S(1)} collective-permute-done((f32[72,128]{1,0:T(8,128)S(1)}, f32[72,128]{1,0:T(8,128)S(1)}, u32[]{:S(2)}, u32[]{:S(2)}) %collective-permute-start.1) | collective-permute-done | bytes 36896 | tf_op jit(solution)/shard_map/ppermute | solution.py:353
  30.5 2.8 %collective-permute-start.3 = (f32[72,128]{1,0:T(8,128)S(1)}, f32[72,128]{1,0:T(8,128)S(1)}, u32[]{:S(2)}, u32[]{:S(2)}) collective-permute-start(f32[72,128]{1,0:T(8,128)S(1)} %pad_maximum_fusion.near), channel_id=1, source_target_pairs={{0,32},{32,0},{1,33},{33,1},{2,34},{34,2},{3,35},{35,3},{4,36},{36... | collective-permute-start | bytes 110600 | tf_op jit(solution)/shard_map/ppermute | solution.py:353
  33.3 2.7 %collective-permute-done.3.far = f32[72,128]{1,0:T(8,128)S(1)} collective-permute-done((f32[72,128]{1,0:T(8,128)S(1)}, f32[72,128]{1,0:T(8,128)S(1)}, u32[]{:S(2)}, u32[]{:S(2)}) %collective-permute-start.3) | collective-permute-done | bytes 36896 | tf_op jit(solution)/shard_map/ppermute | solution.py:353
  36.1 2.8 %collective-permute-start.4 = (bf16[256,1280]{1,0:T(8,128)(2,1)S(1)}, bf16[256,1280]{1,0:T(8,128)(2,1)S(1)}, u32[]{:S(2)}, u32[]{:S(2)}) collective-permute-start(bf16[256,1280]{1,0:T(8,128)(2,1)S(1)} %bitcast.40), channel_id=1, source_target_pairs={{0,32},{32,0},{1,33},{33,1},{2,34},{34,2},{3,35},{35,3},{4,36},{36... | collective-permute-start | bytes 1966088 | tf_op jit(solution)/shard_map/ppermute | solution.py:353
  38.9 1.2 collective-permute-start.8
  40.1 0.9 collective-permute-start.7
  41.1 4.3 %shard_map.113 = (bf16[128,2560]{1,0:T(8,128)(2,1)}, bf16[128,2560]{1,0:T(8,128)(2,1)}, bf16[4,64,640]{2,1,0:T(8,128)(2,1)}, bf16[4,64,640]{2,1,0:T(8,128)(2,1)}) custom-call(s32[1]{0:T(128)} %bitcast.8.place, bf16[128,2560]{1,0:T(8,128)(2,1)} %get-tuple-element.50.normed, bf16[128,2560]{1,0:T(8,128)(2,1)} %bitcast.31, bf16[128,2560]{1,0:T(8,128)(2,1)} %bitcast.36, ...), custom_call_target="tpu_custom_call" | custom-call | flops 251658240 | bytes 6291456 | tf_op jit(solution)/shard_map/pallas_call | solution.py:392
  45.4 1.1 collective-permute-done.8.refs_4_
  46.5 5.5 %collective-permute-done.7.refs_1_ = bf16[128,1280]{1,0:T(8,128)(2,1)S(1)} collective-permute-done((bf16[128,1280]{1,0:T(8,128)(2,1)S(1)}, bf16[128,1280]{1,0:T(8,128)(2,1)S(1)}, u32[]{:S(2)}, u32[]{:S(2)}) %collective-permute-start.7) | collective-permute-done | bytes 327712 | tf_op jit(solution)/shard_map/ppermute | solution.py:353
  52.0 3.2 %collective-permute-start.10 = (bf16[128,1280]{1,0:T(8,128)(2,1)S(1)}, bf16[128,1280]{1,0:T(8,128)(2,1)}, u32[]{:S(2)}, u32[]{:S(2)}) collective-permute-start(bf16[128,1280]{1,0:T(8,128)(2,1)S(1)} %collective-permute-done.8.refs_4_), channel_id=1, source_target_pairs={{0,192},{64,0},{128,64},{192,128},{1,193},{65,1},{129,65},{193,129... | collective-permute-start | bytes 983048 | tf_op jit(solution)/shard_map/ppermute | solution.py:353
  55.5 3.5 %collective-permute-done.13.refs_2_ = bf16[128,1280]{1,0:T(8,128)(2,1)S(1)} collective-permute-done((bf16[128,1280]{1,0:T(8,128)(2,1)S(1)}, bf16[128,1280]{1,0:T(8,128)(2,1)S(1)}, u32[]{:S(2)}, u32[]{:S(2)}) %collective-permute-start.13) | collective-permute-done | bytes 327712 | tf_op jit(solution)/shard_map/ppermute | solution.py:353
  59.0 7.1 %collective-permute-done.9.refs_2_ = bf16[128,1280]{1,0:T(8,128)(2,1)} collective-permute-done((bf16[128,1280]{1,0:T(8,128)(2,1)S(1)}, bf16[128,1280]{1,0:T(8,128)(2,1)}, u32[]{:S(2)}, u32[]{:S(2)}) %collective-permute-start.9) | collective-permute-done | bytes 327712 | tf_op jit(solution)/shard_map/ppermute | solution.py:353
  66.1 0.8 collective-permute-start.11
  66.9 2.7 %collective-permute-start.12 = (bf16[128,1280]{1,0:T(8,128)(2,1)}, bf16[128,1280]{1,0:T(8,128)(2,1)}, u32[]{:S(2)}, u32[]{:S(2)}) collective-permute-start(bf16[128,1280]{1,0:T(8,128)(2,1)} %collective-permute-done.10.refs_3_), channel_id=1, source_target_pairs={{0,32},{32,0},{1,33},{33,1},{2,34},{34,2},{3,35},{35,3},{4,36},{36... | collective-permute-start | bytes 983048 | tf_op jit(solution)/shard_map/ppermute | solution.py:353
  69.7 0.7 collective-permute-done.14.refs_3_
  70.4 0.7 copy-done.20
  71.1 5.7 %shard_map.114 = (bf16[8,128,640]{2,1,0:T(8,128)(2,1)}, bf16[256,2560]{1,0:T(8,128)(2,1)}, bf16[256,2560]{1,0:T(8,128)(2,1)}, bf16[256,256]{1,0:T(8,128)(2,1)}, bf16[256,256]{1,0:T(8,128)(2,1)}) custom-call(bf16[256,1280]{1,0:T(8,128)(2,1)} %bitcast.42, bf16[128,1280]{1,0:T(8,128)(2,1)} %copy-done.18, bf16[128,1280]{1,0:T(8,128)(2,1)} %copy-done.19, ...), custom_call_target="tpu_custom_call" | custom-call | flops 1006632960 | bytes 8388608 | tf_op jit(solution)/shard_map/pallas_call | solution.py:408
  76.9 0.8 collective-permute-start.15
  77.7 0.7 stack.35.at_ref
  78.4 4.7 %collective-permute-done.12.refs_5_ = bf16[128,1280]{1,0:T(8,128)(2,1)} collective-permute-done((bf16[128,1280]{1,0:T(8,128)(2,1)}, bf16[128,1280]{1,0:T(8,128)(2,1)}, u32[]{:S(2)}, u32[]{:S(2)}) %collective-permute-start.12) | collective-permute-done | bytes 327712 | tf_op jit(solution)/shard_map/ppermute | solution.py:353
  83.0 0.8 copy-done.15
  83.9 0.8 copy-done.16
  84.7 6.2 %shard_map.115 = (bf16[8,256,640]{2,1,0:T(8,128)(2,1)}, bf16[256,2560]{1,0:T(8,128)(2,1)}, bf16[256,2560]{1,0:T(8,128)(2,1)}, bf16[256,256]{1,0:T(8,128)(2,1)}, bf16[256,256]{1,0:T(8,128)(2,1)}) custom-call(s32[8]{0:T(128)} %stack.35.at_ref, bf16[256,1280]{1,0:T(8,128)(2,1)} %copy-done.16, bf16[256,1280]{1,0:T(8,128)(2,1)} %copy-done.15, ...), custom_call_target="tpu_custom_call" | custom-call | flops 1006632960 | bytes 12582912 | tf_op jit(solution)/shard_map/pallas_call | solution.py:418
  91.0 3.6 %all-to-all-start.1 = ((bf16[8,256,640]{2,1,0:T(8,128)(2,1)}), bf16[8,256,640]{2,1,0:T(8,128)(2,1)S(1)}, u32[]{:S(2)}, u32[]{:S(2)}) async-start(bf16[8,256,640]{2,1,0:T(8,128)(2,1)} %get-tuple-element.69), calls=%async_computation.1 | async-start | bytes 5242880 | tf_op jit(solution)/shard_map/all_to_all | solution.py:436
  94.6 7.3 %shard_map.116 = bf16[512,2560]{1,0:T(8,128)(2,1)} custom-call(bf16[256,2560]{1,0:T(8,128)(2,1)} %get-tuple-element.70.refs_0_, bf16[256,2560]{1,0:T(8,128)(2,1)} %get-tuple-element.71.refs_1_, bf16[256,256]{1,0:T(8,128)(2,1)} %get-tuple-element.72.refs_2_, bf16[256,256]{1,0:T(8,128)(2,1)} %get-tuple-element.73.refs_3_, ...), custom_call_target="tpu_custom_call" | custom-call | flops 1342177280 | bytes 8388608 | tf_op jit(solution)/shard_map/pallas_call | solution.py:437
  101.9 6.4 %reshape.29 = bf16[1,256,2,2560]{3,2,1,0:T(2,128)(2,1)} reshape(bf16[512,2560]{1,0:T(8,128)(2,1)} %shard_map.116) | data formatting | bytes 5242880 | tf_op jit(solution)/shard_map/reshape | solution.py:446
  108.4 12.0 %all-to-all-done.1.parts = bf16[8,256,640]{2,1,0:T(8,128)(2,1)S(1)} async-done(((bf16[8,256,640]{2,1,0:T(8,128)(2,1)}), bf16[8,256,640]{2,1,0:T(8,128)(2,1)S(1)}, u32[]{:S(2)}, u32[]{:S(2)}) %all-to-all-start.1) | async-done | bytes 2621472 | tf_op jit(solution)/shard_map/all_to_all | solution.py:436
  120.4 1.3 shard_map.117
  121.7 4.9 %all-to-all-start.2 = ((bf16[32,8,640]{2,1,0:T(8,128)(2,1)}), bf16[32,8,640]{2,1,0:T(8,128)(2,1)S(1)}, u32[]{:S(2)}, u32[]{:S(2)}) async-start(bf16[32,8,640]{2,1,0:T(8,128)(2,1)} %bitcast.21), calls=%async_computation.2 | async-start | bytes 655360 | tf_op jit(solution)/shard_map/all_to_all | solution.py:450
  126.7 0.4 collective-permute-start.16
  127.1 2.7 %collective-permute-start.17 = (bf16[64,640]{1,0:T(8,128)(2,1)S(1)}, bf16[64,640]{1,0:T(8,128)(2,1)S(1)}, u32[]{:S(2)}, u32[]{:S(2)}) collective-permute-start(bf16[64,640]{1,0:T(8,128)(2,1)S(1)} %get-tuple-element.87), channel_id=1, source_target_pairs={{0,128},{64,192},{128,0},{192,64},{1,129},{65,193},{129,1},{193,65... | collective-permute-start | bytes 245768 | tf_op jit(solution)/shard_map/ppermute | solution.py:353
  129.8 0.4 collective-permute-start.18
  130.2 4.0 %collective-permute-done.16.below = bf16[64,640]{1,0:T(8,128)(2,1)S(1)} collective-permute-done((bf16[64,640]{1,0:T(8,128)(2,1)S(1)}, bf16[64,640]{1,0:T(8,128)(2,1)S(1)}, u32[]{:S(2)}, u32[]{:S(2)}) %collective-permute-start.16) | collective-permute-done | bytes 81952 | tf_op jit(solution)/shard_map/ppermute | solution.py:353
  134.2 0.6 collective-permute-done.18.above
  134.8 5.3 %all-to-all-done.2 = bf16[32,8,640]{2,1,0:T(8,128)(2,1)S(1)} async-done(((bf16[32,8,640]{2,1,0:T(8,128)(2,1)}), bf16[32,8,640]{2,1,0:T(8,128)(2,1)S(1)}, u32[]{:S(2)}, u32[]{:S(2)}) %all-to-all-start.2) | async-done | bytes 327712 | tf_op jit(solution)/shard_map/all_to_all | solution.py:450
  140.6 15.3 %all_to_all.20.packs = bf16[8,64,640]{2,1,0:T(8,128)(2,1)S(1)} all-to-all(bf16[8,64,640]{2,1,0:T(8,128)(2,1)S(1)} %shard_map.119), channel_id=1, replica_groups=mesh['ctx_0'=4,'ctx_1'=2,'exp'=32] {'ctx_0','ctx_1'}, dimensions={0} | all-to-all | bytes 1310720 | tf_op jit(solution)/shard_map/all_to_all | solution.py:458
  155.9 1.5 shard_map.120
  (61 shorter events, 1.9 us)
Async XLA Ops:
  4.0 32.1 %all-to-all-start = ((bf16[32,8,1280]{2,1,0:T(8,128)(2,1)}), bf16[32,8,1280]{2,1,0:T(8,128)(2,1)S(1)}, u32[]{:S(2)}, u32[]{:S(2)}) async-start(bf16[32,8,1280]{2,1,0:T(8,128)(2,1)} %bitcast.44), calls=%async_computation | async-start | bytes 1310720 | tf_op jit(solution)/shard_map/all_to_all | solution.py:370
  15.7 1.7 %copy-start = (bf16[1,128,2560]{2,1,0:T(8,128)(2,1)S(1)}, bf16[1,128,2560]{2,1,0:T(8,128)(2,1)}, u32[]{:S(2)}) copy-start(bf16[1,128,2560]{2,1,0:T(8,128)(2,1)} %param.9) | copy-start | bytes 1966084
  15.7 1.7 %copy-start.3 = (bf16[1,128,2560]{2,1,0:T(8,128)(2,1)S(1)}, bf16[1,128,2560]{2,1,0:T(8,128)(2,1)}, u32[]{:S(2)}) copy-start(bf16[1,128,2560]{2,1,0:T(8,128)(2,1)} %param.10) | copy-start | bytes 1966084
  15.7 2.4 %copy-start.4 = (bf16[128,2560]{1,0:T(8,128)(2,1)S(1)}, bf16[128,2560]{1,0:T(8,128)(2,1)}, u32[]{:S(2)}) copy-start(bf16[128,2560]{1,0:T(8,128)(2,1)} %get-tuple-element.50.normed) | copy-start | bytes 1966084
  15.7 2.6 %copy-start.7 = (bf16[1,128,2560]{2,1,0:T(8,128)(2,1)S(1)}, bf16[1,128,2560]{2,1,0:T(8,128)(2,1)}, u32[]{:S(2)}) copy-start(bf16[1,128,2560]{2,1,0:T(8,128)(2,1)} %param.11) | copy-start | bytes 1966084
  19.4 1.1 copy-start.5
  20.5 1.1 copy-start.6
  21.6 19.5 %copy-start.9 = (f32[72,128]{1,0:T(8,128)}, f32[72,128]{1,0:T(8,128)S(1)}, u32[]{:S(2)}) copy-start(f32[72,128]{1,0:T(8,128)S(1)} %get-tuple-element.53.local) | copy-start | bytes 110596
  21.6 4.9 %collective-permute-start.2 = (f32[72,128]{1,0:T(8,128)S(1)}, f32[72,128]{1,0:T(8,128)S(1)}, u32[]{:S(2)}, u32[]{:S(2)}) collective-permute-start(f32[72,128]{1,0:T(8,128)S(1)} %get-tuple-element.53.local), channel_id=1, source_target_pairs={{0,192},{64,0},{128,64},{192,128},{1,193},{65,1},{129,65},{193,129... | collective-permute-start | bytes 110600 | tf_op jit(solution)/shard_map/ppermute | solution.py:353
  24.6 5.5 %collective-permute-start.1 = (f32[72,128]{1,0:T(8,128)S(1)}, f32[72,128]{1,0:T(8,128)S(1)}, u32[]{:S(2)}, u32[]{:S(2)}) collective-permute-start(f32[72,128]{1,0:T(8,128)S(1)} %get-tuple-element.53.local), channel_id=1, source_target_pairs={{0,128},{64,192},{128,0},{192,64},{1,129},{65,193},{129,1},{193,65... | collective-permute-start | bytes 110600 | tf_op jit(solution)/shard_map/ppermute | solution.py:353
  25.2 5.2 %collective-permute-start = (f32[72,128]{1,0:T(8,128)S(1)}, f32[72,128]{1,0:T(8,128)S(1)}, u32[]{:S(2)}, u32[]{:S(2)}) collective-permute-start(f32[72,128]{1,0:T(8,128)S(1)} %get-tuple-element.53.local), channel_id=1, source_target_pairs={{0,64},{64,128},{128,192},{192,0},{1,65},{65,129},{129,193},{193,1... | collective-permute-start | bytes 110600 | tf_op jit(solution)/shard_map/ppermute | solution.py:353
  30.5 10.6 %copy-start.21 = (f32[72,128]{1,0:T(8,128)}, f32[72,128]{1,0:T(8,128)S(1)}, u32[]{:S(2)}) copy-start(f32[72,128]{1,0:T(8,128)S(1)} %pad_maximum_fusion.near) | copy-start | bytes 110596
  30.5 5.5 %collective-permute-start.3 = (f32[72,128]{1,0:T(8,128)S(1)}, f32[72,128]{1,0:T(8,128)S(1)}, u32[]{:S(2)}, u32[]{:S(2)}) collective-permute-start(f32[72,128]{1,0:T(8,128)S(1)} %pad_maximum_fusion.near), channel_id=1, source_target_pairs={{0,32},{32,0},{1,33},{33,1},{2,34},{34,2},{3,35},{35,3},{4,36},{36... | collective-permute-start | bytes 110600 | tf_op jit(solution)/shard_map/ppermute | solution.py:353
  36.1 5.0 %copy-start.22 = (f32[72,128]{1,0:T(8,128)}, f32[72,128]{1,0:T(8,128)S(1)}, u32[]{:S(2)}) copy-start(f32[72,128]{1,0:T(8,128)S(1)} %collective-permute-done.3.far) | copy-start | bytes 110596
  36.1 9.4 %copy-start.13 = (bf16[32,8,1280]{2,1,0:T(8,128)(2,1)}, bf16[32,8,1280]{2,1,0:T(8,128)(2,1)S(1)}, u32[]{:S(2)}) copy-start(bf16[32,8,1280]{2,1,0:T(8,128)(2,1)S(1)} %all-to-all-done) | copy-start | bytes 1966084
  36.1 19.2 %collective-permute-start.4 = (bf16[256,1280]{1,0:T(8,128)(2,1)S(1)}, bf16[256,1280]{1,0:T(8,128)(2,1)S(1)}, u32[]{:S(2)}, u32[]{:S(2)}) collective-permute-start(bf16[256,1280]{1,0:T(8,128)(2,1)S(1)} %bitcast.40), channel_id=1, source_target_pairs={{0,32},{32,0},{1,33},{33,1},{2,34},{34,2},{3,35},{35,3},{4,36},{36... | collective-permute-start | bytes 1966088 | tf_op jit(solution)/shard_map/ppermute | solution.py:353
  38.9 7.6 %collective-permute-start.8 = (bf16[128,1280]{1,0:T(8,128)(2,1)S(1)}, bf16[128,1280]{1,0:T(8,128)(2,1)S(1)}, u32[]{:S(2)}, u32[]{:S(2)}) collective-permute-start(bf16[128,1280]{1,0:T(8,128)(2,1)S(1)} %get-tuple-element.96), channel_id=1, source_target_pairs={{0,192},{64,0},{128,64},{192,128},{1,193},{65,1},{129,65},{193,129... | collective-permute-start | bytes 983048 | tf_op jit(solution)/shard_map/ppermute | solution.py:353
  40.1 11.9 %collective-permute-start.7 = (bf16[128,1280]{1,0:T(8,128)(2,1)S(1)}, bf16[128,1280]{1,0:T(8,128)(2,1)S(1)}, u32[]{:S(2)}, u32[]{:S(2)}) collective-permute-start(bf16[128,1280]{1,0:T(8,128)(2,1)S(1)} %get-tuple-element.97), channel_id=1, source_target_pairs={{0,64},{64,128},{128,192},{192,0},{1,65},{65,129},{129,193},{193,1... | collective-permute-start | bytes 983048 | tf_op jit(solution)/shard_map/ppermute | solution.py:353
  41.0 17.9 %collective-permute-start.13 = (bf16[128,1280]{1,0:T(8,128)(2,1)S(1)}, bf16[128,1280]{1,0:T(8,128)(2,1)S(1)}, u32[]{:S(2)}, u32[]{:S(2)}) collective-permute-start(bf16[128,1280]{1,0:T(8,128)(2,1)S(1)} %get-tuple-element.96), channel_id=1, source_target_pairs={{0,64},{64,128},{128,192},{192,0},{1,65},{65,129},{129,193},{193,1... | collective-permute-start | bytes 983048 | tf_op jit(solution)/shard_map/ppermute | solution.py:353
  46.5 23.9 %copy-start.17 = (bf16[128,1280]{1,0:T(8,128)(2,1)}, bf16[128,1280]{1,0:T(8,128)(2,1)S(1)}, u32[]{:S(2)}) copy-start(bf16[128,1280]{1,0:T(8,128)(2,1)S(1)} %collective-permute-done.8.refs_4_) | copy-start | bytes 983044
  52.0 18.4 %copy-start.18 = (bf16[128,1280]{1,0:T(8,128)(2,1)}, bf16[128,1280]{1,0:T(8,128)(2,1)S(1)}, u32[]{:S(2)}) copy-start(bf16[128,1280]{1,0:T(8,128)(2,1)S(1)} %collective-permute-done.7.refs_1_) | copy-start | bytes 983044
  52.0 14.1 %collective-permute-start.9 = (bf16[128,1280]{1,0:T(8,128)(2,1)S(1)}, bf16[128,1280]{1,0:T(8,128)(2,1)}, u32[]{:S(2)}, u32[]{:S(2)}) collective-permute-start(bf16[128,1280]{1,0:T(8,128)(2,1)S(1)} %collective-permute-done.7.refs_1_), channel_id=1, source_target_pairs={{0,64},{64,128},{128,192},{192,0},{1,65},{65,129},{129,193},{193,1... | collective-permute-start | bytes 983048 | tf_op jit(solution)/shard_map/ppermute | solution.py:353
  52.0 14.9 %collective-permute-start.10 = (bf16[128,1280]{1,0:T(8,128)(2,1)S(1)}, bf16[128,1280]{1,0:T(8,128)(2,1)}, u32[]{:S(2)}, u32[]{:S(2)}) collective-permute-start(bf16[128,1280]{1,0:T(8,128)(2,1)S(1)} %collective-permute-done.8.refs_4_), channel_id=1, source_target_pairs={{0,192},{64,0},{128,64},{192,128},{1,193},{65,1},{129,65},{193,129... | collective-permute-start | bytes 983048 | tf_op jit(solution)/shard_map/ppermute | solution.py:353
  55.2 15.2 %collective-permute-start.14 = (bf16[128,1280]{1,0:T(8,128)(2,1)S(1)}, bf16[128,1280]{1,0:T(8,128)(2,1)S(1)}, u32[]{:S(2)}, u32[]{:S(2)}) collective-permute-start(bf16[128,1280]{1,0:T(8,128)(2,1)S(1)} %get-tuple-element.97), channel_id=1, source_target_pairs={{0,192},{64,0},{128,64},{192,128},{1,193},{65,1},{129,65},{193,129... | collective-permute-start | bytes 983048 | tf_op jit(solution)/shard_map/ppermute | solution.py:353
  55.2 15.2 %copy-start.14 = (bf16[256,1280]{1,0:T(8,128)(2,1)}, bf16[256,1280]{1,0:T(8,128)(2,1)S(1)}, u32[]{:S(2)}) copy-start(bf16[256,1280]{1,0:T(8,128)(2,1)S(1)} %collective-permute-done.4.refs_5_) | copy-start | bytes 1966084
  55.3 27.8 %collective-permute-start.6 = (bf16[256,1280]{1,0:T(8,128)(2,1)S(1)}, bf16[256,1280]{1,0:T(8,128)(2,1)S(1)}, u32[]{:S(2)}, u32[]{:S(2)}) collective-permute-start(bf16[256,1280]{1,0:T(8,128)(2,1)S(1)} %collective-permute-done.4.refs_5_), channel_id=1, source_target_pairs={{0,192},{64,0},{128,64},{192,128},{1,193},{65,1},{129,65},{193,129... | collective-permute-start | bytes 1966088 | tf_op jit(solution)/shard_map/ppermute | solution.py:353
  59.0 11.4 %copy-start.19 = (bf16[128,1280]{1,0:T(8,128)(2,1)}, bf16[128,1280]{1,0:T(8,128)(2,1)S(1)}, u32[]{:S(2)}) copy-start(bf16[128,1280]{1,0:T(8,128)(2,1)S(1)} %collective-permute-done.13.refs_2_) | copy-start | bytes 983044
  59.0 24.0 %collective-permute-start.5 = (bf16[256,1280]{1,0:T(8,128)(2,1)S(1)}, bf16[256,1280]{1,0:T(8,128)(2,1)S(1)}, u32[]{:S(2)}, u32[]{:S(2)}) collective-permute-start(bf16[256,1280]{1,0:T(8,128)(2,1)S(1)} %collective-permute-done.4.refs_5_), channel_id=1, source_target_pairs={{0,64},{64,128},{128,192},{192,0},{1,65},{65,129},{129,193},{193,1... | collective-permute-start | bytes 1966088 | tf_op jit(solution)/shard_map/ppermute | solution.py:353
  66.1 12.2 %collective-permute-start.11 = (bf16[128,1280]{1,0:T(8,128)(2,1)}, bf16[128,1280]{1,0:T(8,128)(2,1)}, u32[]{:S(2)}, u32[]{:S(2)}) collective-permute-start(bf16[128,1280]{1,0:T(8,128)(2,1)} %collective-permute-done.9.refs_2_), channel_id=1, source_target_pairs={{0,32},{32,0},{1,33},{33,1},{2,34},{34,2},{3,35},{35,3},{4,36},{36... | collective-permute-start | bytes 983048 | tf_op jit(solution)/shard_map/ppermute | solution.py:353
  66.9 16.1 %collective-permute-start.12 = (bf16[128,1280]{1,0:T(8,128)(2,1)}, bf16[128,1280]{1,0:T(8,128)(2,1)}, u32[]{:S(2)}, u32[]{:S(2)}) collective-permute-start(bf16[128,1280]{1,0:T(8,128)(2,1)} %collective-permute-done.10.refs_3_), channel_id=1, source_target_pairs={{0,32},{32,0},{1,33},{33,1},{2,34},{34,2},{3,35},{35,3},{4,36},{36... | collective-permute-start | bytes 983048 | tf_op jit(solution)/shard_map/ppermute | solution.py:353
  70.4 0.7 copy-start.20
  76.9 14.1 %collective-permute-start.15 = (bf16[4,64,640]{2,1,0:T(8,128)(2,1)}, bf16[4,64,640]{2,1,0:T(8,128)(2,1)S(1)}, u32[]{:S(2)}, u32[]{:S(2)}) collective-permute-start(bf16[4,64,640]{2,1,0:T(8,128)(2,1)} %get-tuple-element.68), channel_id=1, source_target_pairs={{0,32},{32,0},{1,33},{33,1},{2,34},{34,2},{3,35},{35,3},{4,36},{36... | collective-permute-start | bytes 983048 | tf_op jit(solution)/shard_map/ppermute | solution.py:353
  83.0 0.8 copy-start.15
  83.9 0.8 copy-start.16
  91.0 29.4 %all-to-all-start.1 = ((bf16[8,256,640]{2,1,0:T(8,128)(2,1)}), bf16[8,256,640]{2,1,0:T(8,128)(2,1)S(1)}, u32[]{:S(2)}, u32[]{:S(2)}) async-start(bf16[8,256,640]{2,1,0:T(8,128)(2,1)} %get-tuple-element.69), calls=%async_computation.1 | async-start | bytes 5242880 | tf_op jit(solution)/shard_map/all_to_all | solution.py:436
  108.4 18.2 %copy-start.8 = (bf16[4,64,640]{2,1,0:T(8,128)(2,1)S(1)}, bf16[4,64,640]{2,1,0:T(8,128)(2,1)}, u32[]{:S(2)}) copy-start(bf16[4,64,640]{2,1,0:T(8,128)(2,1)} %get-tuple-element.83.own) | copy-start | bytes 983044
  121.7 18.5 %copy-start.10 = (bf16[256,128]{1,0:T(8,128)(2,1)S(1)}, bf16[256,128]{1,0:T(8,128)(2,1)}, u32[]{:S(2)}) copy-start(bf16[256,128]{1,0:T(8,128)(2,1)} %get-tuple-element.81.even) | copy-start | bytes 196612
  121.7 18.5 %copy-start.11 = (bf16[256,128]{1,0:T(8,128)(2,1)S(1)}, bf16[256,128]{1,0:T(8,128)(2,1)}, u32[]{:S(2)}) copy-start(bf16[256,128]{1,0:T(8,128)(2,1)} %get-tuple-element.82.odd) | copy-start | bytes 196612
  121.7 18.5 %all-to-all-start.2 = ((bf16[32,8,640]{2,1,0:T(8,128)(2,1)}), bf16[32,8,640]{2,1,0:T(8,128)(2,1)S(1)}, u32[]{:S(2)}, u32[]{:S(2)}) async-start(bf16[32,8,640]{2,1,0:T(8,128)(2,1)} %bitcast.21), calls=%async_computation.2 | async-start | bytes 655360 | tf_op jit(solution)/shard_map/all_to_all | solution.py:450
  126.7 7.5 %collective-permute-start.16 = (bf16[64,640]{1,0:T(8,128)(2,1)S(1)}, bf16[64,640]{1,0:T(8,128)(2,1)S(1)}, u32[]{:S(2)}, u32[]{:S(2)}) collective-permute-start(bf16[64,640]{1,0:T(8,128)(2,1)S(1)} %get-tuple-element.86), channel_id=1, source_target_pairs={{0,64},{64,128},{128,192},{192,0},{1,65},{65,129},{129,193},{193,1... | collective-permute-start | bytes 245768 | tf_op jit(solution)/shard_map/ppermute | solution.py:353
  127.1 7.1 %collective-permute-start.17 = (bf16[64,640]{1,0:T(8,128)(2,1)S(1)}, bf16[64,640]{1,0:T(8,128)(2,1)S(1)}, u32[]{:S(2)}, u32[]{:S(2)}) collective-permute-start(bf16[64,640]{1,0:T(8,128)(2,1)S(1)} %get-tuple-element.87), channel_id=1, source_target_pairs={{0,128},{64,192},{128,0},{192,64},{1,129},{65,193},{129,1},{193,65... | collective-permute-start | bytes 245768 | tf_op jit(solution)/shard_map/ppermute | solution.py:353
  129.8 5.0 %collective-permute-start.18 = (bf16[64,640]{1,0:T(8,128)(2,1)S(1)}, bf16[64,640]{1,0:T(8,128)(2,1)S(1)}, u32[]{:S(2)}, u32[]{:S(2)}) collective-permute-start(bf16[64,640]{1,0:T(8,128)(2,1)S(1)} %get-tuple-element.88), channel_id=1, source_target_pairs={{0,192},{64,0},{128,64},{192,128},{1,193},{65,1},{129,65},{193,129... | collective-permute-start | bytes 245768 | tf_op jit(solution)/shard_map/ppermute | solution.py:353
  140.1 15.8 %copy-start.1 = (bf16[1,128,2560]{2,1,0:T(8,128)(2,1)S(1)}, bf16[1,128,2560]{2,1,0:T(8,128)(2,1)}, u32[]{:S(2)}) copy-start(bf16[1,128,2560]{2,1,0:T(8,128)(2,1)} %param.9) | copy-start | bytes 1966084
  140.1 15.8 %copy-start.2 = (bf16[1,128,2560]{2,1,0:T(8,128)(2,1)S(1)}, bf16[1,128,2560]{2,1,0:T(8,128)(2,1)}, u32[]{:S(2)}) copy-start(bf16[1,128,2560]{2,1,0:T(8,128)(2,1)} %param.8) | copy-start | bytes 1966084
  140.1 15.8 %copy-start.12 = (f32[2560]{0:T(1024)S(1)}, f32[2560]{0:T(1024)}, u32[]{:S(2)}) copy-start(f32[2560]{0:T(1024)} %gain.3) | copy-start | bytes 30724

commit v10 on v9

--- a/solution.py
+++ b/solution.py
@@ -27,6 +27,7 @@
 F32 = jnp.float32
 VMEM_LIMIT = 24 * 2**20
 VMEM_ALL = 60 * 2**20
+VMEM_MOST = 50 * 2**20
 
 VMEM = pl.BlockSpec(memory_space=pltpu.VMEM)
 SMEM = pl.BlockSpec(memory_space=pltpu.SMEM)
@@ -413,7 +414,7 @@
         moved=8 * 2**20,
         limit=VMEM_ALL,
     )(own, up, up_rest, down_rest, down, partner, w_in, w_out)
-    early_sums, far_pack = lax.optimization_barrier((early_sums, far_pack))
+    *partner_across, far_pack = lax.optimization_barrier((*partner_across, far_pack))
     far_query = moved_by(far_pack, "ctx_1", 1)
     sums, *late = call(
         late_kernel,
@@ -430,7 +431,7 @@
         flops=2 * 3 * SLOTS * UNITS * D,
         moved=12 * 2**20,
         places=[ANY] * 5,
-        limit=VMEM_ALL,
+        limit=VMEM_MOST,
     )(at, partner_up, partner_down, *across, *partner_across, w_in, w_out, early_sums)
     sums, far_query = lax.optimization_barrier((sums, far_query))
     parts = lax.all_to_all(sums, CTX, split_axis=0, concat_axis=0, tiled=True)

time: 158 us -> 168 us (1.063)
  waiting for transfers between devices: 51.5 us -> 58 us
  starting transfers between devices: 42 us -> 47.9 us
  local copies, waits for them, and re-layouts: 16.4 us -> 14.2 us
    all_to_all x1, waiting for transfers between devices: 12 us -> 16.2 us  [on_device(): parts = lax.all_to_all(sums, CTX, split_axis=0, concat_axis=0, tiled=True)]
    ppermute x19, starting transfers between devices: 23.8 us -> 27.8 us  [moved_by(): lax.ppermute(array, axis, [(k, (k + step) % count) for k in range(count)])]
    ppermute x19, waiting for transfers between devices: 34.2 us -> 36.5 us  [moved_by(): lax.ppermute(array, axis, [(k, (k + step) % count) for k in range(count)])]
    slice x1, local copies, waits for them, and re-layouts: 0.04 us -> 1.97 us  [on_device(): low, high = (own[:128], own[128:])]
    all_to_all x1, starting transfers between devices: 4.91 us -> 6.81 us  [on_device(): lax.all_to_all(back.reshape(EXPERTS, 8, CHUNK), 'exp', split_axis=0, conc...]
    optimization_barrier x1, local copies, waits for them, and re-layouts: 2 us -> 0.26 us  [on_device(): normed, expert_weights = lax.optimization_barrier((normed, expert_weights))]
    unnamed x46 -> x40, local copies, waits for them, and re-layouts: 5.53 us -> 3.81 us
  transfers between devices with their start and end apart: 22 -> 22, of which waited for: 14 -> 13; matrix products, arithmetic and copies ran while one was open for 7% -> 5% of each run, Pallas kernels for 16% -> 15%
where the time goes in v10:
time: 168 us
  waiting for transfers between devices  58 us (35%)
  starting transfers between devices  47.9 us (29%)
  Pallas kernels  31.8 us (19%)
  blocking collectives  14.9 us (9%)
  local copies, waits for them, and re-layouts  14.2 us (8%)
    ppermute x19, waiting for transfers between devices, moved_by(): lax.ppermute(array, axis, [(k, (k + step) % count) for k in range(count)])  36.5 us
    ppermute x19, starting transfers between devices, moved_by(): lax.ppermute(array, axis, [(k, (k + step) % count) for k in range(count)])  27.8 us
    all_to_all x1, waiting for transfers between devices, on_device(): parts = lax.all_to_all(sums, CTX, split_axis=0, concat_axis=0, tiled=True)  16.2 us
    all_to_all x1, blocking collectives, on_device(): packs = lax.all_to_all(total, CTX, split_axis=0, concat_axis=0, tiled=True)  14.9 us
    all_to_all x1, starting transfers between devices, on_device(): lax.all_to_all(send.reshape(EXPERTS, 8, HALF), 'exp', split_axis=0, conca...  9.7 us
    pallas_call x1, Pallas kernels, on_device(): call(weights_kernel, [ANY] * 8, [shape((2 * UNITS, D))], [pltpu.VMEM(k.sh...  7.35 us
    all_to_all x1, starting transfers between devices, on_device(): lax.all_to_all(back.reshape(EXPERTS, 8, CHUNK), 'exp', split_axis=0, conc...  6.81 us
    pallas_call x1, Pallas kernels, on_device(): call(late_kernel, [SMEM] + [ANY] * 9, [shape((CTX_COUNT, ROWS, CHUNK)), *...  6.48 us
  transfers between devices with their start and end apart: 22, of which 13 were waited for; matrix products, arithmetic and copies ran while one was open for 5% of the time, Pallas kernels for 15%

profile of v10, /device:TPU:32, one launch (start us, length us, event | category | flops | bytes accessed | tf_op | source)
XLA Modules:
  0.0 167.8 jit_solution(8155853352065682168)
XLA Ops:
  0.7 3.5 %shard_map.111 = (bf16[128,2560]{1,0:T(8,128)(2,1)}, bf16[256,1280]{1,0:T(8,128)(2,1)}, bf16[256,128]{1,0:T(8,128)(2,1)}, bf16[256,128]{1,0:T(8,128)(2,1)}) custom-call(s32[1]{0:T(128)} %bitcast.8.place, bf16[128,2560]{1,0:T(8,128)(2,1)} %bitcast.34, bf16[128,2560]{1,0:T(8,128)(2,1)} %bitcast.30, f32[2560]{0:T(1024)} %gain.3, s32[2,128]{1,0:T(2,128)} %bitcast.42, ...), custom_call_target="tpu_custom_call" | custom-call | flops 335544320 | bytes 3145728 | tf_op jit(solution)/shard_map/pallas_call | solution.py:363
  4.2 9.7 %all-to-all-start = ((bf16[32,8,1280]{2,1,0:T(8,128)(2,1)}), bf16[32,8,1280]{2,1,0:T(8,128)(2,1)}, u32[]{:S(2)}, u32[]{:S(2)}) async-start(bf16[32,8,1280]{2,1,0:T(8,128)(2,1)} %bitcast.41), calls=%async_computation | async-start | bytes 1310720 | tf_op jit(solution)/shard_map/all_to_all | solution.py:371
  13.9 0.3 copy.12
  14.2 1.7 slice_bitcast_fusion
  15.9 0.7 copy-done.4
  16.5 0.2 copy-done.7
  16.8 1.1 shard_map.112
  17.9 1.1 copy-done.5
  19.0 1.1 copy-done.6
  20.0 3.0 %collective-permute-start.2 = (f32[72,128]{1,0:T(8,128)S(1)}, f32[72,128]{1,0:T(8,128)S(1)}, u32[]{:S(2)}, u32[]{:S(2)}) collective-permute-start(f32[72,128]{1,0:T(8,128)S(1)} %get-tuple-element.54.local), channel_id=1, source_target_pairs={{0,192},{64,0},{128,64},{192,128},{1,193},{65,1},{129,65},{193,129... | collective-permute-start | bytes 110600 | tf_op jit(solution)/shard_map/ppermute | solution.py:354
  23.0 0.6 collective-permute-start.1
  23.7 1.0 collective-permute-start
  24.6 0.2 collective-permute-done.2
  24.9 3.6 %collective-permute-done.1 = f32[72,128]{1,0:T(8,128)S(1)} collective-permute-done((f32[72,128]{1,0:T(8,128)S(1)}, f32[72,128]{1,0:T(8,128)S(1)}, u32[]{:S(2)}, u32[]{:S(2)}) %collective-permute-start.1) | collective-permute-done | bytes 36896 | tf_op jit(solution)/shard_map/ppermute | solution.py:354
  28.5 0.4 collective-permute-done
  29.0 2.8 %collective-permute-start.3 = (f32[72,128]{1,0:T(8,128)S(1)}, f32[72,128]{1,0:T(8,128)S(1)}, u32[]{:S(2)}, u32[]{:S(2)}) collective-permute-start(f32[72,128]{1,0:T(8,128)S(1)} %pad_maximum_fusion.near), channel_id=1, source_target_pairs={{0,32},{32,0},{1,33},{33,1},{2,34},{34,2},{3,35},{35,3},{4,36},{36... | collective-permute-start | bytes 110600 | tf_op jit(solution)/shard_map/ppermute | solution.py:354
  31.8 2.7 %collective-permute-done.3.far = f32[72,128]{1,0:T(8,128)S(1)} collective-permute-done((f32[72,128]{1,0:T(8,128)S(1)}, f32[72,128]{1,0:T(8,128)S(1)}, u32[]{:S(2)}, u32[]{:S(2)}) %collective-permute-start.3) | collective-permute-done | bytes 36896 | tf_op jit(solution)/shard_map/ppermute | solution.py:354
  34.5 2.0 %fusion.6 = (bf16[128,1280]{1,0:T(8,128)(2,1)}, bf16[128,1280]{1,0:T(8,128)(2,1)}) fusion(bf16[256,1280]{1,0:T(8,128)(2,1)} %bitcast.16.refs_0_), kind=kLoop, calls=%fused_computation.20 | loop fusion | bytes 1310720 | tf_op jit(solution)/shard_map/slice | solution.py:389
  36.5 3.0 %collective-permute-start.8 = (bf16[128,1280]{1,0:T(8,128)(2,1)}, bf16[128,1280]{1,0:T(8,128)(2,1)S(1)}, u32[]{:S(2)}, u32[]{:S(2)}) collective-permute-start(bf16[128,1280]{1,0:T(8,128)(2,1)} %get-tuple-element.98), channel_id=1, source_target_pairs={{0,192},{64,0},{128,64},{192,128},{1,193},{65,1},{129,65},{193,129... | collective-permute-start | bytes 983048 | tf_op jit(solution)/shard_map/ppermute | solution.py:354
  39.5 2.7 %collective-permute-start.4 = (bf16[256,1280]{1,0:T(8,128)(2,1)}, bf16[256,1280]{1,0:T(8,128)(2,1)}, u32[]{:S(2)}, u32[]{:S(2)}) collective-permute-start(bf16[256,1280]{1,0:T(8,128)(2,1)} %bitcast.16.refs_0_), channel_id=1, source_target_pairs={{0,32},{32,0},{1,33},{33,1},{2,34},{34,2},{3,35},{35,3},{4,36},{36... | collective-permute-start | bytes 1966088 | tf_op jit(solution)/shard_map/ppermute | solution.py:354
  42.2 4.3 %shard_map.113 = (bf16[128,2560]{1,0:T(8,128)(2,1)}, bf16[128,2560]{1,0:T(8,128)(2,1)}, bf16[4,64,640]{2,1,0:T(8,128)(2,1)}, bf16[4,64,640]{2,1,0:T(8,128)(2,1)}) custom-call(s32[1]{0:T(128)} %bitcast.8.place, bf16[128,2560]{1,0:T(8,128)(2,1)} %get-tuple-element.51.normed, bf16[128,2560]{1,0:T(8,128)(2,1)} %bitcast.31, bf16[128,2560]{1,0:T(8,128)(2,1)} %bitcast.36, ...), custom_call_target="tpu_custom_call" | custom-call | flops 251658240 | bytes 6291456 | tf_op jit(solution)/shard_map/pallas_call | solution.py:393
  46.6 2.7 %collective-permute-done.7.refs_1_ = bf16[128,1280]{1,0:T(8,128)(2,1)S(1)} collective-permute-done((bf16[128,1280]{1,0:T(8,128)(2,1)}, bf16[128,1280]{1,0:T(8,128)(2,1)S(1)}, u32[]{:S(2)}, u32[]{:S(2)}) %collective-permute-start.7) | collective-permute-done | bytes 327712 | tf_op jit(solution)/shard_map/ppermute | solution.py:354
  49.2 3.2 %collective-permute-start.10 = (bf16[128,1280]{1,0:T(8,128)(2,1)S(1)}, bf16[128,1280]{1,0:T(8,128)(2,1)S(1)}, u32[]{:S(2)}, u32[]{:S(2)}) collective-permute-start(bf16[128,1280]{1,0:T(8,128)(2,1)S(1)} %collective-permute-done.8.refs_4_), channel_id=1, source_target_pairs={{0,192},{64,0},{128,64},{192,128},{1,193},{65,1},{129,65},{193,129... | collective-permute-start | bytes 983048 | tf_op jit(solution)/shard_map/ppermute | solution.py:354
  52.5 5.5 %collective-permute-done.9.refs_2_ = bf16[128,1280]{1,0:T(8,128)(2,1)S(1)} collective-permute-done((bf16[128,1280]{1,0:T(8,128)(2,1)S(1)}, bf16[128,1280]{1,0:T(8,128)(2,1)S(1)}, u32[]{:S(2)}, u32[]{:S(2)}) %collective-permute-start.9) | collective-permute-done | bytes 327712 | tf_op jit(solution)/shard_map/ppermute | solution.py:354
  58.0 2.6 %collective-permute-start.11 = (bf16[128,1280]{1,0:T(8,128)(2,1)S(1)}, bf16[128,1280]{1,0:T(8,128)(2,1)S(1)}, u32[]{:S(2)}, u32[]{:S(2)}) collective-permute-start(bf16[128,1280]{1,0:T(8,128)(2,1)S(1)} %collective-permute-done.9.refs_2_), channel_id=1, source_target_pairs={{0,32},{32,0},{1,33},{33,1},{2,34},{34,2},{3,35},{35,3},{4,36},{36... | collective-permute-start | bytes 983048 | tf_op jit(solution)/shard_map/ppermute | solution.py:354
  60.6 2.0 %collective-permute-start.5 = (bf16[256,1280]{1,0:T(8,128)(2,1)}, bf16[256,1280]{1,0:T(8,128)(2,1)S(1)}, u32[]{:S(2)}, u32[]{:S(2)}) collective-permute-start(bf16[256,1280]{1,0:T(8,128)(2,1)} %collective-permute-done.4.refs_5_), channel_id=1, source_target_pairs={{0,64},{64,128},{128,192},{192,0},{1,65},{65,129},{129,193},{193,1... | collective-permute-start | bytes 1966088 | tf_op jit(solution)/shard_map/ppermute | solution.py:354
  62.6 0.9 collective-permute-start.12
  63.6 6.3 %collective-permute-done.11.refs_4_ = bf16[128,1280]{1,0:T(8,128)(2,1)S(1)} collective-permute-done((bf16[128,1280]{1,0:T(8,128)(2,1)S(1)}, bf16[128,1280]{1,0:T(8,128)(2,1)S(1)}, u32[]{:S(2)}, u32[]{:S(2)}) %collective-permute-start.11) | collective-permute-done | bytes 327712 | tf_op jit(solution)/shard_map/ppermute | solution.py:354
  69.8 3.5 %collective-permute-done.12.refs_5_ = bf16[128,1280]{1,0:T(8,128)(2,1)S(1)} collective-permute-done((bf16[128,1280]{1,0:T(8,128)(2,1)S(1)}, bf16[128,1280]{1,0:T(8,128)(2,1)S(1)}, u32[]{:S(2)}, u32[]{:S(2)}) %collective-permute-start.12) | collective-permute-done | bytes 327712 | tf_op jit(solution)/shard_map/ppermute | solution.py:354
  73.3 2.3 %collective-permute-start.15 = (bf16[4,64,640]{2,1,0:T(8,128)(2,1)}, bf16[4,64,640]{2,1,0:T(8,128)(2,1)S(1)}, u32[]{:S(2)}, u32[]{:S(2)}) collective-permute-start(bf16[4,64,640]{2,1,0:T(8,128)(2,1)} %get-tuple-element.70), channel_id=1, source_target_pairs={{0,32},{32,0},{1,33},{33,1},{2,34},{34,2},{3,35},{35,3},{4,36},{36... | collective-permute-start | bytes 983048 | tf_op jit(solution)/shard_map/ppermute | solution.py:354
  75.7 6.9 %collective-permute-done.13.refs_2_ = bf16[128,1280]{1,0:T(8,128)(2,1)} collective-permute-done((bf16[128,1280]{1,0:T(8,128)(2,1)}, bf16[128,1280]{1,0:T(8,128)(2,1)}, u32[]{:S(2)}, u32[]{:S(2)}) %collective-permute-start.13) | collective-permute-done | bytes 327712 | tf_op jit(solution)/shard_map/ppermute | solution.py:354
  82.7 5.8 %shard_map.114 = (bf16[8,128,640]{2,1,0:T(8,128)(2,1)}, bf16[256,2560]{1,0:T(8,128)(2,1)}, bf16[256,2560]{1,0:T(8,128)(2,1)}, bf16[256,256]{1,0:T(8,128)(2,1)}, bf16[256,256]{1,0:T(8,128)(2,1)}) custom-call(bf16[256,1280]{1,0:T(8,128)(2,1)} %bitcast.16.refs_0_, bf16[128,1280]{1,0:T(8,128)(2,1)} %copy-done.17, ...), custom_call_target="tpu_custom_call" | custom-call | flops 1006632960 | bytes 8388608 | tf_op jit(solution)/shard_map/pallas_call | solution.py:409
  88.4 6.5 %shard_map.115 = (bf16[8,256,640]{2,1,0:T(8,128)(2,1)}, bf16[256,2560]{1,0:T(8,128)(2,1)}, bf16[256,2560]{1,0:T(8,128)(2,1)}, bf16[256,256]{1,0:T(8,128)(2,1)S(1)}, bf16[256,256]{1,0:T(8,128)(2,1)S(1)}) custom-call(s32[8]{0:T(128)S(1)} %stack.35.at_ref, bf16[256,1280]{1,0:T(8,128)(2,1)S(1)} %collective-permute-done.5.refs_0_, ...), custom_call_target="tpu_custom_call" | custom-call | flops 1006632960 | bytes 12582912 | tf_op jit(solution)/shard_map/pallas_call | solution.py:419
  95.0 0.6 copy-done.10
  95.6 3.6 %all-to-all-start.1 = ((bf16[8,256,640]{2,1,0:T(8,128)(2,1)}), bf16[8,256,640]{2,1,0:T(8,128)(2,1)S(1)}, u32[]{:S(2)}, u32[]{:S(2)}) async-start(bf16[8,256,640]{2,1,0:T(8,128)(2,1)} %get-tuple-element.71), calls=%async_computation.1 | async-start | bytes 5242880 | tf_op jit(solution)/shard_map/all_to_all | solution.py:437
  99.3 7.4 %shard_map.116 = bf16[512,2560]{1,0:T(8,128)(2,1)} custom-call(bf16[256,2560]{1,0:T(8,128)(2,1)} %get-tuple-element.72.refs_0_, bf16[256,2560]{1,0:T(8,128)(2,1)} %get-tuple-element.73.refs_1_, bf16[256,256]{1,0:T(8,128)(2,1)} %get-tuple-element.74.refs_2_, bf16[256,256]{1,0:T(8,128)(2,1)} %get-tuple-element.75.refs_3_, ...), custom_call_target="tpu_custom_call" | custom-call | flops 1342177280 | bytes 8388608 | tf_op jit(solution)/shard_map/pallas_call | solution.py:438
  106.6 6.4 %reshape.29 = bf16[1,256,2,2560]{3,2,1,0:T(2,128)(2,1)} reshape(bf16[512,2560]{1,0:T(8,128)(2,1)} %shard_map.116) | data formatting | bytes 5242880 | tf_op jit(solution)/shard_map/reshape | solution.py:447
  113.1 16.2 %all-to-all-done.1.parts = bf16[8,256,640]{2,1,0:T(8,128)(2,1)S(1)} async-done(((bf16[8,256,640]{2,1,0:T(8,128)(2,1)}), bf16[8,256,640]{2,1,0:T(8,128)(2,1)S(1)}, u32[]{:S(2)}, u32[]{:S(2)}) %all-to-all-start.1) | async-done | bytes 2621472 | tf_op jit(solution)/shard_map/all_to_all | solution.py:437
  129.3 1.3 shard_map.117
  130.6 6.8 %all-to-all-start.2 = ((bf16[32,8,640]{2,1,0:T(8,128)(2,1)}), bf16[32,8,640]{2,1,0:T(8,128)(2,1)S(1)}, u32[]{:S(2)}, u32[]{:S(2)}) async-start(bf16[32,8,640]{2,1,0:T(8,128)(2,1)} %bitcast.21), calls=%async_computation.2 | async-start | bytes 655360 | tf_op jit(solution)/shard_map/all_to_all | solution.py:451
  137.6 2.3 %collective-permute-start.17 = (bf16[64,640]{1,0:T(8,128)(2,1)S(1)}, bf16[64,640]{1,0:T(8,128)(2,1)S(1)}, u32[]{:S(2)}, u32[]{:S(2)}) collective-permute-start(bf16[64,640]{1,0:T(8,128)(2,1)S(1)} %get-tuple-element.89), channel_id=1, source_target_pairs={{0,128},{64,192},{128,0},{192,64},{1,129},{65,193},{129,1},{193,65... | collective-permute-start | bytes 245768 | tf_op jit(solution)/shard_map/ppermute | solution.py:354
  139.9 1.1 collective-permute-start.18
  141.0 4.0 %collective-permute-done.16.below = bf16[64,640]{1,0:T(8,128)(2,1)S(1)} collective-permute-done((bf16[64,640]{1,0:T(8,128)(2,1)S(1)}, bf16[64,640]{1,0:T(8,128)(2,1)S(1)}, u32[]{:S(2)}, u32[]{:S(2)}) %collective-permute-start.16) | collective-permute-done | bytes 81952 | tf_op jit(solution)/shard_map/ppermute | solution.py:354
  145.0 0.6 collective-permute-done.18.above
  145.6 5.3 %all-to-all-done.2 = bf16[32,8,640]{2,1,0:T(8,128)(2,1)S(1)} async-done(((bf16[32,8,640]{2,1,0:T(8,128)(2,1)}), bf16[32,8,640]{2,1,0:T(8,128)(2,1)S(1)}, u32[]{:S(2)}, u32[]{:S(2)}) %all-to-all-start.2) | async-done | bytes 327712 | tf_op jit(solution)/shard_map/all_to_all | solution.py:451
  151.0 0.4 shard_map.119
  151.4 14.9 %all_to_all.20.packs = bf16[8,64,640]{2,1,0:T(8,128)(2,1)S(1)} all-to-all(bf16[8,64,640]{2,1,0:T(8,128)(2,1)S(1)} %shard_map.119), channel_id=1, replica_groups=mesh['ctx_0'=4,'ctx_1'=2,'exp'=32] {'ctx_0','ctx_1'}, dimensions={0} | all-to-all | bytes 1310720 | tf_op jit(solution)/shard_map/all_to_all | solution.py:459
  166.3 1.5 shard_map.120
  (55 shorter events, 0.5 us)
Async XLA Ops:
  0.6 13.2 %copy-start.15 = (bf16[1,256,2,2560]{3,2,1,0:T(2,128)(2,1)S(1)}, bf16[1,256,2,2560]{3,2,1,0:T(2,128)(2,1)}, u32[]{:S(2)}) copy-start(bf16[1,256,2,2560]{3,2,1,0:T(2,128)(2,1)} %param.15) | copy-start | bytes 7864324
  4.2 30.4 %all-to-all-start = ((bf16[32,8,1280]{2,1,0:T(8,128)(2,1)}), bf16[32,8,1280]{2,1,0:T(8,128)(2,1)}, u32[]{:S(2)}, u32[]{:S(2)}) async-start(bf16[32,8,1280]{2,1,0:T(8,128)(2,1)} %bitcast.41), calls=%async_computation | async-start | bytes 1310720 | tf_op jit(solution)/shard_map/all_to_all | solution.py:371
  14.2 1.7 %copy-start = (bf16[1,128,2560]{2,1,0:T(8,128)(2,1)S(1)}, bf16[1,128,2560]{2,1,0:T(8,128)(2,1)}, u32[]{:S(2)}) copy-start(bf16[1,128,2560]{2,1,0:T(8,128)(2,1)} %param.9) | copy-start | bytes 1966084
  14.2 1.7 %copy-start.3 = (bf16[1,128,2560]{2,1,0:T(8,128)(2,1)S(1)}, bf16[1,128,2560]{2,1,0:T(8,128)(2,1)}, u32[]{:S(2)}) copy-start(bf16[1,128,2560]{2,1,0:T(8,128)(2,1)} %param.10) | copy-start | bytes 1966084
  14.2 2.4 %copy-start.4 = (bf16[128,2560]{1,0:T(8,128)(2,1)S(1)}, bf16[128,2560]{1,0:T(8,128)(2,1)}, u32[]{:S(2)}) copy-start(bf16[128,2560]{1,0:T(8,128)(2,1)} %get-tuple-element.51.normed) | copy-start | bytes 1966084
  14.2 2.6 %copy-start.7 = (bf16[1,128,2560]{2,1,0:T(8,128)(2,1)S(1)}, bf16[1,128,2560]{2,1,0:T(8,128)(2,1)}, u32[]{:S(2)}) copy-start(bf16[1,128,2560]{2,1,0:T(8,128)(2,1)} %param.11) | copy-start | bytes 1966084
  17.9 1.1 copy-start.5
  19.0 1.1 copy-start.6
  20.0 22.2 %copy-start.9 = (f32[72,128]{1,0:T(8,128)}, f32[72,128]{1,0:T(8,128)S(1)}, u32[]{:S(2)}) copy-start(f32[72,128]{1,0:T(8,128)S(1)} %get-tuple-element.54.local) | copy-start | bytes 110596
  20.0 4.9 %collective-permute-start.2 = (f32[72,128]{1,0:T(8,128)S(1)}, f32[72,128]{1,0:T(8,128)S(1)}, u32[]{:S(2)}, u32[]{:S(2)}) collective-permute-start(f32[72,128]{1,0:T(8,128)S(1)} %get-tuple-element.54.local), channel_id=1, source_target_pairs={{0,192},{64,0},{128,64},{192,128},{1,193},{65,1},{129,65},{193,129... | collective-permute-start | bytes 110600 | tf_op jit(solution)/shard_map/ppermute | solution.py:354
  23.0 5.5 %collective-permute-start.1 = (f32[72,128]{1,0:T(8,128)S(1)}, f32[72,128]{1,0:T(8,128)S(1)}, u32[]{:S(2)}, u32[]{:S(2)}) collective-permute-start(f32[72,128]{1,0:T(8,128)S(1)} %get-tuple-element.54.local), channel_id=1, source_target_pairs={{0,128},{64,192},{128,0},{192,64},{1,129},{65,193},{129,1},{193,65... | collective-permute-start | bytes 110600 | tf_op jit(solution)/shard_map/ppermute | solution.py:354
  23.7 5.2 %collective-permute-start = (f32[72,128]{1,0:T(8,128)S(1)}, f32[72,128]{1,0:T(8,128)S(1)}, u32[]{:S(2)}, u32[]{:S(2)}) collective-permute-start(f32[72,128]{1,0:T(8,128)S(1)} %get-tuple-element.54.local), channel_id=1, source_target_pairs={{0,64},{64,128},{128,192},{192,0},{1,65},{65,129},{129,193},{193,1... | collective-permute-start | bytes 110600 | tf_op jit(solution)/shard_map/ppermute | solution.py:354
  29.0 13.2 %copy-start.18 = (f32[72,128]{1,0:T(8,128)}, f32[72,128]{1,0:T(8,128)S(1)}, u32[]{:S(2)}) copy-start(f32[72,128]{1,0:T(8,128)S(1)} %pad_maximum_fusion.near) | copy-start | bytes 110596
  29.0 5.5 %collective-permute-start.3 = (f32[72,128]{1,0:T(8,128)S(1)}, f32[72,128]{1,0:T(8,128)S(1)}, u32[]{:S(2)}, u32[]{:S(2)}) collective-permute-start(f32[72,128]{1,0:T(8,128)S(1)} %pad_maximum_fusion.near), channel_id=1, source_target_pairs={{0,32},{32,0},{1,33},{33,1},{2,34},{34,2},{3,35},{35,3},{4,36},{36... | collective-permute-start | bytes 110600 | tf_op jit(solution)/shard_map/ppermute | solution.py:354
  34.5 7.7 %copy-start.19 = (f32[72,128]{1,0:T(8,128)}, f32[72,128]{1,0:T(8,128)S(1)}, u32[]{:S(2)}) copy-start(f32[72,128]{1,0:T(8,128)S(1)} %collective-permute-done.3.far) | copy-start | bytes 110596
  36.5 10.0 %collective-permute-start.8 = (bf16[128,1280]{1,0:T(8,128)(2,1)}, bf16[128,1280]{1,0:T(8,128)(2,1)S(1)}, u32[]{:S(2)}, u32[]{:S(2)}) collective-permute-start(bf16[128,1280]{1,0:T(8,128)(2,1)} %get-tuple-element.98), channel_id=1, source_target_pairs={{0,192},{64,0},{128,64},{192,128},{1,193},{65,1},{129,65},{193,129... | collective-permute-start | bytes 983048 | tf_op jit(solution)/shard_map/ppermute | solution.py:354
  39.5 9.8 %collective-permute-start.7 = (bf16[128,1280]{1,0:T(8,128)(2,1)}, bf16[128,1280]{1,0:T(8,128)(2,1)S(1)}, u32[]{:S(2)}, u32[]{:S(2)}) collective-permute-start(bf16[128,1280]{1,0:T(8,128)(2,1)} %get-tuple-element.99), channel_id=1, source_target_pairs={{0,64},{64,128},{128,192},{192,0},{1,65},{65,129},{129,193},{193,1... | collective-permute-start | bytes 983048 | tf_op jit(solution)/shard_map/ppermute | solution.py:354
  39.5 21.1 %collective-permute-start.4 = (bf16[256,1280]{1,0:T(8,128)(2,1)}, bf16[256,1280]{1,0:T(8,128)(2,1)}, u32[]{:S(2)}, u32[]{:S(2)}) collective-permute-start(bf16[256,1280]{1,0:T(8,128)(2,1)} %bitcast.16.refs_0_), channel_id=1, source_target_pairs={{0,32},{32,0},{1,33},{33,1},{2,34},{34,2},{3,35},{35,3},{4,36},{36... | collective-permute-start | bytes 1966088 | tf_op jit(solution)/shard_map/ppermute | solution.py:354
  46.6 26.8 %copy-start.16 = (bf16[128,1280]{1,0:T(8,128)(2,1)}, bf16[128,1280]{1,0:T(8,128)(2,1)S(1)}, u32[]{:S(2)}) copy-start(bf16[128,1280]{1,0:T(8,128)(2,1)S(1)} %collective-permute-done.8.refs_4_) | copy-start | bytes 983044
  49.2 11.4 %copy-start.17 = (bf16[128,1280]{1,0:T(8,128)(2,1)}, bf16[128,1280]{1,0:T(8,128)(2,1)S(1)}, u32[]{:S(2)}) copy-start(bf16[128,1280]{1,0:T(8,128)(2,1)S(1)} %collective-permute-done.7.refs_1_) | copy-start | bytes 983044
  49.2 8.7 %collective-permute-start.9 = (bf16[128,1280]{1,0:T(8,128)(2,1)S(1)}, bf16[128,1280]{1,0:T(8,128)(2,1)S(1)}, u32[]{:S(2)}, u32[]{:S(2)}) collective-permute-start(bf16[128,1280]{1,0:T(8,128)(2,1)S(1)} %collective-permute-done.7.refs_1_), channel_id=1, source_target_pairs={{0,64},{64,128},{128,192},{192,0},{1,65},{65,129},{129,193},{193,1... | collective-permute-start | bytes 983048 | tf_op jit(solution)/shard_map/ppermute | solution.py:354
  49.2 13.4 %collective-permute-start.10 = (bf16[128,1280]{1,0:T(8,128)(2,1)S(1)}, bf16[128,1280]{1,0:T(8,128)(2,1)S(1)}, u32[]{:S(2)}, u32[]{:S(2)}) collective-permute-start(bf16[128,1280]{1,0:T(8,128)(2,1)S(1)} %collective-permute-done.8.refs_4_), channel_id=1, source_target_pairs={{0,192},{64,0},{128,64},{192,128},{1,193},{65,1},{129,65},{193,129... | collective-permute-start | bytes 983048 | tf_op jit(solution)/shard_map/ppermute | solution.py:354
  58.0 11.8 %collective-permute-start.11 = (bf16[128,1280]{1,0:T(8,128)(2,1)S(1)}, bf16[128,1280]{1,0:T(8,128)(2,1)S(1)}, u32[]{:S(2)}, u32[]{:S(2)}) collective-permute-start(bf16[128,1280]{1,0:T(8,128)(2,1)S(1)} %collective-permute-done.9.refs_2_), channel_id=1, source_target_pairs={{0,32},{32,0},{1,33},{33,1},{2,34},{34,2},{3,35},{35,3},{4,36},{36... | collective-permute-start | bytes 983048 | tf_op jit(solution)/shard_map/ppermute | solution.py:354
  60.6 27.8 %collective-permute-start.6 = (bf16[256,1280]{1,0:T(8,128)(2,1)}, bf16[256,1280]{1,0:T(8,128)(2,1)S(1)}, u32[]{:S(2)}, u32[]{:S(2)}) collective-permute-start(bf16[256,1280]{1,0:T(8,128)(2,1)} %collective-permute-done.4.refs_5_), channel_id=1, source_target_pairs={{0,192},{64,0},{128,64},{192,128},{1,193},{65,1},{129,65},{193,129... | collective-permute-start | bytes 1966088 | tf_op jit(solution)/shard_map/ppermute | solution.py:354
  60.6 27.8 %collective-permute-start.5 = (bf16[256,1280]{1,0:T(8,128)(2,1)}, bf16[256,1280]{1,0:T(8,128)(2,1)S(1)}, u32[]{:S(2)}, u32[]{:S(2)}) collective-permute-start(bf16[256,1280]{1,0:T(8,128)(2,1)} %collective-permute-done.4.refs_5_), channel_id=1, source_target_pairs={{0,64},{64,128},{128,192},{192,0},{1,65},{65,129},{129,193},{193,1... | collective-permute-start | bytes 1966088 | tf_op jit(solution)/shard_map/ppermute | solution.py:354
  62.6 10.7 %collective-permute-start.12 = (bf16[128,1280]{1,0:T(8,128)(2,1)S(1)}, bf16[128,1280]{1,0:T(8,128)(2,1)S(1)}, u32[]{:S(2)}, u32[]{:S(2)}) collective-permute-start(bf16[128,1280]{1,0:T(8,128)(2,1)S(1)} %collective-permute-done.10.refs_3_), channel_id=1, source_target_pairs={{0,32},{32,0},{1,33},{33,1},{2,34},{34,2},{3,35},{35,3},{4,36},{36... | collective-permute-start | bytes 983048 | tf_op jit(solution)/shard_map/ppermute | solution.py:354
  63.5 19.1 %collective-permute-start.13 = (bf16[128,1280]{1,0:T(8,128)(2,1)}, bf16[128,1280]{1,0:T(8,128)(2,1)}, u32[]{:S(2)}, u32[]{:S(2)}) collective-permute-start(bf16[128,1280]{1,0:T(8,128)(2,1)} %get-tuple-element.98), channel_id=1, source_target_pairs={{0,64},{64,128},{128,192},{192,0},{1,65},{65,129},{129,193},{193,1... | collective-permute-start | bytes 983048 | tf_op jit(solution)/shard_map/ppermute | solution.py:354
  69.8 12.9 %collective-permute-start.14 = (bf16[128,1280]{1,0:T(8,128)(2,1)}, bf16[128,1280]{1,0:T(8,128)(2,1)}, u32[]{:S(2)}, u32[]{:S(2)}) collective-permute-start(bf16[128,1280]{1,0:T(8,128)(2,1)} %get-tuple-element.99), channel_id=1, source_target_pairs={{0,192},{64,0},{128,64},{192,128},{1,193},{65,1},{129,65},{193,129... | collective-permute-start | bytes 983048 | tf_op jit(solution)/shard_map/ppermute | solution.py:354
  73.3 21.6 %collective-permute-start.15 = (bf16[4,64,640]{2,1,0:T(8,128)(2,1)}, bf16[4,64,640]{2,1,0:T(8,128)(2,1)S(1)}, u32[]{:S(2)}, u32[]{:S(2)}) collective-permute-start(bf16[4,64,640]{2,1,0:T(8,128)(2,1)} %get-tuple-element.70), channel_id=1, source_target_pairs={{0,32},{32,0},{1,33},{33,1},{2,34},{34,2},{3,35},{35,3},{4,36},{36... | collective-permute-start | bytes 983048 | tf_op jit(solution)/shard_map/ppermute | solution.py:354
  94.9 0.7 copy-start.10
  95.0 0.7 copy-start.11
  95.6 33.6 %all-to-all-start.1 = ((bf16[8,256,640]{2,1,0:T(8,128)(2,1)}), bf16[8,256,640]{2,1,0:T(8,128)(2,1)S(1)}, u32[]{:S(2)}, u32[]{:S(2)}) async-start(bf16[8,256,640]{2,1,0:T(8,128)(2,1)} %get-tuple-element.71), calls=%async_computation.1 | async-start | bytes 5242880 | tf_op jit(solution)/shard_map/all_to_all | solution.py:437
  113.1 24.3 %copy-start.8 = (bf16[4,64,640]{2,1,0:T(8,128)(2,1)S(1)}, bf16[4,64,640]{2,1,0:T(8,128)(2,1)}, u32[]{:S(2)}) copy-start(bf16[4,64,640]{2,1,0:T(8,128)(2,1)} %get-tuple-element.85.own) | copy-start | bytes 983044
  130.6 20.4 %copy-start.12 = (bf16[256,128]{1,0:T(8,128)(2,1)S(1)}, bf16[256,128]{1,0:T(8,128)(2,1)}, u32[]{:S(2)}) copy-start(bf16[256,128]{1,0:T(8,128)(2,1)} %get-tuple-element.83.even) | copy-start | bytes 196612
  130.6 20.4 %copy-start.13 = (bf16[256,128]{1,0:T(8,128)(2,1)S(1)}, bf16[256,128]{1,0:T(8,128)(2,1)}, u32[]{:S(2)}) copy-start(bf16[256,128]{1,0:T(8,128)(2,1)} %get-tuple-element.84.odd) | copy-start | bytes 196612
  130.6 20.4 %all-to-all-start.2 = ((bf16[32,8,640]{2,1,0:T(8,128)(2,1)}), bf16[32,8,640]{2,1,0:T(8,128)(2,1)S(1)}, u32[]{:S(2)}, u32[]{:S(2)}) async-start(bf16[32,8,640]{2,1,0:T(8,128)(2,1)} %bitcast.21), calls=%async_computation.2 | async-start | bytes 655360 | tf_op jit(solution)/shard_map/all_to_all | solution.py:451
  137.5 7.5 %collective-permute-start.16 = (bf16[64,640]{1,0:T(8,128)(2,1)S(1)}, bf16[64,640]{1,0:T(8,128)(2,1)S(1)}, u32[]{:S(2)}, u32[]{:S(2)}) collective-permute-start(bf16[64,640]{1,0:T(8,128)(2,1)S(1)} %get-tuple-element.88), channel_id=1, source_target_pairs={{0,64},{64,128},{128,192},{192,0},{1,65},{65,129},{129,193},{193,1... | collective-permute-start | bytes 245768 | tf_op jit(solution)/shard_map/ppermute | solution.py:354
  137.6 7.5 %collective-permute-start.17 = (bf16[64,640]{1,0:T(8,128)(2,1)S(1)}, bf16[64,640]{1,0:T(8,128)(2,1)S(1)}, u32[]{:S(2)}, u32[]{:S(2)}) collective-permute-start(bf16[64,640]{1,0:T(8,128)(2,1)S(1)} %get-tuple-element.89), channel_id=1, source_target_pairs={{0,128},{64,192},{128,0},{192,64},{1,129},{65,193},{129,1},{193,65... | collective-permute-start | bytes 245768 | tf_op jit(solution)/shard_map/ppermute | solution.py:354
  139.9 5.7 %collective-permute-start.18 = (bf16[64,640]{1,0:T(8,128)(2,1)S(1)}, bf16[64,640]{1,0:T(8,128)(2,1)S(1)}, u32[]{:S(2)}, u32[]{:S(2)}) collective-permute-start(bf16[64,640]{1,0:T(8,128)(2,1)S(1)} %get-tuple-element.90), channel_id=1, source_target_pairs={{0,192},{64,0},{128,64},{192,128},{1,193},{65,1},{129,65},{193,129... | collective-permute-start | bytes 245768 | tf_op jit(solution)/shard_map/ppermute | solution.py:354
  150.9 15.3 %copy-start.1 = (bf16[1,128,2560]{2,1,0:T(8,128)(2,1)S(1)}, bf16[1,128,2560]{2,1,0:T(8,128)(2,1)}, u32[]{:S(2)}) copy-start(bf16[1,128,2560]{2,1,0:T(8,128)(2,1)} %param.9) | copy-start | bytes 1966084
  151.0 15.3 %copy-start.2 = (bf16[1,128,2560]{2,1,0:T(8,128)(2,1)S(1)}, bf16[1,128,2560]{2,1,0:T(8,128)(2,1)}, u32[]{:S(2)}) copy-start(bf16[1,128,2560]{2,1,0:T(8,128)(2,1)} %param.8) | copy-start | bytes 1966084
  151.0 15.3 %copy-start.14 = (f32[2560]{0:T(1024)S(1)}, f32[2560]{0:T(1024)}, u32[]{:S(2)}) copy-start(f32[2560]{0:T(1024)} %gain.3) | copy-start | bytes 30724

commit v11 on v10

--- a/solution.py
+++ b/solution.py
@@ -414,7 +414,9 @@
         moved=8 * 2**20,
         limit=VMEM_ALL,
     )(own, up, up_rest, down_rest, down, partner, w_in, w_out)
-    *partner_across, far_pack = lax.optimization_barrier((*partner_across, far_pack))
+    *partner_across, early_sums, far_pack = lax.optimization_barrier(
+        (*partner_across, early_sums, far_pack)
+    )
     far_query = moved_by(far_pack, "ctx_1", 1)
     sums, *late = call(
         late_kernel,

time: 168 us -> 161 us (0.958)
  starting transfers between devices: 47.9 us -> 44.3 us
  waiting for transfers between devices: 58 us -> 55 us
    ppermute x19, starting transfers between devices: 27.8 us -> 25.1 us  [moved_by(): lax.ppermute(array, axis, [(k, (k + step) % count) for k in range(count)])]
    all_to_all x1, waiting for transfers between devices: 16.2 us -> 13.7 us  [on_device(): parts = lax.all_to_all(sums, CTX, split_axis=0, concat_axis=0, tiled=True)]
    unnamed x40 -> x42, local copies, waits for them, and re-layouts: 3.81 us -> 3.18 us
  transfers between devices with their start and end apart: 22 -> 22, of which waited for: 13 -> 15; matrix products, arithmetic and copies ran while one was open for 5% -> 6% of each run, Pallas kernels for 15% -> 16%
where the time goes in v11:
time: 161 us; the launch traced here: 160 us
  waiting for transfers between devices  55 us (34%)
  starting transfers between devices  44.3 us (28%)
  Pallas kernels  31.8 us (20%)
  blocking collectives  14.9 us (9%)
  local copies, waits for them, and re-layouts  13.5 us (8%)
    ppermute x19, waiting for transfers between devices, moved_by(): lax.ppermute(array, axis, [(k, (k + step) % count) for k in range(count)])  36 us
    ppermute x19, starting transfers between devices, moved_by(): lax.ppermute(array, axis, [(k, (k + step) % count) for k in range(count)])  25.1 us
    all_to_all x1, blocking collectives, on_device(): packs = lax.all_to_all(total, CTX, split_axis=0, concat_axis=0, tiled=True)  14.9 us
    all_to_all x1, waiting for transfers between devices, on_device(): parts = lax.all_to_all(sums, CTX, split_axis=0, concat_axis=0, tiled=True)  13.7 us
    all_to_all x1, starting transfers between devices, on_device(): lax.all_to_all(send.reshape(EXPERTS, 8, HALF), 'exp', split_axis=0, conca...  9.7 us
    pallas_call x1, Pallas kernels, on_device(): call(weights_kernel, [ANY] * 8, [shape((2 * UNITS, D))], [pltpu.VMEM(k.sh...  7.34 us
    pallas_call x1, Pallas kernels, on_device(): call(late_kernel, [SMEM] + [ANY] * 9, [shape((CTX_COUNT, ROWS, CHUNK)), *...  6.48 us
    reshape x1, local copies, waits for them, and re-layouts, on_device(): weights_grad = weights_grad.reshape(1, UNITS, 2, D)  6.45 us
  transfers between devices with their start and end apart: 22, of which 15 were waited for; matrix products, arithmetic and copies ran while one was open for 6% of the time, Pallas kernels for 16%

profile of v11, /device:TPU:32, one launch (start us, length us, event | category | flops | bytes accessed | tf_op | source)
XLA Modules:
  0.0 160.4 jit_solution(10041685654257757040)
XLA Ops:
  0.7 3.5 %shard_map.111 = (bf16[128,2560]{1,0:T(8,128)(2,1)}, bf16[256,1280]{1,0:T(8,128)(2,1)}, bf16[256,128]{1,0:T(8,128)(2,1)}, bf16[256,128]{1,0:T(8,128)(2,1)}) custom-call(s32[1]{0:T(128)} %bitcast.8.place, bf16[128,2560]{1,0:T(8,128)(2,1)} %bitcast.34, bf16[128,2560]{1,0:T(8,128)(2,1)} %bitcast.30, f32[2560]{0:T(1024)} %gain.3, s32[2,128]{1,0:T(2,128)} %bitcast.42, ...), custom_call_target="tpu_custom_call" | custom-call | flops 335544320 | bytes 3145728 | tf_op jit(solution)/shard_map/pallas_call | solution.py:363
  4.2 9.7 %all-to-all-start = ((bf16[32,8,1280]{2,1,0:T(8,128)(2,1)}), bf16[32,8,1280]{2,1,0:T(8,128)(2,1)}, u32[]{:S(2)}, u32[]{:S(2)}) async-start(bf16[32,8,1280]{2,1,0:T(8,128)(2,1)} %bitcast.41), calls=%async_computation | async-start | bytes 1310720 | tf_op jit(solution)/shard_map/all_to_all | solution.py:371
  13.9 0.3 copy.12
  14.2 1.7 %slice_bitcast_fusion = (bf16[256,2560]{1,0:T(8,128)(2,1)}, bf16[256,2560]{1,0:T(8,128)(2,1)}) fusion(bf16[1,256,2,2560]{3,1,2,0:T(8,128)(2,1)S(1)} %copy.12), kind=kLoop, calls=%fused_computation | loop fusion | bytes 5242880 | tf_op jit(solution)/shard_map/squeeze | solution.py:376
  15.9 0.7 copy-done.4
  16.6 0.2 copy-done.7
  16.8 1.1 shard_map.112
  17.9 1.1 copy-done.5
  19.0 1.1 copy-done.6
  20.1 3.0 %collective-permute-start.2 = (f32[72,128]{1,0:T(8,128)S(1)}, f32[72,128]{1,0:T(8,128)S(1)}, u32[]{:S(2)}, u32[]{:S(2)}) collective-permute-start(f32[72,128]{1,0:T(8,128)S(1)} %get-tuple-element.55.local), channel_id=1, source_target_pairs={{0,192},{64,0},{128,64},{192,128},{1,193},{65,1},{129,65},{193,129... | collective-permute-start | bytes 110600 | tf_op jit(solution)/shard_map/ppermute | solution.py:354
  23.1 0.6 collective-permute-start.1
  23.7 1.0 collective-permute-start
  24.9 3.6 %collective-permute-done.1 = f32[72,128]{1,0:T(8,128)S(1)} collective-permute-done((f32[72,128]{1,0:T(8,128)S(1)}, f32[72,128]{1,0:T(8,128)S(1)}, u32[]{:S(2)}, u32[]{:S(2)}) %collective-permute-start.1) | collective-permute-done | bytes 36896 | tf_op jit(solution)/shard_map/ppermute | solution.py:354
  28.5 0.4 collective-permute-done
  29.0 2.8 %collective-permute-start.3 = (f32[72,128]{1,0:T(8,128)S(1)}, f32[72,128]{1,0:T(8,128)S(1)}, u32[]{:S(2)}, u32[]{:S(2)}) collective-permute-start(f32[72,128]{1,0:T(8,128)S(1)} %pad_maximum_fusion.near), channel_id=1, source_target_pairs={{0,32},{32,0},{1,33},{33,1},{2,34},{34,2},{3,35},{35,3},{4,36},{36... | collective-permute-start | bytes 110600 | tf_op jit(solution)/shard_map/ppermute | solution.py:354
  31.8 2.7 %collective-permute-done.3.far = f32[72,128]{1,0:T(8,128)S(1)} collective-permute-done((f32[72,128]{1,0:T(8,128)S(1)}, f32[72,128]{1,0:T(8,128)S(1)}, u32[]{:S(2)}, u32[]{:S(2)}) %collective-permute-start.3) | collective-permute-done | bytes 36896 | tf_op jit(solution)/shard_map/ppermute | solution.py:354
  34.6 2.7 %collective-permute-start.4 = (bf16[256,1280]{1,0:T(8,128)(2,1)}, bf16[256,1280]{1,0:T(8,128)(2,1)}, u32[]{:S(2)}, u32[]{:S(2)}) collective-permute-start(bf16[256,1280]{1,0:T(8,128)(2,1)} %bitcast.16.refs_0_), channel_id=1, source_target_pairs={{0,32},{32,0},{1,33},{33,1},{2,34},{34,2},{3,35},{35,3},{4,36},{36... | collective-permute-start | bytes 1966088 | tf_op jit(solution)/shard_map/ppermute | solution.py:354
  37.3 1.8 %fusion.6 = (bf16[128,1280]{1,0:T(8,128)(2,1)S(1)}, bf16[128,1280]{1,0:T(8,128)(2,1)}) fusion(bf16[256,1280]{1,0:T(8,128)(2,1)} %bitcast.16.refs_0_), kind=kLoop, calls=%fused_computation.20 | loop fusion | bytes 1310720 | tf_op jit(solution)/shard_map/slice | solution.py:389
  39.1 3.0 %collective-permute-start.8 = (bf16[128,1280]{1,0:T(8,128)(2,1)S(1)}, bf16[128,1280]{1,0:T(8,128)(2,1)S(1)}, u32[]{:S(2)}, u32[]{:S(2)}) collective-permute-start(bf16[128,1280]{1,0:T(8,128)(2,1)S(1)} %get-tuple-element.100), channel_id=1, source_target_pairs={{0,192},{64,0},{128,64},{192,128},{1,193},{65,1},{129,65},{193,129... | collective-permute-start | bytes 983048 | tf_op jit(solution)/shard_map/ppermute | solution.py:354
  42.1 0.6 collective-permute-start.13
  42.7 4.3 %shard_map.113 = (bf16[128,2560]{1,0:T(8,128)(2,1)}, bf16[128,2560]{1,0:T(8,128)(2,1)}, bf16[4,64,640]{2,1,0:T(8,128)(2,1)}, bf16[4,64,640]{2,1,0:T(8,128)(2,1)}) custom-call(s32[1]{0:T(128)} %bitcast.8.place, bf16[128,2560]{1,0:T(8,128)(2,1)} %get-tuple-element.52.normed, bf16[128,2560]{1,0:T(8,128)(2,1)} %bitcast.31, bf16[128,2560]{1,0:T(8,128)(2,1)} %bitcast.36, ...), custom_call_target="tpu_custom_call" | custom-call | flops 251658240 | bytes 6291456 | tf_op jit(solution)/shard_map/pallas_call | solution.py:393
  47.0 0.9 collective-permute-done.8.refs_4_
  48.0 6.2 %collective-permute-done.7.refs_1_ = bf16[128,1280]{1,0:T(8,128)(2,1)S(1)} collective-permute-done((bf16[128,1280]{1,0:T(8,128)(2,1)}, bf16[128,1280]{1,0:T(8,128)(2,1)S(1)}, u32[]{:S(2)}, u32[]{:S(2)}) %collective-permute-start.7) | collective-permute-done | bytes 327712 | tf_op jit(solution)/shard_map/ppermute | solution.py:354
  54.2 3.2 %collective-permute-start.10 = (bf16[128,1280]{1,0:T(8,128)(2,1)S(1)}, bf16[128,1280]{1,0:T(8,128)(2,1)S(1)}, u32[]{:S(2)}, u32[]{:S(2)}) collective-permute-start(bf16[128,1280]{1,0:T(8,128)(2,1)S(1)} %collective-permute-done.8.refs_4_), channel_id=1, source_target_pairs={{0,192},{64,0},{128,64},{192,128},{1,193},{65,1},{129,65},{193,129... | collective-permute-start | bytes 983048 | tf_op jit(solution)/shard_map/ppermute | solution.py:354
  57.7 3.5 %collective-permute-done.13.refs_2_ = bf16[128,1280]{1,0:T(8,128)(2,1)S(1)} collective-permute-done((bf16[128,1280]{1,0:T(8,128)(2,1)S(1)}, bf16[128,1280]{1,0:T(8,128)(2,1)S(1)}, u32[]{:S(2)}, u32[]{:S(2)}) %collective-permute-start.13) | collective-permute-done | bytes 327712 | tf_op jit(solution)/shard_map/ppermute | solution.py:354
  61.2 7.0 %collective-permute-done.9.refs_2_ = bf16[128,1280]{1,0:T(8,128)(2,1)S(1)} collective-permute-done((bf16[128,1280]{1,0:T(8,128)(2,1)S(1)}, bf16[128,1280]{1,0:T(8,128)(2,1)S(1)}, u32[]{:S(2)}, u32[]{:S(2)}) %collective-permute-start.9) | collective-permute-done | bytes 327712 | tf_op jit(solution)/shard_map/ppermute | solution.py:354
  68.2 0.8 collective-permute-start.11
  69.0 2.7 %collective-permute-start.12 = (bf16[128,1280]{1,0:T(8,128)(2,1)S(1)}, bf16[128,1280]{1,0:T(8,128)(2,1)S(1)}, u32[]{:S(2)}, u32[]{:S(2)}) collective-permute-start(bf16[128,1280]{1,0:T(8,128)(2,1)S(1)} %collective-permute-done.10.refs_3_), channel_id=1, source_target_pairs={{0,32},{32,0},{1,33},{33,1},{2,34},{34,2},{3,35},{35,3},{4,36},{36... | collective-permute-start | bytes 983048 | tf_op jit(solution)/shard_map/ppermute | solution.py:354
  71.7 1.0 collective-permute-done.14.refs_3_
  72.7 5.8 %shard_map.114 = (bf16[8,128,640]{2,1,0:T(8,128)(2,1)}, bf16[256,2560]{1,0:T(8,128)(2,1)}, bf16[256,2560]{1,0:T(8,128)(2,1)}, bf16[256,256]{1,0:T(8,128)(2,1)}, bf16[256,256]{1,0:T(8,128)(2,1)}) custom-call(bf16[256,1280]{1,0:T(8,128)(2,1)} %bitcast.16.refs_0_, bf16[128,1280]{1,0:T(8,128)(2,1)} %copy-done.17, bf16[128,1280]{1,0:T(8,128)(2,1)} %copy-done.18, ...), custom_call_target="tpu_custom_call" | custom-call | flops 1006632960 | bytes 8388608 | tf_op jit(solution)/shard_map/pallas_call | solution.py:409
  78.5 4.4 %collective-permute-done.12.refs_5_ = bf16[128,1280]{1,0:T(8,128)(2,1)S(1)} collective-permute-done((bf16[128,1280]{1,0:T(8,128)(2,1)S(1)}, bf16[128,1280]{1,0:T(8,128)(2,1)S(1)}, u32[]{:S(2)}, u32[]{:S(2)}) %collective-permute-start.12) | collective-permute-done | bytes 327712 | tf_op jit(solution)/shard_map/ppermute | solution.py:354
  82.9 0.8 collective-permute-start.15
  83.8 6.5 %shard_map.115 = (bf16[8,256,640]{2,1,0:T(8,128)(2,1)}, bf16[256,2560]{1,0:T(8,128)(2,1)}, bf16[256,2560]{1,0:T(8,128)(2,1)}, bf16[256,256]{1,0:T(8,128)(2,1)S(1)}, bf16[256,256]{1,0:T(8,128)(2,1)S(1)}) custom-call(s32[8]{0:T(128)S(1)} %stack.35.at_ref, bf16[256,1280]{1,0:T(8,128)(2,1)S(1)} %collective-permute-done.5.refs_0_, ...), custom_call_target="tpu_custom_call" | custom-call | flops 1006632960 | bytes 12582912 | tf_op jit(solution)/shard_map/pallas_call | solution.py:421
  90.3 1.4 collective-permute-done.15.far
  91.7 3.6 %all-to-all-start.1 = ((bf16[8,256,640]{2,1,0:T(8,128)(2,1)}), bf16[8,256,640]{2,1,0:T(8,128)(2,1)S(1)}, u32[]{:S(2)}, u32[]{:S(2)}) async-start(bf16[8,256,640]{2,1,0:T(8,128)(2,1)} %get-tuple-element.73), calls=%async_computation.1 | async-start | bytes 5242880 | tf_op jit(solution)/shard_map/all_to_all | solution.py:439
  95.3 7.3 %shard_map.116 = bf16[512,2560]{1,0:T(8,128)(2,1)} custom-call(bf16[256,2560]{1,0:T(8,128)(2,1)} %get-tuple-element.74.refs_0_, bf16[256,2560]{1,0:T(8,128)(2,1)} %get-tuple-element.75.refs_1_, bf16[256,256]{1,0:T(8,128)(2,1)} %get-tuple-element.76.refs_2_, bf16[256,256]{1,0:T(8,128)(2,1)} %get-tuple-element.77.refs_3_, ...), custom_call_target="tpu_custom_call" | custom-call | flops 1342177280 | bytes 8388608 | tf_op jit(solution)/shard_map/pallas_call | solution.py:440
  102.7 6.4 %reshape.29 = bf16[1,256,2,2560]{3,2,1,0:T(2,128)(2,1)} reshape(bf16[512,2560]{1,0:T(8,128)(2,1)} %shard_map.116) | data formatting | bytes 5242880 | tf_op jit(solution)/shard_map/reshape | solution.py:449
  109.1 13.7 %all-to-all-done.1.parts = bf16[8,256,640]{2,1,0:T(8,128)(2,1)S(1)} async-done(((bf16[8,256,640]{2,1,0:T(8,128)(2,1)}), bf16[8,256,640]{2,1,0:T(8,128)(2,1)S(1)}, u32[]{:S(2)}, u32[]{:S(2)}) %all-to-all-start.1) | async-done | bytes 2621472 | tf_op jit(solution)/shard_map/all_to_all | solution.py:439
  122.8 1.3 shard_map.117
  124.1 5.9 %all-to-all-start.2 = ((bf16[32,8,640]{2,1,0:T(8,128)(2,1)}), bf16[32,8,640]{2,1,0:T(8,128)(2,1)S(1)}, u32[]{:S(2)}, u32[]{:S(2)}) async-start(bf16[32,8,640]{2,1,0:T(8,128)(2,1)} %bitcast.21), calls=%async_computation.2 | async-start | bytes 655360 | tf_op jit(solution)/shard_map/all_to_all | solution.py:453
  130.2 2.4 %collective-permute-start.17 = (bf16[64,640]{1,0:T(8,128)(2,1)S(1)}, bf16[64,640]{1,0:T(8,128)(2,1)S(1)}, u32[]{:S(2)}, u32[]{:S(2)}) collective-permute-start(bf16[64,640]{1,0:T(8,128)(2,1)S(1)} %get-tuple-element.91), channel_id=1, source_target_pairs={{0,128},{64,192},{128,0},{192,64},{1,129},{65,193},{129,1},{193,65... | collective-permute-start | bytes 245768 | tf_op jit(solution)/shard_map/ppermute | solution.py:354
  132.6 1.0 collective-permute-start.18
  133.6 4.0 %collective-permute-done.16.below = bf16[64,640]{1,0:T(8,128)(2,1)S(1)} collective-permute-done((bf16[64,640]{1,0:T(8,128)(2,1)S(1)}, bf16[64,640]{1,0:T(8,128)(2,1)S(1)}, u32[]{:S(2)}, u32[]{:S(2)}) %collective-permute-start.16) | collective-permute-done | bytes 81952 | tf_op jit(solution)/shard_map/ppermute | solution.py:354
  137.6 0.6 collective-permute-done.18.above
  138.2 5.3 %all-to-all-done.2 = bf16[32,8,640]{2,1,0:T(8,128)(2,1)S(1)} async-done(((bf16[32,8,640]{2,1,0:T(8,128)(2,1)}), bf16[32,8,640]{2,1,0:T(8,128)(2,1)S(1)}, u32[]{:S(2)}, u32[]{:S(2)}) %all-to-all-start.2) | async-done | bytes 327712 | tf_op jit(solution)/shard_map/all_to_all | solution.py:453
  143.6 0.4 shard_map.119
  144.0 14.9 %all_to_all.20.packs = bf16[8,64,640]{2,1,0:T(8,128)(2,1)S(1)} all-to-all(bf16[8,64,640]{2,1,0:T(8,128)(2,1)S(1)} %shard_map.119), channel_id=1, replica_groups=mesh['ctx_0'=4,'ctx_1'=2,'exp'=32] {'ctx_0','ctx_1'}, dimensions={0} | all-to-all | bytes 1310720 | tf_op jit(solution)/shard_map/all_to_all | solution.py:461
  158.9 1.5 shard_map.120
  (57 shorter events, 0.9 us)
Async XLA Ops:
  0.6 13.2 %copy-start.15 = (bf16[1,256,2,2560]{3,2,1,0:T(2,128)(2,1)S(1)}, bf16[1,256,2,2560]{3,2,1,0:T(2,128)(2,1)}, u32[]{:S(2)}) copy-start(bf16[1,256,2,2560]{3,2,1,0:T(2,128)(2,1)} %param.15) | copy-start | bytes 7864324
  4.2 30.4 %all-to-all-start = ((bf16[32,8,1280]{2,1,0:T(8,128)(2,1)}), bf16[32,8,1280]{2,1,0:T(8,128)(2,1)}, u32[]{:S(2)}, u32[]{:S(2)}) async-start(bf16[32,8,1280]{2,1,0:T(8,128)(2,1)} %bitcast.41), calls=%async_computation | async-start | bytes 1310720 | tf_op jit(solution)/shard_map/all_to_all | solution.py:371
  14.2 1.7 %copy-start = (bf16[1,128,2560]{2,1,0:T(8,128)(2,1)S(1)}, bf16[1,128,2560]{2,1,0:T(8,128)(2,1)}, u32[]{:S(2)}) copy-start(bf16[1,128,2560]{2,1,0:T(8,128)(2,1)} %param.9) | copy-start | bytes 1966084
  14.2 1.7 %copy-start.3 = (bf16[1,128,2560]{2,1,0:T(8,128)(2,1)S(1)}, bf16[1,128,2560]{2,1,0:T(8,128)(2,1)}, u32[]{:S(2)}) copy-start(bf16[1,128,2560]{2,1,0:T(8,128)(2,1)} %param.10) | copy-start | bytes 1966084
  14.2 2.4 %copy-start.4 = (bf16[128,2560]{1,0:T(8,128)(2,1)S(1)}, bf16[128,2560]{1,0:T(8,128)(2,1)}, u32[]{:S(2)}) copy-start(bf16[128,2560]{1,0:T(8,128)(2,1)} %get-tuple-element.52.normed) | copy-start | bytes 1966084
  14.2 2.6 %copy-start.7 = (bf16[1,128,2560]{2,1,0:T(8,128)(2,1)S(1)}, bf16[1,128,2560]{2,1,0:T(8,128)(2,1)}, u32[]{:S(2)}) copy-start(bf16[1,128,2560]{2,1,0:T(8,128)(2,1)} %param.11) | copy-start | bytes 1966084
  17.9 1.1 copy-start.5
  19.0 1.1 copy-start.6
  20.1 22.6 %copy-start.9 = (f32[72,128]{1,0:T(8,128)}, f32[72,128]{1,0:T(8,128)S(1)}, u32[]{:S(2)}) copy-start(f32[72,128]{1,0:T(8,128)S(1)} %get-tuple-element.55.local) | copy-start | bytes 110596
  20.1 4.9 %collective-permute-start.2 = (f32[72,128]{1,0:T(8,128)S(1)}, f32[72,128]{1,0:T(8,128)S(1)}, u32[]{:S(2)}, u32[]{:S(2)}) collective-permute-start(f32[72,128]{1,0:T(8,128)S(1)} %get-tuple-element.55.local), channel_id=1, source_target_pairs={{0,192},{64,0},{128,64},{192,128},{1,193},{65,1},{129,65},{193,129... | collective-permute-start | bytes 110600 | tf_op jit(solution)/shard_map/ppermute | solution.py:354
  23.1 5.5 %collective-permute-start.1 = (f32[72,128]{1,0:T(8,128)S(1)}, f32[72,128]{1,0:T(8,128)S(1)}, u32[]{:S(2)}, u32[]{:S(2)}) collective-permute-start(f32[72,128]{1,0:T(8,128)S(1)} %get-tuple-element.55.local), channel_id=1, source_target_pairs={{0,128},{64,192},{128,0},{192,64},{1,129},{65,193},{129,1},{193,65... | collective-permute-start | bytes 110600 | tf_op jit(solution)/shard_map/ppermute | solution.py:354
  23.7 5.2 %collective-permute-start = (f32[72,128]{1,0:T(8,128)S(1)}, f32[72,128]{1,0:T(8,128)S(1)}, u32[]{:S(2)}, u32[]{:S(2)}) collective-permute-start(f32[72,128]{1,0:T(8,128)S(1)} %get-tuple-element.55.local), channel_id=1, source_target_pairs={{0,64},{64,128},{128,192},{192,0},{1,65},{65,129},{129,193},{193,1... | collective-permute-start | bytes 110600 | tf_op jit(solution)/shard_map/ppermute | solution.py:354
  29.0 13.7 %copy-start.19 = (f32[72,128]{1,0:T(8,128)}, f32[72,128]{1,0:T(8,128)S(1)}, u32[]{:S(2)}) copy-start(f32[72,128]{1,0:T(8,128)S(1)} %pad_maximum_fusion.near) | copy-start | bytes 110596
  29.0 5.6 %collective-permute-start.3 = (f32[72,128]{1,0:T(8,128)S(1)}, f32[72,128]{1,0:T(8,128)S(1)}, u32[]{:S(2)}, u32[]{:S(2)}) collective-permute-start(f32[72,128]{1,0:T(8,128)S(1)} %pad_maximum_fusion.near), channel_id=1, source_target_pairs={{0,32},{32,0},{1,33},{33,1},{2,34},{34,2},{3,35},{35,3},{4,36},{36... | collective-permute-start | bytes 110600 | tf_op jit(solution)/shard_map/ppermute | solution.py:354
  34.6 8.1 %copy-start.20 = (f32[72,128]{1,0:T(8,128)}, f32[72,128]{1,0:T(8,128)S(1)}, u32[]{:S(2)}) copy-start(f32[72,128]{1,0:T(8,128)S(1)} %collective-permute-done.3.far) | copy-start | bytes 110596
  34.6 22.9 %collective-permute-start.4 = (bf16[256,1280]{1,0:T(8,128)(2,1)}, bf16[256,1280]{1,0:T(8,128)(2,1)}, u32[]{:S(2)}, u32[]{:S(2)}) collective-permute-start(bf16[256,1280]{1,0:T(8,128)(2,1)} %bitcast.16.refs_0_), channel_id=1, source_target_pairs={{0,32},{32,0},{1,33},{33,1},{2,34},{34,2},{3,35},{35,3},{4,36},{36... | collective-permute-start | bytes 1966088 | tf_op jit(solution)/shard_map/ppermute | solution.py:354
  39.1 8.8 %collective-permute-start.8 = (bf16[128,1280]{1,0:T(8,128)(2,1)S(1)}, bf16[128,1280]{1,0:T(8,128)(2,1)S(1)}, u32[]{:S(2)}, u32[]{:S(2)}) collective-permute-start(bf16[128,1280]{1,0:T(8,128)(2,1)S(1)} %get-tuple-element.100), channel_id=1, source_target_pairs={{0,192},{64,0},{128,64},{192,128},{1,193},{65,1},{129,65},{193,129... | collective-permute-start | bytes 983048 | tf_op jit(solution)/shard_map/ppermute | solution.py:354
  42.1 12.1 %collective-permute-start.7 = (bf16[128,1280]{1,0:T(8,128)(2,1)}, bf16[128,1280]{1,0:T(8,128)(2,1)S(1)}, u32[]{:S(2)}, u32[]{:S(2)}) collective-permute-start(bf16[128,1280]{1,0:T(8,128)(2,1)} %get-tuple-element.101), channel_id=1, source_target_pairs={{0,64},{64,128},{128,192},{192,0},{1,65},{65,129},{129,193},{193,1... | collective-permute-start | bytes 983048 | tf_op jit(solution)/shard_map/ppermute | solution.py:354
  42.1 19.1 %collective-permute-start.13 = (bf16[128,1280]{1,0:T(8,128)(2,1)S(1)}, bf16[128,1280]{1,0:T(8,128)(2,1)S(1)}, u32[]{:S(2)}, u32[]{:S(2)}) collective-permute-start(bf16[128,1280]{1,0:T(8,128)(2,1)S(1)} %get-tuple-element.100), channel_id=1, source_target_pairs={{0,64},{64,128},{128,192},{192,0},{1,65},{65,129},{129,193},{193,1... | collective-permute-start | bytes 983048 | tf_op jit(solution)/shard_map/ppermute | solution.py:354
  48.0 24.7 %copy-start.16 = (bf16[128,1280]{1,0:T(8,128)(2,1)}, bf16[128,1280]{1,0:T(8,128)(2,1)S(1)}, u32[]{:S(2)}) copy-start(bf16[128,1280]{1,0:T(8,128)(2,1)S(1)} %collective-permute-done.8.refs_4_) | copy-start | bytes 983044
  54.2 18.5 %copy-start.17 = (bf16[128,1280]{1,0:T(8,128)(2,1)}, bf16[128,1280]{1,0:T(8,128)(2,1)S(1)}, u32[]{:S(2)}) copy-start(bf16[128,1280]{1,0:T(8,128)(2,1)S(1)} %collective-permute-done.7.refs_1_) | copy-start | bytes 983044
  54.2 14.0 %collective-permute-start.9 = (bf16[128,1280]{1,0:T(8,128)(2,1)S(1)}, bf16[128,1280]{1,0:T(8,128)(2,1)S(1)}, u32[]{:S(2)}, u32[]{:S(2)}) collective-permute-start(bf16[128,1280]{1,0:T(8,128)(2,1)S(1)} %collective-permute-done.7.refs_1_), channel_id=1, source_target_pairs={{0,64},{64,128},{128,192},{192,0},{1,65},{65,129},{129,193},{193,1... | collective-permute-start | bytes 983048 | tf_op jit(solution)/shard_map/ppermute | solution.py:354
  54.2 14.8 %collective-permute-start.10 = (bf16[128,1280]{1,0:T(8,128)(2,1)S(1)}, bf16[128,1280]{1,0:T(8,128)(2,1)S(1)}, u32[]{:S(2)}, u32[]{:S(2)}) collective-permute-start(bf16[128,1280]{1,0:T(8,128)(2,1)S(1)} %collective-permute-done.8.refs_4_), channel_id=1, source_target_pairs={{0,192},{64,0},{128,64},{192,128},{1,193},{65,1},{129,65},{193,129... | collective-permute-start | bytes 983048 | tf_op jit(solution)/shard_map/ppermute | solution.py:354
  57.4 15.3 %collective-permute-start.14 = (bf16[128,1280]{1,0:T(8,128)(2,1)}, bf16[128,1280]{1,0:T(8,128)(2,1)}, u32[]{:S(2)}, u32[]{:S(2)}) collective-permute-start(bf16[128,1280]{1,0:T(8,128)(2,1)} %get-tuple-element.101), channel_id=1, source_target_pairs={{0,192},{64,0},{128,64},{192,128},{1,193},{65,1},{129,65},{193,129... | collective-permute-start | bytes 983048 | tf_op jit(solution)/shard_map/ppermute | solution.py:354
  57.4 26.3 %collective-permute-start.6 = (bf16[256,1280]{1,0:T(8,128)(2,1)}, bf16[256,1280]{1,0:T(8,128)(2,1)S(1)}, u32[]{:S(2)}, u32[]{:S(2)}) collective-permute-start(bf16[256,1280]{1,0:T(8,128)(2,1)} %collective-permute-done.4.refs_5_), channel_id=1, source_target_pairs={{0,192},{64,0},{128,64},{192,128},{1,193},{65,1},{129,65},{193,129... | collective-permute-start | bytes 1966088 | tf_op jit(solution)/shard_map/ppermute | solution.py:354
  61.2 11.5 %copy-start.18 = (bf16[128,1280]{1,0:T(8,128)(2,1)}, bf16[128,1280]{1,0:T(8,128)(2,1)S(1)}, u32[]{:S(2)}) copy-start(bf16[128,1280]{1,0:T(8,128)(2,1)S(1)} %collective-permute-done.13.refs_2_) | copy-start | bytes 983044
  61.2 22.6 %collective-permute-start.5 = (bf16[256,1280]{1,0:T(8,128)(2,1)}, bf16[256,1280]{1,0:T(8,128)(2,1)S(1)}, u32[]{:S(2)}, u32[]{:S(2)}) collective-permute-start(bf16[256,1280]{1,0:T(8,128)(2,1)} %collective-permute-done.4.refs_5_), channel_id=1, source_target_pairs={{0,64},{64,128},{128,192},{192,0},{1,65},{65,129},{129,193},{193,1... | collective-permute-start | bytes 1966088 | tf_op jit(solution)/shard_map/ppermute | solution.py:354
  68.2 10.3 %collective-permute-start.11 = (bf16[128,1280]{1,0:T(8,128)(2,1)S(1)}, bf16[128,1280]{1,0:T(8,128)(2,1)S(1)}, u32[]{:S(2)}, u32[]{:S(2)}) collective-permute-start(bf16[128,1280]{1,0:T(8,128)(2,1)S(1)} %collective-permute-done.9.refs_2_), channel_id=1, source_target_pairs={{0,32},{32,0},{1,33},{33,1},{2,34},{34,2},{3,35},{35,3},{4,36},{36... | collective-permute-start | bytes 983048 | tf_op jit(solution)/shard_map/ppermute | solution.py:354
  69.0 13.9 %collective-permute-start.12 = (bf16[128,1280]{1,0:T(8,128)(2,1)S(1)}, bf16[128,1280]{1,0:T(8,128)(2,1)S(1)}, u32[]{:S(2)}, u32[]{:S(2)}) collective-permute-start(bf16[128,1280]{1,0:T(8,128)(2,1)S(1)} %collective-permute-done.10.refs_3_), channel_id=1, source_target_pairs={{0,32},{32,0},{1,33},{33,1},{2,34},{34,2},{3,35},{35,3},{4,36},{36... | collective-permute-start | bytes 983048 | tf_op jit(solution)/shard_map/ppermute | solution.py:354
  82.9 8.8 %collective-permute-start.15 = (bf16[4,64,640]{2,1,0:T(8,128)(2,1)}, bf16[4,64,640]{2,1,0:T(8,128)(2,1)S(1)}, u32[]{:S(2)}, u32[]{:S(2)}) collective-permute-start(bf16[4,64,640]{2,1,0:T(8,128)(2,1)} %get-tuple-element.72), channel_id=1, source_target_pairs={{0,32},{32,0},{1,33},{33,1},{2,34},{34,2},{3,35},{35,3},{4,36},{36... | collective-permute-start | bytes 983048 | tf_op jit(solution)/shard_map/ppermute | solution.py:354
  90.3 1.4 copy-start.10
  90.3 1.4 copy-start.11
  91.7 31.1 %all-to-all-start.1 = ((bf16[8,256,640]{2,1,0:T(8,128)(2,1)}), bf16[8,256,640]{2,1,0:T(8,128)(2,1)S(1)}, u32[]{:S(2)}, u32[]{:S(2)}) async-start(bf16[8,256,640]{2,1,0:T(8,128)(2,1)} %get-tuple-element.73), calls=%async_computation.1 | async-start | bytes 5242880 | tf_op jit(solution)/shard_map/all_to_all | solution.py:439
  109.1 20.9 %copy-start.8 = (bf16[4,64,640]{2,1,0:T(8,128)(2,1)S(1)}, bf16[4,64,640]{2,1,0:T(8,128)(2,1)}, u32[]{:S(2)}) copy-start(bf16[4,64,640]{2,1,0:T(8,128)(2,1)} %get-tuple-element.87.own) | copy-start | bytes 983044
  124.1 19.5 %copy-start.12 = (bf16[256,128]{1,0:T(8,128)(2,1)S(1)}, bf16[256,128]{1,0:T(8,128)(2,1)}, u32[]{:S(2)}) copy-start(bf16[256,128]{1,0:T(8,128)(2,1)} %get-tuple-element.85.even) | copy-start | bytes 196612
  124.1 19.5 %copy-start.13 = (bf16[256,128]{1,0:T(8,128)(2,1)S(1)}, bf16[256,128]{1,0:T(8,128)(2,1)}, u32[]{:S(2)}) copy-start(bf16[256,128]{1,0:T(8,128)(2,1)} %get-tuple-element.86.odd) | copy-start | bytes 196612
  124.1 19.5 %all-to-all-start.2 = ((bf16[32,8,640]{2,1,0:T(8,128)(2,1)}), bf16[32,8,640]{2,1,0:T(8,128)(2,1)S(1)}, u32[]{:S(2)}, u32[]{:S(2)}) async-start(bf16[32,8,640]{2,1,0:T(8,128)(2,1)} %bitcast.21), calls=%async_computation.2 | async-start | bytes 655360 | tf_op jit(solution)/shard_map/all_to_all | solution.py:453
  130.1 7.5 %collective-permute-start.16 = (bf16[64,640]{1,0:T(8,128)(2,1)S(1)}, bf16[64,640]{1,0:T(8,128)(2,1)S(1)}, u32[]{:S(2)}, u32[]{:S(2)}) collective-permute-start(bf16[64,640]{1,0:T(8,128)(2,1)S(1)} %get-tuple-element.90), channel_id=1, source_target_pairs={{0,64},{64,128},{128,192},{192,0},{1,65},{65,129},{129,193},{193,1... | collective-permute-start | bytes 245768 | tf_op jit(solution)/shard_map/ppermute | solution.py:354
  130.2 7.5 %collective-permute-start.17 = (bf16[64,640]{1,0:T(8,128)(2,1)S(1)}, bf16[64,640]{1,0:T(8,128)(2,1)S(1)}, u32[]{:S(2)}, u32[]{:S(2)}) collective-permute-start(bf16[64,640]{1,0:T(8,128)(2,1)S(1)} %get-tuple-element.91), channel_id=1, source_target_pairs={{0,128},{64,192},{128,0},{192,64},{1,129},{65,193},{129,1},{193,65... | collective-permute-start | bytes 245768 | tf_op jit(solution)/shard_map/ppermute | solution.py:354
  132.6 5.6 %collective-permute-start.18 = (bf16[64,640]{1,0:T(8,128)(2,1)S(1)}, bf16[64,640]{1,0:T(8,128)(2,1)S(1)}, u32[]{:S(2)}, u32[]{:S(2)}) collective-permute-start(bf16[64,640]{1,0:T(8,128)(2,1)S(1)} %get-tuple-element.92), channel_id=1, source_target_pairs={{0,192},{64,0},{128,64},{192,128},{1,193},{65,1},{129,65},{193,129... | collective-permute-start | bytes 245768 | tf_op jit(solution)/shard_map/ppermute | solution.py:354
  143.5 15.3 %copy-start.1 = (bf16[1,128,2560]{2,1,0:T(8,128)(2,1)S(1)}, bf16[1,128,2560]{2,1,0:T(8,128)(2,1)}, u32[]{:S(2)}) copy-start(bf16[1,128,2560]{2,1,0:T(8,128)(2,1)} %param.9) | copy-start | bytes 1966084
  143.5 15.3 %copy-start.2 = (bf16[1,128,2560]{2,1,0:T(8,128)(2,1)S(1)}, bf16[1,128,2560]{2,1,0:T(8,128)(2,1)}, u32[]{:S(2)}) copy-start(bf16[1,128,2560]{2,1,0:T(8,128)(2,1)} %param.8) | copy-start | bytes 1966084
  143.5 15.3 %copy-start.14 = (f32[2560]{0:T(1024)S(1)}, f32[2560]{0:T(1024)}, u32[]{:S(2)}) copy-start(f32[2560]{0:T(1024)} %gain.3) | copy-start | bytes 30724

commit v12 on v10

--- a/solution.py
+++ b/solution.py
@@ -414,7 +414,7 @@
         moved=8 * 2**20,
         limit=VMEM_ALL,
     )(own, up, up_rest, down_rest, down, partner, w_in, w_out)
-    *partner_across, far_pack = lax.optimization_barrier((*partner_across, far_pack))
+    early_sums, far_pack = lax.optimization_barrier((early_sums, far_pack))
     far_query = moved_by(far_pack, "ctx_1", 1)
     sums, *late = call(
         late_kernel,

time: 168 us -> 161 us (0.958)
  waiting for transfers between devices: 58 us -> 53.8 us
  starting transfers between devices: 47.9 us -> 44.3 us
    all_to_all x1, waiting for transfers between devices: 16.2 us -> 12.9 us  [on_device(): parts = lax.all_to_all(sums, CTX, split_axis=0, concat_axis=0, tiled=True)]
    ppermute x19, starting transfers between devices: 27.8 us -> 25.1 us  [moved_by(): lax.ppermute(array, axis, [(k, (k + step) % count) for k in range(count)])]
    unnamed x40 -> x42, local copies, waits for them, and re-layouts: 3.81 us -> 3.84 us
  transfers between devices with their start and end apart: 22 -> 22, of which waited for: 13 -> 14; matrix products, arithmetic and copies ran while one was open for 5% -> 6% of each run, Pallas kernels for 15% -> 16%
where the time goes in v12:
time: 161 us; the launch traced here: 160 us
  waiting for transfers between devices  53.8 us (33%)
  starting transfers between devices  44.3 us (28%)
  Pallas kernels  31.8 us (20%)
  blocking collectives  14.9 us (9%)
  local copies, waits for them, and re-layouts  14.1 us (9%)
    ppermute x19, waiting for transfers between devices, moved_by(): lax.ppermute(array, axis, [(k, (k + step) % count) for k in range(count)])  35.6 us
    ppermute x19, starting transfers between devices, moved_by(): lax.ppermute(array, axis, [(k, (k + step) % count) for k in range(count)])  25.1 us
    all_to_all x1, blocking collectives, on_device(): packs = lax.all_to_all(total, CTX, split_axis=0, concat_axis=0, tiled=True)  14.9 us
    all_to_all x1, waiting for transfers between devices, on_device(): parts = lax.all_to_all(sums, CTX, split_axis=0, concat_axis=0, tiled=True)  12.9 us
    all_to_all x1, starting transfers between devices, on_device(): lax.all_to_all(send.reshape(EXPERTS, 8, HALF), 'exp', split_axis=0, conca...  9.7 us
    pallas_call x1, Pallas kernels, on_device(): call(weights_kernel, [ANY] * 8, [shape((2 * UNITS, D))], [pltpu.VMEM(k.sh...  7.34 us
    pallas_call x1, Pallas kernels, on_device(): call(late_kernel, [SMEM] + [ANY] * 9, [shape((CTX_COUNT, ROWS, CHUNK)), *...  6.47 us
    reshape x1, local copies, waits for them, and re-layouts, on_device(): weights_grad = weights_grad.reshape(1, UNITS, 2, D)  6.45 us
  transfers between devices with their start and end apart: 22, of which 14 were waited for; matrix products, arithmetic and copies ran while one was open for 6% of the time, Pallas kernels for 16%

profile of v12, /device:TPU:32, one launch (start us, length us, event | category | flops | bytes accessed | tf_op | source)
XLA Modules:
  0.0 159.9 jit_solution(2169143515890100846)
XLA Ops:
  0.7 3.5 %shard_map.111 = (bf16[128,2560]{1,0:T(8,128)(2,1)}, bf16[256,1280]{1,0:T(8,128)(2,1)}, bf16[256,128]{1,0:T(8,128)(2,1)}, bf16[256,128]{1,0:T(8,128)(2,1)}) custom-call(s32[1]{0:T(128)} %bitcast.8.place, bf16[128,2560]{1,0:T(8,128)(2,1)} %bitcast.34, bf16[128,2560]{1,0:T(8,128)(2,1)} %bitcast.30, f32[2560]{0:T(1024)} %gain.3, s32[2,128]{1,0:T(2,128)} %bitcast.42, ...), custom_call_target="tpu_custom_call" | custom-call | flops 335544320 | bytes 3145728 | tf_op jit(solution)/shard_map/pallas_call | solution.py:363
  4.2 9.7 %all-to-all-start = ((bf16[32,8,1280]{2,1,0:T(8,128)(2,1)}), bf16[32,8,1280]{2,1,0:T(8,128)(2,1)}, u32[]{:S(2)}, u32[]{:S(2)}) async-start(bf16[32,8,1280]{2,1,0:T(8,128)(2,1)} %bitcast.41), calls=%async_computation | async-start | bytes 1310720 | tf_op jit(solution)/shard_map/all_to_all | solution.py:371
  13.9 0.3 copy.12
  14.2 1.7 %slice_bitcast_fusion = (bf16[256,2560]{1,0:T(8,128)(2,1)}, bf16[256,2560]{1,0:T(8,128)(2,1)}) fusion(bf16[1,256,2,2560]{3,1,2,0:T(8,128)(2,1)S(1)} %copy.12), kind=kLoop, calls=%fused_computation | loop fusion | bytes 5242880 | tf_op jit(solution)/shard_map/squeeze | solution.py:376
  15.9 0.7 copy-done.4
  16.8 1.1 shard_map.112
  17.9 1.1 copy-done.5
  19.0 1.1 copy-done.6
  20.1 3.0 %collective-permute-start.2 = (f32[72,128]{1,0:T(8,128)S(1)}, f32[72,128]{1,0:T(8,128)S(1)}, u32[]{:S(2)}, u32[]{:S(2)}) collective-permute-start(f32[72,128]{1,0:T(8,128)S(1)} %get-tuple-element.53.local), channel_id=1, source_target_pairs={{0,192},{64,0},{128,64},{192,128},{1,193},{65,1},{129,65},{193,129... | collective-permute-start | bytes 110600 | tf_op jit(solution)/shard_map/ppermute | solution.py:354
  23.1 0.6 collective-permute-start.1
  23.7 1.0 collective-permute-start
  24.9 3.6 %collective-permute-done.1 = f32[72,128]{1,0:T(8,128)S(1)} collective-permute-done((f32[72,128]{1,0:T(8,128)S(1)}, f32[72,128]{1,0:T(8,128)S(1)}, u32[]{:S(2)}, u32[]{:S(2)}) %collective-permute-start.1) | collective-permute-done | bytes 36896 | tf_op jit(solution)/shard_map/ppermute | solution.py:354
  28.5 0.4 collective-permute-done
  29.0 2.8 %collective-permute-start.3 = (f32[72,128]{1,0:T(8,128)S(1)}, f32[72,128]{1,0:T(8,128)S(1)}, u32[]{:S(2)}, u32[]{:S(2)}) collective-permute-start(f32[72,128]{1,0:T(8,128)S(1)} %pad_maximum_fusion.near), channel_id=1, source_target_pairs={{0,32},{32,0},{1,33},{33,1},{2,34},{34,2},{3,35},{35,3},{4,36},{36... | collective-permute-start | bytes 110600 | tf_op jit(solution)/shard_map/ppermute | solution.py:354
  31.8 2.7 %collective-permute-done.3.far = f32[72,128]{1,0:T(8,128)S(1)} collective-permute-done((f32[72,128]{1,0:T(8,128)S(1)}, f32[72,128]{1,0:T(8,128)S(1)}, u32[]{:S(2)}, u32[]{:S(2)}) %collective-permute-start.3) | collective-permute-done | bytes 36896 | tf_op jit(solution)/shard_map/ppermute | solution.py:354
  34.6 2.7 %collective-permute-start.4 = (bf16[256,1280]{1,0:T(8,128)(2,1)}, bf16[256,1280]{1,0:T(8,128)(2,1)}, u32[]{:S(2)}, u32[]{:S(2)}) collective-permute-start(bf16[256,1280]{1,0:T(8,128)(2,1)} %bitcast.16.refs_0_), channel_id=1, source_target_pairs={{0,32},{32,0},{1,33},{33,1},{2,34},{34,2},{3,35},{35,3},{4,36},{36... | collective-permute-start | bytes 1966088 | tf_op jit(solution)/shard_map/ppermute | solution.py:354
  37.3 1.8 %fusion.6 = (bf16[128,1280]{1,0:T(8,128)(2,1)S(1)}, bf16[128,1280]{1,0:T(8,128)(2,1)}) fusion(bf16[256,1280]{1,0:T(8,128)(2,1)} %bitcast.16.refs_0_), kind=kLoop, calls=%fused_computation.20 | loop fusion | bytes 1310720 | tf_op jit(solution)/shard_map/slice | solution.py:389
  39.1 3.0 %collective-permute-start.8 = (bf16[128,1280]{1,0:T(8,128)(2,1)S(1)}, bf16[128,1280]{1,0:T(8,128)(2,1)S(1)}, u32[]{:S(2)}, u32[]{:S(2)}) collective-permute-start(bf16[128,1280]{1,0:T(8,128)(2,1)S(1)} %get-tuple-element.96), channel_id=1, source_target_pairs={{0,192},{64,0},{128,64},{192,128},{1,193},{65,1},{129,65},{193,129... | collective-permute-start | bytes 983048 | tf_op jit(solution)/shard_map/ppermute | solution.py:354
  42.1 0.6 collective-permute-start.13
  42.7 4.3 %shard_map.113 = (bf16[128,2560]{1,0:T(8,128)(2,1)}, bf16[128,2560]{1,0:T(8,128)(2,1)}, bf16[4,64,640]{2,1,0:T(8,128)(2,1)}, bf16[4,64,640]{2,1,0:T(8,128)(2,1)}) custom-call(s32[1]{0:T(128)} %bitcast.8.place, bf16[128,2560]{1,0:T(8,128)(2,1)} %get-tuple-element.50.normed, bf16[128,2560]{1,0:T(8,128)(2,1)} %bitcast.31, bf16[128,2560]{1,0:T(8,128)(2,1)} %bitcast.36, ...), custom_call_target="tpu_custom_call" | custom-call | flops 251658240 | bytes 6291456 | tf_op jit(solution)/shard_map/pallas_call | solution.py:393
  47.0 0.9 collective-permute-done.8.refs_4_
  48.0 6.2 %collective-permute-done.7.refs_1_ = bf16[128,1280]{1,0:T(8,128)(2,1)S(1)} collective-permute-done((bf16[128,1280]{1,0:T(8,128)(2,1)}, bf16[128,1280]{1,0:T(8,128)(2,1)S(1)}, u32[]{:S(2)}, u32[]{:S(2)}) %collective-permute-start.7) | collective-permute-done | bytes 327712 | tf_op jit(solution)/shard_map/ppermute | solution.py:354
  54.2 3.2 %collective-permute-start.10 = (bf16[128,1280]{1,0:T(8,128)(2,1)S(1)}, bf16[128,1280]{1,0:T(8,128)(2,1)S(1)}, u32[]{:S(2)}, u32[]{:S(2)}) collective-permute-start(bf16[128,1280]{1,0:T(8,128)(2,1)S(1)} %collective-permute-done.8.refs_4_), channel_id=1, source_target_pairs={{0,192},{64,0},{128,64},{192,128},{1,193},{65,1},{129,65},{193,129... | collective-permute-start | bytes 983048 | tf_op jit(solution)/shard_map/ppermute | solution.py:354
  57.7 3.5 %collective-permute-done.13.refs_2_ = bf16[128,1280]{1,0:T(8,128)(2,1)S(1)} collective-permute-done((bf16[128,1280]{1,0:T(8,128)(2,1)S(1)}, bf16[128,1280]{1,0:T(8,128)(2,1)S(1)}, u32[]{:S(2)}, u32[]{:S(2)}) %collective-permute-start.13) | collective-permute-done | bytes 327712 | tf_op jit(solution)/shard_map/ppermute | solution.py:354
  61.2 7.0 %collective-permute-done.9.refs_2_ = bf16[128,1280]{1,0:T(8,128)(2,1)S(1)} collective-permute-done((bf16[128,1280]{1,0:T(8,128)(2,1)S(1)}, bf16[128,1280]{1,0:T(8,128)(2,1)S(1)}, u32[]{:S(2)}, u32[]{:S(2)}) %collective-permute-start.9) | collective-permute-done | bytes 327712 | tf_op jit(solution)/shard_map/ppermute | solution.py:354
  68.2 0.8 collective-permute-start.11
  69.0 2.7 %collective-permute-start.12 = (bf16[128,1280]{1,0:T(8,128)(2,1)S(1)}, bf16[128,1280]{1,0:T(8,128)(2,1)S(1)}, u32[]{:S(2)}, u32[]{:S(2)}) collective-permute-start(bf16[128,1280]{1,0:T(8,128)(2,1)S(1)} %collective-permute-done.10.refs_3_), channel_id=1, source_target_pairs={{0,32},{32,0},{1,33},{33,1},{2,34},{34,2},{3,35},{35,3},{4,36},{36... | collective-permute-start | bytes 983048 | tf_op jit(solution)/shard_map/ppermute | solution.py:354
  71.7 1.0 collective-permute-done.14.refs_3_
  72.7 5.8 %shard_map.114 = (bf16[8,128,640]{2,1,0:T(8,128)(2,1)}, bf16[256,2560]{1,0:T(8,128)(2,1)}, bf16[256,2560]{1,0:T(8,128)(2,1)}, bf16[256,256]{1,0:T(8,128)(2,1)}, bf16[256,256]{1,0:T(8,128)(2,1)}) custom-call(bf16[256,1280]{1,0:T(8,128)(2,1)} %bitcast.16.refs_0_, bf16[128,1280]{1,0:T(8,128)(2,1)} %copy-done.17, bf16[128,1280]{1,0:T(8,128)(2,1)} %copy-done.18, ...), custom_call_target="tpu_custom_call" | custom-call | flops 1006632960 | bytes 8388608 | tf_op jit(solution)/shard_map/pallas_call | solution.py:409
  78.5 0.8 collective-permute-start.15
  79.4 5.4 %collective-permute-done.12.refs_5_ = bf16[128,1280]{1,0:T(8,128)(2,1)S(1)} collective-permute-done((bf16[128,1280]{1,0:T(8,128)(2,1)S(1)}, bf16[128,1280]{1,0:T(8,128)(2,1)S(1)}, u32[]{:S(2)}, u32[]{:S(2)}) %collective-permute-start.12) | collective-permute-done | bytes 327712 | tf_op jit(solution)/shard_map/ppermute | solution.py:354
  84.8 6.5 %shard_map.115 = (bf16[8,256,640]{2,1,0:T(8,128)(2,1)}, bf16[256,2560]{1,0:T(8,128)(2,1)}, bf16[256,2560]{1,0:T(8,128)(2,1)}, bf16[256,256]{1,0:T(8,128)(2,1)S(1)}, bf16[256,256]{1,0:T(8,128)(2,1)S(1)}) custom-call(s32[8]{0:T(128)S(1)} %stack.35.at_ref, bf16[256,1280]{1,0:T(8,128)(2,1)S(1)} %collective-permute-done.5.refs_0_, ...), custom_call_target="tpu_custom_call" | custom-call | flops 1006632960 | bytes 12582912 | tf_op jit(solution)/shard_map/pallas_call | solution.py:419
  91.3 0.6 copy-done.10
  92.0 3.8 %all-to-all-start.1 = ((bf16[8,256,640]{2,1,0:T(8,128)(2,1)}), bf16[8,256,640]{2,1,0:T(8,128)(2,1)S(1)}, u32[]{:S(2)}, u32[]{:S(2)}) async-start(bf16[8,256,640]{2,1,0:T(8,128)(2,1)} %get-tuple-element.69), calls=%async_computation.1 | async-start | bytes 5242880 | tf_op jit(solution)/shard_map/all_to_all | solution.py:437
  95.8 7.3 %shard_map.116 = bf16[512,2560]{1,0:T(8,128)(2,1)} custom-call(bf16[256,2560]{1,0:T(8,128)(2,1)} %get-tuple-element.70.refs_0_, bf16[256,2560]{1,0:T(8,128)(2,1)} %get-tuple-element.71.refs_1_, bf16[256,256]{1,0:T(8,128)(2,1)} %get-tuple-element.72.refs_2_, bf16[256,256]{1,0:T(8,128)(2,1)} %get-tuple-element.73.refs_3_, ...), custom_call_target="tpu_custom_call" | custom-call | flops 1342177280 | bytes 8388608 | tf_op jit(solution)/shard_map/pallas_call | solution.py:438
  103.2 6.4 %reshape.29 = bf16[1,256,2,2560]{3,2,1,0:T(2,128)(2,1)} reshape(bf16[512,2560]{1,0:T(8,128)(2,1)} %shard_map.116) | data formatting | bytes 5242880 | tf_op jit(solution)/shard_map/reshape | solution.py:447
  109.6 12.9 %all-to-all-done.1.parts = bf16[8,256,640]{2,1,0:T(8,128)(2,1)S(1)} async-done(((bf16[8,256,640]{2,1,0:T(8,128)(2,1)}), bf16[8,256,640]{2,1,0:T(8,128)(2,1)S(1)}, u32[]{:S(2)}, u32[]{:S(2)}) %all-to-all-start.1) | async-done | bytes 2621472 | tf_op jit(solution)/shard_map/all_to_all | solution.py:437
  122.5 1.3 shard_map.117
  123.8 5.7 %all-to-all-start.2 = ((bf16[32,8,640]{2,1,0:T(8,128)(2,1)}), bf16[32,8,640]{2,1,0:T(8,128)(2,1)S(1)}, u32[]{:S(2)}, u32[]{:S(2)}) async-start(bf16[32,8,640]{2,1,0:T(8,128)(2,1)} %bitcast.21), calls=%async_computation.2 | async-start | bytes 655360 | tf_op jit(solution)/shard_map/all_to_all | solution.py:451
  129.6 0.3 collective-permute-start.16
  129.9 2.7 %collective-permute-start.17 = (bf16[64,640]{1,0:T(8,128)(2,1)S(1)}, bf16[64,640]{1,0:T(8,128)(2,1)S(1)}, u32[]{:S(2)}, u32[]{:S(2)}) collective-permute-start(bf16[64,640]{1,0:T(8,128)(2,1)S(1)} %get-tuple-element.87), channel_id=1, source_target_pairs={{0,128},{64,192},{128,0},{192,64},{1,129},{65,193},{129,1},{193,65... | collective-permute-start | bytes 245768 | tf_op jit(solution)/shard_map/ppermute | solution.py:354
  132.6 0.6 collective-permute-start.18
  133.2 4.0 %collective-permute-done.16.below = bf16[64,640]{1,0:T(8,128)(2,1)S(1)} collective-permute-done((bf16[64,640]{1,0:T(8,128)(2,1)S(1)}, bf16[64,640]{1,0:T(8,128)(2,1)S(1)}, u32[]{:S(2)}, u32[]{:S(2)}) %collective-permute-start.16) | collective-permute-done | bytes 81952 | tf_op jit(solution)/shard_map/ppermute | solution.py:354
  137.1 0.6 collective-permute-done.18.above
  137.7 5.3 %all-to-all-done.2 = bf16[32,8,640]{2,1,0:T(8,128)(2,1)S(1)} async-done(((bf16[32,8,640]{2,1,0:T(8,128)(2,1)}), bf16[32,8,640]{2,1,0:T(8,128)(2,1)S(1)}, u32[]{:S(2)}, u32[]{:S(2)}) %all-to-all-start.2) | async-done | bytes 327712 | tf_op jit(solution)/shard_map/all_to_all | solution.py:451
  143.1 0.4 shard_map.119
  143.5 14.9 %all_to_all.20.packs = bf16[8,64,640]{2,1,0:T(8,128)(2,1)S(1)} all-to-all(bf16[8,64,640]{2,1,0:T(8,128)(2,1)S(1)} %shard_map.119), channel_id=1, replica_groups=mesh['ctx_0'=4,'ctx_1'=2,'exp'=32] {'ctx_0','ctx_1'}, dimensions={0} | all-to-all | bytes 1310720 | tf_op jit(solution)/shard_map/all_to_all | solution.py:459
  158.4 1.5 shard_map.120
  (57 shorter events, 1.1 us)
Async XLA Ops:
  0.6 13.2 %copy-start.15 = (bf16[1,256,2,2560]{3,2,1,0:T(2,128)(2,1)S(1)}, bf16[1,256,2,2560]{3,2,1,0:T(2,128)(2,1)}, u32[]{:S(2)}) copy-start(bf16[1,256,2,2560]{3,2,1,0:T(2,128)(2,1)} %param.15) | copy-start | bytes 7864324
  4.2 30.4 %all-to-all-start = ((bf16[32,8,1280]{2,1,0:T(8,128)(2,1)}), bf16[32,8,1280]{2,1,0:T(8,128)(2,1)}, u32[]{:S(2)}, u32[]{:S(2)}) async-start(bf16[32,8,1280]{2,1,0:T(8,128)(2,1)} %bitcast.41), calls=%async_computation | async-start | bytes 1310720 | tf_op jit(solution)/shard_map/all_to_all | solution.py:371
  14.2 1.7 %copy-start = (bf16[1,128,2560]{2,1,0:T(8,128)(2,1)S(1)}, bf16[1,128,2560]{2,1,0:T(8,128)(2,1)}, u32[]{:S(2)}) copy-start(bf16[1,128,2560]{2,1,0:T(8,128)(2,1)} %param.9) | copy-start | bytes 1966084
  14.2 1.7 %copy-start.3 = (bf16[1,128,2560]{2,1,0:T(8,128)(2,1)S(1)}, bf16[1,128,2560]{2,1,0:T(8,128)(2,1)}, u32[]{:S(2)}) copy-start(bf16[1,128,2560]{2,1,0:T(8,128)(2,1)} %param.10) | copy-start | bytes 1966084
  14.2 2.4 %copy-start.4 = (bf16[128,2560]{1,0:T(8,128)(2,1)S(1)}, bf16[128,2560]{1,0:T(8,128)(2,1)}, u32[]{:S(2)}) copy-start(bf16[128,2560]{1,0:T(8,128)(2,1)} %get-tuple-element.50.normed) | copy-start | bytes 1966084
  14.2 2.6 %copy-start.7 = (bf16[1,128,2560]{2,1,0:T(8,128)(2,1)S(1)}, bf16[1,128,2560]{2,1,0:T(8,128)(2,1)}, u32[]{:S(2)}) copy-start(bf16[1,128,2560]{2,1,0:T(8,128)(2,1)} %param.11) | copy-start | bytes 1966084
  17.9 1.1 copy-start.5
  19.0 1.1 copy-start.6
  20.1 22.6 %copy-start.9 = (f32[72,128]{1,0:T(8,128)}, f32[72,128]{1,0:T(8,128)S(1)}, u32[]{:S(2)}) copy-start(f32[72,128]{1,0:T(8,128)S(1)} %get-tuple-element.53.local) | copy-start | bytes 110596
  20.1 4.9 %collective-permute-start.2 = (f32[72,128]{1,0:T(8,128)S(1)}, f32[72,128]{1,0:T(8,128)S(1)}, u32[]{:S(2)}, u32[]{:S(2)}) collective-permute-start(f32[72,128]{1,0:T(8,128)S(1)} %get-tuple-element.53.local), channel_id=1, source_target_pairs={{0,192},{64,0},{128,64},{192,128},{1,193},{65,1},{129,65},{193,129... | collective-permute-start | bytes 110600 | tf_op jit(solution)/shard_map/ppermute | solution.py:354
  23.1 5.5 %collective-permute-start.1 = (f32[72,128]{1,0:T(8,128)S(1)}, f32[72,128]{1,0:T(8,128)S(1)}, u32[]{:S(2)}, u32[]{:S(2)}) collective-permute-start(f32[72,128]{1,0:T(8,128)S(1)} %get-tuple-element.53.local), channel_id=1, source_target_pairs={{0,128},{64,192},{128,0},{192,64},{1,129},{65,193},{129,1},{193,65... | collective-permute-start | bytes 110600 | tf_op jit(solution)/shard_map/ppermute | solution.py:354
  23.7 5.2 %collective-permute-start = (f32[72,128]{1,0:T(8,128)S(1)}, f32[72,128]{1,0:T(8,128)S(1)}, u32[]{:S(2)}, u32[]{:S(2)}) collective-permute-start(f32[72,128]{1,0:T(8,128)S(1)} %get-tuple-element.53.local), channel_id=1, source_target_pairs={{0,64},{64,128},{128,192},{192,0},{1,65},{65,129},{129,193},{193,1... | collective-permute-start | bytes 110600 | tf_op jit(solution)/shard_map/ppermute | solution.py:354
  29.0 13.7 %copy-start.19 = (f32[72,128]{1,0:T(8,128)}, f32[72,128]{1,0:T(8,128)S(1)}, u32[]{:S(2)}) copy-start(f32[72,128]{1,0:T(8,128)S(1)} %pad_maximum_fusion.near) | copy-start | bytes 110596
  29.0 5.6 %collective-permute-start.3 = (f32[72,128]{1,0:T(8,128)S(1)}, f32[72,128]{1,0:T(8,128)S(1)}, u32[]{:S(2)}, u32[]{:S(2)}) collective-permute-start(f32[72,128]{1,0:T(8,128)S(1)} %pad_maximum_fusion.near), channel_id=1, source_target_pairs={{0,32},{32,0},{1,33},{33,1},{2,34},{34,2},{3,35},{35,3},{4,36},{36... | collective-permute-start | bytes 110600 | tf_op jit(solution)/shard_map/ppermute | solution.py:354
  34.6 8.1 %copy-start.20 = (f32[72,128]{1,0:T(8,128)}, f32[72,128]{1,0:T(8,128)S(1)}, u32[]{:S(2)}) copy-start(f32[72,128]{1,0:T(8,128)S(1)} %collective-permute-done.3.far) | copy-start | bytes 110596
  34.6 22.9 %collective-permute-start.4 = (bf16[256,1280]{1,0:T(8,128)(2,1)}, bf16[256,1280]{1,0:T(8,128)(2,1)}, u32[]{:S(2)}, u32[]{:S(2)}) collective-permute-start(bf16[256,1280]{1,0:T(8,128)(2,1)} %bitcast.16.refs_0_), channel_id=1, source_target_pairs={{0,32},{32,0},{1,33},{33,1},{2,34},{34,2},{3,35},{35,3},{4,36},{36... | collective-permute-start | bytes 1966088 | tf_op jit(solution)/shard_map/ppermute | solution.py:354
  39.1 8.8 %collective-permute-start.8 = (bf16[128,1280]{1,0:T(8,128)(2,1)S(1)}, bf16[128,1280]{1,0:T(8,128)(2,1)S(1)}, u32[]{:S(2)}, u32[]{:S(2)}) collective-permute-start(bf16[128,1280]{1,0:T(8,128)(2,1)S(1)} %get-tuple-element.96), channel_id=1, source_target_pairs={{0,192},{64,0},{128,64},{192,128},{1,193},{65,1},{129,65},{193,129... | collective-permute-start | bytes 983048 | tf_op jit(solution)/shard_map/ppermute | solution.py:354
  42.1 12.1 %collective-permute-start.7 = (bf16[128,1280]{1,0:T(8,128)(2,1)}, bf16[128,1280]{1,0:T(8,128)(2,1)S(1)}, u32[]{:S(2)}, u32[]{:S(2)}) collective-permute-start(bf16[128,1280]{1,0:T(8,128)(2,1)} %get-tuple-element.97), channel_id=1, source_target_pairs={{0,64},{64,128},{128,192},{192,0},{1,65},{65,129},{129,193},{193,1... | collective-permute-start | bytes 983048 | tf_op jit(solution)/shard_map/ppermute | solution.py:354
  42.1 19.1 %collective-permute-start.13 = (bf16[128,1280]{1,0:T(8,128)(2,1)S(1)}, bf16[128,1280]{1,0:T(8,128)(2,1)S(1)}, u32[]{:S(2)}, u32[]{:S(2)}) collective-permute-start(bf16[128,1280]{1,0:T(8,128)(2,1)S(1)} %get-tuple-element.96), channel_id=1, source_target_pairs={{0,64},{64,128},{128,192},{192,0},{1,65},{65,129},{129,193},{193,1... | collective-permute-start | bytes 983048 | tf_op jit(solution)/shard_map/ppermute | solution.py:354
  48.0 24.7 %copy-start.16 = (bf16[128,1280]{1,0:T(8,128)(2,1)}, bf16[128,1280]{1,0:T(8,128)(2,1)S(1)}, u32[]{:S(2)}) copy-start(bf16[128,1280]{1,0:T(8,128)(2,1)S(1)} %collective-permute-done.8.refs_4_) | copy-start | bytes 983044
  54.2 18.5 %copy-start.17 = (bf16[128,1280]{1,0:T(8,128)(2,1)}, bf16[128,1280]{1,0:T(8,128)(2,1)S(1)}, u32[]{:S(2)}) copy-start(bf16[128,1280]{1,0:T(8,128)(2,1)S(1)} %collective-permute-done.7.refs_1_) | copy-start | bytes 983044
  54.2 14.0 %collective-permute-start.9 = (bf16[128,1280]{1,0:T(8,128)(2,1)S(1)}, bf16[128,1280]{1,0:T(8,128)(2,1)S(1)}, u32[]{:S(2)}, u32[]{:S(2)}) collective-permute-start(bf16[128,1280]{1,0:T(8,128)(2,1)S(1)} %collective-permute-done.7.refs_1_), channel_id=1, source_target_pairs={{0,64},{64,128},{128,192},{192,0},{1,65},{65,129},{129,193},{193,1... | collective-permute-start | bytes 983048 | tf_op jit(solution)/shard_map/ppermute | solution.py:354
  54.2 14.8 %collective-permute-start.10 = (bf16[128,1280]{1,0:T(8,128)(2,1)S(1)}, bf16[128,1280]{1,0:T(8,128)(2,1)S(1)}, u32[]{:S(2)}, u32[]{:S(2)}) collective-permute-start(bf16[128,1280]{1,0:T(8,128)(2,1)S(1)} %collective-permute-done.8.refs_4_), channel_id=1, source_target_pairs={{0,192},{64,0},{128,64},{192,128},{1,193},{65,1},{129,65},{193,129... | collective-permute-start | bytes 983048 | tf_op jit(solution)/shard_map/ppermute | solution.py:354
  57.4 15.3 %collective-permute-start.14 = (bf16[128,1280]{1,0:T(8,128)(2,1)}, bf16[128,1280]{1,0:T(8,128)(2,1)}, u32[]{:S(2)}, u32[]{:S(2)}) collective-permute-start(bf16[128,1280]{1,0:T(8,128)(2,1)} %get-tuple-element.97), channel_id=1, source_target_pairs={{0,192},{64,0},{128,64},{192,128},{1,193},{65,1},{129,65},{193,129... | collective-permute-start | bytes 983048 | tf_op jit(solution)/shard_map/ppermute | solution.py:354
  57.4 27.4 %collective-permute-start.6 = (bf16[256,1280]{1,0:T(8,128)(2,1)}, bf16[256,1280]{1,0:T(8,128)(2,1)S(1)}, u32[]{:S(2)}, u32[]{:S(2)}) collective-permute-start(bf16[256,1280]{1,0:T(8,128)(2,1)} %collective-permute-done.4.refs_5_), channel_id=1, source_target_pairs={{0,192},{64,0},{128,64},{192,128},{1,193},{65,1},{129,65},{193,129... | collective-permute-start | bytes 1966088 | tf_op jit(solution)/shard_map/ppermute | solution.py:354
  61.2 11.5 %copy-start.18 = (bf16[128,1280]{1,0:T(8,128)(2,1)}, bf16[128,1280]{1,0:T(8,128)(2,1)S(1)}, u32[]{:S(2)}) copy-start(bf16[128,1280]{1,0:T(8,128)(2,1)S(1)} %collective-permute-done.13.refs_2_) | copy-start | bytes 983044
  61.2 23.6 %collective-permute-start.5 = (bf16[256,1280]{1,0:T(8,128)(2,1)}, bf16[256,1280]{1,0:T(8,128)(2,1)S(1)}, u32[]{:S(2)}, u32[]{:S(2)}) collective-permute-start(bf16[256,1280]{1,0:T(8,128)(2,1)} %collective-permute-done.4.refs_5_), channel_id=1, source_target_pairs={{0,64},{64,128},{128,192},{192,0},{1,65},{65,129},{129,193},{193,1... | collective-permute-start | bytes 1966088 | tf_op jit(solution)/shard_map/ppermute | solution.py:354
  68.2 11.2 %collective-permute-start.11 = (bf16[128,1280]{1,0:T(8,128)(2,1)S(1)}, bf16[128,1280]{1,0:T(8,128)(2,1)S(1)}, u32[]{:S(2)}, u32[]{:S(2)}) collective-permute-start(bf16[128,1280]{1,0:T(8,128)(2,1)S(1)} %collective-permute-done.9.refs_2_), channel_id=1, source_target_pairs={{0,32},{32,0},{1,33},{33,1},{2,34},{34,2},{3,35},{35,3},{4,36},{36... | collective-permute-start | bytes 983048 | tf_op jit(solution)/shard_map/ppermute | solution.py:354
  69.0 15.8 %collective-permute-start.12 = (bf16[128,1280]{1,0:T(8,128)(2,1)S(1)}, bf16[128,1280]{1,0:T(8,128)(2,1)S(1)}, u32[]{:S(2)}, u32[]{:S(2)}) collective-permute-start(bf16[128,1280]{1,0:T(8,128)(2,1)S(1)} %collective-permute-done.10.refs_3_), channel_id=1, source_target_pairs={{0,32},{32,0},{1,33},{33,1},{2,34},{34,2},{3,35},{35,3},{4,36},{36... | collective-permute-start | bytes 983048 | tf_op jit(solution)/shard_map/ppermute | solution.py:354
  78.5 12.8 %collective-permute-start.15 = (bf16[4,64,640]{2,1,0:T(8,128)(2,1)}, bf16[4,64,640]{2,1,0:T(8,128)(2,1)S(1)}, u32[]{:S(2)}, u32[]{:S(2)}) collective-permute-start(bf16[4,64,640]{2,1,0:T(8,128)(2,1)} %get-tuple-element.68), channel_id=1, source_target_pairs={{0,32},{32,0},{1,33},{33,1},{2,34},{34,2},{3,35},{35,3},{4,36},{36... | collective-permute-start | bytes 983048 | tf_op jit(solution)/shard_map/ppermute | solution.py:354
  91.3 0.7 copy-start.10
  91.3 0.7 copy-start.11
  92.0 30.5 %all-to-all-start.1 = ((bf16[8,256,640]{2,1,0:T(8,128)(2,1)}), bf16[8,256,640]{2,1,0:T(8,128)(2,1)S(1)}, u32[]{:S(2)}, u32[]{:S(2)}) async-start(bf16[8,256,640]{2,1,0:T(8,128)(2,1)} %get-tuple-element.69), calls=%async_computation.1 | async-start | bytes 5242880 | tf_op jit(solution)/shard_map/all_to_all | solution.py:437
  109.6 19.9 %copy-start.8 = (bf16[4,64,640]{2,1,0:T(8,128)(2,1)S(1)}, bf16[4,64,640]{2,1,0:T(8,128)(2,1)}, u32[]{:S(2)}) copy-start(bf16[4,64,640]{2,1,0:T(8,128)(2,1)} %get-tuple-element.83.own) | copy-start | bytes 983044
  123.8 19.2 %copy-start.12 = (bf16[256,128]{1,0:T(8,128)(2,1)S(1)}, bf16[256,128]{1,0:T(8,128)(2,1)}, u32[]{:S(2)}) copy-start(bf16[256,128]{1,0:T(8,128)(2,1)} %get-tuple-element.81.even) | copy-start | bytes 196612
  123.8 19.2 %copy-start.13 = (bf16[256,128]{1,0:T(8,128)(2,1)S(1)}, bf16[256,128]{1,0:T(8,128)(2,1)}, u32[]{:S(2)}) copy-start(bf16[256,128]{1,0:T(8,128)(2,1)} %get-tuple-element.82.odd) | copy-start | bytes 196612
  123.8 19.2 %all-to-all-start.2 = ((bf16[32,8,640]{2,1,0:T(8,128)(2,1)}), bf16[32,8,640]{2,1,0:T(8,128)(2,1)S(1)}, u32[]{:S(2)}, u32[]{:S(2)}) async-start(bf16[32,8,640]{2,1,0:T(8,128)(2,1)} %bitcast.21), calls=%async_computation.2 | async-start | bytes 655360 | tf_op jit(solution)/shard_map/all_to_all | solution.py:451
  129.6 7.5 %collective-permute-start.16 = (bf16[64,640]{1,0:T(8,128)(2,1)S(1)}, bf16[64,640]{1,0:T(8,128)(2,1)S(1)}, u32[]{:S(2)}, u32[]{:S(2)}) collective-permute-start(bf16[64,640]{1,0:T(8,128)(2,1)S(1)} %get-tuple-element.86), channel_id=1, source_target_pairs={{0,64},{64,128},{128,192},{192,0},{1,65},{65,129},{129,193},{193,1... | collective-permute-start | bytes 245768 | tf_op jit(solution)/shard_map/ppermute | solution.py:354
  129.9 7.2 %collective-permute-start.17 = (bf16[64,640]{1,0:T(8,128)(2,1)S(1)}, bf16[64,640]{1,0:T(8,128)(2,1)S(1)}, u32[]{:S(2)}, u32[]{:S(2)}) collective-permute-start(bf16[64,640]{1,0:T(8,128)(2,1)S(1)} %get-tuple-element.87), channel_id=1, source_target_pairs={{0,128},{64,192},{128,0},{192,64},{1,129},{65,193},{129,1},{193,65... | collective-permute-start | bytes 245768 | tf_op jit(solution)/shard_map/ppermute | solution.py:354
  132.6 5.1 %collective-permute-start.18 = (bf16[64,640]{1,0:T(8,128)(2,1)S(1)}, bf16[64,640]{1,0:T(8,128)(2,1)S(1)}, u32[]{:S(2)}, u32[]{:S(2)}) collective-permute-start(bf16[64,640]{1,0:T(8,128)(2,1)S(1)} %get-tuple-element.88), channel_id=1, source_target_pairs={{0,192},{64,0},{128,64},{192,128},{1,193},{65,1},{129,65},{193,129... | collective-permute-start | bytes 245768 | tf_op jit(solution)/shard_map/ppermute | solution.py:354
  143.0 15.3 %copy-start.1 = (bf16[1,128,2560]{2,1,0:T(8,128)(2,1)S(1)}, bf16[1,128,2560]{2,1,0:T(8,128)(2,1)}, u32[]{:S(2)}) copy-start(bf16[1,128,2560]{2,1,0:T(8,128)(2,1)} %param.9) | copy-start | bytes 1966084
  143.0 15.3 %copy-start.2 = (bf16[1,128,2560]{2,1,0:T(8,128)(2,1)S(1)}, bf16[1,128,2560]{2,1,0:T(8,128)(2,1)}, u32[]{:S(2)}) copy-start(bf16[1,128,2560]{2,1,0:T(8,128)(2,1)} %param.8) | copy-start | bytes 1966084
  143.1 15.3 %copy-start.14 = (f32[2560]{0:T(1024)S(1)}, f32[2560]{0:T(1024)}, u32[]{:S(2)}) copy-start(f32[2560]{0:T(1024)} %gain.3) | copy-start | bytes 30724
